TPU v7x, 32 devices: a whole 2x2x4 slice. The times are simulated.
32 devices in a mesh: section: 2 (over core), seq: 4 (over z), wshard: 4 (over y, x).
Axes of the slice: x: 2, y: 2, z: 4, core: 2. Of those that a mesh axis runs over, the one named last changes fastest.
Arguments:
- ends_in: bfloat16 [2, 2, 4, 1024, 1024], P('section', None, 'wshard', 'seq'), may hold values from -6 to 6
- seq_lengths: int32 [2, 4, 4], P(None, 'wshard'), may hold values from 1 to 512, 1024 in all within a row
- deal_order: int32 [2, 4, 1024], P(None, 'wshard'), may hold values from 0 to 1023, each once within a row
- norm_w: float32 [2, 1024], P('section'), may hold values from 0.1 to 1.9
- in_w: bfloat16 [2, 1024, 4384], P('section', 'wshard'), may hold values from -0.1875 to 0.1875
- conv_w: float32 [2, 4, 2304], P('section'), may hold values from -3 to 3
- conv_b: float32 [2, 2304], P('section'), may hold values from -3 to 3
- dt_bias: float32 [2, 32], P('section'), may hold values from -5 to -3
- a_log: float32 [2, 32], P('section'), may hold values from -6 to 2
- d_skip: float32 [2, 32], P('section'), may hold values from 0.1 to 1.9
- gnorm_w: float32 [2, 2048], P('section'), may hold values from 0.1 to 1.9
- out_w: bfloat16 [2, 2048, 1024], P('section', 'wshard'), may hold values from -0.125 to 0.125
Outputs:
- ends_out: float32 [2, 2, 4, 1024, 1024], P('section', None, 'wshard', 'seq')
- g_norm_w: float32 [2, 1024], P('section')
- g_in_w: float32 [2, 1024, 4384], P('section', ('seq', 'wshard'))
- g_conv_w: float32 [2, 4, 2304], P('section')
- g_conv_b: float32 [2, 2304], P('section')
- g_dt_bias: float32 [2, 32], P('section')
- g_a_log: float32 [2, 32], P('section')
- g_d_skip: float32 [2, 32], P('section')
- g_gnorm_w: float32 [2, 2048], P('section')
- g_out_w: float32 [2, 2048, 1024], P('section', ('seq', 'wshard'))
Inputs may be any that keep to these rules, and one draw needn't show every extreme that they name: `seq_lengths`: the 4 lengths of a micro-batch and group add up to 1024, and the largest is exactly 512. `deal_order`: each row of a micro-batch and group is a permutation of the positions 0 to 1023.
All inputs are finite; a program needn't handle non-finite values.
Results may differ from a plain program's by a relative error of at most 0.015.
The roundings to bfloat16 on the way count: a program that leaves them out, or rounds other values in their place, can miss the bound.
Values may be sent and summed in bfloat16 or wider, within the bound.
No kernel may reach another device: no remote copies, remote signals or barrier semaphores. Data moves between devices by JAX's collectives and lax.ppermute only.
A program may use at most 320 MiB of HBM per device.

v0:
```python
import jax
import jax.numpy as jnp
from jax import lax
from jax.sharding import PartitionSpec as P

D = 1024
HEADDIM = 64
STATE = 128
KCONV = 4
BLOCK = 256
INNER = 2048
HEADS = 32
PROJ = 4384


EPS = 1e-05
HIGH = lax.Precision.HIGHEST


def passed_along(value, axis, steps):
    count = lax.axis_size(axis)
    leading, last = (max(0, -steps), min(count, count - steps))
    return lax.ppermute(value, axis, [(source, source + steps) for source in range(leading, last)])


def prenorm(tokens, gain):
    return (
        tokens * lax.rsqrt(jnp.mean(tokens * tokens, axis=-1, keepdims=True) + EPS) * gain[None, :]
    )


def gated(values, gate, gain):
    mixed = values * jax.nn.silu(gate)
    return mixed * lax.rsqrt(jnp.mean(mixed * mixed, axis=-1, keepdims=True) + EPS) * gain[None, :]


def segments(lengths, total):
    ends = jnp.cumsum(lengths)
    place = lax.broadcasted_iota(jnp.int32, (total,), 0)
    passed = place[:, None] >= ends[None, :]
    label = jnp.sum(passed.astype(jnp.int32), axis=1)
    begin = jnp.max(jnp.where(passed, ends[None, :], 0), axis=1)
    return (label, place - begin)


def invert(order):
    total = order.shape[0]
    return (
        jnp.zeros((total,), jnp.int32).at[order].set(lax.broadcasted_iota(jnp.int32, (total,), 0))
    )


def convolve(values, kernel, shift, offset):
    count = values.shape[0]
    taps = kernel.shape[0]
    total = jnp.zeros(values.shape, jnp.float32) + shift[None, :]
    for index in range(taps):
        delay = taps - 1 - index
        moved = jnp.pad(values, ((delay, 0), (0, 0)))[:count]
        inside = (offset >= delay).astype(jnp.float32)
        total = total + kernel[index][None, :] * moved * inside[:, None]
    return jax.nn.silu(total)


def decays(raw, bias, log_rate, label, before):
    rate = jax.nn.softplus(raw + bias[None, :])
    level = jnp.cumsum(rate * (-jnp.exp(log_rate))[None, :], axis=0)
    length = raw.shape[0]
    rows = lax.broadcasted_iota(jnp.int32, (length, length), 0)
    column = lax.broadcasted_iota(jnp.int32, (length, length), 1)
    inside = (label[:, None] == label[None, :]) & (column <= rows)
    gap = level.T[:, :, None] - level.T[:, None, :]
    weight = (
        jnp.exp(jnp.where(inside[None], gap, 0.0))
        * inside[None].astype(jnp.float32)
        * rate.T[:, None, :]
    )
    final = label[length - 1]
    tail = (
        jnp.exp(level[length - 1][None, :] - level)
        * (label == final).astype(jnp.float32)[:, None]
        * rate
    )
    head = jnp.exp(level) * (label == before).astype(jnp.float32)[:, None]
    carry = jnp.exp(level[length - 1]) * (final == before).astype(jnp.float32)
    return (weight, tail, head, carry)


def on_device(
    ends_in,
    seq_lengths,
    deal_order,
    norm_w,
    in_w,
    conv_w,
    conv_b,
    dt_bias,
    a_log,
    d_skip,
    gnorm_w,
    out_w,
):
    section = lax.axis_index("section")
    shards = lax.axis_size("seq")
    shard = lax.axis_index("seq")
    heads_here = HEADS // shards
    width = heads_here * HEADDIM
    batches = ends_in.shape[1]
    tok_rows = ends_in.shape[3]
    group = tok_rows * shards
    count = group // BLOCK
    in_full, out_full = (
        lax.all_gather(in_w[0], "wshard", axis=0, tiled=True),
        lax.all_gather(out_w[0], "wshard", axis=0, tiled=True),
    )
    norm_gain = norm_w[0]
    gated_gain = gnorm_w[0]
    kernel = conv_w[0]
    conv_bias = conv_b[0]
    first_channel = shard * width
    first_head = shard * heads_here
    kernel_input = lax.dynamic_slice_in_dim(kernel, first_channel, width, 1)
    shift_input = lax.dynamic_slice_in_dim(conv_bias, first_channel, width, 0)
    kernel_pair = kernel[:, INNER:]
    shift_pair = conv_bias[INNER:]
    rate_bias = lax.dynamic_slice_in_dim(dt_bias[0], first_head, heads_here, 0)
    log_rate = lax.dynamic_slice_in_dim(a_log[0], first_head, heads_here, 0)
    skip = lax.dynamic_slice_in_dim(d_skip[0], first_head, heads_here, 0)

    def previous_labels(label):
        label_parts = label.reshape(count, BLOCK)
        before = jnp.concatenate([jnp.full((1,), -1, jnp.int32), label_parts[:-1, BLOCK - 1]])
        return (label_parts, before)

    def head_forward(input_ordered, pair_ordered, raw_ordered, label, offset):
        input_conv = convolve(
            input_ordered.astype(jnp.float32), kernel_input, shift_input, offset
        ).astype(jnp.bfloat16)
        pair_conv = convolve(
            pair_ordered.astype(jnp.float32), kernel_pair, shift_pair, offset
        ).astype(jnp.bfloat16)
        label_parts, before = previous_labels(label)

        def advance(state, piece):
            inputs, pair, raw, label_part, prior_label = piece
            weight, tail, head, carry = decays(
                raw.astype(jnp.float32), rate_bias, log_rate, label_part, prior_label
            )
            inputs_three = inputs.reshape(BLOCK, heads_here, HEADDIM)
            write_part = pair[:, :STATE]
            read_part = pair[:, STATE:]
            gram = jnp.dot(read_part, write_part.T, preferred_element_type=jnp.float32)
            mixing = (gram[None] * weight).astype(jnp.bfloat16)
            output = jnp.einsum(
                "hij,jhp->ihp", mixing, inputs_three, preferred_element_type=jnp.float32
            )
            inputs_float = inputs_three.astype(jnp.float32)
            output = output + head[:, :, None] * jnp.einsum(
                "in,hnp->ihp", read_part.astype(jnp.float32), state, precision=HIGH
            )
            output = output + skip[None, :, None] * inputs_float
            fresh = carry[:, None, None] * state + jnp.einsum(
                "jn,jhp->hnp",
                write_part.astype(jnp.float32),
                tail[:, :, None] * inputs_float,
                precision=HIGH,
            )
            return (fresh, (output.reshape(BLOCK, width), state))

        start = jnp.zeros((heads_here, STATE, HEADDIM), jnp.float32)
        pieces = (
            input_conv.reshape(count, BLOCK, width),
            pair_conv.reshape(count, BLOCK, 2 * STATE),
            raw_ordered.reshape(count, BLOCK, heads_here),
            label_parts,
            before,
        )
        _, (outputs, states) = lax.scan(advance, start, pieces)
        return (outputs.reshape(group, width), states)

    def head_backward(
        input_ordered, pair_ordered, raw_ordered, label, offset, states, grad_ordered
    ):
        input_conv, input_pull = jax.vjp(
            lambda values, taps, shift: convolve(values, taps, shift, offset),
            input_ordered.astype(jnp.float32),
            kernel_input,
            shift_input,
        )
        pair_conv, pair_pull = jax.vjp(
            lambda values, taps, shift: convolve(values, taps, shift, offset),
            pair_ordered.astype(jnp.float32),
            kernel_pair,
            shift_pair,
        )
        label_parts, before = previous_labels(label)

        def retreat(grad_state, piece):
            inputs, pair, raw, label_part, prior_label, state, grad_part = piece

            def local(raw_values, bias_values, log_values):
                return decays(raw_values, bias_values, log_values, label_part, prior_label)

            (weight, tail, head, carry), decay_pull = jax.vjp(
                local, raw.astype(jnp.float32), rate_bias, log_rate
            )
            inputs_three = inputs.reshape(BLOCK, heads_here, HEADDIM)
            grad_three = grad_part.reshape(BLOCK, heads_here, HEADDIM)
            write_part = pair[:, :STATE]
            read_part = pair[:, STATE:]
            write_float = write_part.astype(jnp.float32)
            read_float = read_part.astype(jnp.float32)
            inputs_float = inputs_three.astype(jnp.float32)
            grad_float = grad_three.astype(jnp.float32)
            gram = jnp.dot(read_part, write_part.T, preferred_element_type=jnp.float32)
            mixing = (gram[None] * weight).astype(jnp.bfloat16)
            grad_mix = jnp.einsum(
                "ihp,jhp->hij", grad_three, inputs_three, preferred_element_type=jnp.float32
            )
            grad_weight = grad_mix * gram[None]
            grad_gram = jnp.sum(grad_mix * weight, axis=0)
            from_state = jnp.einsum("in,hnp->ihp", read_float, state, precision=HIGH)
            grad_head = jnp.sum(grad_float * from_state, axis=2)
            scaled = grad_float * head[:, :, None]
            grad_read = jnp.dot(grad_gram, write_float, precision=HIGH) + jnp.einsum(
                "ihp,hnp->in", scaled, state, precision=HIGH
            )
            through = jnp.einsum("jn,hnp->jhp", write_float, grad_state, precision=HIGH)
            grad_write = jnp.dot(grad_gram.T, read_float, precision=HIGH) + jnp.einsum(
                "jhp,hnp->jn", tail[:, :, None] * inputs_float, grad_state, precision=HIGH
            )
            grad_tail = jnp.sum(inputs_float * through, axis=2)
            grad_inputs = jnp.einsum(
                "hij,ihp->jhp", mixing, grad_three, preferred_element_type=jnp.float32
            )
            grad_inputs = (
                grad_inputs + skip[None, :, None] * grad_float + tail[:, :, None] * through
            )
            grad_skip = jnp.sum(grad_float * inputs_float, axis=(0, 2))
            grad_carry = jnp.sum(state * grad_state, axis=(1, 2))
            prior = carry[:, None, None] * grad_state + jnp.einsum(
                "in,ihp->hnp", read_float, scaled, precision=HIGH
            )
            grad_raw, grad_bias, grad_log = decay_pull(
                (grad_weight, grad_tail, grad_head, grad_carry)
            )
            grad_pair = jnp.concatenate([grad_write, grad_read], axis=1)
            return (
                prior,
                (
                    grad_inputs.reshape(BLOCK, width),
                    grad_pair,
                    grad_raw,
                    grad_bias,
                    grad_log,
                    grad_skip,
                ),
            )

        start = jnp.zeros((heads_here, STATE, HEADDIM), jnp.float32)
        pieces = (
            input_conv.astype(jnp.bfloat16).reshape(count, BLOCK, width),
            pair_conv.astype(jnp.bfloat16).reshape(count, BLOCK, 2 * STATE),
            raw_ordered.reshape(count, BLOCK, heads_here),
            label_parts,
            before,
            states,
            grad_ordered.reshape(count, BLOCK, width),
        )
        _, (grad_inputs, grad_pair, grad_raw, grad_bias, grad_log, grad_skip) = lax.scan(
            retreat, start, pieces, reverse=True
        )
        grad_input_rows, grad_kernel_input, grad_shift_input = input_pull(
            grad_inputs.reshape(group, width)
        )
        grad_pair_rows, grad_kernel_pair, grad_shift_pair = pair_pull(
            grad_pair.reshape(group, 2 * STATE)
        )
        smalls = (
            grad_kernel_input,
            grad_shift_input,
            grad_kernel_pair,
            grad_shift_pair,
            jnp.sum(grad_bias, axis=0),
            jnp.sum(grad_log, axis=0),
            jnp.sum(grad_skip, axis=0),
        )
        return (grad_input_rows, grad_pair_rows, grad_raw.reshape(group, heads_here), smalls)

    def layer_backward(saved, grad_rows, order):
        (
            tokens,
            normed,
            gate,
            mixed_rows,
            input_rows,
            pair_rows,
            raw_rows,
            kept_heads,
            states,
            inverse,
            label,
            offset,
        ) = saved
        grad_low = grad_rows.astype(jnp.bfloat16)
        normed_out, gate_pull = jax.vjp(gated, mixed_rows.astype(jnp.float32), gate, gated_gain)
        out_grad = jnp.dot(
            normed_out.astype(jnp.bfloat16).T, grad_low, preferred_element_type=jnp.float32
        )
        grad_normed_out = jnp.dot(grad_low, out_full.T, preferred_element_type=jnp.float32)
        grad_mixed, grad_gate, grad_gated_gain = gate_pull(grad_normed_out)
        grad_dealt = lax.all_to_all(
            grad_mixed.astype(jnp.bfloat16).reshape(tok_rows, shards, width),
            "seq",
            split_axis=1,
            concat_axis=0,
            tiled=True,
        ).reshape(group, width)
        input_ordered, pair_ordered, raw_ordered = kept_heads
        grad_input, grad_pair, grad_raw, smalls = head_backward(
            input_ordered, pair_ordered, raw_ordered, label, offset, states, grad_dealt[inverse]
        )
        input_back, raw_back = (
            lax.all_to_all(
                grad_input[order].astype(jnp.bfloat16).reshape(group, 1, width),
                "seq",
                split_axis=0,
                concat_axis=1,
                tiled=True,
            ),
            lax.all_to_all(
                grad_raw[order].astype(jnp.bfloat16).reshape(group, 1, heads_here),
                "seq",
                split_axis=0,
                concat_axis=1,
                tiled=True,
            ),
        )
        pair_back = lax.psum_scatter(
            grad_pair[order].astype(jnp.bfloat16), "seq", scatter_dimension=0, tiled=True
        )
        grad_proj = jnp.concatenate(
            [
                grad_gate.astype(jnp.bfloat16),
                input_back.reshape(tok_rows, INNER),
                pair_back,
                raw_back.reshape(tok_rows, HEADS),
            ],
            axis=1,
        )
        in_grad = jnp.dot(normed.T, grad_proj, preferred_element_type=jnp.float32)
        grad_normed = jnp.dot(grad_proj, in_full.T, preferred_element_type=jnp.float32)
        _, norm_pull = jax.vjp(prenorm, tokens, norm_gain)
        grad_tokens, grad_norm_gain = norm_pull(grad_normed)
        return (
            grad_rows + grad_tokens,
            in_grad,
            out_grad,
            (grad_norm_gain, grad_gated_gain) + smalls,
        )

    kept = []
    results = []
    sent = None
    for slot in range(batches + 1):
        if slot == 0:
            arrived = jnp.zeros((tok_rows, D), jnp.float32)
        else:
            arrived = passed_along(sent, "section", 1).astype(jnp.float32)
        local = ends_in[0, min(slot, batches - 1), 0].astype(jnp.float32)
        tokens = jnp.where(section == 0, local, arrived)
        batch = jnp.clip(slot - section, 0, batches - 1)
        order = lax.dynamic_index_in_dim(deal_order[:, 0], batch, 0, keepdims=False)
        lengths = lax.dynamic_index_in_dim(seq_lengths[:, 0], batch, 0, keepdims=False)
        layer_normed = prenorm(tokens, norm_gain).astype(jnp.bfloat16)
        projected = jnp.dot(layer_normed, in_full, preferred_element_type=jnp.float32)
        layer_gate = projected[:, :INNER]
        layer_input_rows = projected[:, INNER : 2 * INNER].astype(jnp.bfloat16)
        layer_pair_rows = projected[:, 2 * INNER : 2 * INNER + 2 * STATE].astype(jnp.bfloat16)
        layer_raw_rows = projected[:, 2 * INNER + 2 * STATE :].astype(jnp.bfloat16)
        input_dealt = lax.all_to_all(
            layer_input_rows.reshape(tok_rows, shards, width),
            "seq",
            split_axis=1,
            concat_axis=0,
            tiled=True,
        )
        raw_dealt = lax.all_to_all(
            layer_raw_rows.reshape(tok_rows, shards, heads_here),
            "seq",
            split_axis=1,
            concat_axis=0,
            tiled=True,
        )
        pair_dealt = lax.all_gather(layer_pair_rows, "seq", axis=0, tiled=True)
        layer_input_dealt = input_dealt.reshape(group, width)
        layer_raw_dealt = raw_dealt.reshape(group, heads_here)
        layer_inverse = invert(order)
        layer_label, layer_offset = segments(lengths, group)
        layer_input_ordered = layer_input_dealt[layer_inverse]
        layer_pair_ordered = pair_dealt[layer_inverse]
        layer_raw_ordered = layer_raw_dealt[layer_inverse]
        mixed_ordered, layer_states = head_forward(
            layer_input_ordered, layer_pair_ordered, layer_raw_ordered, layer_label, layer_offset
        )
        mixed_dealt = mixed_ordered[order].astype(jnp.bfloat16)
        layer_mixed_rows = lax.all_to_all(
            mixed_dealt.reshape(group, 1, width), "seq", split_axis=0, concat_axis=1, tiled=True
        ).reshape(tok_rows, INNER)
        layer_normed_out = gated(
            layer_mixed_rows.astype(jnp.float32), layer_gate, gated_gain
        ).astype(jnp.bfloat16)
        result = tokens + jnp.dot(layer_normed_out, out_full, preferred_element_type=jnp.float32)
        layer_saved = (
            tokens,
            layer_normed,
            layer_gate,
            layer_mixed_rows,
            layer_input_rows,
            layer_pair_rows,
            layer_raw_rows,
            (layer_input_ordered, layer_pair_ordered, layer_raw_ordered),
            layer_states,
            layer_inverse,
            layer_label,
            layer_offset,
        )
        result, saved = (result, layer_saved)
        kept.append((saved, order))
        results.append(result)
        sent = result.astype(jnp.bfloat16)
    in_total = jnp.zeros((D, PROJ), jnp.float32)
    out_total = jnp.zeros((INNER, D), jnp.float32)
    small_totals = (
        jnp.zeros((D,), jnp.float32),
        jnp.zeros((INNER,), jnp.float32),
        jnp.zeros((KCONV, width), jnp.float32),
        jnp.zeros((width,), jnp.float32),
        jnp.zeros((KCONV, 2 * STATE), jnp.float32),
        jnp.zeros((2 * STATE,), jnp.float32),
        jnp.zeros((heads_here,), jnp.float32),
        jnp.zeros((heads_here,), jnp.float32),
        jnp.zeros((heads_here,), jnp.float32),
    )
    input_grads = [None] * batches
    back = None
    for step in range(batches + 1):
        back_slot = batches - step
        if step == 0:
            arrived = jnp.zeros((tok_rows, D), jnp.float32)
        else:
            arrived = passed_along(back, "section", -1).astype(jnp.float32)
        cotangent = ends_in[0, max(batches - 1 - step, 0), 0].astype(jnp.float32)
        live = jnp.where(section == 1, 1.0 if step < batches else 0.0, 1.0 if step >= 1 else 0.0)
        grad_rows = jnp.where(section == 1, cotangent, arrived) * live
        saved, order = kept[back_slot]
        grad_tokens, in_grad, out_grad, smalls = layer_backward(saved, grad_rows, order)
        in_total = in_total + in_grad
        out_total = out_total + out_grad
        small_totals = tuple((total + term for total, term in zip(small_totals, smalls)))
        back = grad_tokens.astype(jnp.bfloat16)
        if step >= 1:
            input_grads[batches - step] = grad_tokens
    in_shard, out_shard = (
        lax.psum_scatter(in_total, ("seq", "wshard"), scatter_dimension=0, tiled=True),
        lax.psum_scatter(out_total, ("seq", "wshard"), scatter_dimension=0, tiled=True),
    )
    anchor = jnp.zeros((), jnp.int32)
    (
        norm_total,
        gated_total,
        kernel_in_total,
        shift_in_total,
        kernel_pair_total,
        shift_pair_total,
        bias_total,
        log_total,
        skip_total,
    ) = small_totals
    kernel_full = jnp.concatenate(
        [
            lax.dynamic_update_slice(
                jnp.zeros((KCONV, INNER), jnp.float32), kernel_in_total, (anchor, first_channel)
            ),
            kernel_pair_total,
        ],
        axis=1,
    )
    shift_full = jnp.concatenate(
        [
            lax.dynamic_update_slice(
                jnp.zeros((INNER,), jnp.float32), shift_in_total, (first_channel,)
            ),
            shift_pair_total,
        ],
        axis=0,
    )
    bias_full = lax.dynamic_update_slice(
        jnp.zeros((HEADS,), jnp.float32), bias_total, (first_head,)
    )
    log_full = lax.dynamic_update_slice(jnp.zeros((HEADS,), jnp.float32), log_total, (first_head,))
    skip_full = lax.dynamic_update_slice(
        jnp.zeros((HEADS,), jnp.float32), skip_total, (first_head,)
    )
    sums = lax.psum(
        (norm_total, gated_total, kernel_full, shift_full, bias_full, log_full, skip_full),
        ("seq", "wshard"),
    )
    ends_out = jnp.stack(
        [
            jnp.where(section == 1, results[index + 1], input_grads[index])
            for index in range(batches)
        ]
    )
    ends_out = ends_out[None, :, None]
    return (
        ends_out,
        sums[0][None],
        in_shard[None],
        sums[2][None],
        sums[3][None],
        sums[4][None],
        sums[5][None],
        sums[6][None],
        sums[1][None],
        out_shard[None],
    )


def solution(mesh):
    placed = (
        P("section", None, "wshard", "seq", None),
        P(None, "wshard", None),
        P(None, "wshard", None),
        P("section", None),
        P("section", "wshard", None),
        P("section", None, None),
        P("section", None),
        P("section", None),
        P("section", None),
        P("section", None),
        P("section", None),
        P("section", "wshard", None),
    )
    return jax.shard_map(
        on_device,
        mesh=mesh,
        in_specs=placed,
        out_specs=(
            P("section", None, "wshard", "seq", None),
            P("section", None),
            P("section", ("seq", "wshard"), None),
            P("section", None, None),
            P("section", None),
            P("section", None),
            P("section", None),
            P("section", None),
            P("section", None),
            P("section", ("seq", "wshard"), None),
        ),
        check_vma=False,
    )
```

profile of v0, /device:TPU:0, one launch (start us, length us, event | category | flops | bytes accessed | tf_op | source)
XLA Modules:
  0.0 1906.7 jit_solution(2763156946009968585)
XLA Ops:
  12.4 92.6 %all-gather.5.cloned.1.call-done = bf16[1,1024,4384]{1,2,0:T(8,128)(2,1)} async-done(((bf16[1,256,4384]{1,2,0:T(8,128)(2,1)}), bf16[1,1024,4384]{1,2,0:T(8,128)(2,1)}) %all-gather.5.cloned.1.call-update) | async-done | bytes 8978448 | tf_op jit(solution)/shard_map/all_gather | solution.py:113
  105.0 8.2 fusion.416
  115.3 4.6 all-to-all-start
  121.2 4.3 scatter_custom_fusion
  127.7 5.1 all-to-all-start.1
  135.4 32.8 %all_gather.16 = bf16[1024,256]{0,1:T(8,128)(2,1)S(1)} all-gather(bf16[256,256]{0,1:T(8,128)(2,1)S(1)} %slice.741), channel_id=1, replica_groups=mesh['section'=2,'seq'=4,'wshard'=4] {'seq'}, dimensions={0}, use_global_device_ids=true | all-gather | bytes 655360 | tf_op jit(solution)/shard_map/all_gather | solution.py:395
  179.2 4.0 gather_fusion.1
  183.6 4.1 multiply_convert_fusion.20
  191.2 42.3 %while.135 = (s32[]{:T(128)}, f32[8,128,64]{1,2,0:T(8,128)S(1)}, bf16[4,256,512]{2,1,0:T(8,128)(2,1)S(1)}, f32[4,8,128,64]{2,3,1,0:T(8,128)}, bf16[4,256,8]{1,2,...) while((s32[]{:T(128)}, f32[8,128,64]{1,2,0:T(8,128)S(1)}, ...), condition=%wide.region_8.9_spmd.clone, body=%wide.region_5.8_spmd.clone.sunk | while | flops 491500576 | bytes 6826045 | solution.py:178
  233.5 4.0 gather_fusion.3
  240.2 26.6 %all_to_all.252 = bf16[4,2,65536]{2,1,0:T(2,128)(2,1)S(1)} all-to-all(bf16[4,2,65536]{2,1,0:T(2,128)(2,1)S(1)} %reshape.2823), channel_id=1, replica_groups=mesh['section'=2,'seq'=4,'wshard'=4] {'seq'}, dimensions={0} | all-to-all | bytes 2097152 | tf_op jit(solution)/shard_map/all_to_all | solution.py:407
  269.2 6.1 copy.397
  275.3 4.3 multiply_reduce_fusion.26
  279.7 4.2 fusion.301
  287.0 8.3 fusion.417
  309.8 4.3 scatter_custom_fusion.1
  315.4 29.8 %all_gather.18 = bf16[1024,256]{0,1:T(8,128)(2,1)S(1)} all-gather(bf16[256,256]{0,1:T(8,128)(2,1)S(1)} %slice.749), channel_id=1, replica_groups=mesh['section'=2,'seq'=4,'wshard'=4] {'seq'}, dimensions={0}, use_global_device_ids=true | all-gather | bytes 655360 | tf_op jit(solution)/shard_map/all_gather | solution.py:395
  356.3 4.0 gather_fusion.5
  360.6 4.1 multiply_convert_fusion.18
  368.2 42.2 %while.136 = (s32[]{:T(128)}, f32[8,128,64]{1,2,0:T(8,128)S(1)}, bf16[4,256,512]{2,1,0:T(8,128)(2,1)S(1)}, f32[4,8,128,64]{2,3,1,0:T(8,128)}, bf16[4,256,8]{1,2,...) while((s32[]{:T(128)}, f32[8,128,64]{1,2,0:T(8,128)S(1)}, ...), condition=%wide.region_18.19_spmd.clone, body=%wide.region_15.18_spmd.clone.sunk | while | flops 491500576 | bytes 6826045 | solution.py:178
  410.5 4.0 gather_fusion.7
  416.8 27.1 %all_to_all.253 = bf16[4,2,65536]{2,1,0:T(2,128)(2,1)S(1)} all-to-all(bf16[4,2,65536]{2,1,0:T(2,128)(2,1)S(1)} %reshape.2825), channel_id=1, replica_groups=mesh['section'=2,'seq'=4,'wshard'=4] {'seq'}, dimensions={0} | all-to-all | bytes 2097152 | tf_op jit(solution)/shard_map/all_to_all | solution.py:407
  446.1 6.2 copy.405
  455.4 5.9 fusion.418
  464.5 4.9 fusion.419
  483.8 4.3 scatter_custom_fusion.2
  489.2 30.2 %all_gather.19 = bf16[1024,256]{0,1:T(8,128)(2,1)S(1)} all-gather(bf16[256,256]{0,1:T(8,128)(2,1)S(1)} %slice.754), channel_id=1, replica_groups=mesh['section'=2,'seq'=4,'wshard'=4] {'seq'}, dimensions={0}, use_global_device_ids=true | all-gather | bytes 655360 | tf_op jit(solution)/shard_map/all_gather | solution.py:395
  534.7 4.2 multiply_convert_fusion.16
  542.3 42.3 %while.137 = (s32[]{:T(128)}, f32[8,128,64]{1,2,0:T(8,128)S(1)}, bf16[4,256,512]{2,1,0:T(8,128)(2,1)S(1)}, f32[4,8,128,64]{2,3,1,0:T(8,128)}, bf16[4,256,8]{1,2,...) while((s32[]{:T(128)}, f32[8,128,64]{1,2,0:T(8,128)S(1)}, ...), condition=%wide.region_28.29_spmd.clone, body=%wide.region_25.28_spmd.clone.sunk | while | flops 491500576 | bytes 6826045 | solution.py:178
  592.0 4.6 all-to-all-start.8
  596.6 22.2 %all-to-all-done.8 = bf16[4,2,65536]{2,1,0:T(2,128)(2,1)S(1)} async-done(((bf16[4,2,65536]{2,1,0:T(2,128)(2,1)}), bf16[4,2,65536]{2,1,0:T(2,128)(2,1)S(1)}, u32[]{:S(2)}, u32[]{:S(2)}) %all-to-all-start.8) | async-done | bytes 1048608 | tf_op jit(solution)/shard_map/all_to_all | solution.py:407
  621.2 6.1 copy.413
  640.7 24.1 %all-to-all-done.9 = bf16[256,4,512]{0,2,1:T(8,128)(2,1)S(1)} async-done(((bf16[256,4,512]{0,2,1:T(8,128)(2,1)}), bf16[256,4,512]{0,2,1:T(8,128)(2,1)S(1)}, u32[]{:S(2)}, u32[]{:S(2)}) %all-to-all-start.9) | async-done | bytes 1048608 | tf_op jit(solution)/shard_map/all_to_all | solution.py:312
  665.3 5.1 gather_fusion.12
  675.4 111.9 %while.138 = (s32[]{:T(128)}, f32[8,128,64]{1,2,0:T(8,128)S(1)}, f32[4,256,512]{2,1,0:T(8,128)}, f32[4,256,256]{2,1,0:T(8,128)}, bf16[4,256,8]{1,2,0:T(8,128)(2,...) while((s32[]{:T(128)}, f32[8,128,64]{1,2,0:T(8,128)S(1)}, ...), condition=%wide.region_48.50_spmd.clone, body=%wide.region_31.49_spmd.clone.sunk | while | flops 1373899776 | bytes 18148180 | solution.py:270
  787.4 6.8 fusion.393
  813.8 4.0 gather_fusion.13
  821.2 5.1 all-to-all-start.10
  833.9 25.6 %all-to-all-done.10 = bf16[4,2,65536]{2,1,0:T(2,128)(2,1)} async-done(((bf16[4,2,65536]{2,1,0:T(2,128)(2,1)}), bf16[4,2,65536]{2,1,0:T(2,128)(2,1)}, u32[]{:S(2)}, u32[]{:S(2)}) %all-to-all-start.10) | async-done | bytes 1048608 | tf_op jit(solution)/shard_map/all_to_all | solution.py:324
  868.7 7.5 multiply_reduce_fusion.40
  890.9 26.2 %all-to-all-done.12 = bf16[256,4,512]{0,2,1:T(8,128)(2,1)S(1)} async-done(((bf16[256,4,512]{0,2,1:T(8,128)(2,1)}), bf16[256,4,512]{0,2,1:T(8,128)(2,1)S(1)}, u32[]{:S(2)}, u32[]{:S(2)}) %all-to-all-start.12) | async-done | bytes 1048608 | tf_op jit(solution)/shard_map/all_to_all | solution.py:312
  917.7 5.1 gather_fusion.16
  927.8 116.1 %while.139 = (s32[]{:T(128)}, f32[8,128,64]{1,2,0:T(8,128)S(1)}, f32[4,256,512]{2,1,0:T(8,128)}, f32[4,256,256]{2,1,0:T(8,128)}, bf16[4,256,8]{1,2,0:T(8,128)(2,...) while((s32[]{:T(128)}, f32[8,128,64]{1,2,0:T(8,128)S(1)}, ...), condition=%wide.region_69.71_spmd.clone, body=%wide.region_52.70_spmd.clone.sunk | while | flops 1373899776 | bytes 18148068 | solution.py:270
  1043.9 6.8 fusion.392
  1077.7 5.1 all-to-all-start.13
  1090.3 25.8 %all-to-all-done.13 = bf16[4,2,65536]{2,1,0:T(2,128)(2,1)} async-done(((bf16[4,2,65536]{2,1,0:T(2,128)(2,1)}), bf16[4,2,65536]{2,1,0:T(2,128)(2,1)}, u32[]{:S(2)}, u32[]{:S(2)}) %all-to-all-start.13) | async-done | bytes 1048608 | tf_op jit(solution)/shard_map/all_to_all | solution.py:324
  1125.4 7.4 multiply_reduce_fusion.39
  1138.1 5.3 multiply_reduce_fusion.6
  1151.3 6.1 fusion.337
  1157.5 19.7 %all-to-all-done.15 = bf16[256,4,512]{0,2,1:T(8,128)(2,1)S(1)} async-done(((bf16[256,4,512]{0,2,1:T(8,128)(2,1)}), bf16[256,4,512]{0,2,1:T(8,128)(2,1)S(1)}, u32[]{:S(2)}, u32[]{:S(2)}) %all-to-all-start.15) | async-done | bytes 1048608 | tf_op jit(solution)/shard_map/all_to_all | solution.py:312
  1177.7 5.1 gather_fusion.20
  1187.8 116.0 %while.140 = (s32[]{:T(128)}, f32[8,128,64]{1,2,0:T(8,128)S(1)}, f32[4,256,512]{2,1,0:T(8,128)}, f32[4,256,256]{2,1,0:T(8,128)}, bf16[4,256,8]{1,2,0:T(8,128)(2,...) while((s32[]{:T(128)}, f32[8,128,64]{1,2,0:T(8,128)S(1)}, ...), condition=%wide.region_90.92_spmd.clone, body=%wide.region_73.91_spmd.clone.sunk | while | flops 1373899776 | bytes 18148068 | solution.py:270
  1303.9 4.1 fusion.397
  1318.1 6.3 add_add_fusion.1
  1333.5 6.1 fusion.394
  1352.5 5.0 all-to-all-start.16
  1357.9 10.5 fusion.341
  1368.4 13.6 fusion.340
  1382.9 11.0 all-to-all-done.16
  1403.2 20.0 %add_add_fusion = f32[1024,4384]{1,0:T(8,128)} fusion(f32[1024,4384]{1,0:T(8,128)} %fusion.341, f32[1024,4384]{1,0:T(8,128)} %fusion.340, bf16[256,32]{0,1:T(8,128)(2,1)S(1)} %bitcast.1455, bf16[256,256]{0,1:T(8,128)(2,1)} %reduce-scatter.10.cloned.1.call-done, bf16[256,2048]{0,1:T(8,128)(2,1)} %bitcast.1388, bf16[256,2048]{0,1:T(8,128)(2,1)S(1)} %copy-done.52, ...), kind=kOutput, calls=%fused_computation.495 | convolution fusion | flops 2317746176 | bytes 56644608 | tf_op jit(solution)/shard_map/dot_general | solution.py:351
  1424.3 5.5 fusion.298
  1431.2 7.6 fusion.316
  1438.9 76.9 %all-reduce.66 = (f32[1,1024]{1,0:T(1,128)}, f32[1,4,2304]{2,1,0:T(4,128)}, f32[1,2304]{1,0:T(1,128)}, f32[1,32]{1,0:T(1,128)}, f32[1,32]{1,0:T(1,128)}, /*index=5*/f32[1,32]{1,0:T(1,128)}, f32[1,2048]{1,0:T(1,128)}) all-reduce(f32[1,1024]{1,0:T(1,128)S(1)} %bitcast.1494, ...), channel_id=1, replica_groups=mesh['section'=2,'seq'=4,'wshard'=4] {'seq','wshard'}, use_global_device_ids=true, to_apply=%region_96.98 | all-reduce | flops 14688 | bytes 117504 | tf_op jit(solution)/shard_map/psum | solution.py:505
  1519.1 380.5 %reduce-scatter.12.cloned.1.call-done = f32[64,4384]{1,0:T(8,128)} async-done(((f32[1024,4384]{1,0:T(8,128)}), f32[64,4384]{1,0:T(8,128)}) %reduce-scatter.12.cloned.1.call-update) | async-done | bytes 1122320 | tf_op jit(solution)/shard_map/reduce_scatter | solution.py:465
  (1774 shorter events, 745.8 us)
Async XLA Ops:
  7.2 97.8 %copy-start.40 = (f32[1,1024]{1,0:T(1,128)S(1)}, f32[1,1024]{1,0:T(1,128)}, u32[]{:S(2)}) copy-start(f32[1,1024]{1,0:T(1,128)} %param.28) | copy-start | bytes 12292
  7.2 97.8 %all-gather.5.cloned.1.call-start = ((), (), s32[]{:S(2)}) async-start(), calls=%async_computation.28 | async-start | bytes 11223040 | tf_op jit(solution)/shard_map/all_gather | solution.py:113
  8.0 271.7 %all-gather.7.cloned.1.call-start = ((), (), s32[]{:S(2)}) async-start(), calls=%async_computation.29 | async-start | bytes 5242880 | tf_op jit(solution)/shard_map/all_gather | solution.py:114
  8.8 112.3 %copy-start = (bf16[4,256,512]{2,1,0:T(8,128)(2,1)}, bf16[4,256,512]{2,1,0:T(8,128)(2,1)S(1)}, u32[]{:S(2)}) copy-start(bf16[4,256,512]{2,1,0:T(8,128)(2,1)S(1)} %fusion.414) | copy-start | bytes 3145732
  9.0 104.2 %copy-start.156 = (f32[256]{0:T(256)}, f32[256]{0:T(256)S(1)}, u32[]{:S(2)}) copy-start(f32[256]{0:T(256)S(1)} %fusion.329) | copy-start | bytes 3076
  9.1 104.2 %copy-start.133 = (f32[256]{0:T(256)}, f32[256]{0:T(256)S(1)}, u32[]{:S(2)}) copy-start(f32[256]{0:T(256)S(1)} %fusion.358) | copy-start | bytes 3076
  105.0 14.9 copy-start.203
  105.0 14.9 copy-start.204
  115.3 12.5 all-to-all-start
  127.7 50.9 %all-to-all-start.1 = ((bf16[256,4,512]{0,2,1:T(8,128)(2,1)}), bf16[256,4,512]{0,2,1:T(8,128)(2,1)S(1)}, u32[]{:S(2)}, u32[]{:S(2)}) async-start(bf16[256,4,512]{0,2,1:T(8,128)(2,1)} %bitcast.16), calls=%async_computation.1 | async-start | bytes 2097152 | tf_op jit(solution)/shard_map/all_to_all | solution.py:381
  132.9 100.5 %copy-start.107 = (s32[1024]{0:T(1024)}, s32[1024]{0:T(1024)S(1)}, u32[]{:S(2)}) copy-start(s32[1024]{0:T(1024)S(1)} %broadcast_clamp_fusion.2) | copy-start | bytes 12292
  132.9 46.3 %copy-start.109 = (s32[1024]{0:T(1024)}, s32[1024]{0:T(1024)S(1)}, u32[]{:S(2)}) copy-start(s32[1024]{0:T(1024)S(1)} %fusion.349) | copy-start | bytes 12292
  134.4 389.3 %copy-start.135 = (f32[1,256]{1,0:T(1,128)}, f32[1,256]{1,0:T(1,128)S(1)}, u32[]{:S(2)}) copy-start(f32[1,256]{1,0:T(1,128)S(1)} %get-tuple-element.3049) | copy-start | bytes 3076
  134.4 389.3 %copy-start.139 = (f32[1,256]{1,0:T(1,128)}, f32[1,256]{1,0:T(1,128)S(1)}, u32[]{:S(2)}) copy-start(f32[1,256]{1,0:T(1,128)S(1)} %get-tuple-element.3048) | copy-start | bytes 3076
  134.4 49.2 %copy-start.76 = (f32[1024]{0:T(1024)}, f32[1024]{0:T(1024)S(1)}, u32[]{:S(2)}) copy-start(f32[1024]{0:T(1024)S(1)} %get-tuple-element.3067) | copy-start | bytes 12292
  134.4 49.2 %copy-start.78 = (f32[1024]{0:T(1024)}, f32[1024]{0:T(1024)S(1)}, u32[]{:S(2)}) copy-start(f32[1024]{0:T(1024)S(1)} %get-tuple-element.3068) | copy-start | bytes 12292
  134.4 49.2 %copy-start.80 = (f32[1024]{0:T(1024)}, f32[1024]{0:T(1024)S(1)}, u32[]{:S(2)}) copy-start(f32[1024]{0:T(1024)S(1)} %get-tuple-element.3069) | copy-start | bytes 12292
  134.4 49.2 %copy-start.94 = (f32[1024]{0:T(1024)}, f32[1024]{0:T(1024)S(1)}, u32[]{:S(2)}) copy-start(f32[1024]{0:T(1024)S(1)} %get-tuple-element.3070) | copy-start | bytes 12292
  283.9 2.8 collective-permute-start
  297.3 8.9 all-to-all-start.3
  306.1 49.6 %all-to-all-start.4 = ((bf16[256,4,512]{0,2,1:T(8,128)(2,1)}), bf16[256,4,512]{0,2,1:T(8,128)(2,1)S(1)}, u32[]{:S(2)}, u32[]{:S(2)}) async-start(bf16[256,4,512]{0,2,1:T(8,128)(2,1)} %bitcast.48), calls=%async_computation.4 | async-start | bytes 2097152 | tf_op jit(solution)/shard_map/all_to_all | solution.py:381
  314.4 96.1 %copy-start.111 = (s32[1024]{0:T(1024)}, s32[1024]{0:T(1024)S(1)}, u32[]{:S(2)}) copy-start(s32[1024]{0:T(1024)S(1)} %broadcast_clamp_fusion.1) | copy-start | bytes 12292
  314.4 41.9 %copy-start.113 = (s32[1024]{0:T(1024)}, s32[1024]{0:T(1024)S(1)}, u32[]{:S(2)}) copy-start(s32[1024]{0:T(1024)S(1)} %fusion.350) | copy-start | bytes 12292
  314.4 46.1 %copy-start.82 = (f32[1024]{0:T(1024)}, f32[1024]{0:T(1024)S(1)}, u32[]{:S(2)}) copy-start(f32[1024]{0:T(1024)S(1)} %get-tuple-element.3063) | copy-start | bytes 12292
  314.5 46.1 %copy-start.84 = (f32[1024]{0:T(1024)}, f32[1024]{0:T(1024)S(1)}, u32[]{:S(2)}) copy-start(f32[1024]{0:T(1024)S(1)} %get-tuple-element.3064) | copy-start | bytes 12292
  314.5 46.1 %copy-start.86 = (f32[1024]{0:T(1024)}, f32[1024]{0:T(1024)S(1)}, u32[]{:S(2)}) copy-start(f32[1024]{0:T(1024)S(1)} %get-tuple-element.3065) | copy-start | bytes 12292
  314.5 46.1 %copy-start.96 = (f32[1024]{0:T(1024)}, f32[1024]{0:T(1024)S(1)}, u32[]{:S(2)}) copy-start(f32[1024]{0:T(1024)S(1)} %get-tuple-element.3066) | copy-start | bytes 12292
  452.3 12.1 slice-start
  452.3 12.2 slice-start.1
  461.3 2.8 collective-permute-start.1
  471.4 8.9 all-to-all-start.6
  480.3 49.6 %all-to-all-start.7 = ((bf16[256,4,512]{0,2,1:T(8,128)(2,1)}), bf16[256,4,512]{0,2,1:T(8,128)(2,1)S(1)}, u32[]{:S(2)}, u32[]{:S(2)}) async-start(bf16[256,4,512]{0,2,1:T(8,128)(2,1)} %bitcast.70), calls=%async_computation.7 | async-start | bytes 2097152 | tf_op jit(solution)/shard_map/all_to_all | solution.py:381
  488.2 96.4 %copy-start.115 = (s32[1024]{0:T(1024)}, s32[1024]{0:T(1024)S(1)}, u32[]{:S(2)}) copy-start(s32[1024]{0:T(1024)S(1)} %broadcast_clamp_fusion) | copy-start | bytes 12292
  488.2 46.5 %copy-start.88 = (f32[1024]{0:T(1024)}, f32[1024]{0:T(1024)S(1)}, u32[]{:S(2)}) copy-start(f32[1024]{0:T(1024)S(1)} %get-tuple-element.3059) | copy-start | bytes 12292
  488.2 46.5 %copy-start.90 = (f32[1024]{0:T(1024)}, f32[1024]{0:T(1024)S(1)}, u32[]{:S(2)}) copy-start(f32[1024]{0:T(1024)S(1)} %get-tuple-element.3060) | copy-start | bytes 12292
  488.3 46.5 %copy-start.92 = (f32[1024]{0:T(1024)}, f32[1024]{0:T(1024)S(1)}, u32[]{:S(2)}) copy-start(f32[1024]{0:T(1024)S(1)} %get-tuple-element.3061) | copy-start | bytes 12292
  488.3 46.5 %copy-start.98 = (f32[1024]{0:T(1024)}, f32[1024]{0:T(1024)S(1)}, u32[]{:S(2)}) copy-start(f32[1024]{0:T(1024)S(1)} %get-tuple-element.3062) | copy-start | bytes 12292
  592.0 26.8 %all-to-all-start.8 = ((bf16[4,2,65536]{2,1,0:T(2,128)(2,1)}), bf16[4,2,65536]{2,1,0:T(2,128)(2,1)S(1)}, u32[]{:S(2)}, u32[]{:S(2)}) async-start(bf16[4,2,65536]{2,1,0:T(2,128)(2,1)} %reshape.2827), calls=%async_computation.8 | async-start | bytes 2097152 | tf_op jit(solution)/shard_map/all_to_all | solution.py:407
  637.0 27.8 %all-to-all-start.9 = ((bf16[256,4,512]{0,2,1:T(8,128)(2,1)}), bf16[256,4,512]{0,2,1:T(8,128)(2,1)S(1)}, u32[]{:S(2)}, u32[]{:S(2)}) async-start(bf16[256,4,512]{0,2,1:T(8,128)(2,1)} %bitcast.82), calls=%async_computation.9 | async-start | bytes 2097152 | tf_op jit(solution)/shard_map/all_to_all | solution.py:312
  803.0 18.2 all-to-all-start.11
  821.2 38.3 %all-to-all-start.10 = ((bf16[4,2,65536]{2,1,0:T(2,128)(2,1)}), bf16[4,2,65536]{2,1,0:T(2,128)(2,1)}, u32[]{:S(2)}, u32[]{:S(2)}) async-start(bf16[4,2,65536]{2,1,0:T(2,128)(2,1)} %reshape.2831), calls=%async_computation.10 | async-start | bytes 2097152 | tf_op jit(solution)/shard_map/all_to_all | solution.py:324
  826.3 42.4 %reduce-scatter.6.cloned.1.call-start = ((), (), s32[]{:S(2)}) async-start(), calls=%async_computation.23 | async-start | bytes 655360 | tf_op jit(solution)/shard_map/reduce_scatter | solution.py:339
  833.9 34.8 %copy-start.123 = (bf16[1024,1,8]{0,2,1:T(8,128)(2,1)}, bf16[1024,1,8]{0,2,1:T(8,128)(2,1)S(1)}, u32[]{:S(2)}) copy-start(bf16[1024,1,8]{0,2,1:T(8,128)(2,1)S(1)} %copy.426) | copy-start | bytes 49156
  868.7 12.1 copy-start.210
  876.7 4.1 collective-permute-start.2
  887.0 30.6 %copy-start.114 = (s32[1024]{0:T(1024)S(1)}, s32[1024]{0:T(1024)}, u32[]{:S(2)}) copy-start(s32[1024]{0:T(1024)} %copy-done.113) | copy-start | bytes 12292
  887.0 30.1 %all-to-all-start.12 = ((bf16[256,4,512]{0,2,1:T(8,128)(2,1)}), bf16[256,4,512]{0,2,1:T(8,128)(2,1)S(1)}, u32[]{:S(2)}, u32[]{:S(2)}) async-start(bf16[256,4,512]{0,2,1:T(8,128)(2,1)} %bitcast.98), calls=%async_computation.13 | async-start | bytes 2097152 | tf_op jit(solution)/shard_map/all_to_all | solution.py:312
  927.8 116.1 %copy-start.83 = (f32[1024]{0:T(1024)S(1)}, f32[1024]{0:T(1024)}, u32[]{:S(2)}) copy-start(f32[1024]{0:T(1024)} %copy-done.82) | copy-start | bytes 12292
  1059.7 18.0 all-to-all-start.14
  1077.7 38.5 %all-to-all-start.13 = ((bf16[4,2,65536]{2,1,0:T(2,128)(2,1)}), bf16[4,2,65536]{2,1,0:T(2,128)(2,1)}, u32[]{:S(2)}, u32[]{:S(2)}) async-start(bf16[4,2,65536]{2,1,0:T(2,128)(2,1)} %reshape.2835), calls=%async_computation.14 | async-start | bytes 2097152 | tf_op jit(solution)/shard_map/all_to_all | solution.py:324
  1082.8 42.6 %reduce-scatter.8.cloned.1.call-start = ((), (), s32[]{:S(2)}) async-start(), calls=%async_computation.24 | async-start | bytes 655360 | tf_op jit(solution)/shard_map/reduce_scatter | solution.py:339
  1090.3 35.0 %copy-start.125 = (bf16[1024,1,8]{0,2,1:T(8,128)(2,1)}, bf16[1024,1,8]{0,2,1:T(8,128)(2,1)S(1)}, u32[]{:S(2)}) copy-start(bf16[1024,1,8]{0,2,1:T(8,128)(2,1)S(1)} %copy.439) | copy-start | bytes 49156
  1134.3 3.8 collective-permute-start.3
  1147.2 29.9 %all-to-all-start.15 = ((bf16[256,4,512]{0,2,1:T(8,128)(2,1)}), bf16[256,4,512]{0,2,1:T(8,128)(2,1)S(1)}, u32[]{:S(2)}, u32[]{:S(2)}) async-start(bf16[256,4,512]{0,2,1:T(8,128)(2,1)} %bitcast.114), calls=%async_computation.17 | async-start | bytes 2097152 | tf_op jit(solution)/shard_map/all_to_all | solution.py:312
  1150.9 252.3 %reduce-scatter.10.cloned.1.call-start = ((), (), s32[]{:S(2)}) async-start(), calls=%async_computation.25 | async-start | bytes 655360 | tf_op jit(solution)/shard_map/reduce_scatter | solution.py:339
  1157.5 20.2 %copy-start.110 = (s32[1024]{0:T(1024)S(1)}, s32[1024]{0:T(1024)}, u32[]{:S(2)}) copy-start(s32[1024]{0:T(1024)} %copy-done.109) | copy-start | bytes 12292
  1187.8 116.0 %copy-start.77 = (f32[1024]{0:T(1024)S(1)}, f32[1024]{0:T(1024)}, u32[]{:S(2)}) copy-start(f32[1024]{0:T(1024)} %copy-done.76) | copy-start | bytes 12292
  1314.8 204.3 %reduce-scatter.14.cloned.1.call-start = ((), (), s32[]{:S(2)}) async-start(), calls=%async_computation.27 | async-start | bytes 8912896 | tf_op jit(solution)/shard_map/reduce_scatter | solution.py:466
  1330.2 22.3 %all-to-all-start.17 = ((bf16[4,2,1024]{2,1,0:T(2,128)(2,1)}), bf16[4,2,1024]{2,1,0:T(2,128)(2,1)S(1)}, u32[]{:S(2)}, u32[]{:S(2)}) async-start(bf16[4,2,1024]{2,1,0:T(2,128)(2,1)} %reshape.2837), calls=%async_computation.20 | async-start | bytes 32768 | tf_op jit(solution)/shard_map/all_to_all | solution.py:331
  1352.5 41.5 %all-to-all-start.16 = ((bf16[4,2,65536]{2,1,0:T(2,128)(2,1)}), bf16[4,2,65536]{2,1,0:T(2,128)(2,1)}, u32[]{:S(2)}, u32[]{:S(2)}) async-start(bf16[4,2,65536]{2,1,0:T(2,128)(2,1)} %reshape.2839), calls=%async_computation.18 | async-start | bytes 2097152 | tf_op jit(solution)/shard_map/all_to_all | solution.py:324
  1357.5 10.9 copy-start.126
  1357.5 542.1 %reduce-scatter.12.cloned.1.call-start = ((), (), s32[]{:S(2)}) async-start(), calls=%async_computation.26 | async-start | bytes 19496960 | tf_op jit(solution)/shard_map/reduce_scatter | solution.py:465
  1431.2 84.5 %copy-start.157 = (f32[256]{0:T(256)S(1)}, f32[256]{0:T(256)}, u32[]{:S(2)}) copy-start(f32[256]{0:T(256)} %copy-done.156) | copy-start | bytes 3076
  1431.2 84.5 %copy-start.63 = (bf16[256,1024]{1,0:T(8,128)(2,1)S(1)}, bf16[256,1024]{1,0:T(8,128)(2,1)}, u32[]{:S(2)}) copy-start(bf16[256,1024]{1,0:T(8,128)(2,1)} %copy-done.61) | copy-start | bytes 1572868
  (263 other events, 1184.9 us)
Sparse Core Ops, SparseCore 0:
  9.9 95.0 all-gather.4
  106.8 52.6 all-gather.6
  833.0 26.0 reduce-scatter.5
  1089.5 26.2 reduce-scatter.7
  1314.9 19.8 reduce-scatter.9
  1337.5 178.6 reduce-scatter.13
  1519.1 380.4 reduce-scatter.11
where the time goes:
time: 1920 us; the launch traced here: 1910 us
  waiting for transfers between devices  643 us (33%)
  local copies, waits for them, and re-layouts  409 us (21%)
  other arithmetic  255 us (13%)
  matrix products  252 us (13%)
  blocking collectives  223 us (12%)
  starting transfers between devices  71.3 us (4%)
  loops' own time  34.8 us (2%)
    reduce_scatter x1, waiting for transfers between devices, on_device(): lax.psum_scatter(in_total, ('seq', 'wshard'), scatter_dimension=0, tiled=...  381 us
    all_gather x3, blocking collectives, on_device(): pair_dealt = lax.all_gather(layer_pair_rows, 'seq', axis=0, tiled=True)  92.8 us
    all_gather x1, waiting for transfers between devices, on_device(): lax.all_gather(in_w[0], 'wshard', axis=0, tiled=True)  92.6 us
    psum x1, blocking collectives, on_device(): lax.psum((norm_total, gated_total, kernel_full, shift_full, bias_full, lo...  76.9 us
    all_to_all x3, waiting for transfers between devices, layer_backward(): lax.all_to_all(grad_mixed.astype(jnp.bfloat16).reshape(tok_rows, shards,...  70 us
    dynamic_update_slice x72, local copies, waits for them, and re-layouts, head_backward(): lax.scan(retreat, start, pieces, reverse=True)  63 us
    all_to_all x3, waiting for transfers between devices, layer_backward(): lax.all_to_all(grad_input[order].astype(jnp.bfloat16).reshape(group, 1, w...  62.4 us
    unnamed x419, local copies, waits for them, and re-layouts  58 us
  transfers between devices with their start and end apart: 27, of which 15 were waited for; matrix products, arithmetic and copies ran while one was open for 16% of the time, Pallas kernels for 0%

commit v1 on v0

v1 whole, which is shorter than its diff:
```python
import functools

import jax
import jax.numpy as jnp
from jax import lax
from jax.experimental import pallas as pl
from jax.experimental.pallas import tpu as pltpu
from jax.sharding import PartitionSpec as P

D = 1024
HEADDIM = 64
STATE = 128
KCONV = 4
BLOCK = 256
INNER = 2048
HEADS = 32
PAIR = 2 * STATE
LANES = 128
EPS = 1e-05
NEG = -1e30
BF = jnp.bfloat16
F32 = jnp.float32
HIGH = lax.Precision.HIGHEST
AXES = ("section", "seq", "wshard")
VMEM_LIMIT = 58 << 20


def params():
    return pltpu.CompilerParams(
        dimension_semantics=("arbitrary",), vmem_limit_bytes=VMEM_LIMIT
    )


def cost(flops, nbytes, trans=0):
    return pl.CostEstimate(flops=flops, bytes_accessed=nbytes, transcendentals=trans)


def nn(a, b, precision=None):
    return lax.dot_general(
        a, b, (((1,), (0,)), ((), ())), preferred_element_type=F32, precision=precision
    )


def nt(a, b):
    return lax.dot_general(a, b, (((1,), (1,)), ((), ())), preferred_element_type=F32)


def tn(a, b):
    return lax.dot_general(a, b, (((0,), (0,)), ((), ())), preferred_element_type=F32)


def two(x):
    hi = x.astype(BF)
    lo = (x - hi.astype(F32)).astype(BF)
    return jnp.concatenate([hi, lo], axis=1)


def iota(shape, dim):
    return lax.broadcasted_iota(jnp.int32, shape, dim)


def column(row):
    return jnp.broadcast_to(row, (LANES, row.shape[1])).T[:, :1]


def as_row(col):
    return jnp.broadcast_to(col, (col.shape[0], LANES)).T[:1]


def sigmoid(x):
    return 1.0 / (1.0 + jnp.exp(-x))


def softplus(x):
    return jnp.maximum(x, 0.0) + jnp.log1p(jnp.exp(-jnp.abs(x)))


def full(shape):
    return pl.BlockSpec(shape, lambda i: (0,) * len(shape))


def place_kernel(with_norm, order_ref, x_ref, gain_ref, *outs):
    base = pl.program_id(0) * BLOCK
    total = x_ref.shape[0]
    hot = (order_ref[...] == base + iota((BLOCK, total), 0)).astype(BF)
    tokens = nn(hot, x_ref[...])
    outs[0][...] = tokens.astype(BF)
    if with_norm:
        scale = lax.rsqrt(jnp.mean(tokens * tokens, axis=1, keepdims=True) + EPS)
        outs[1][...] = (tokens * scale * gain_ref[...]).astype(BF)


def place(order_row, x, gain, with_norm):
    total = x.shape[0]
    count = total // BLOCK
    out = jax.ShapeDtypeStruct((total, D), BF)
    number = 2 if with_norm else 1
    return pl.pallas_call(
        functools.partial(place_kernel, with_norm),
        grid=(count,),
        in_specs=[full((1, total)), full((total, D)), full((1, D))],
        out_specs=[pl.BlockSpec((BLOCK, D), lambda i: (i, 0))] * number,
        out_shape=[out] * number,
        compiler_params=params(),
        cost_estimate=cost(2 * total * total * D, 6 * total * D),
        name="place",
    )(order_row, x, gain)


def unplace_kernel(order_ref, x_ref, out_ref):
    total = x_ref.shape[0]
    hot = (order_ref[...] == iota((BLOCK, total), 1)).astype(BF)
    out_ref[...] = nn(hot, x_ref[...]).astype(BF)


def unplace(order_col, x):
    total = x.shape[0]
    return pl.pallas_call(
        unplace_kernel,
        grid=(total // BLOCK,),
        in_specs=[pl.BlockSpec((BLOCK, 1), lambda i: (i, 0)), full((total, D))],
        out_specs=pl.BlockSpec((BLOCK, D), lambda i: (i, 0)),
        out_shape=jax.ShapeDtypeStruct((total, D), BF),
        compiler_params=params(),
        cost_estimate=cost(2 * total * total * D, 4 * total * D),
        name="unplace",
    )(order_col, x)


def block_terms(raw, dtb, rate_sign, label_col, offset):
    rate = softplus(raw + dtb)
    rows = iota((BLOCK, BLOCK), 0)
    cols = iota((BLOCK, BLOCK), 1)
    lower = (cols <= rows).astype(F32)
    level = nn(lower, rate * rate_sign, HIGH)
    local = iota((BLOCK, 1), 0)
    end = level[BLOCK - 1 :]
    end_offset = offset[BLOCK - 1 :]
    head = jnp.where(offset > local, jnp.exp(level), 0.0)
    fade = jnp.where(local >= BLOCK - 1 - end_offset, jnp.exp(end - level), 0.0)
    carry = jnp.where(end_offset > BLOCK - 1, jnp.exp(end), 0.0)
    return rate, level, head, fade, carry


def forward_kernel(
    heads,
    normed_ref,
    wg_ref,
    wc_ref,
    wr_ref,
    taps_ref,
    bias_ref,
    dtb_ref,
    sign_ref,
    skip_ref,
    spread_ref,
    pos_ref,
    label_ref,
    gate_ref,
    pre_ref,
    cin_ref,
    raw_ref,
    mixed_ref,
    states_ref,
    square_ref,
    state_ref,
    halo_ref,
):
    width = heads * HEADDIM

    @pl.when(pl.program_id(0) == 0)
    def _():
        state_ref[...] = jnp.zeros_like(state_ref)
        halo_ref[...] = jnp.zeros_like(halo_ref)

    x = normed_ref[...]
    gate = nn(x, wg_ref[...])
    gate_ref[...] = gate
    cin_low = nn(x, wc_ref[...]).astype(BF)
    cin_ref[...] = cin_low
    raw_low = nn(x, wr_ref[...]).astype(BF)
    raw_ref[...] = raw_low
    pos = pos_ref[...]
    label_col = pos[:, 0:1]
    offset = pos[:, 1:2]
    cin = cin_low.astype(F32)
    longer = jnp.concatenate([halo_ref[...], cin], axis=0)
    halo_ref[...] = cin[BLOCK - 8 :]
    taps = taps_ref[...]
    pre = bias_ref[...] + taps[KCONV - 1 : KCONV] * cin
    for index in range(KCONV - 1):
        delay = KCONV - 1 - index
        moved = longer[8 - delay : 8 - delay + BLOCK]
        pre = pre + jnp.where(offset >= delay, taps[index : index + 1] * moved, 0.0)
    pre_ref[...] = pre
    conv = (pre * sigmoid(pre)).astype(BF)
    write = conv[:, :STATE]
    read = conv[:, STATE:PAIR]
    xs = conv[:, PAIR:]
    xs_float = xs.astype(F32)
    rate, level, head, fade, carry = block_terms(
        raw_low.astype(F32), dtb_ref[...], sign_ref[...], label_col, offset
    )
    tail = fade * rate
    level_rows = level.T
    rate_rows = rate.T
    spread = spread_ref[...]
    state = state_ref[...]
    states_ref[0] = state
    mixed = nn(two(head), spread) * nn(read, state.astype(BF)) + skip_ref[...] * xs_float
    gram = nt(read, write)
    inside = (label_col == label_ref[0]) & (iota((BLOCK, BLOCK), 1) <= iota((BLOCK, BLOCK), 0))
    closed = jnp.where(inside, 0.0, NEG)
    step = 2 if heads % 2 == 0 else 1
    parts = []
    for first in range(0, heads, step):
        span = xs[:, first * HEADDIM : (first + step) * HEADDIM]
        mixing = []
        values = []
        for h in range(first, first + step):
            weight = jnp.exp(level[:, h : h + 1] - level_rows[h : h + 1] + closed)
            mixing.append((gram * (weight * rate_rows[h : h + 1])).astype(BF))
            if step == 1:
                values.append(span)
            else:
                own = iota(span.shape, 1) // HEADDIM == h - first
                values.append(jnp.where(own, span, jnp.zeros_like(span)))
        parts.append(nn(jnp.concatenate(mixing, axis=1), jnp.concatenate(values, axis=0)))
    mixed = mixed + jnp.concatenate(parts, axis=1)
    mixed_low = mixed.astype(BF)
    mixed_ref[...] = mixed_low
    gv = mixed_low.astype(F32) * (gate * sigmoid(gate))
    square_ref[0] = as_row(jnp.sum(gv * gv, axis=1, keepdims=True))
    carry_rows = jnp.broadcast_to(carry, (8, LANES))
    carry_wide = nn(two(carry_rows), spread)[:1]
    written = (nn(two(tail), spread) * xs_float).astype(BF)
    state_ref[...] = carry_wide * state + tn(write, written)


def forward(heads, normed, weights, vectors, spread, pos, label_row):
    total = normed.shape[0]
    count = total // BLOCK
    width = heads * HEADDIM
    conv = PAIR + width
    wg, wc, wr = weights
    block = lambda n: pl.BlockSpec((BLOCK, n), lambda i: (i, 0))
    row = pl.BlockSpec((1, 1, BLOCK), lambda i: (i, 0, 0))
    return pl.pallas_call(
        functools.partial(forward_kernel, heads),
        grid=(count,),
        in_specs=[
            block(D),
            full((D, width)),
            full((D, conv)),
            full((D, LANES)),
            full((KCONV, conv)),
            full((1, conv)),
            full((1, LANES)),
            full((1, LANES)),
            full((1, width)),
            full((2 * LANES, width)),
            block(3),
            row,
        ],
        out_specs=[
            block(width),
            block(conv),
            block(conv),
            block(LANES),
            block(width),
            pl.BlockSpec((1, STATE, width), lambda i: (i, 0, 0)),
            row,
        ],
        out_shape=[
            jax.ShapeDtypeStruct((total, width), F32),
            jax.ShapeDtypeStruct((total, conv), F32),
            jax.ShapeDtypeStruct((total, conv), BF),
            jax.ShapeDtypeStruct((total, LANES), BF),
            jax.ShapeDtypeStruct((total, width), BF),
            jax.ShapeDtypeStruct((count, STATE, width), F32),
            jax.ShapeDtypeStruct((count, 1, BLOCK), F32),
        ],
        scratch_shapes=[pltpu.VMEM((STATE, width), F32), pltpu.VMEM((8, conv), F32)],
        compiler_params=params(),
        cost_estimate=cost(
            2 * total * D * (width + conv + LANES) * 2, total * D * 12, total * BLOCK * heads
        ),
        name="forward",
    )(
        normed,
        wg,
        wc,
        wr,
        vectors["taps"],
        vectors["bias"],
        vectors["dtb"],
        vectors["sign"],
        vectors["skip"],
        spread,
        pos,
        label_row,
    )


def project_kernel(with_rest, own_ref, mixed_ref, gate_ref, square_ref, gain_ref, w_ref, rest_ref, out_ref):
    gate = gate_ref[...]
    gv = mixed_ref[...].astype(F32) * (gate * sigmoid(gate))
    scale = lax.rsqrt(column(square_ref[0]) / INNER + EPS)
    normed_out = (gv * scale * gain_ref[...]).astype(BF)
    out = nn(normed_out, w_ref[...])
    if with_rest:
        own = (own_ref[0] == pl.program_id(0)).astype(F32)
        out = out + own * rest_ref[...].astype(F32)
    out_ref[...] = out.astype(BF)


def project(mixed, gate, square, gain, w, own, rest, with_rest):
    total, width = mixed.shape
    block = lambda n: pl.BlockSpec((BLOCK, n), lambda i: (i, 0))
    return pl.pallas_call(
        functools.partial(project_kernel, with_rest),
        grid=(total // BLOCK,),
        in_specs=[
            pl.BlockSpec(memory_space=pltpu.SMEM),
            block(width),
            block(width),
            pl.BlockSpec((1, 1, BLOCK), lambda i: (i, 0, 0)),
            full((1, width)),
            full((width, D)),
            full((BLOCK, D)),
        ],
        out_specs=block(D),
        out_shape=jax.ShapeDtypeStruct((total, D), BF),
        compiler_params=params(),
        cost_estimate=cost(2 * total * D * width, total * (width * 6 + D * 2)),
        name="project",
    )(own, mixed, gate, square, gain, w, rest)


def dots_kernel(dout_ref, w_ref, mixed_ref, gate_ref, gain_ref, out_ref):
    gate = gate_ref[...]
    gv = mixed_ref[...].astype(F32) * (gate * sigmoid(gate))
    grad = nt(dout_ref[...], w_ref[...]) * gain_ref[...]
    out_ref[0] = as_row(jnp.sum(grad * gv, axis=1, keepdims=True))


def dots(dout, w, mixed, gate, gain):
    total, width = mixed.shape
    block = lambda n: pl.BlockSpec((BLOCK, n), lambda i: (i, 0))
    row = pl.BlockSpec((1, 1, BLOCK), lambda i: (i, 0, 0))
    return pl.pallas_call(
        dots_kernel,
        grid=(total // BLOCK,),
        in_specs=[block(D), full((width, D)), block(width), block(width), full((1, width))],
        out_specs=row,
        out_shape=jax.ShapeDtypeStruct((total // BLOCK, 1, BLOCK), F32),
        compiler_params=params(),
        cost_estimate=cost(2 * total * D * width, total * (width * 6 + D * 2)),
        name="dots",
    )(dout, w, mixed, gate, gain)


def ungate_kernel(
    dout_ref,
    w_ref,
    mixed_ref,
    gate_ref,
    gain_ref,
    square_ref,
    dot_ref,
    normed_ref,
    dmixed_ref,
    dgate_ref,
    ggain_ref,
    gout_ref,
    gin_ref,
    out_total,
    in_total,
):
    step = pl.program_id(0)

    @pl.when(step == 0)
    def _():
        ggain_ref[...] = jnp.zeros_like(ggain_ref)
        out_total[...] = jnp.zeros_like(out_total)
        in_total[...] = jnp.zeros_like(in_total)

    gate = gate_ref[...]
    gain = gain_ref[...]
    mixed = mixed_ref[...].astype(F32)
    sig = sigmoid(gate)
    act = gate * sig
    scale = lax.rsqrt(column(square_ref[0]) / INNER + EPS)
    normal = mixed * act * scale
    dout = dout_ref[...]
    grad_out = nt(dout, w_ref[...])
    grad_normal = grad_out * gain
    shared = column(dot_ref[0]) * scale / INNER
    grad_gv = scale * (grad_normal - normal * shared)
    dmixed_ref[...] = (grad_gv * act).astype(BF)
    dgate = (grad_gv * mixed * (sig * (1.0 + gate * (1.0 - sig)))).astype(BF)
    dgate_ref[...] = dgate
    ggain_ref[...] += jnp.sum(grad_out * normal, axis=0, keepdims=True)
    out_total[...] += tn((normal * gain).astype(BF), dout)
    in_total[...] += tn(normed_ref[...], dgate)

    @pl.when(step == pl.num_programs(0) - 1)
    def _():
        gout_ref[...] = out_total[...].astype(BF)
        gin_ref[...] = in_total[...].astype(BF)


def ungate(dout, w, mixed, gate, gain, square, dot, normed):
    total, width = mixed.shape
    block = lambda n: pl.BlockSpec((BLOCK, n), lambda i: (i, 0))
    row = pl.BlockSpec((1, 1, BLOCK), lambda i: (i, 0, 0))
    return pl.pallas_call(
        ungate_kernel,
        grid=(total // BLOCK,),
        in_specs=[
            block(D),
            full((width, D)),
            block(width),
            block(width),
            full((1, width)),
            row,
            row,
            block(D),
        ],
        out_specs=[
            block(width),
            block(width),
            full((1, width)),
            full((width, D)),
            full((D, width)),
        ],
        out_shape=[
            jax.ShapeDtypeStruct((total, width), BF),
            jax.ShapeDtypeStruct((total, width), BF),
            jax.ShapeDtypeStruct((1, width), F32),
            jax.ShapeDtypeStruct((width, D), BF),
            jax.ShapeDtypeStruct((D, width), BF),
        ],
        scratch_shapes=[pltpu.VMEM((width, D), F32), pltpu.VMEM((D, width), F32)],
        compiler_params=params(),
        cost_estimate=cost(6 * total * D * width, total * (width * 10 + D * 4)),
        name="ungate",
    )(dout, w, mixed, gate, gain, square, dot, normed)


def backward_kernel(
    heads,
    normed_ref,
    wg_ref,
    wc_ref,
    wr_ref,
    taps_ref,
    dtb_ref,
    sign_ref,
    skip_ref,
    spread_ref,
    fold_ref,
    pos_ref,
    label_ref,
    pre_ref,
    cin_ref,
    raw_ref,
    states_ref,
    dmixed_ref,
    dgate_ref,
    dnormed_ref,
    gconv_ref,
    graw_ref,
    gtaps_ref,
    gheads_ref,
    gskip_ref,
    dstate_ref,
    halo_ref,
    conv_total,
    raw_total,
):
    step = pl.program_id(0)

    @pl.when(step == 0)
    def _():
        dstate_ref[...] = jnp.zeros_like(dstate_ref)
        halo_ref[...] = jnp.zeros_like(halo_ref)
        conv_total[...] = jnp.zeros_like(conv_total)
        raw_total[...] = jnp.zeros_like(raw_total)
        gtaps_ref[...] = jnp.zeros_like(gtaps_ref)
        gheads_ref[...] = jnp.zeros_like(gheads_ref)
        gskip_ref[...] = jnp.zeros_like(gskip_ref)

    pos = pos_ref[...]
    label_col = pos[:, 0:1]
    offset = pos[:, 1:2]
    remain = pos[:, 2:3]
    pre = pre_ref[...]
    sig = sigmoid(pre)
    conv = (pre * sig).astype(BF)
    write = conv[:, :STATE]
    read = conv[:, STATE:PAIR]
    xs = conv[:, PAIR:]
    xs_float = xs.astype(F32)
    raw = raw_ref[...].astype(F32)
    sign = sign_ref[...]
    rate, level, head, fade, carry = block_terms(raw, dtb_ref[...], sign, label_col, offset)
    tail = fade * rate
    level_rows = level.T
    spread = spread_ref[...]
    fold = fold_ref[...]
    skip = skip_ref[...]
    dy = dmixed_ref[...]
    dy_float = dy.astype(F32)
    state = states_ref[0]
    state_low = state.astype(BF)
    dstate = dstate_ref[...]
    dstate_low = dstate.astype(BF)
    from_state = nn(read, state_low)
    dhead = nn(two(dy_float * from_state), fold)
    tail_wide = nn(two(tail), spread)
    scaled = (nn(two(head), spread) * dy_float).astype(BF)
    written = (tail_wide * xs_float).astype(BF)
    through = nn(write, dstate_low)
    dtail = nn(two(xs_float * through), fold)
    gskip_ref[...] += jnp.sum(dy_float * xs_float, axis=0, keepdims=True)
    carry_rows = jnp.broadcast_to(carry, (8, LANES))
    carry_wide = nn(two(carry_rows), spread)[:1]
    held = jnp.broadcast_to(jnp.sum(state * dstate, axis=0, keepdims=True), (8, heads * HEADDIM))
    dcarry = nn(two(held), fold)[:1]

    gram = nt(write, read)
    inside = (label_col == label_ref[0]) & (iota((BLOCK, BLOCK), 0) <= iota((BLOCK, BLOCK), 1))
    closed = jnp.where(inside, 0.0, NEG)
    pair_size = 2 if heads % 2 == 0 else 1
    lane = iota((1, LANES), 1)
    drate = jnp.zeros((BLOCK, LANES), F32)
    level_sums = []
    parts = []
    dgram = jnp.zeros((BLOCK, BLOCK), F32)
    for first in range(0, heads, pair_size):
        cut = slice(first * HEADDIM, (first + pair_size) * HEADDIM)
        xs_span = xs[:, cut]
        dy_span = dy[:, cut]
        mixing = []
        values = []
        for h in range(first, first + pair_size):
            if pair_size == 1:
                xs_own = xs_span
                dy_own = dy_span
            else:
                own = iota(xs_span.shape, 1) // HEADDIM == h - first
                xs_own = jnp.where(own, xs_span, jnp.zeros_like(xs_span))
                dy_own = jnp.where(own, dy_span, jnp.zeros_like(dy_span))
            decay = jnp.exp(level_rows[h : h + 1] - level[:, h : h + 1] + closed)
            rate_col = rate[:, h : h + 1]
            weight = decay * rate_col
            mixing.append((gram * weight).astype(BF))
            values.append(dy_own)
            dmix = nt(xs_own, dy_span)
            dgram = dgram + dmix * weight
            bare = dmix * gram * decay
            drate = drate + jnp.sum(bare, axis=1, keepdims=True) * (lane == h).astype(F32)
            level_sums.append(jnp.sum(bare * rate_col, axis=0, keepdims=True))
        parts.append(nn(jnp.concatenate(mixing, axis=1), jnp.concatenate(values, axis=0)))
    dxs = jnp.concatenate(parts, axis=1) + skip * dy_float + tail_wide * through
    dgram_low = dgram.astype(BF)
    dread = tn(dgram_low, write) + nt(scaled, state_low)
    dwrite = nn(dgram_low, read) + nt(written, dstate_low)
    dstate_ref[...] = carry_wide * dstate + tn(read, scaled)

    level_sums.append(jnp.zeros((LANES - heads, BLOCK), F32))
    tail_flow = dtail * tail
    local = iota((BLOCK, 1), 0)
    last = jnp.sum(tail_flow, axis=0, keepdims=True) + dcarry * carry
    dlevel = jnp.concatenate(level_sums, axis=0).T - rate * drate + dhead * head - tail_flow
    dlevel = dlevel + jnp.where(local == BLOCK - 1, last, 0.0)
    upper = (iota((BLOCK, BLOCK), 0) <= iota((BLOCK, BLOCK), 1)).astype(F32)
    dsum = nn(upper, dlevel, HIGH)
    drate = drate + dtail * fade + sign * dsum
    draw = drate * sigmoid(raw + dtb_ref[...])
    gheads_ref[0:1] += jnp.sum(draw, axis=0, keepdims=True)
    gheads_ref[1:2] += jnp.sum(rate * dsum, axis=0, keepdims=True) * sign

    dpre = jnp.concatenate([dwrite, dread, dxs], axis=1) * (sig * (1.0 + pre * (1.0 - sig)))
    longer = jnp.concatenate([dpre, halo_ref[...]], axis=0)
    halo_ref[...] = dpre[:8]
    cin = cin_ref[...].astype(F32)
    taps = taps_ref[...]
    gtaps_ref[KCONV : KCONV + 1] += jnp.sum(dpre, axis=0, keepdims=True)
    gtaps_ref[KCONV - 1 : KCONV] += jnp.sum(dpre * cin, axis=0, keepdims=True)
    dcin = taps[KCONV - 1 : KCONV] * dpre
    for index in range(KCONV - 1):
        delay = KCONV - 1 - index
        moved = jnp.where(remain >= delay, longer[delay : delay + BLOCK], 0.0)
        dcin = dcin + taps[index : index + 1] * moved
        gtaps_ref[index : index + 1] += jnp.sum(moved * cin, axis=0, keepdims=True)
    dcin_low = dcin.astype(BF)
    draw_low = draw.astype(BF)
    dnormed = (
        nt(dgate_ref[...], wg_ref[...]) + nt(dcin_low, wc_ref[...]) + nt(draw_low, wr_ref[...])
    )
    dnormed_ref[...] = dnormed.astype(BF)
    x = normed_ref[...]
    conv_total[...] += tn(x, dcin_low)
    raw_total[...] += tn(x, draw_low)

    @pl.when(step == pl.num_programs(0) - 1)
    def _():
        gconv_ref[...] = conv_total[...].astype(BF)
        graw_ref[...] = raw_total[...].astype(BF)


def backward(heads, normed, weights, vectors, spread, fold, pos, label_row, kept, dmixed, dgate):
    total = normed.shape[0]
    count = total // BLOCK
    width = heads * HEADDIM
    conv = PAIR + width
    wg, wc, wr = weights
    pre, cin, raw, states = kept
    block = lambda n: pl.BlockSpec((BLOCK, n), lambda i: (count - 1 - i, 0))
    return pl.pallas_call(
        functools.partial(backward_kernel, heads),
        grid=(count,),
        in_specs=[
            block(D),
            full((D, width)),
            full((D, conv)),
            full((D, LANES)),
            full((KCONV, conv)),
            full((1, LANES)),
            full((1, LANES)),
            full((1, width)),
            full((2 * LANES, width)),
            full((2 * width, LANES)),
            block(3),
            pl.BlockSpec((1, 1, BLOCK), lambda i: (count - 1 - i, 0, 0)),
            block(conv),
            block(conv),
            block(LANES),
            pl.BlockSpec((1, STATE, width), lambda i: (count - 1 - i, 0, 0)),
            block(width),
            block(width),
        ],
        out_specs=[
            block(D),
            full((D, conv)),
            full((D, LANES)),
            full((8, conv)),
            full((8, LANES)),
            full((1, width)),
        ],
        out_shape=[
            jax.ShapeDtypeStruct((total, D), BF),
            jax.ShapeDtypeStruct((D, conv), BF),
            jax.ShapeDtypeStruct((D, LANES), BF),
            jax.ShapeDtypeStruct((8, conv), F32),
            jax.ShapeDtypeStruct((8, LANES), F32),
            jax.ShapeDtypeStruct((1, width), F32),
        ],
        scratch_shapes=[
            pltpu.VMEM((STATE, width), F32),
            pltpu.VMEM((8, conv), F32),
            pltpu.VMEM((D, conv), F32),
            pltpu.VMEM((D, LANES), F32),
        ],
        compiler_params=params(),
        cost_estimate=cost(
            4 * total * D * (width + conv + LANES) * 2, total * D * 16, total * BLOCK * heads
        ),
        name="backward",
    )(
        normed,
        wg,
        wc,
        wr,
        vectors["taps"],
        vectors["dtb"],
        vectors["sign"],
        vectors["skip"],
        spread,
        fold,
        pos,
        label_row,
        pre,
        cin,
        raw,
        states,
        dmixed,
        dgate,
    )


class Plan:
    def __init__(self):
        self.seq = lax.axis_size("seq")
        self.shards = lax.axis_size("wshard")
        self.half = self.seq // 2
        self.core = lax.axis_index("section")
        self.z = lax.axis_index("seq")
        self.w = lax.axis_index("wshard")
        self.batch = self.z // self.half
        self.place = self.z % self.half
        self.rank = 2 * self.place + self.core

    def send(self, value, route, cores=(0, 1)):
        pairs = []
        for c in range(2):
            for z in range(self.seq):
                for w in range(self.shards):
                    target = route(c, z, w)
                    if c in cores and target is not None:
                        source = (c * self.seq + z) * self.shards + w
                        tc, tz, tw = target
                        pairs.append((source, (tc * self.seq + tz) * self.shards + tw))
        return lax.ppermute(value, AXES, pairs)

    def swap(self, value, cores=(0, 1)):
        return self.send(value, lambda c, z, w: (1 - c, z, w), cores)

    def turn(self, value, k, cores=(0, 1)):
        half = self.half
        return self.send(
            value, lambda c, z, w: (c, z // half * half + (z % half + k) % half, w), cores
        )

    def across(self, value, cores=(0, 1)):
        return self.send(value, lambda c, z, w: (c, (z + self.half) % self.seq, w), cores)

    def beside(self, value, bit, cores=(0, 1)):
        return self.send(value, lambda c, z, w: (c, z, w ^ bit), cores)

    def along(self, value, k):
        return self.send(value, lambda c, z, w: (c, z ^ k, w))

    def gather(self, value):
        rows, width = value.shape
        half = self.half
        whole = jnp.zeros((half, 2, rows, width), value.dtype)

        def put(whole, piece, place, core):
            return lax.dynamic_update_slice(whole, piece[None, None], (place, core, 0, 0))

        zero = jnp.int32(0)
        whole = put(whole, value, self.place, self.core)
        whole = put(whole, self.swap(value), self.place, 1 - self.core)
        for k in range(1, half):
            piece = self.turn(value, k)
            source = (self.place - k + half) % half + zero
            whole = put(whole, piece, source, self.core)
            whole = put(whole, self.swap(piece), source, 1 - self.core)
        return whole.reshape(half * 2 * rows, width)

    def scatter(self, value):
        half = self.half
        rows = value.shape[0] // (2 * half)
        parts = value.reshape(half, 2, rows, value.shape[1])

        def chip_sum(place):
            mine = pick(pick(parts, place), self.core)
            theirs = pick(pick(parts, place), 1 - self.core)
            return mine.astype(F32) + self.swap(theirs).astype(F32)

        arrived = []
        for k in range(1, half):
            term = chip_sum((self.place + k) % half).astype(BF)
            arrived.append(self.turn(term, k))
        total = chip_sum(self.place)
        for term in arrived:
            total = total + term.astype(F32)
        return total

    def total(self, value):
        chip = value + self.swap(value)
        whole = chip
        for k in range(1, self.half):
            whole = whole + self.turn(chip, k)
        return whole

    def shards_of(self, chunk, core):
        rows, width = chunk.shape
        low, high = chunk[: rows // 2], chunk[rows // 2 :]
        low_x = self.beside(low, 1, (core,))
        high_y = self.beside(high, 2, (core,))
        low_y = self.beside(jnp.stack([low, low_x]), 2, (core,))
        high_x = self.beside(jnp.stack([high, high_y]), 1, (core,))
        whole = jnp.zeros((self.shards, 2, rows // 2, width), chunk.dtype)

        def put(whole, piece, shard, part):
            return lax.dynamic_update_slice(whole, piece[None, None], (shard, part, 0, 0))

        w = self.w
        whole = put(whole, low, w, 0)
        whole = put(whole, low_x, w ^ 1, 0)
        whole = put(whole, low_y[0], w ^ 2, 0)
        whole = put(whole, low_y[1], w ^ 3, 0)
        whole = put(whole, high, w, 1)
        whole = put(whole, high_y, w ^ 2, 1)
        whole = put(whole, high_x[0], w ^ 1, 1)
        whole = put(whole, high_x[1], w ^ 3, 1)
        return whole.reshape(self.shards * rows, width)

    def reduce_shards(self, low, high):
        results = []
        firsts = []
        for value, bit in ((low, 1), (high, 2)):
            keep = jnp.stack([pick(value, self.w, 1), pick(value, self.w ^ (3 - bit), 1)])
            away = jnp.stack([pick(value, self.w ^ bit, 1), pick(value, self.w ^ 3, 1)])
            firsts.append((keep, self.beside(away, bit)))
        for (keep, came), bit in zip(firsts, (1, 2)):
            total = keep.astype(F32) + came.astype(F32)
            other = self.beside(total[1].astype(BF), 3 - bit)
            results.append((total[0] + other.astype(F32)).astype(BF))
        return results

    def spread_rows(self, value):
        pieces = [pick(value, self.z)]
        for k in range(1, self.seq):
            pieces.append(self.along(pick(value, self.z ^ k), k))
        half = self.half
        whole = jnp.zeros((half,) + value.shape[1:], BF)
        for k in range(half):
            term = (pieces[k].astype(F32) + pieces[k + half].astype(F32)).astype(BF)
            place = (self.place ^ k) if half > 1 else self.place
            whole = lax.dynamic_update_slice(whole, term[None], (place, 0, 0))
        return whole

    def home(self, value, batch, layer):
        half = self.half

        def route(c, z, w):
            if z // half != batch:
                return None
            return (layer, 2 * (z % half) + c, w)

        return self.send(value, route)


def pick(value, index, axis=0):
    return lax.dynamic_index_in_dim(value, index, axis, keepdims=False)


def cut(value, start, size, axis):
    return lax.dynamic_slice_in_dim(value, start, size, axis)


def prenorm(tokens, gain):
    scale = lax.rsqrt(jnp.mean(tokens * tokens, axis=-1, keepdims=True) + EPS)
    return tokens * scale * gain[None, :]


def on_device(
    ends_in,
    seq_lengths,
    deal_order,
    norm_w,
    in_w,
    conv_w,
    conv_b,
    dt_bias,
    a_log,
    d_skip,
    gnorm_w,
    out_w,
):
    plan = Plan()
    core = plan.core
    half = plan.half
    rank = plan.rank
    rows = ends_in.shape[3]
    total = rows * plan.seq
    count = total // BLOCK
    heads = HEADS // plan.seq
    width = heads * HEADDIM
    conv = PAIR + width

    order = pick(deal_order[:, 0], plan.batch)
    lengths = pick(seq_lengths[:, 0], plan.batch)
    ends = jnp.cumsum(lengths)
    at = iota((total,), 0)
    passed = at[:, None] >= ends[None, :]
    label = jnp.sum(passed.astype(jnp.int32), axis=1)
    begin = jnp.max(jnp.where(passed, ends[None, :], 0), axis=1)
    finish = jnp.min(jnp.where(passed, total, ends[None, :]), axis=1)
    pos = jnp.stack([label, at - begin, finish - 1 - at], axis=1)
    label_row = label.reshape(count, 1, BLOCK)
    order_row = order.reshape(1, total)
    order_col = order.reshape(total, 1)

    def collect(held, slot):
        only = (slot,)
        own = pick(held, plan.batch)
        far = plan.across(pick(held, 1 - plan.batch), only)
        whole = jnp.zeros((2, half, rows, D), BF)

        def put(whole, piece, batch, place):
            return lax.dynamic_update_slice(whole, piece[None, None], (batch, place, 0, 0))

        whole = put(whole, own, plan.batch, plan.place)
        whole = put(whole, far, 1 - plan.batch, plan.place)
        for k in range(1, half):
            source = (plan.place - k + half) % half
            whole = put(whole, plan.turn(own, k, only), plan.batch, source)
            whole = put(whole, plan.turn(far, k, only), 1 - plan.batch, source)
        whole = whole.reshape(total, D)
        return jnp.where(core == slot, whole, plan.swap(whole, only))

    held = ends_in[0, :, 0]
    started = collect(held, 0)
    held_later, _ = lax.optimization_barrier((held, started))
    cotangent = collect(held_later, 1)

    own_small = jnp.concatenate(
        [
            norm_w[0],
            conv_w[0].reshape(-1),
            conv_b[0],
            dt_bias[0],
            a_log[0],
            d_skip[0],
            gnorm_w[0],
        ]
    )
    other_small = plan.swap(own_small)

    def vectors_of(layer):
        flat = jnp.where(core == layer, own_small, other_small)
        sizes = (D, KCONV * (INNER + PAIR), INNER + PAIR, HEADS, HEADS, HEADS, INNER)
        pieces = []
        start = 0
        for size in sizes:
            pieces.append(flat[start : start + size])
            start += size
        gain, taps, bias, dtb, log_rate, skip, gated = pieces
        taps = taps.reshape(KCONV, INNER + PAIR)
        bias = bias.reshape(1, INNER + PAIR)

        def channels(value):
            return jnp.concatenate(
                [value[:, INNER:], cut(value, rank * width, width, 1)], axis=1
            )

        def lanes(value):
            own = cut(value, rank * heads, heads, 0)
            return jnp.pad(own, (0, LANES - heads)).reshape(1, LANES)

        return {
            "gain": gain,
            "taps": channels(taps),
            "bias": channels(bias),
            "dtb": lanes(dtb),
            "sign": lanes(-jnp.exp(log_rate)),
            "skip": jnp.repeat(cut(skip, rank * heads, heads, 0), HEADDIM).reshape(1, width),
            "gated": cut(gated, rank * width, width, 0).reshape(1, width),
        }

    vectors = [vectors_of(0), vectors_of(1)]

    first = 2 * width * plan.place
    gate_cols = cut(in_w[0], first, 2 * width, 1)
    input_cols = cut(in_w[0], INNER + first, 2 * width, 1)
    pair_cols = in_w[0][:, 2 * INNER : 2 * INNER + PAIR]
    raw_cols = cut(in_w[0], 2 * INNER + PAIR + 2 * heads * plan.place, 2 * heads, 1)
    raw_cols = jnp.pad(raw_cols, ((0, 0), (0, LANES - 2 * heads)))
    chunk = jnp.concatenate(
        [
            gate_cols[:, :width],
            input_cols[:, :width],
            gate_cols[:, width:],
            input_cols[:, width:],
            pair_cols,
            raw_cols,
        ],
        axis=1,
    )
    out_chunk = out_w[0]

    def in_weights(chunk, layer):
        whole = plan.shards_of(chunk, layer)
        shared = whole[:, 4 * width :]
        mine = whole[:, 2 * width * layer : 2 * width * (layer + 1)]
        theirs = whole[:, 2 * width * (1 - layer) : 2 * width * (2 - layer)]
        came = plan.swap(jnp.concatenate([theirs, shared], axis=1), (layer,))
        got = jnp.where(core == layer, jnp.concatenate([mine, shared], axis=1), came)
        raw = cut(got[:, 2 * width + PAIR :], core * heads, heads, 1)
        return (
            got[:, :width],
            jnp.concatenate([got[:, 2 * width : 2 * width + PAIR], got[:, width : 2 * width]], axis=1),
            jnp.pad(raw, ((0, 0), (0, LANES - heads))),
        )

    def out_weights(chunk, layer):
        whole = plan.shards_of(chunk, layer)
        mine = cut(whole, width * rank, width, 0)
        theirs = cut(whole, width * (rank ^ 1), width, 0)
        return jnp.where(core == layer, mine, plan.swap(theirs, (layer,)))

    in_first = in_weights(chunk, 0)
    out_chunk_0, _ = lax.optimization_barrier((out_chunk, in_first))
    out_first = out_weights(out_chunk_0, 0)
    chunk_1, _ = lax.optimization_barrier((chunk, out_first))
    in_second = in_weights(chunk_1, 1)
    out_chunk_1, _ = lax.optimization_barrier((out_chunk, in_second))
    out_second = out_weights(out_chunk_1, 1)
    in_parts = [in_first, in_second]
    out_parts = [out_first, out_second]

    channel_head = iota((LANES, width), 1) // HEADDIM
    hot = (channel_head == iota((LANES, width), 0)).astype(BF)
    spread = jnp.concatenate([hot, hot], axis=0)
    fold = jnp.concatenate([hot.T, hot.T], axis=0)

    own_rank = rank.reshape(1).astype(jnp.int32)
    tokens, normed = place(order_row, started, vectors[0]["gain"][None], True)
    saved = []
    unused = jnp.zeros((BLOCK, D), BF)
    own_tokens = cut(tokens, rank * rows, rows, 0)
    rank_tokens = [own_tokens]
    result = None
    for layer in range(2):
        gate, pre, cin, raw, mixed, states, square = forward(
            heads, normed, in_parts[layer], vectors[layer], spread, pos, label_row
        )
        square = plan.total(square)
        saved.append((normed, gate, pre, cin, raw, mixed, states, square))
        rest = unused if layer == 0 else own_tokens
        partial = project(
            mixed, gate, square, vectors[layer]["gated"], out_parts[layer], own_rank, rest, layer == 1
        )
        if layer == 0:
            summed = plan.scatter(partial) + own_tokens.astype(F32)
            own_tokens = summed.astype(BF)
            rank_tokens.append(own_tokens)
            mine = prenorm(own_tokens.astype(F32), vectors[1]["gain"]).astype(BF)
            normed = plan.gather(mine)
        else:
            result = plan.scatter(unplace(order_col, partial)).astype(BF)

    small_terms = []
    weight_terms = []
    (dout,) = place(order_row, cotangent, vectors[0]["gain"][None], False)
    own_dout = cut(dout, rank * rows, rows, 0)
    start_grad = None
    for layer in (1, 0):
        normed, gate, pre, cin, raw, mixed, states, square = saved[layer]
        gated = vectors[layer]["gated"]
        w = out_parts[layer]
        dot = plan.total(dots(dout, w, mixed, gate, gated))
        dmixed, dgate, ggated, gout, ggate = ungate(
            dout, w, mixed, gate, gated, square, dot, normed
        )
        dnormed, gconv, graw, gtaps, gheads, gskip = backward(
            heads,
            normed,
            in_parts[layer],
            vectors[layer],
            spread,
            fold,
            pos,
            label_row,
            (pre, cin, raw, states),
            dmixed,
            dgate,
        )
        if layer == 0:
            dnormed = unplace(order_col, dnormed)
            dout_rows = unplace(order_col, dout)
            own_dout = cut(dout_rows, rank * rows, rows, 0)
            own_in = cut(started, rank * rows, rows, 0)
        else:
            own_in = rank_tokens[1]
        grad = plan.scatter(dnormed)
        _, pull = jax.vjp(prenorm, own_in.astype(F32), vectors[layer]["gain"])
        dtokens, ggain = pull(grad)
        dtokens = (own_dout.astype(F32) + dtokens).astype(BF)
        if layer == 1:
            own_dout = dtokens
            dout = plan.gather(dtokens)
        else:
            start_grad = dtokens
        small_terms.append((ggain, gtaps, gheads, gskip, ggated))
        weight_terms.append((gout, ggate, gconv, graw))
    small_terms.reverse()
    weight_terms.reverse()

    def reduced_in(value):
        share = value.shape[0] // (plan.seq * plan.shards)
        parts = value.reshape(plan.seq, plan.shards, share, value.shape[1])
        cut_at = plan.seq // 2
        low, high = plan.reduce_shards(parts[:cut_at], parts[cut_at:])
        return plan.spread_rows(jnp.concatenate([low, high], axis=0))

    def reduced_out(value):
        share = value.shape[0] // plan.shards
        parts = value.reshape(1, plan.shards, share, D)
        low, high = plan.reduce_shards(parts[..., : D // 2], parts[..., D // 2 :])
        return jnp.concatenate([low[0], high[0]], axis=1)

    in_grads = []
    out_grads = []
    for layer in range(2):
        gout, ggate, gconv, graw = weight_terms[layer]
        gout = reduced_out(gout)
        out_grads.append(
            plan.home(gout, 0, layer).astype(F32) + plan.home(gout, 1, layer).astype(F32)
        )

        def both(value):
            came = plan.swap(value, (1 - layer,))
            return (value, came) if layer == 0 else (came, value)

        gate_even, gate_odd = both(reduced_in(ggate))
        rest_even, rest_odd = both(reduced_in(jnp.concatenate([gconv, graw], axis=1)))
        ranks = [(even, odd) for even, odd in zip(range(half), range(half))]
        gates = []
        inputs = []
        raws = []
        pair = None
        for even, odd in ranks:
            gates += [gate_even[even], gate_odd[odd]]
            for part in (rest_even[even], rest_odd[odd]):
                term = part[:, :PAIR].astype(F32)
                pair = term if pair is None else pair + term
                inputs.append(part[:, PAIR:conv])
                raws.append(part[:, conv : conv + heads])
        in_grads.append(
            jnp.concatenate(
                [item.astype(F32) for item in gates + inputs] + [pair] + [item.astype(F32) for item in raws],
                axis=1,
            )
        )
    g_in = jnp.where(core == 0, in_grads[0], in_grads[1])
    g_out = jnp.where(core == 0, out_grads[0], out_grads[1])

    def flat_of(terms):
        ggain, gtaps, gheads, gskip, ggated = terms
        zeros = lambda *shape: jnp.zeros(shape, F32)

        def channels(value):
            whole = zeros(value.shape[0], INNER)
            whole = lax.dynamic_update_slice_in_dim(whole, value[:, PAIR:], rank * width, 1)
            return jnp.concatenate([whole, value[:, :PAIR]], axis=1)

        def per_head(value):
            return lax.dynamic_update_slice_in_dim(zeros(HEADS), value, rank * heads, 0)

        spread_gated = lax.dynamic_update_slice_in_dim(zeros(INNER), ggated[0], rank * width, 0)
        return jnp.concatenate(
            [
                ggain,
                channels(gtaps[: KCONV + 1]).reshape(-1),
                per_head(gheads[0, :heads]),
                per_head(gheads[1, :heads]),
                per_head(jnp.sum(gskip.reshape(heads, HEADDIM), axis=1)),
                spread_gated,
            ]
        )

    flat = [flat_of(terms) for terms in small_terms]
    sums = jnp.where(core == 0, flat[0], flat[1]) + plan.swap(jnp.where(core == 0, flat[1], flat[0]))
    for bit in (1, 2):
        sums = sums + plan.beside(sums, bit)
    hop = 1
    while hop < plan.seq:
        sums = sums + plan.along(sums, hop)
        hop *= 2
    sizes = (D, (KCONV + 1) * (INNER + PAIR), HEADS, HEADS, HEADS, INNER)
    pieces = []
    start = 0
    for size in sizes:
        pieces.append(sums[start : start + size])
        start += size
    g_norm, g_taps, g_dt, g_log, g_skip, g_gated = pieces
    g_taps = g_taps.reshape(KCONV + 1, INNER + PAIR)

    outs = []
    for batch in range(2):
        last = plan.home(result, batch, 1)
        first_grad = plan.home(start_grad, batch, 0)
        outs.append(jnp.where(core == 1, last, first_grad).astype(F32))
    ends_out = jnp.stack(outs)[None, :, None]
    return (
        ends_out,
        g_norm[None],
        g_in[None],
        g_taps[None, :KCONV],
        g_taps[KCONV][None],
        g_dt[None],
        g_log[None],
        g_skip[None],
        g_gated[None],
        g_out[None],
    )


def solution(mesh):
    placed = (
        P("section", None, "wshard", "seq", None),
        P(None, "wshard", None),
        P(None, "wshard", None),
        P("section", None),
        P("section", "wshard", None),
        P("section", None, None),
        P("section", None),
        P("section", None),
        P("section", None),
        P("section", None),
        P("section", None),
        P("section", "wshard", None),
    )
    return jax.shard_map(
        on_device,
        mesh=mesh,
        in_specs=placed,
        out_specs=(
            P("section", None, "wshard", "seq", None),
            P("section", None),
            P("section", ("seq", "wshard"), None),
            P("section", None, None),
            P("section", None),
            P("section", None),
            P("section", None),
            P("section", None),
            P("section", None),
            P("section", ("seq", "wshard"), None),
        ),
        check_vma=False,
    )
```

time: 1920 us -> 783 us (0.41)
  waiting for transfers between devices: 643 us -> 203 us
  local copies, waits for them, and re-layouts: 409 us -> 107 us
  matrix products: 252 us -> 0 us
  blocking collectives: 223 us -> 0 us
  other arithmetic: 255 us -> 81.9 us
  Pallas kernels: 0 us -> 161 us
  starting transfers between devices: 71.3 us -> 213 us
  loops' own time: 34.8 us -> 0 us
    reduce_scatter x5 -> x0, waiting for transfers between devices: 381 us -> none  [the longest x1 381 us: on_device(): lax.psum_scatter(in_total, ('seq', 'wshard'), scatter_dimension=0, tiled=...]
    dot_general x150 -> x0, matrix products: 229 us -> none  [the longest x3 44.1 us: layer_backward(): in_grad = jnp.dot(normed.T, grad_proj, preferred_element_type=jnp.float32)]
    ppermute x4 -> x108, starting transfers between devices: 5.69 us -> 213 us  [send(): return lax.ppermute(value, AXES, pairs)]
    ppermute x4 -> x108, waiting for transfers between devices: 7.55 us -> 203 us  [send(): return lax.ppermute(value, AXES, pairs)]
    pallas_call x0 -> x15, Pallas kernels: none -> 161 us  [the longest x2 56.2 us: backward(): pl.pallas_call(functools.partial(backward_kernel, heads), grid=(count,),...]
    all_to_all x16 -> x0, waiting for transfers between devices: 161 us -> none  [the longest x3 70 us: layer_backward(): lax.all_to_all(grad_mixed.astype(jnp.bfloat16).reshape(tok_rows, shards,...]
    gather x27 -> x0, local copies, waits for them, and re-layouts: 96.8 us -> none  [the longest x3 15.2 us: layer_backward(): grad_dealt[inverse]]
    all_gather x3 -> x0, blocking collectives: 92.8 us -> none  [on_device(): pair_dealt = lax.all_gather(layer_pair_rows, 'seq', axis=0, tiled=True)]
  transfers between devices with their start and end apart: 27 -> 108, of which waited for: 15 -> 47; matrix products, arithmetic and copies ran while one was open for 16% -> 20% of each run, Pallas kernels for 0% -> 19%
where the time goes in v1:
time: 783 us; the launch traced here: 770 us
  starting transfers between devices  213 us (27%)
  waiting for transfers between devices  203 us (26%)
  Pallas kernels  161 us (21%)
  local copies, waits for them, and re-layouts  107 us (14%)
  other arithmetic  81.9 us (10%)
    ppermute x108, starting transfers between devices, send(): return lax.ppermute(value, AXES, pairs)  213 us
    ppermute x108, waiting for transfers between devices, send(): return lax.ppermute(value, AXES, pairs)  203 us
    pallas_call x2, Pallas kernels, backward(): pl.pallas_call(functools.partial(backward_kernel, heads), grid=(count,),...  56.2 us
    pallas_call x2, Pallas kernels, forward(): pl.pallas_call(functools.partial(forward_kernel, heads), grid=(count,), i...  32.6 us
    pallas_call x2, Pallas kernels, ungate(): pl.pallas_call(ungate_kernel, grid=(total // BLOCK,), in_specs=[block(D),...  19.9 us
    pallas_call x3, Pallas kernels, unplace(): pl.pallas_call(unplace_kernel, grid=(total // BLOCK,), in_specs=[pl.Block...  17.8 us
  transfers between devices with their start and end apart: 108, of which 47 were waited for; matrix products, arithmetic and copies ran while one was open for 20% of the time, Pallas kernels for 19%

profile of v1, /device:TPU:0, one launch (start us, length us, event | category | flops | bytes accessed | tf_op | source)
XLA Modules:
  0.0 770.4 jit_solution(12551762083059088940)
XLA Ops:
  8.0 4.8 collective-permute-start.5
  12.8 3.4 collective-permute-start.7
  16.2 5.1 collective-permute-done.5
  23.6 3.9 collective-permute-start.6
  31.1 3.4 collective-permute-start.8
  36.5 6.2 collective-permute-done.6
  51.7 3.8 concatenate.282
  59.8 4.5 collective-permute-start
  64.3 3.5 collective-permute-start.1
  79.4 3.4 collective-permute-start.12
  95.7 3.4 collective-permute-start.13
  109.0 5.5 collective-permute-done.13
  114.7 7.5 collective-permute-done.15
  141.2 6.0 place.2
  158.8 16.3 %forward.2 = (f32[1024,512]{1,0:T(8,128)}, f32[1024,768]{1,0:T(8,128)}, bf16[1024,768]{1,0:T(8,128)(2,1)}, bf16[1024,128]{1,0:T(8,128)(2,1)}, bf16[1024,512]{1,0...) custom-call(bf16[1024,1024]{1,0:T(8,128)(2,1)} %get-tuple-element.52.normed_ref, ...), custom_call_target="tpu_custom_call" | custom-call | flops 5905580032 | bytes 12582912 | tf_op jit(solution)/shard_map/forward/pallas_call | solution.py:248
  175.1 25.3 %collective-permute-start.10 = (f32[4,1,256]{2,1,0:T(1,128)}, f32[4,1,256]{2,1,0:T(1,128)S(1)}, u32[]{:S(2)}, u32[]{:S(2)}) collective-permute-start(f32[4,1,256]{2,1,0:T(1,128)} %get-tuple-element.55), channel_id=1, source_target_pairs={{0,16},{1,17},{2,18},{3,19},{4,20},{5,21},{6,22},{7,23},{8,24},{9,... | collective-permute-start | bytes 12296 | tf_op jit(solution)/shard_map/ppermute | solution.py:716
  207.2 6.1 project.2
  230.7 11.6 %collective-permute-done.19 = bf16[256,1024]{1,0:T(8,128)(2,1)S(1)} collective-permute-done((bf16[256,1024]{1,0:T(8,128)(2,1)S(1)}, bf16[256,1024]{1,0:T(8,128)(2,1)S(1)}, u32[]{:S(2)}, u32[]{:S(2)}) %collective-permute-start.19) | collective-permute-done | bytes 524320 | tf_op jit(solution)/shard_map/ppermute | solution.py:716
  254.6 4.6 collective-permute-done.21
  259.3 5.0 collective-permute-start.22
  272.3 16.3 %forward.3 = (f32[1024,512]{1,0:T(8,128)}, f32[1024,768]{1,0:T(8,128)}, bf16[1024,768]{1,0:T(8,128)(2,1)}, bf16[1024,128]{1,0:T(8,128)(2,1)}, bf16[1024,512]{1,0...) custom-call(bf16[1024,1024]{1,0:T(8,128)(2,1)} %bitcast.699, bf16[1024,512]{1,0:T(8,128)(2,1)} %get-tuple-element.148.wg_ref, ...), custom_call_target="tpu_custom_call" | custom-call | flops 5905580032 | bytes 12582912 | tf_op jit(solution)/shard_map/forward/pallas_call | solution.py:248
  288.7 21.5 %collective-permute-start.28 = (f32[4,1,256]{2,1,0:T(1,128)}, f32[4,1,256]{2,1,0:T(1,128)S(1)}, u32[]{:S(2)}, u32[]{:S(2)}) collective-permute-start(f32[4,1,256]{2,1,0:T(1,128)} %get-tuple-element.61), channel_id=1, source_target_pairs={{0,16},{1,17},{2,18},{3,19},{4,20},{5,21},{6,22},{7,23},{8,24},{9,... | collective-permute-start | bytes 12296 | tf_op jit(solution)/shard_map/ppermute | solution.py:716
  310.2 3.2 broadcast_select_fusion.x_ref
  313.5 5.4 place.3.dout_ref
  322.1 6.0 project.3.x_ref
  328.1 5.6 dots.2
  333.7 5.9 unplace.3
  344.8 10.0 %ungate.2 = (bf16[1024,512]{1,0:T(8,128)(2,1)}, bf16[1024,512]{1,0:T(8,128)(2,1)}, f32[1,512]{1,0:T(1,128)}, bf16[512,1024]{1,0:T(8,128)(2,1)}, bf16[1024,512]{1,0:T(8,128)(2,1)}) custom-call(bf16[1024,1024]{1,0:T(8,128)(2,1)} %place.3.dout_ref, bf16[512,1024]{1,0:T(8,128)(2,1)} %dynamic-slice_select_fusion.w_ref, ...), custom_call_target="tpu_custom_call" | custom-call | flops 3221225472 | bytes 9437184 | tf_op jit(solution)/shard_map/ungate/pallas_call | solution.py:417
  354.8 28.2 %backward.2 = (bf16[1024,1024]{1,0:T(8,128)(2,1)}, bf16[1024,768]{1,0:T(8,128)(2,1)}, bf16[1024,128]{1,0:T(8,128)(2,1)}, f32[8,768]{1,0:T(8,128)}, f32[8,128]{1,0:T(8,128)}, /*index=5*/f32[1,512]{1,0:T(1,128)}) custom-call(bf16[1024,1024]{1,0:T(8,128)(2,1)} %bitcast.701, bf16[1024,512]{1,0:T(8,128)(2,1)} %get-tuple-element.148.wg_ref, ...), custom_call_target="tpu_custom_call" | custom-call | flops 11811160064 | bytes 16777216 | tf_op jit(solution)/shard_map/backward/pallas_call | solution.py:622
  403.8 3.9 collective-permute-done.104
  408.4 11.5 %collective-permute-done.102 = bf16[2,1,128,512]{3,2,1,0:T(8,128)(2,1)S(1)} collective-permute-done((bf16[2,1,128,512]{3,2,1,0:T(8,128)(2,1)S(1)}, bf16[2,1,128,512]{3,2,1,0:T(8,128)(2,1)S(1)}, u32[]{:S(2)}, u32[]{:S(2)}) %collective-permute-start.102) | collective-permute-done | bytes 262176 | tf_op jit(solution)/shard_map/ppermute | solution.py:716
  421.6 3.4 collective-permute-done.81
  425.5 5.5 collective-permute-done.83
  431.7 4.4 collective-permute-done.105
  436.6 5.9 collective-permute-done.103
  443.8 3.5 collective-permute-start.84
  451.0 4.1 collective-permute-start.86
  460.8 4.8 collective-permute-done.89
  466.1 5.4 collective-permute-done.91
  476.1 3.9 collective-permute-done.92
  480.2 6.1 collective-permute-start.94
  498.8 5.9 collective-permute-done.37
  507.8 5.3 collective-permute-done.47
  521.3 10.4 %collective-permute-done.49 = bf16[256,1024]{1,0:T(8,128)(2,1)} collective-permute-done((bf16[256,1024]{1,0:T(8,128)(2,1)}, bf16[256,1024]{1,0:T(8,128)(2,1)}, u32[]{:S(2)}, u32[]{:S(2)}) %collective-permute-start.49) | collective-permute-done | bytes 524320 | tf_op jit(solution)/shard_map/ppermute | solution.py:716
  535.2 5.8 dots.3
  544.3 5.9 unplace.4
  550.8 9.9 %ungate.3 = (bf16[1024,512]{1,0:T(8,128)(2,1)}, bf16[1024,512]{1,0:T(8,128)(2,1)}, f32[1,512]{1,0:T(1,128)}, bf16[512,1024]{1,0:T(8,128)(2,1)}, bf16[1024,512]{1,0:T(8,128)(2,1)}) custom-call(bf16[1024,1024]{1,0:T(8,128)(2,1)} %bitcast.680, bf16[512,1024]{1,0:T(8,128)(2,1)} %dynamic-slice_select_fusion.1.w_ref, ...), custom_call_target="tpu_custom_call" | custom-call | flops 3221225472 | bytes 9437184 | tf_op jit(solution)/shard_map/ungate/pallas_call | solution.py:417
  560.7 28.1 %backward.3 = (bf16[1024,1024]{1,0:T(8,128)(2,1)}, bf16[1024,768]{1,0:T(8,128)(2,1)}, bf16[1024,128]{1,0:T(8,128)(2,1)}, f32[8,768]{1,0:T(8,128)}, f32[8,128]{1,0:T(8,128)}, /*index=5*/f32[1,512]{1,0:T(1,128)}) custom-call(bf16[1024,1024]{1,0:T(8,128)(2,1)} %get-tuple-element.52.normed_ref, bf16[1024,512]{1,0:T(8,128)(2,1)} %get-tuple-element.150.wg_ref, ...), custom_call_target="tpu_custom_call" | custom-call | flops 11811160064 | bytes 16777216 | tf_op jit(solution)/shard_map/backward/pallas_call | solution.py:622
  588.8 5.9 unplace.5
  616.5 4.7 collective-permute-done.98
  622.8 9.4 %collective-permute-done.96 = bf16[2,1,128,512]{3,2,1,0:T(8,128)(2,1)S(1)} collective-permute-done((bf16[2,1,128,512]{3,2,1,0:T(8,128)(2,1)S(1)}, bf16[2,1,128,512]{3,2,1,0:T(8,128)(2,1)S(1)}, u32[]{:S(2)}, u32[]{:S(2)}) %collective-permute-start.96) | collective-permute-done | bytes 262176 | tf_op jit(solution)/shard_map/ppermute | solution.py:716
  638.7 4.2 collective-permute-done.67
  644.3 3.5 collective-permute-done.99
  655.0 4.2 collective-permute-done.68
  662.2 5.4 collective-permute-done.74
  675.9 5.6 collective-permute-done.73
  683.0 6.1 collective-permute-done.75
  693.1 7.8 %collective-permute-done.76 = bf16[64,896]{1,0:T(8,128)(2,1)S(1)} collective-permute-done((bf16[64,896]{1,0:T(8,128)(2,1)S(1)}, bf16[64,896]{1,0:T(8,128)(2,1)S(1)}, u32[]{:S(2)}, u32[]{:S(2)}) %collective-permute-start.76) | collective-permute-done | bytes 114720 | tf_op jit(solution)/shard_map/ppermute | solution.py:716
  704.8 4.4 collective-permute-start.78
  713.4 6.6 collective-permute-start.55
  724.0 5.9 collective-permute-done.55
  732.8 3.6 collective-permute-start.59
  750.8 6.0 collective-permute-start.62
  760.5 3.7 collective-permute-done.63
  (693 shorter events, 311.1 us)
Async XLA Ops:
  8.0 13.4 %collective-permute-start.5 = (bf16[128,2432]{1,0:T(8,128)(2,1)}, bf16[128,2432]{1,0:T(8,128)(2,1)}, u32[]{:S(2)}, u32[]{:S(2)}) collective-permute-start(bf16[128,2432]{1,0:T(8,128)(2,1)} %get-tuple-element.172), channel_id=1, source_target_pairs={{0,1},{1,0},{2,3},{3,2},{4,5},{5,4},{6,7},{7,6},{8,9},{9,8},{10,11... | collective-permute-start | bytes 1867784 | tf_op jit(solution)/shard_map/ppermute | solution.py:716
  12.8 18.1 %collective-permute-start.7 = (bf16[128,2432]{1,0:T(8,128)(2,1)}, bf16[128,2432]{1,0:T(8,128)(2,1)S(1)}, u32[]{:S(2)}, u32[]{:S(2)}) collective-permute-start(bf16[128,2432]{1,0:T(8,128)(2,1)} %get-tuple-element.171), channel_id=1, source_target_pairs={{0,2},{1,3},{2,0},{3,1},{4,6},{5,7},{6,4},{7,5},{8,10},{9,11},{10,... | collective-permute-start | bytes 1867784 | tf_op jit(solution)/shard_map/ppermute | solution.py:716
  23.6 19.1 %collective-permute-start.6 = (bf16[2,128,2432]{2,1,0:T(8,128)(2,1)}, bf16[2,128,2432]{2,1,0:T(8,128)(2,1)}, u32[]{:S(2)}, u32[]{:S(2)}) collective-permute-start(bf16[2,128,2432]{2,1,0:T(8,128)(2,1)} %pad_maximum_fusion.3), channel_id=1, source_target_pairs={{0,2},{1,3},{2,0},{3,1},{4,6},{5,7},{6,4},{7,5},{8,10},{9,11},{10,... | collective-permute-start | bytes 3735560 | tf_op jit(solution)/shard_map/ppermute | solution.py:716
  31.1 18.8 %collective-permute-start.8 = (bf16[2,128,2432]{2,1,0:T(8,128)(2,1)S(1)}, bf16[2,128,2432]{2,1,0:T(8,128)(2,1)S(1)}, u32[]{:S(2)}, u32[]{:S(2)}) collective-permute-start(bf16[2,128,2432]{2,1,0:T(8,128)(2,1)S(1)} %pad_maximum_fusion.4), channel_id=1, source_target_pairs={{0,1},{1,0},{2,3},{3,2},{4,5},{5,4},{6,7},{7,6},{8,9},{9,8},{10,11... | collective-permute-start | bytes 3735560 | tf_op jit(solution)/shard_map/ppermute | solution.py:716
  55.5 17.5 %collective-permute-start.9 = (bf16[1024,1408]{1,0:T(8,128)(2,1)}, bf16[1024,1408]{1,0:T(8,128)(2,1)}, u32[]{:S(2)}, u32[]{:S(2)}) collective-permute-start(bf16[1024,1408]{1,0:T(8,128)(2,1)} %concatenate.282), channel_id=1, source_target_pairs={{0,16},{1,17},{2,18},{3,19},{4,20},{5,21},{6,22},{7,23},{8,24},{9,... | collective-permute-start | bytes 8650760 | tf_op jit(solution)/shard_map/ppermute | solution.py:716
  58.7 68.9 %collective-permute-start.4 = (f32[14688]{0:T(1024)S(1)}, f32[14688]{0:T(1024)}, u32[]{:S(2)}, u32[]{:S(2)}) collective-permute-start(f32[14688]{0:T(1024)S(1)} %concatenate.202), channel_id=1, source_target_pairs={{0,16},{1,17},{2,18},{3,19},{4,20},{5,21},{6,22},{7,23},{8,24},{9,... | collective-permute-start | bytes 176264 | tf_op jit(solution)/shard_map/ppermute | solution.py:716
  59.8 28.1 %collective-permute-start = (bf16[256,1024]{1,0:T(8,128)(2,1)}, bf16[256,1024]{1,0:T(8,128)(2,1)}, u32[]{:S(2)}, u32[]{:S(2)}) collective-permute-start(bf16[256,1024]{1,0:T(8,128)(2,1)} %get-tuple-element.192), channel_id=1, source_target_pairs={{0,8},{1,9},{2,10},{3,11},{4,12},{5,13},{6,14},{7,15},{8,0},{9,1},... | collective-permute-start | bytes 1572872 | tf_op jit(solution)/shard_map/ppermute | solution.py:716
  64.3 34.9 %collective-permute-start.1 = (bf16[256,1024]{1,0:T(8,128)(2,1)}, bf16[256,1024]{1,0:T(8,128)(2,1)}, u32[]{:S(2)}, u32[]{:S(2)}) collective-permute-start(bf16[256,1024]{1,0:T(8,128)(2,1)} %get-tuple-element.191), channel_id=1, source_target_pairs={{0,4},{1,5},{2,6},{3,7},{4,0},{5,1},{6,2},{7,3},{8,12},{9,13},{10,... | collective-permute-start | bytes 1572872 | tf_op jit(solution)/shard_map/ppermute | solution.py:716
  79.4 15.2 %collective-permute-start.12 = (bf16[256,1024]{1,0:T(8,128)(2,1)}, bf16[256,1024]{1,0:T(8,128)(2,1)}, u32[]{:S(2)}, u32[]{:S(2)}) collective-permute-start(bf16[256,1024]{1,0:T(8,128)(2,1)} %get-tuple-element.190), channel_id=1, source_target_pairs={{0,1},{1,0},{2,3},{3,2},{4,5},{5,4},{6,7},{7,6},{8,9},{9,8},{10,11... | collective-permute-start | bytes 1572872 | tf_op jit(solution)/shard_map/ppermute | solution.py:716
  87.9 13.1 %collective-permute-start.2 = (bf16[256,1024]{1,0:T(8,128)(2,1)}, bf16[256,1024]{1,0:T(8,128)(2,1)S(1)}, u32[]{:S(2)}, u32[]{:S(2)}) collective-permute-start(bf16[256,1024]{1,0:T(8,128)(2,1)} %collective-permute-done), channel_id=1, source_target_pairs={{0,4},{1,5},{2,6},{3,7},{4,0},{5,1},{6,2},{7,3},{8,12},{9,13},{10,... | collective-permute-start | bytes 1572872 | tf_op jit(solution)/shard_map/ppermute | solution.py:716
  92.2 13.1 %collective-permute-start.14 = (bf16[256,1024]{1,0:T(8,128)(2,1)S(1)}, bf16[256,1024]{1,0:T(8,128)(2,1)S(1)}, u32[]{:S(2)}, u32[]{:S(2)}) collective-permute-start(bf16[256,1024]{1,0:T(8,128)(2,1)S(1)} %copy-done.33), channel_id=1, source_target_pairs={{0,2},{1,3},{2,0},{3,1},{4,6},{5,7},{6,4},{7,5},{8,10},{9,11},{10,... | collective-permute-start | bytes 1572872 | tf_op jit(solution)/shard_map/ppermute | solution.py:716
  95.7 18.7 %collective-permute-start.13 = (bf16[2,256,1024]{2,1,0:T(8,128)(2,1)S(1)}, bf16[2,256,1024]{2,1,0:T(8,128)(2,1)S(1)}, u32[]{:S(2)}, u32[]{:S(2)}) collective-permute-start(bf16[2,256,1024]{2,1,0:T(8,128)(2,1)S(1)} %pad_maximum_fusion.7), channel_id=1, source_target_pairs={{0,2},{1,3},{2,0},{3,1},{4,6},{5,7},{6,4},{7,5},{8,10},{9,11},{10,... | collective-permute-start | bytes 3145736 | tf_op jit(solution)/shard_map/ppermute | solution.py:716
  101.9 36.2 %collective-permute-start.3 = (bf16[1024,1024]{1,0:T(8,128)(2,1)}, bf16[1024,1024]{1,0:T(8,128)(2,1)}, u32[]{:S(2)}, u32[]{:S(2)}) collective-permute-start(bf16[1024,1024]{1,0:T(8,128)(2,1)} %bitcast.9), channel_id=1, source_target_pairs={{0,16},{1,17},{2,18},{3,19},{4,20},{5,21},{6,22},{7,23},{8,24},{9,... | collective-permute-start | bytes 6291464 | tf_op jit(solution)/shard_map/ppermute | solution.py:716
  105.4 16.7 %collective-permute-start.15 = (bf16[2,256,1024]{2,1,0:T(8,128)(2,1)S(1)}, bf16[2,256,1024]{2,1,0:T(8,128)(2,1)S(1)}, u32[]{:S(2)}, u32[]{:S(2)}) collective-permute-start(bf16[2,256,1024]{2,1,0:T(8,128)(2,1)S(1)} %pad_maximum_fusion.8), channel_id=1, source_target_pairs={{0,1},{1,0},{2,3},{3,2},{4,5},{5,4},{6,7},{7,6},{8,9},{9,8},{10,11... | collective-permute-start | bytes 3145736 | tf_op jit(solution)/shard_map/ppermute | solution.py:716
  134.7 13.3 %collective-permute-start.23 = (bf16[128,2432]{1,0:T(8,128)(2,1)}, bf16[128,2432]{1,0:T(8,128)(2,1)}, u32[]{:S(2)}, u32[]{:S(2)}) collective-permute-start(bf16[128,2432]{1,0:T(8,128)(2,1)} %get-tuple-element.168), channel_id=1, source_target_pairs={{16,17},{17,16},{18,19},{19,18},{20,21},{21,20},{22,23},{23,22},{2... | collective-permute-start | bytes 1867784 | tf_op jit(solution)/shard_map/ppermute | solution.py:716
  157.5 86.9 %collective-permute-start.27 = (bf16[1024,1408]{1,0:T(8,128)(2,1)}, bf16[1024,1408]{1,0:T(8,128)(2,1)}, u32[]{:S(2)}, u32[]{:S(2)}) collective-permute-start(bf16[1024,1408]{1,0:T(8,128)(2,1)} %pad_maximum_fusion), channel_id=1, source_target_pairs={{16,0},{17,1},{18,2},{19,3},{20,4},{21,5},{22,6},{23,7},{24,8},{25... | collective-permute-start | bytes 8650760 | tf_op jit(solution)/shard_map/ppermute | solution.py:716
  175.1 26.3 %collective-permute-start.10 = (f32[4,1,256]{2,1,0:T(1,128)}, f32[4,1,256]{2,1,0:T(1,128)S(1)}, u32[]{:S(2)}, u32[]{:S(2)}) collective-permute-start(f32[4,1,256]{2,1,0:T(1,128)} %get-tuple-element.55), channel_id=1, source_target_pairs={{0,16},{1,17},{2,18},{3,19},{4,20},{5,21},{6,22},{7,23},{8,24},{9,... | collective-permute-start | bytes 12296 | tf_op jit(solution)/shard_map/ppermute | solution.py:716
  219.2 10.0 %collective-permute-start.39 = (bf16[256,1024]{1,0:T(8,128)(2,1)S(1)}, bf16[256,1024]{1,0:T(8,128)(2,1)S(1)}, u32[]{:S(2)}, u32[]{:S(2)}) collective-permute-start(bf16[256,1024]{1,0:T(8,128)(2,1)S(1)} %get-tuple-element.182), channel_id=1, source_target_pairs={{16,24},{17,25},{18,26},{19,27},{20,28},{21,29},{22,30},{23,31},{2... | collective-permute-start | bytes 1572872 | tf_op jit(solution)/shard_map/ppermute | solution.py:716
  219.9 10.8 %collective-permute-start.17 = (bf16[256,1024]{1,0:T(8,128)(2,1)}, bf16[256,1024]{1,0:T(8,128)(2,1)S(1)}, u32[]{:S(2)}, u32[]{:S(2)}) collective-permute-start(bf16[256,1024]{1,0:T(8,128)(2,1)} %get-tuple-element.159), channel_id=1, source_target_pairs={{0,16},{1,17},{2,18},{3,19},{4,20},{5,21},{6,22},{7,23},{8,24},{9,... | collective-permute-start | bytes 1572872 | tf_op jit(solution)/shard_map/ppermute | solution.py:716
  223.0 19.4 %collective-permute-start.19 = (bf16[256,1024]{1,0:T(8,128)(2,1)S(1)}, bf16[256,1024]{1,0:T(8,128)(2,1)S(1)}, u32[]{:S(2)}, u32[]{:S(2)}) collective-permute-start(bf16[256,1024]{1,0:T(8,128)(2,1)S(1)} %fusion.22), channel_id=1, source_target_pairs={{0,4},{1,5},{2,6},{3,7},{4,0},{5,1},{6,2},{7,3},{8,12},{9,13},{10,... | collective-permute-start | bytes 1572872 | tf_op jit(solution)/shard_map/ppermute | solution.py:716
  227.1 24.6 %collective-permute-start.40 = (bf16[256,1024]{1,0:T(8,128)(2,1)S(1)}, bf16[256,1024]{1,0:T(8,128)(2,1)S(1)}, u32[]{:S(2)}, u32[]{:S(2)}) collective-permute-start(bf16[256,1024]{1,0:T(8,128)(2,1)S(1)} %get-tuple-element.181), channel_id=1, source_target_pairs={{16,20},{17,21},{18,22},{19,23},{20,16},{21,17},{22,18},{23,19},{2... | collective-permute-start | bytes 1572872 | tf_op jit(solution)/shard_map/ppermute | solution.py:716
  229.2 23.3 %collective-permute-start.41 = (bf16[256,1024]{1,0:T(8,128)(2,1)S(1)}, bf16[256,1024]{1,0:T(8,128)(2,1)S(1)}, u32[]{:S(2)}, u32[]{:S(2)}) collective-permute-start(bf16[256,1024]{1,0:T(8,128)(2,1)S(1)} %collective-permute-done.39), channel_id=1, source_target_pairs={{16,20},{17,21},{18,22},{19,23},{20,16},{21,17},{22,18},{23,19},{2... | collective-permute-start | bytes 1572872 | tf_op jit(solution)/shard_map/ppermute | solution.py:716
  244.3 20.0 %collective-permute-start.20 = (bf16[256,1024]{1,0:T(8,128)(2,1)S(1)}, bf16[256,1024]{1,0:T(8,128)(2,1)S(1)}, u32[]{:S(2)}, u32[]{:S(2)}) collective-permute-start(bf16[256,1024]{1,0:T(8,128)(2,1)S(1)} %get-tuple-element.144), channel_id=1, source_target_pairs={{0,16},{1,17},{2,18},{3,19},{4,20},{5,21},{6,22},{7,23},{8,24},{9,... | collective-permute-start | bytes 1572872 | tf_op jit(solution)/shard_map/ppermute | solution.py:716
  244.3 14.9 %collective-permute-start.21 = (bf16[256,1024]{1,0:T(8,128)(2,1)S(1)}, bf16[256,1024]{1,0:T(8,128)(2,1)S(1)}, u32[]{:S(2)}, u32[]{:S(2)}) collective-permute-start(bf16[256,1024]{1,0:T(8,128)(2,1)S(1)} %get-tuple-element.144), channel_id=1, source_target_pairs={{0,4},{1,5},{2,6},{3,7},{4,0},{5,1},{6,2},{7,3},{8,12},{9,13},{10,... | collective-permute-start | bytes 1572872 | tf_op jit(solution)/shard_map/ppermute | solution.py:716
  250.9 14.0 %collective-permute-start.30 = (bf16[256,1024]{1,0:T(8,128)(2,1)S(1)}, bf16[256,1024]{1,0:T(8,128)(2,1)S(1)}, u32[]{:S(2)}, u32[]{:S(2)}) collective-permute-start(bf16[256,1024]{1,0:T(8,128)(2,1)S(1)} %get-tuple-element.186), channel_id=1, source_target_pairs={{16,17},{17,16},{18,19},{19,18},{20,21},{21,20},{22,23},{23,22},{2... | collective-permute-start | bytes 1572872 | tf_op jit(solution)/shard_map/ppermute | solution.py:716
  253.4 56.9 %collective-permute-start.42 = (bf16[1024,1024]{1,0:T(8,128)(2,1)}, bf16[1024,1024]{1,0:T(8,128)(2,1)S(1)}, u32[]{:S(2)}, u32[]{:S(2)}) collective-permute-start(bf16[1024,1024]{1,0:T(8,128)(2,1)} %bitcast.109), channel_id=1, source_target_pairs={{16,0},{17,1},{18,2},{19,3},{20,4},{21,5},{22,6},{23,7},{24,8},{25... | collective-permute-start | bytes 6291464 | tf_op jit(solution)/shard_map/ppermute | solution.py:716
  270.6 48.9 %collective-permute-start.34 = (bf16[512,1024]{1,0:T(8,128)(2,1)S(1)}, bf16[512,1024]{1,0:T(8,128)(2,1)S(1)}, u32[]{:S(2)}, u32[]{:S(2)}) collective-permute-start(bf16[512,1024]{1,0:T(8,128)(2,1)S(1)} %constant_dynamic-slice_fusion.16), channel_id=1, source_target_pairs={{16,0},{17,1},{18,2},{19,3},{20,4},{21,5},{22,6},{23,7},{24,8},{25... | collective-permute-start | bytes 3145736 | tf_op jit(solution)/shard_map/ppermute | solution.py:716
  288.7 24.7 %collective-permute-start.28 = (f32[4,1,256]{2,1,0:T(1,128)}, f32[4,1,256]{2,1,0:T(1,128)S(1)}, u32[]{:S(2)}, u32[]{:S(2)}) collective-permute-start(f32[4,1,256]{2,1,0:T(1,128)} %get-tuple-element.61), channel_id=1, source_target_pairs={{0,16},{1,17},{2,18},{3,19},{4,20},{5,21},{6,22},{7,23},{8,24},{9,... | collective-permute-start | bytes 12296 | tf_op jit(solution)/shard_map/ppermute | solution.py:716
  343.7 111.4 %collective-permute-start.36 = (bf16[256,1024]{1,0:T(8,128)(2,1)}, bf16[256,1024]{1,0:T(8,128)(2,1)S(1)}, u32[]{:S(2)}, u32[]{:S(2)}) collective-permute-start(bf16[256,1024]{1,0:T(8,128)(2,1)} %get-tuple-element.158), channel_id=1, source_target_pairs={{0,16},{1,17},{2,18},{3,19},{4,20},{5,21},{6,22},{7,23},{8,24},{9,... | collective-permute-start | bytes 1572872 | tf_op jit(solution)/shard_map/ppermute | solution.py:716
  343.9 152.9 %collective-permute-start.35 = (bf16[256,1024]{1,0:T(8,128)(2,1)S(1)}, bf16[256,1024]{1,0:T(8,128)(2,1)S(1)}, u32[]{:S(2)}, u32[]{:S(2)}) collective-permute-start(bf16[256,1024]{1,0:T(8,128)(2,1)S(1)} %get-tuple-element.157), channel_id=1, source_target_pairs={{0,16},{1,17},{2,18},{3,19},{4,20},{5,21},{6,22},{7,23},{8,24},{9,... | collective-permute-start | bytes 1572872 | tf_op jit(solution)/shard_map/ppermute | solution.py:716
  385.2 87.8 %collective-permute-start.46 = (bf16[256,1024]{1,0:T(8,128)(2,1)}, bf16[256,1024]{1,0:T(8,128)(2,1)}, u32[]{:S(2)}, u32[]{:S(2)}) collective-permute-start(bf16[256,1024]{1,0:T(8,128)(2,1)} %get-tuple-element.156), channel_id=1, source_target_pairs={{0,16},{1,17},{2,18},{3,19},{4,20},{5,21},{6,22},{7,23},{8,24},{9,... | collective-permute-start | bytes 1572872 | tf_op jit(solution)/shard_map/ppermute | solution.py:716
  387.0 12.5 %collective-permute-start.80 = (bf16[2,2,64,512]{3,2,1,0:T(8,128)(2,1)}, bf16[2,2,64,512]{3,2,1,0:T(8,128)(2,1)}, u32[]{:S(2)}, u32[]{:S(2)}) collective-permute-start(bf16[2,2,64,512]{3,2,1,0:T(8,128)(2,1)} %pad_maximum_fusion.17), channel_id=1, source_target_pairs={{0,1},{1,0},{2,3},{3,2},{4,5},{5,4},{6,7},{7,6},{8,9},{9,8},{10,11... | collective-permute-start | bytes 786440 | tf_op jit(solution)/shard_map/ppermute | solution.py:716
  389.2 13.0 %collective-permute-start.82 = (bf16[2,2,64,512]{3,2,1,0:T(8,128)(2,1)}, bf16[2,2,64,512]{3,2,1,0:T(8,128)(2,1)}, u32[]{:S(2)}, u32[]{:S(2)}) collective-permute-start(bf16[2,2,64,512]{3,2,1,0:T(8,128)(2,1)} %pad_maximum_fusion.18), channel_id=1, source_target_pairs={{0,2},{1,3},{2,0},{3,1},{4,6},{5,7},{6,4},{7,5},{8,10},{9,11},{10,... | collective-permute-start | bytes 786440 | tf_op jit(solution)/shard_map/ppermute | solution.py:716
  402.2 41.6 %collective-permute-start.88 = (bf16[2,2,64,896]{3,2,1,0:T(8,128)(2,1)}, bf16[2,2,64,896]{3,2,1,0:T(8,128)(2,1)S(1)}, u32[]{:S(2)}, u32[]{:S(2)}) collective-permute-start(bf16[2,2,64,896]{3,2,1,0:T(8,128)(2,1)} %pad_maximum_fusion.13), channel_id=1, source_target_pairs={{0,1},{1,0},{2,3},{3,2},{4,5},{5,4},{6,7},{7,6},{8,9},{9,8},{10,11... | collective-permute-start | bytes 1376264 | tf_op jit(solution)/shard_map/ppermute | solution.py:716
  407.7 12.2 %collective-permute-start.102 = (bf16[2,1,128,512]{3,2,1,0:T(8,128)(2,1)S(1)}, bf16[2,1,128,512]{3,2,1,0:T(8,128)(2,1)S(1)}, u32[]{:S(2)}, u32[]{:S(2)}) collective-permute-start(bf16[2,1,128,512]{3,2,1,0:T(8,128)(2,1)S(1)} %copy-done.47), channel_id=1, source_target_pairs={{0,1},{1,0},{2,3},{3,2},{4,5},{5,4},{6,7},{7,6},{8,9},{9,8},{10,11... | collective-permute-start | bytes 786440 | tf_op jit(solution)/shard_map/ppermute | solution.py:716
  442.5 8.5 %collective-permute-start.90 = (bf16[2,2,64,896]{3,2,1,0:T(8,128)(2,1)S(1)}, bf16[2,2,64,896]{3,2,1,0:T(8,128)(2,1)S(1)}, u32[]{:S(2)}, u32[]{:S(2)}) collective-permute-start(bf16[2,2,64,896]{3,2,1,0:T(8,128)(2,1)S(1)} %copy-done.44), channel_id=1, source_target_pairs={{0,2},{1,3},{2,0},{3,1},{4,6},{5,7},{6,4},{7,5},{8,10},{9,11},{10,... | collective-permute-start | bytes 1376264 | tf_op jit(solution)/shard_map/ppermute | solution.py:716
  450.2 57.6 %collective-permute-start.45 = (bf16[256,1024]{1,0:T(8,128)(2,1)S(1)}, bf16[256,1024]{1,0:T(8,128)(2,1)S(1)}, u32[]{:S(2)}, u32[]{:S(2)}) collective-permute-start(bf16[256,1024]{1,0:T(8,128)(2,1)S(1)} %get-tuple-element.155), channel_id=1, source_target_pairs={{0,16},{1,17},{2,18},{3,19},{4,20},{5,21},{6,22},{7,23},{8,24},{9,... | collective-permute-start | bytes 1572872 | tf_op jit(solution)/shard_map/ppermute | solution.py:716
  457.5 245.1 %collective-permute-start.107 = (bf16[128,1024]{1,0:T(8,128)(2,1)}, bf16[128,1024]{1,0:T(8,128)(2,1)}, u32[]{:S(2)}, u32[]{:S(2)}) collective-permute-start(bf16[128,1024]{1,0:T(8,128)(2,1)} %pad_maximum_fusion.24), channel_id=1, source_target_pairs={{8,16},{9,17},{10,18},{11,19},{12,24},{13,25},{14,26},{15,27},{24,... | collective-permute-start | bytes 786440 | tf_op jit(solution)/shard_map/ppermute | solution.py:716
  471.6 14.7 %collective-permute-start.87 = (bf16[2,64,512]{2,1,0:T(8,128)(2,1)S(1)}, bf16[2,64,512]{2,1,0:T(8,128)(2,1)S(1)}, u32[]{:S(2)}, u32[]{:S(2)}) collective-permute-start(bf16[2,64,512]{2,1,0:T(8,128)(2,1)S(1)} %fusion.113), channel_id=1, source_target_pairs={{0,16},{1,17},{2,18},{3,19},{4,20},{5,21},{6,22},{7,23},{8,24},{9,... | collective-permute-start | bytes 393224 | tf_op jit(solution)/shard_map/ppermute | solution.py:716
  480.2 9.7 %collective-permute-start.94 = (bf16[64,896]{1,0:T(8,128)(2,1)S(1)}, bf16[64,896]{1,0:T(8,128)(2,1)S(1)}, u32[]{:S(2)}, u32[]{:S(2)}) collective-permute-start(bf16[64,896]{1,0:T(8,128)(2,1)S(1)} %get-tuple-element.243), channel_id=1, source_target_pairs={{0,12},{1,13},{2,14},{3,15},{4,8},{5,9},{6,10},{7,11},{8,4},{9,5},... | collective-permute-start | bytes 344072 | tf_op jit(solution)/shard_map/ppermute | solution.py:716
  489.9 14.9 %collective-permute-start.37 = (bf16[256,1024]{1,0:T(8,128)(2,1)S(1)}, bf16[256,1024]{1,0:T(8,128)(2,1)S(1)}, u32[]{:S(2)}, u32[]{:S(2)}) collective-permute-start(bf16[256,1024]{1,0:T(8,128)(2,1)S(1)} %fusion.19), channel_id=1, source_target_pairs={{0,4},{1,5},{2,6},{3,7},{4,0},{5,1},{6,2},{7,3},{8,12},{9,13},{10,... | collective-permute-start | bytes 1572872 | tf_op jit(solution)/shard_map/ppermute | solution.py:716
  492.4 20.7 %collective-permute-start.47 = (bf16[256,1024]{1,0:T(8,128)(2,1)S(1)}, bf16[256,1024]{1,0:T(8,128)(2,1)S(1)}, u32[]{:S(2)}, u32[]{:S(2)}) collective-permute-start(bf16[256,1024]{1,0:T(8,128)(2,1)S(1)} %fusion.17), channel_id=1, source_target_pairs={{0,4},{1,5},{2,6},{3,7},{4,0},{5,1},{6,2},{7,3},{8,12},{9,13},{10,... | collective-permute-start | bytes 1572872 | tf_op jit(solution)/shard_map/ppermute | solution.py:716
  496.8 207.9 %collective-permute-start.106 = (bf16[128,1024]{1,0:T(8,128)(2,1)}, bf16[128,1024]{1,0:T(8,128)(2,1)}, u32[]{:S(2)}, u32[]{:S(2)}) collective-permute-start(bf16[128,1024]{1,0:T(8,128)(2,1)} %pad_maximum_fusion.24), channel_id=1, source_target_pairs={{0,16},{1,17},{2,18},{3,19},{4,24},{5,25},{6,26},{7,27},{16,20},{1... | collective-permute-start | bytes 786440 | tf_op jit(solution)/shard_map/ppermute | solution.py:716
  504.7 14.2 %collective-permute-start.95 = (bf16[2,64,896]{2,1,0:T(8,128)(2,1)S(1)}, bf16[2,64,896]{2,1,0:T(8,128)(2,1)}, u32[]{:S(2)}, u32[]{:S(2)}) collective-permute-start(bf16[2,64,896]{2,1,0:T(8,128)(2,1)S(1)} %fusion.89), channel_id=1, source_target_pairs={{0,16},{1,17},{2,18},{3,19},{4,20},{5,21},{6,22},{7,23},{8,24},{9,... | collective-permute-start | bytes 688136 | tf_op jit(solution)/shard_map/ppermute | solution.py:716
  516.3 16.0 %collective-permute-start.48 = (bf16[256,1024]{1,0:T(8,128)(2,1)}, bf16[256,1024]{1,0:T(8,128)(2,1)S(1)}, u32[]{:S(2)}, u32[]{:S(2)}) collective-permute-start(bf16[256,1024]{1,0:T(8,128)(2,1)} %get-tuple-element.142), channel_id=1, source_target_pairs={{0,16},{1,17},{2,18},{3,19},{4,20},{5,21},{6,22},{7,23},{8,24},{9,... | collective-permute-start | bytes 1572872 | tf_op jit(solution)/shard_map/ppermute | solution.py:716
  516.3 15.4 %collective-permute-start.49 = (bf16[256,1024]{1,0:T(8,128)(2,1)}, bf16[256,1024]{1,0:T(8,128)(2,1)}, u32[]{:S(2)}, u32[]{:S(2)}) collective-permute-start(bf16[256,1024]{1,0:T(8,128)(2,1)} %get-tuple-element.142), channel_id=1, source_target_pairs={{0,4},{1,5},{2,6},{3,7},{4,0},{5,1},{6,2},{7,3},{8,12},{9,13},{10,... | collective-permute-start | bytes 1572872 | tf_op jit(solution)/shard_map/ppermute | solution.py:716
  597.1 76.3 %collective-permute-start.54 = (bf16[256,1024]{1,0:T(8,128)(2,1)}, bf16[256,1024]{1,0:T(8,128)(2,1)}, u32[]{:S(2)}, u32[]{:S(2)}) collective-permute-start(bf16[256,1024]{1,0:T(8,128)(2,1)} %get-tuple-element.154), channel_id=1, source_target_pairs={{0,16},{1,17},{2,18},{3,19},{4,20},{5,21},{6,22},{7,23},{8,24},{9,... | collective-permute-start | bytes 1572872 | tf_op jit(solution)/shard_map/ppermute | solution.py:716
  598.9 14.0 %collective-permute-start.64 = (bf16[2,2,64,512]{3,2,1,0:T(8,128)(2,1)}, bf16[2,2,64,512]{3,2,1,0:T(8,128)(2,1)}, u32[]{:S(2)}, u32[]{:S(2)}) collective-permute-start(bf16[2,2,64,512]{3,2,1,0:T(8,128)(2,1)} %pad_maximum_fusion.15), channel_id=1, source_target_pairs={{0,1},{1,0},{2,3},{3,2},{4,5},{5,4},{6,7},{7,6},{8,9},{9,8},{10,11... | collective-permute-start | bytes 786440 | tf_op jit(solution)/shard_map/ppermute | solution.py:716
  600.2 13.8 %collective-permute-start.66 = (bf16[2,2,64,512]{3,2,1,0:T(8,128)(2,1)}, bf16[2,2,64,512]{3,2,1,0:T(8,128)(2,1)}, u32[]{:S(2)}, u32[]{:S(2)}) collective-permute-start(bf16[2,2,64,512]{3,2,1,0:T(8,128)(2,1)} %pad_maximum_fusion.16), channel_id=1, source_target_pairs={{0,2},{1,3},{2,0},{3,1},{4,6},{5,7},{6,4},{7,5},{8,10},{9,11},{10,... | collective-permute-start | bytes 786440 | tf_op jit(solution)/shard_map/ppermute | solution.py:716
  614.0 46.6 %collective-permute-start.72 = (bf16[2,2,64,896]{3,2,1,0:T(8,128)(2,1)}, bf16[2,2,64,896]{3,2,1,0:T(8,128)(2,1)S(1)}, u32[]{:S(2)}, u32[]{:S(2)}) collective-permute-start(bf16[2,2,64,896]{3,2,1,0:T(8,128)(2,1)} %pad_maximum_fusion.11), channel_id=1, source_target_pairs={{0,1},{1,0},{2,3},{3,2},{4,5},{5,4},{6,7},{7,6},{8,9},{9,8},{10,11... | collective-permute-start | bytes 1376264 | tf_op jit(solution)/shard_map/ppermute | solution.py:716
  621.2 11.0 %collective-permute-start.96 = (bf16[2,1,128,512]{3,2,1,0:T(8,128)(2,1)S(1)}, bf16[2,1,128,512]{3,2,1,0:T(8,128)(2,1)S(1)}, u32[]{:S(2)}, u32[]{:S(2)}) collective-permute-start(bf16[2,1,128,512]{3,2,1,0:T(8,128)(2,1)S(1)} %copy-done.46), channel_id=1, source_target_pairs={{0,1},{1,0},{2,3},{3,2},{4,5},{5,4},{6,7},{7,6},{8,9},{9,8},{10,11... | collective-permute-start | bytes 786440 | tf_op jit(solution)/shard_map/ppermute | solution.py:716
  659.2 8.5 %collective-permute-start.74 = (bf16[2,2,64,896]{3,2,1,0:T(8,128)(2,1)S(1)}, bf16[2,2,64,896]{3,2,1,0:T(8,128)(2,1)S(1)}, u32[]{:S(2)}, u32[]{:S(2)}) collective-permute-start(bf16[2,2,64,896]{3,2,1,0:T(8,128)(2,1)S(1)} %copy-done.43), channel_id=1, source_target_pairs={{0,2},{1,3},{2,0},{3,1},{4,6},{5,7},{6,4},{7,5},{8,10},{9,11},{10,... | collective-permute-start | bytes 1376264 | tf_op jit(solution)/shard_map/ppermute | solution.py:716
  667.8 37.0 %collective-permute-start.101 = (bf16[128,1024]{1,0:T(8,128)(2,1)S(1)}, bf16[128,1024]{1,0:T(8,128)(2,1)S(1)}, u32[]{:S(2)}, u32[]{:S(2)}) collective-permute-start(bf16[128,1024]{1,0:T(8,128)(2,1)S(1)} %pad_maximum_fusion.21), channel_id=1, source_target_pairs={{8,0},{9,1},{10,2},{11,3},{12,8},{13,9},{14,10},{15,11},{24,4},{25... | collective-permute-start | bytes 786440 | tf_op jit(solution)/shard_map/ppermute | solution.py:716
  671.9 37.2 %collective-permute-start.100 = (bf16[128,1024]{1,0:T(8,128)(2,1)S(1)}, bf16[128,1024]{1,0:T(8,128)(2,1)S(1)}, u32[]{:S(2)}, u32[]{:S(2)}) collective-permute-start(bf16[128,1024]{1,0:T(8,128)(2,1)S(1)} %pad_maximum_fusion.21), channel_id=1, source_target_pairs={{0,0},{1,1},{2,2},{3,3},{4,8},{5,9},{6,10},{7,11},{16,4},{17,5},{1... | collective-permute-start | bytes 786440 | tf_op jit(solution)/shard_map/ppermute | solution.py:716
  692.4 8.6 %collective-permute-start.76 = (bf16[64,896]{1,0:T(8,128)(2,1)S(1)}, bf16[64,896]{1,0:T(8,128)(2,1)S(1)}, u32[]{:S(2)}, u32[]{:S(2)}) collective-permute-start(bf16[64,896]{1,0:T(8,128)(2,1)S(1)} %fusion.107), channel_id=1, source_target_pairs={{0,8},{1,9},{2,10},{3,11},{4,12},{5,13},{6,14},{7,15},{8,0},{9,1},... | collective-permute-start | bytes 344072 | tf_op jit(solution)/shard_map/ppermute | solution.py:716
  700.9 66.4 %collective-permute-start.57 = (bf16[256,1024]{1,0:T(8,128)(2,1)}, bf16[256,1024]{1,0:T(8,128)(2,1)}, u32[]{:S(2)}, u32[]{:S(2)}) collective-permute-start(bf16[256,1024]{1,0:T(8,128)(2,1)} %fusion.21), channel_id=1, source_target_pairs={{8,16},{9,17},{10,18},{11,19},{12,24},{13,25},{14,26},{15,27},{24,... | collective-permute-start | bytes 1572872 | tf_op jit(solution)/shard_map/ppermute | solution.py:716
  702.6 65.8 %collective-permute-start.38 = (bf16[256,1024]{1,0:T(8,128)(2,1)}, bf16[256,1024]{1,0:T(8,128)(2,1)}, u32[]{:S(2)}, u32[]{:S(2)}) collective-permute-start(bf16[256,1024]{1,0:T(8,128)(2,1)} %fusion.21), channel_id=1, source_target_pairs={{0,16},{1,17},{2,18},{3,19},{4,24},{5,25},{6,26},{7,27},{16,20},{1... | collective-permute-start | bytes 1572872 | tf_op jit(solution)/shard_map/ppermute | solution.py:716
  704.7 19.2 %collective-permute-start.53 = (bf16[256,1024]{1,0:T(8,128)(2,1)S(1)}, bf16[256,1024]{1,0:T(8,128)(2,1)S(1)}, u32[]{:S(2)}, u32[]{:S(2)}) collective-permute-start(bf16[256,1024]{1,0:T(8,128)(2,1)S(1)} %copy-done.32), channel_id=1, source_target_pairs={{0,16},{1,17},{2,18},{3,19},{4,20},{5,21},{6,22},{7,23},{8,24},{9,... | collective-permute-start | bytes 1572872 | tf_op jit(solution)/shard_map/ppermute | solution.py:716
  704.8 8.7 %collective-permute-start.78 = (bf16[64,896]{1,0:T(8,128)(2,1)S(1)}, bf16[64,896]{1,0:T(8,128)(2,1)S(1)}, u32[]{:S(2)}, u32[]{:S(2)}) collective-permute-start(bf16[64,896]{1,0:T(8,128)(2,1)S(1)} %get-tuple-element.246), channel_id=1, source_target_pairs={{0,12},{1,13},{2,14},{3,15},{4,8},{5,9},{6,10},{7,11},{8,4},{9,5},... | collective-permute-start | bytes 344072 | tf_op jit(solution)/shard_map/ppermute | solution.py:716
  709.1 10.9 %collective-permute-start.77 = (bf16[64,896]{1,0:T(8,128)(2,1)S(1)}, bf16[64,896]{1,0:T(8,128)(2,1)S(1)}, u32[]{:S(2)}, u32[]{:S(2)}) collective-permute-start(bf16[64,896]{1,0:T(8,128)(2,1)S(1)} %get-tuple-element.244), channel_id=1, source_target_pairs={{0,4},{1,5},{2,6},{3,7},{4,0},{5,1},{6,2},{7,3},{8,12},{9,13},{10,... | collective-permute-start | bytes 344072 | tf_op jit(solution)/shard_map/ppermute | solution.py:716
  713.4 16.5 %collective-permute-start.55 = (bf16[256,1024]{1,0:T(8,128)(2,1)S(1)}, bf16[256,1024]{1,0:T(8,128)(2,1)S(1)}, u32[]{:S(2)}, u32[]{:S(2)}) collective-permute-start(bf16[256,1024]{1,0:T(8,128)(2,1)S(1)} %fusion.15), channel_id=1, source_target_pairs={{0,4},{1,5},{2,6},{3,7},{4,0},{5,1},{6,2},{7,3},{8,12},{9,13},{10,... | collective-permute-start | bytes 1572872 | tf_op jit(solution)/shard_map/ppermute | solution.py:716
  720.1 22.1 %collective-permute-start.79 = (bf16[2,64,896]{2,1,0:T(8,128)(2,1)S(1)}, bf16[2,64,896]{2,1,0:T(8,128)(2,1)}, u32[]{:S(2)}, u32[]{:S(2)}) collective-permute-start(bf16[2,64,896]{2,1,0:T(8,128)(2,1)S(1)} %fusion.87), channel_id=1, source_target_pairs={{16,0},{17,1},{18,2},{19,3},{20,4},{21,5},{22,6},{23,7},{24,8},{25... | collective-permute-start | bytes 688136 | tf_op jit(solution)/shard_map/ppermute | solution.py:716
  739.2 28.1 %collective-permute-start.58 = (bf16[256,1024]{1,0:T(8,128)(2,1)}, bf16[256,1024]{1,0:T(8,128)(2,1)}, u32[]{:S(2)}, u32[]{:S(2)}) collective-permute-start(bf16[256,1024]{1,0:T(8,128)(2,1)} %fusion.7), channel_id=1, source_target_pairs={{8,0},{9,1},{10,2},{11,3},{12,8},{13,9},{14,10},{15,11},{24,4},{25... | collective-permute-start | bytes 1572872 | tf_op jit(solution)/shard_map/ppermute | solution.py:716
  740.5 28.0 %collective-permute-start.56 = (bf16[256,1024]{1,0:T(8,128)(2,1)}, bf16[256,1024]{1,0:T(8,128)(2,1)S(1)}, u32[]{:S(2)}, u32[]{:S(2)}) collective-permute-start(bf16[256,1024]{1,0:T(8,128)(2,1)} %fusion.7), channel_id=1, source_target_pairs={{0,0},{1,1},{2,2},{3,3},{4,8},{5,9},{6,10},{7,11},{16,4},{17,5},{1... | collective-permute-start | bytes 1572872 | tf_op jit(solution)/shard_map/ppermute | solution.py:716
  (128 other events, 1052.6 us)

commit v2 on v0

v2 whole, which is shorter than its diff:
```python
import functools
import types

import jax
import jax.numpy as jnp
from jax import lax
from jax.experimental import pallas as pl
from jax.experimental.pallas import tpu as pltpu
from jax.sharding import PartitionSpec as P

D = 1024
HEADDIM = 64
STATE = 128
KCONV = 4
BLOCK = 256
INNER = 2048
HEADS = 32
PAIR = 2 * STATE
LANES = 128
EPS = 1e-05
NEG = -1e30
BF = jnp.bfloat16
F32 = jnp.float32
HIGH = lax.Precision.HIGHEST
AXES = ("section", "seq", "wshard")
VMEM_LIMIT = 58 << 20


def nn(a, b, precision=None):
    return lax.dot_general(
        a, b, (((1,), (0,)), ((), ())), preferred_element_type=F32, precision=precision
    )


def nt(a, b):
    return lax.dot_general(a, b, (((1,), (1,)), ((), ())), preferred_element_type=F32)


def tn(a, b):
    return lax.dot_general(a, b, (((0,), (0,)), ((), ())), preferred_element_type=F32)


def two(x):
    hi = x.astype(BF)
    lo = (x - hi.astype(F32)).astype(BF)
    return jnp.concatenate([hi, lo], axis=1)


def iota(shape, dim):
    return lax.broadcasted_iota(jnp.int32, shape, dim)


def column(row):
    return jnp.broadcast_to(row, (LANES, row.shape[1])).T[:, :1]


def as_row(col):
    return jnp.broadcast_to(col, (col.shape[0], LANES)).T[:1]


def sigmoid(x):
    return 1.0 / (1.0 + jnp.exp(-x))


def softplus(x):
    return jnp.maximum(x, 0.0) + jnp.log1p(jnp.exp(-jnp.abs(x)))


def full(shape):
    return pl.BlockSpec(shape, lambda i: (0,) * len(shape))


def launch(name, body, grid, ins, outs, scratch=(), flops=0, nbytes=0):
    names = [item[0] for item in ins] + [item[0] for item in outs] + [item[0] for item in scratch]

    def kernel(*refs):
        body(types.SimpleNamespace(**dict(zip(names, refs))))

    results = pl.pallas_call(
        kernel,
        grid=grid,
        in_specs=[item[2] for item in ins],
        out_specs=[item[3] for item in outs],
        out_shape=[jax.ShapeDtypeStruct(item[1], item[2]) for item in outs],
        scratch_shapes=[item[1] for item in scratch],
        compiler_params=pltpu.CompilerParams(
            dimension_semantics=("arbitrary",) * len(grid), vmem_limit_bytes=VMEM_LIMIT
        ),
        cost_estimate=pl.CostEstimate(flops=flops, bytes_accessed=nbytes, transcendentals=0),
        name=name,
    )(*[item[1] for item in ins])
    return types.SimpleNamespace(**dict(zip([item[0] for item in outs], results)))


def small():
    return pl.BlockSpec(memory_space=pltpu.SMEM)


def rows_of(width, first=0):
    return pl.BlockSpec((BLOCK, width), lambda i: (first + i, 0))


def turned(width, last):
    return pl.BlockSpec((BLOCK, width), lambda i: (last - i, 0))


def place(orders, halves):
    mine, theirs = halves
    total = 2 * mine.shape[0]

    def body(r):
        at = pl.program_id(0) * BLOCK + iota((BLOCK, total // 2), 0)
        first = (r.mine_order[...] == at).astype(BF)
        second = (r.their_order[...] == at).astype(BF)
        r.out[...] = (nn(first, r.mine[...]) + nn(second, r.theirs[...])).astype(BF)

    return launch(
        "place",
        body,
        (total // BLOCK,),
        [
            ("mine_order", orders[0], full((1, total // 2))),
            ("their_order", orders[1], full((1, total // 2))),
            ("mine", mine, full((total // 2, D))),
            ("theirs", theirs, full((total // 2, D))),
        ],
        [("out", (total, D), BF, rows_of(D))],
        flops=2 * total * total * D,
        nbytes=4 * total * D,
    ).out


def assemble(spot, part, near, far, theirs, wide):
    rows = part.shape[0]
    side = 2 * wide + LANES
    total = PAIR + side

    def body(r):
        w = r.spot[1]

        def move(source, row, base, pair):
            place_at = pl.ds(pl.multiple_of(row, rows), rows)
            r.out[place_at, :wide] = source[:, base : base + wide]
            r.out[place_at, wide : wide + PAIR] = source[:, pair : pair + PAIR]
            r.out[place_at, wide + PAIR :] = source[:, base + wide : base + side]

        for core in range(2):

            @pl.when(r.spot[0] == core)
            def _():
                own = core * (side + PAIR)
                shards = (w, w ^ (1 + core), w ^ (2 - core), w ^ 3)
                sources = (r.part, r.near, r.far.at[0], r.far.at[1])
                for source, shard in zip(sources, shards):
                    move(source, (2 * shard + core) * rows, own, side)
                shards = (w, w ^ (2 - core), w ^ (1 + core), w ^ 3)
                for index, shard in enumerate(shards):
                    source = r.theirs.at[index]
                    move(source, (2 * shard + 1 - core) * rows, core * PAIR, (1 - core) * side)

    return launch(
        "assemble",
        body,
        (1,),
        [
            ("spot", spot, small()),
            ("part", part, full(part.shape)),
            ("near", near, full(near.shape)),
            ("far", far, full(far.shape)),
            ("theirs", theirs, full(theirs.shape)),
        ],
        [("out", (8 * rows, total), BF, full((8 * rows, total)))],
        nbytes=32 * rows * total,
    ).out


def block_terms(raw, dtb, rate_sign, offset):
    rate = softplus(raw + dtb)
    lower = (iota((BLOCK, BLOCK), 1) <= iota((BLOCK, BLOCK), 0)).astype(F32)
    level = nn(lower, rate * rate_sign, HIGH)
    local = iota((BLOCK, 1), 0)
    end = level[BLOCK - 1 :]
    end_offset = offset[BLOCK - 1 :]
    head = jnp.where(offset > local, jnp.exp(level), 0.0)
    fade = jnp.where(local >= BLOCK - 1 - end_offset, jnp.exp(end - level), 0.0)
    carry = jnp.where(end_offset > BLOCK - 1, jnp.exp(end), 0.0)
    return rate, level, head, fade, carry


def either(flag, first, second):
    chosen = flag.astype(F32)
    return chosen * first.astype(F32) + (1.0 - chosen) * second.astype(F32)


def keep_or_give(r, core, block, split, value):
    slot = pl.ds(pl.multiple_of(block % split * BLOCK, BLOCK), BLOCK)

    @pl.when(block // split == core)
    def _():
        r.keep[slot] = value

    @pl.when(block // split != core)
    def _():
        r.away[slot] = value


def forward_body(layer, begin, wide, split, r):
    heads = wide // HEADDIM
    conv = PAIR + wide
    step = pl.program_id(0)
    core = r.spot[0]

    @pl.when(step == 0)
    def _():
        if begin:
            r.state[...] = jnp.zeros_like(r.state)
            r.halo[...] = jnp.zeros_like(r.halo)
        else:
            r.state[...] = r.state_in[...]
            r.halo[...] = r.halo_in[...]

    tokens = r.tokens[...].astype(F32)
    if layer == 1:
        scale = lax.rsqrt(column(r.last_rows[0][0:1]) / INNER + EPS)
        summed = either(step // split == core, r.mine[...], r.theirs[...])
        low = (tokens + summed * scale).astype(BF)
        r.next[...] = low
        tokens = low.astype(F32)
    scale = lax.rsqrt(jnp.mean(tokens * tokens, axis=1, keepdims=True) + EPS)
    x = (tokens * scale * r.gain[...]).astype(BF)
    r.normed[...] = x
    projected = nn(x, r.w[...])
    gate = projected[:, :wide]
    r.gate[...] = gate
    cin_low = projected[:, wide : wide + conv].astype(BF)
    r.cin[...] = cin_low
    raw_low = projected[:, wide + conv :].astype(BF)
    r.raw[...] = raw_low
    pos = r.pos[...]
    label_col = pos[:, 0:1]
    offset = pos[:, 1:2]
    cin = cin_low.astype(F32)
    longer = jnp.concatenate([r.halo[...], cin], axis=0)
    r.halo[...] = cin[BLOCK - 8 :]
    taps = r.taps[...]
    pre = taps[KCONV : KCONV + 1] + taps[KCONV - 1 : KCONV] * cin
    for index in range(KCONV - 1):
        delay = KCONV - 1 - index
        moved = longer[8 - delay : 8 - delay + BLOCK]
        pre = pre + jnp.where(offset >= delay, taps[index : index + 1] * moved, 0.0)
    r.pre[...] = pre
    mixed_conv = (pre * sigmoid(pre)).astype(BF)
    write = mixed_conv[:, :STATE]
    read = mixed_conv[:, STATE:PAIR]
    xs = mixed_conv[:, PAIR:]
    xs_float = xs.astype(F32)
    terms = r.terms[...]
    rate, level, head, fade, carry = block_terms(
        raw_low.astype(F32), terms[0:1], terms[1:2], offset
    )
    level_rows = level.T
    rate_rows = rate.T
    spread = r.spread[...]
    state = r.state[...]
    r.states[0] = state
    wides = r.wides[...]
    mixed = nn(two(head), spread) * nn(read, state.astype(BF)) + wides[0:1] * xs_float
    gram = nt(read, write)
    inside = (label_col == r.label[0]) & (iota((BLOCK, BLOCK), 1) <= iota((BLOCK, BLOCK), 0))
    closed = jnp.where(inside, 0.0, NEG)
    parts = []
    for first in range(0, heads, 2):
        span = xs[:, first * HEADDIM : (first + 2) * HEADDIM]
        mixing = []
        values = []
        for h in range(first, first + 2):
            weight = jnp.exp(level[:, h : h + 1] - level_rows[h : h + 1] + closed)
            mixing.append((gram * (weight * rate_rows[h : h + 1])).astype(BF))
            own = iota(span.shape, 1) // HEADDIM == h - first
            values.append(jnp.where(own, span, jnp.zeros_like(span)))
        parts.append(nn(jnp.concatenate(mixing, axis=1), jnp.concatenate(values, axis=0)))
    mixed = mixed + jnp.concatenate(parts, axis=1)
    mixed_low = mixed.astype(BF)
    r.mixed[...] = mixed_low
    carry_wide = nn(two(jnp.broadcast_to(carry, (8, LANES))), spread)[:1]
    written = (nn(two(fade * rate), spread) * xs_float).astype(BF)
    r.state[...] = carry_wide * state + tn(write, written)
    gv = mixed_low.astype(F32) * (gate * sigmoid(gate))
    r.rows[0, 0:1] = as_row(jnp.sum(gv * gv, axis=1, keepdims=True))
    scaled = gv * wides[1:2]
    if layer == 1:
        dotted = nt(r.dout[...], r.w_out[...]) * scaled
        r.rows[0, 1:2] = as_row(jnp.sum(dotted, axis=1, keepdims=True))
    else:
        r.rows[0, 1:2] = jnp.zeros((1, BLOCK), F32)
    keep_or_give(r, core, step, split, nn(scaled.astype(BF), r.w_out[...]).astype(BF))


def forward(layer, part, spot, env, tokens, before, weights, vectors, carried, dout):
    w, w_out = weights
    wide = w_out.shape[0]
    conv = PAIR + wide
    count = tokens.shape[0] // BLOCK // 2
    split = count // 2
    first = part * count
    total = count * BLOCK
    row = pl.BlockSpec((1, 2, BLOCK), lambda i: (i, 0, 0))
    ins = [
        ("spot", spot, small()),
        ("tokens", tokens, rows_of(D, first)),
        ("gain", vectors["gain"], full((1, D))),
        ("w", w, full(w.shape)),
        ("w_out", w_out, full(w_out.shape)),
        ("taps", vectors["taps"], full((8, conv))),
        ("terms", vectors["terms"], full((8, LANES))),
        ("wides", vectors["wides"], full((8, wide))),
        ("spread", env.spread, full(env.spread.shape)),
        ("pos", env.pos, rows_of(3, first)),
        ("label", env.label_row, pl.BlockSpec((1, 1, BLOCK), lambda i: (first + i, 0, 0))),
    ]
    outs = [
        ("normed", (total, D), BF, rows_of(D)),
        ("gate", (total, wide), F32, rows_of(wide)),
        ("pre", (total, conv), F32, rows_of(conv)),
        ("cin", (total, conv), BF, rows_of(conv)),
        ("raw", (total, LANES), BF, rows_of(LANES)),
        ("mixed", (total, wide), BF, rows_of(wide)),
        ("states", (count, STATE, wide), F32, pl.BlockSpec((1, STATE, wide), lambda i: (i, 0, 0))),
        ("rows", (count, 2, BLOCK), F32, row),
        ("keep", (total // 2, D), BF, full((total // 2, D))),
        ("away", (total // 2, D), BF, full((total // 2, D))),
        ("state", (STATE, wide), F32, full((STATE, wide))),
        ("halo", (8, conv), F32, full((8, conv))),
    ]
    if part == 1:
        ins += [
            ("state_in", carried.state, full((STATE, wide))),
            ("halo_in", carried.halo, full((8, conv))),
        ]
    if layer == 1:
        block = pl.BlockSpec((BLOCK, D), lambda i: (i % split, 0))
        mine, theirs, last_rows = before
        ins += [
            ("mine", mine, block),
            ("theirs", theirs, block),
            ("last_rows", last_rows, row),
            ("dout", dout, rows_of(D, first)),
        ]
        outs.append(("next", (total, D), BF, rows_of(D)))
    return launch(
        "forward",
        functools.partial(forward_body, layer, part == 0, wide, split),
        (count,),
        ins,
        outs,
        flops=4 * total * D * (2 * wide + conv),
        nbytes=total * D * 16,
    )


def ungate_body(layer, wide, count, split, r):
    step = pl.program_id(0)
    block = count - 1 - step
    core = r.spot[0]

    @pl.when(step == 0)
    def _():
        r.ggated[...] = jnp.zeros_like(r.ggated)
        if layer == 0:
            r.ggain[...] = jnp.zeros_like(r.ggain)

    scale = lax.rsqrt(column(r.rows[0][0:1]) / INNER + EPS)
    if layer == 1:
        dout = r.dout[...]
        dots = column(r.rows[0][1:2])
    else:
        flag = block // split == core
        grad = either(flag, r.grad_mine[...], r.grad_theirs[...])
        dtokens, dgain = unnorm(r.tokens[...].astype(F32), r.gain[...], grad)
        r.ggain[...] += dgain
        dout = (r.dlater[...].astype(F32) + dtokens).astype(BF)
        r.dout[...] = dout
        summed = either(flag, r.mine[...], r.theirs[...])
        dots = jnp.sum(dout.astype(F32) * summed, axis=1, keepdims=True)
    gate = r.gate[...]
    gain = r.wides[1:2]
    mixed = r.mixed[...].astype(F32)
    sig = sigmoid(gate)
    act = gate * sig
    normal = mixed * act * scale
    grad_out = nt(dout, r.w_out[...])
    shared = dots * scale / INNER
    grad_gv = scale * (grad_out * gain - normal * shared)
    r.dmixed[...] = (grad_gv * act).astype(BF)
    r.dgate[...] = (grad_gv * mixed * (sig * (1.0 + gate * (1.0 - sig)))).astype(BF)
    r.ggated[...] += jnp.sum(grad_out * normal, axis=0, keepdims=True)
    r.normed_out[...] = (normal * gain).astype(BF)


def unnorm(tokens, gain, grad):
    scale = lax.rsqrt(jnp.mean(tokens * tokens, axis=1, keepdims=True) + EPS)
    normal = tokens * scale
    inner = grad * gain
    dtokens = scale * (inner - normal * jnp.mean(inner * normal, axis=1, keepdims=True))
    return dtokens, jnp.sum(grad * normal, axis=0, keepdims=True)


def ungate(layer, part, spot, kept, rows, w_out, vectors, above):
    total, wide = kept.mixed.shape
    count = total // BLOCK
    split = count // 2
    last = count - 1
    row = pl.BlockSpec((1, 2, BLOCK), lambda i: (last - i, 0, 0))
    ins = [
        ("spot", spot, small()),
        ("rows", rows, row),
        ("gate", kept.gate, turned(wide, last)),
        ("mixed", kept.mixed, turned(wide, last)),
        ("wides", vectors["wides"], full((8, wide))),
        ("w_out", w_out, full((wide, D))),
    ]
    outs = [
        ("dmixed", (total, wide), BF, turned(wide, last)),
        ("dgate", (total, wide), BF, turned(wide, last)),
        ("normed_out", (total, wide), BF, turned(wide, last)),
        ("ggated", (1, wide), F32, full((1, wide))),
    ]
    if layer == 1:
        ins.append(("dout", above.dout, turned(D, part * count + last)))
    else:
        block = pl.BlockSpec((BLOCK, D), lambda i: ((last - i) % split, 0))
        ins += [
            ("grad_mine", above.grad[0], block),
            ("grad_theirs", above.grad[1], block),
            ("mine", above.summed[0], block),
            ("theirs", above.summed[1], block),
            ("tokens", above.tokens, turned(D, last)),
            ("gain", above.gain, full((1, D))),
            ("dlater", above.dout, turned(D, part * count + last)),
        ]
        outs += [("dout", (total, D), BF, turned(D, last)), ("ggain", (1, D), F32, full((1, D)))]
    return launch(
        "ungate",
        functools.partial(ungate_body, layer, wide, count, split),
        (count,),
        ins,
        outs,
        flops=2 * total * D * wide,
        nbytes=total * (wide * 10 + D * 4),
    )


def backward_body(begin, wide, count, split, r):
    heads = wide // HEADDIM
    conv = PAIR + wide
    step = pl.program_id(0)
    block = count - 1 - step
    core = r.spot[0]

    @pl.when(step == 0)
    def _():
        if begin:
            r.dstate[...] = jnp.zeros_like(r.dstate)
            r.halo[...] = jnp.zeros_like(r.halo)
        else:
            r.dstate[...] = r.dstate_in[...]
            r.halo[...] = r.halo_in[...]
        r.gtaps[...] = jnp.zeros_like(r.gtaps)
        r.gheads[...] = jnp.zeros_like(r.gheads)
        r.gskip[...] = jnp.zeros_like(r.gskip)

    pos = r.pos[...]
    label_col = pos[:, 0:1]
    offset = pos[:, 1:2]
    remain = pos[:, 2:3]
    pre = r.pre[...]
    sig = sigmoid(pre)
    mixed_conv = (pre * sig).astype(BF)
    write = mixed_conv[:, :STATE]
    read = mixed_conv[:, STATE:PAIR]
    xs = mixed_conv[:, PAIR:]
    xs_float = xs.astype(F32)
    raw = r.raw[...].astype(F32)
    terms = r.terms[...]
    dtb = terms[0:1]
    sign = terms[1:2]
    rate, level, head, fade, carry = block_terms(raw, dtb, sign, offset)
    tail = fade * rate
    level_rows = level.T
    spread = r.spread[...]
    fold = r.fold[...]
    dy = r.dmixed[...]
    dy_float = dy.astype(F32)
    state = r.states[0]
    state_low = state.astype(BF)
    dstate = r.dstate[...]
    dstate_low = dstate.astype(BF)
    dhead = nn(two(dy_float * nn(read, state_low)), fold)
    tail_wide = nn(two(tail), spread)
    scaled = (nn(two(head), spread) * dy_float).astype(BF)
    written = (tail_wide * xs_float).astype(BF)
    through = nn(write, dstate_low)
    dtail = nn(two(xs_float * through), fold)
    r.gskip[...] += jnp.sum(dy_float * xs_float, axis=0, keepdims=True)
    carry_wide = nn(two(jnp.broadcast_to(carry, (8, LANES))), spread)[:1]
    held = jnp.broadcast_to(jnp.sum(state * dstate, axis=0, keepdims=True), (8, wide))
    dcarry = nn(two(held), fold)[:1]

    gram = nt(write, read)
    inside = (label_col == r.label[0]) & (iota((BLOCK, BLOCK), 0) <= iota((BLOCK, BLOCK), 1))
    closed = jnp.where(inside, 0.0, NEG)
    lane = iota((1, LANES), 1)
    drate = jnp.zeros((BLOCK, LANES), F32)
    level_sums = []
    parts = []
    dgram = jnp.zeros((BLOCK, BLOCK), F32)
    for first in range(0, heads, 2):
        cut_at = slice(first * HEADDIM, (first + 2) * HEADDIM)
        xs_span = xs[:, cut_at]
        dy_span = dy[:, cut_at]
        mixing = []
        values = []
        for h in range(first, first + 2):
            own = iota(xs_span.shape, 1) // HEADDIM == h - first
            xs_own = jnp.where(own, xs_span, jnp.zeros_like(xs_span))
            values.append(jnp.where(own, dy_span, jnp.zeros_like(dy_span)))
            decay = jnp.exp(level_rows[h : h + 1] - level[:, h : h + 1] + closed)
            rate_col = rate[:, h : h + 1]
            weight = decay * rate_col
            mixing.append((gram * weight).astype(BF))
            dmix = nt(xs_own, dy_span)
            dgram = dgram + dmix * weight
            bare = dmix * gram * decay
            drate = drate + jnp.sum(bare, axis=1, keepdims=True) * (lane == h).astype(F32)
            level_sums.append(jnp.sum(bare * rate_col, axis=0, keepdims=True))
        parts.append(nn(jnp.concatenate(mixing, axis=1), jnp.concatenate(values, axis=0)))
    dxs = jnp.concatenate(parts, axis=1) + r.wides[0:1] * dy_float + tail_wide * through
    dgram_low = dgram.astype(BF)
    dread = tn(dgram_low, write) + nt(scaled, state_low)
    dwrite = nn(dgram_low, read) + nt(written, dstate_low)
    r.dstate[...] = carry_wide * dstate + tn(read, scaled)

    level_sums.append(jnp.zeros((LANES - heads, BLOCK), F32))
    tail_flow = dtail * tail
    local = iota((BLOCK, 1), 0)
    last = jnp.sum(tail_flow, axis=0, keepdims=True) + dcarry * carry
    dlevel = jnp.concatenate(level_sums, axis=0).T - rate * drate + dhead * head - tail_flow
    dlevel = dlevel + jnp.where(local == BLOCK - 1, last, 0.0)
    upper = (iota((BLOCK, BLOCK), 0) <= iota((BLOCK, BLOCK), 1)).astype(F32)
    dsum = nn(upper, dlevel, HIGH)
    drate = drate + dtail * fade + sign * dsum
    draw = drate * sigmoid(raw + dtb)
    r.gheads[0:1] += jnp.sum(draw, axis=0, keepdims=True)
    r.gheads[1:2] += jnp.sum(rate * dsum, axis=0, keepdims=True) * sign

    dpre = jnp.concatenate([dwrite, dread, dxs], axis=1) * (sig * (1.0 + pre * (1.0 - sig)))
    longer = jnp.concatenate([dpre, r.halo[...]], axis=0)
    r.halo[...] = dpre[:8]
    cin = r.cin[...].astype(F32)
    taps = r.taps[...]
    r.gtaps[KCONV : KCONV + 1] += jnp.sum(dpre, axis=0, keepdims=True)
    r.gtaps[KCONV - 1 : KCONV] += jnp.sum(dpre * cin, axis=0, keepdims=True)
    dcin = taps[KCONV - 1 : KCONV] * dpre
    for index in range(KCONV - 1):
        delay = KCONV - 1 - index
        moved = jnp.where(remain >= delay, longer[delay : delay + BLOCK], 0.0)
        dcin = dcin + taps[index : index + 1] * moved
        r.gtaps[index : index + 1] += jnp.sum(moved * cin, axis=0, keepdims=True)
    rest = jnp.concatenate([dcin, draw], axis=1).astype(BF)
    r.rest[...] = rest
    w = r.w[...]
    dnormed = nt(r.dgate[...], w[:, :wide]) + nt(rest, w[:, wide:])
    keep_or_give(r, core, block, split, dnormed.astype(BF))


def backward(part, spot, env, kept, grads, w, vectors, carried):
    total, wide = kept.mixed.shape
    conv = PAIR + wide
    count = total // BLOCK
    split = count // 2
    last = count - 1
    top = part * count + last
    ins = [
        ("spot", spot, small()),
        ("w", w, full(w.shape)),
        ("taps", vectors["taps"], full((8, conv))),
        ("terms", vectors["terms"], full((8, LANES))),
        ("wides", vectors["wides"], full((8, wide))),
        ("spread", env.spread, full(env.spread.shape)),
        ("fold", env.fold, full(env.fold.shape)),
        ("pos", env.pos, turned(3, top)),
        ("label", env.label_row, pl.BlockSpec((1, 1, BLOCK), lambda i: (top - i, 0, 0))),
        ("pre", kept.pre, turned(conv, last)),
        ("cin", kept.cin, turned(conv, last)),
        ("raw", kept.raw, turned(LANES, last)),
        ("states", kept.states, pl.BlockSpec((1, STATE, wide), lambda i: (last - i, 0, 0))),
        ("dmixed", grads.dmixed, turned(wide, last)),
        ("dgate", grads.dgate, turned(wide, last)),
    ]
    if part == 0:
        ins += [
            ("dstate_in", carried.dstate, full((STATE, wide))),
            ("halo_in", carried.halo, full((8, conv))),
        ]
    outs = [
        ("keep", (total // 2, D), BF, full((total // 2, D))),
        ("away", (total // 2, D), BF, full((total // 2, D))),
        ("rest", (total, conv + LANES), BF, turned(conv + LANES, last)),
        ("gtaps", (8, conv), F32, full((8, conv))),
        ("gheads", (8, LANES), F32, full((8, LANES))),
        ("gskip", (1, wide), F32, full((1, wide))),
        ("dstate", (STATE, wide), F32, full((STATE, wide))),
        ("halo", (8, conv), F32, full((8, conv))),
    ]
    return launch(
        "backward",
        functools.partial(backward_body, part == 1, wide, count, split),
        (count,),
        ins,
        outs,
        flops=6 * total * D * (2 * wide + conv),
        nbytes=total * D * 16,
    )


def weight_grads(spot, lefts, rights, seq, outer=None, size=0):
    depth = lefts[0].shape[1]
    wide = rights[0].shape[1]
    share = depth // (4 * seq)
    rows = depth // 4
    extra = size * (D // wide)

    def body(r):
        w = r.spot[1]
        z = r.spot[2]
        sides = ((r.keep, (0, r.spot[5])), (r.away, (r.spot[4], 3)))
        r.total[...] = tn(r.left0[...], r.right0[...]) + tn(r.left1[...], r.right1[...])
        for ref, shards in sides:
            for index, shard in enumerate(shards):
                for turn in range(seq):
                    start = ((z ^ turn) * 4 + (w ^ shard)) * share
                    piece = r.total[pl.ds(pl.multiple_of(start, share), share)]
                    ref[index, turn * share : (turn + 1) * share] = piece.astype(BF)
        if outer is None:
            return
        for part in range(D // wide):
            cols = slice(part * wide, (part + 1) * wide)
            r.outer[...] = tn(r.out0[...], r.dout0[...][:, cols]) + tn(
                r.out1[...], r.dout1[...][:, cols]
            )
            for ref, shards in sides:
                for index, shard in enumerate(shards):
                    start = pl.multiple_of((w ^ shard) * size, size)
                    begin = rows + part * size
                    ref[index, begin : begin + size] = r.outer[pl.ds(start, size)].astype(BF)

    ins = [("spot", spot, small())]
    for name, pair in (("left", lefts), ("right", rights)):
        for index in range(2):
            ins.append((name + str(index), pair[index], full(pair[index].shape)))
    scratch = [("total", pltpu.VMEM((depth, wide), F32))]
    if outer is not None:
        outs, douts = outer
        height = outs[0].shape[0]
        for index in range(2):
            ins.append(("out" + str(index), outs[index], full(outs[index].shape)))
            array, at = douts[index]
            spec = pl.BlockSpec((height, D), functools.partial(lambda at, i: (at, 0), at))
            ins.append(("dout" + str(index), array, spec))
        scratch.append(("outer", pltpu.VMEM((outs[0].shape[1], wide), F32)))
    height = rows + extra
    return launch(
        "weight_grads",
        body,
        (1,),
        ins,
        [
            ("keep", (2, height, wide), BF, full((2, height, wide))),
            ("away", (2, height, wide), BF, full((2, height, wide))),
        ],
        scratch=scratch,
        flops=4 * lefts[0].shape[0] * depth * wide,
        nbytes=4 * depth * wide,
    )


def finish(kind, part, spot, orders, values, before):
    count = values.count
    split = count // 2
    total = count * BLOCK

    def body(r):
        step = pl.program_id(0)
        core = r.spot[0]

        @pl.when(step == 0)
        def _():
            if before is None:
                r.own[...] = jnp.zeros_like(r.own)
                r.across[...] = jnp.zeros_like(r.across)
            else:
                r.own[...] = r.own_in[...]
                r.across[...] = r.across_in[...]
            if kind == "grad":
                r.ggain[...] = jnp.zeros_like(r.ggain)

        summed = either(step // split == core, r.mine[...], r.theirs[...])
        if kind == "grad":
            dtokens, dgain = unnorm(r.tokens[...].astype(F32), r.gain[...], summed)
            r.ggain[...] += dgain
            value = r.rest[...].astype(F32) + dtokens
        else:
            scale = lax.rsqrt(column(r.rows[0][0:1]) / INNER + EPS)
            value = r.rest[...].astype(F32) + summed * scale
        low = value.astype(BF)
        at = (part * count + step) * BLOCK + iota((BLOCK, BLOCK), 1)
        r.own[...] += nn((r.own_order[...] == at).astype(BF), low)
        r.across[...] += nn((r.far_order[...] == at).astype(BF), low)

    block = pl.BlockSpec((BLOCK, D), lambda i: (i % split, 0))
    ins = [
        ("spot", spot, small()),
        ("own_order", orders[0], full((BLOCK, 1))),
        ("far_order", orders[1], full((BLOCK, 1))),
        ("mine", values.summed[0], block),
        ("theirs", values.summed[1], block),
        ("rest", values.rest, rows_of(D)),
    ]
    outs = [
        ("own", (BLOCK, D), F32, full((BLOCK, D))),
        ("across", (BLOCK, D), F32, full((BLOCK, D))),
    ]
    if kind == "grad":
        ins += [
            ("tokens", values.tokens, rows_of(D, part * count)),
            ("gain", values.gain, full((1, D))),
        ]
        outs.append(("ggain", (1, D), F32, full((1, D))))
    else:
        ins.append(("rows", values.rows, pl.BlockSpec((1, 2, BLOCK), lambda i: (i, 0, 0))))
    if before is not None:
        ins += [
            ("own_in", before.own, full((BLOCK, D))),
            ("across_in", before.across, full((BLOCK, D))),
        ]
    return launch(
        "finish", body, (count,), ins, outs, flops=4 * total * BLOCK * D, nbytes=total * D * 8
    )


class Plan:
    def __init__(self):
        self.seq = lax.axis_size("seq")
        self.shards = lax.axis_size("wshard")
        self.half = self.seq // 2
        self.core = lax.axis_index("section")
        self.z = lax.axis_index("seq")
        self.w = lax.axis_index("wshard")
        self.batch = self.z // self.half
        self.place = self.z % self.half
        self.rank = 2 * self.place + self.core

    def send(self, value, route, cores=(0, 1)):
        pairs = []
        for c in range(2):
            for z in range(self.seq):
                for w in range(self.shards):
                    target = route(c, z, w)
                    if c in cores and target is not None:
                        source = (c * self.seq + z) * self.shards + w
                        tc, tz, tw = target
                        pairs.append((source, (tc * self.seq + tz) * self.shards + tw))
        return lax.ppermute(value, AXES, pairs)

    def swap(self, value, cores=(0, 1)):
        return self.send(value, lambda c, z, w: (1 - c, z, w), cores)

    def along(self, value, k, cores=(0, 1)):
        return self.send(value, lambda c, z, w: (c, z ^ k, w), cores)

    def first_side(self, value):
        return self.send(value, lambda c, z, w: (c, z, w ^ (1 + c)))

    def second_side(self, value):
        return self.send(value, lambda c, z, w: (c, z, w ^ (2 - c)))

    def own(self, first, second):
        return jnp.where(self.core == 0, first, second)

    def collect(self, near, far):
        pieces = [near]
        came = self.along(far, self.half)
        for k in range(1, self.half):
            pieces.append(self.along(near, k))
        pieces.append(came)
        for k in range(1, self.half):
            pieces.append(self.along(came, k))
        mine = jnp.concatenate(pieces, axis=0)
        return mine, self.swap(mine)

    def fold(self, terms):
        return add(terms.keep, self.swap(terms.away))

    def reduce(self, total):
        hop = 1
        while hop < self.half:
            total = add(total, self.along(total, hop))
            hop *= 2
        return total, self.swap(total)

    def total(self, value):
        value = value + self.swap(value)
        hop = 1
        while hop < self.half:
            value = value + self.along(value, hop)
            hop *= 2
        return value

    def home(self, value, batch, layer):
        half = self.half

        def route(c, z, w):
            if z // half != batch:
                return None
            return (layer, 2 * (z % half) + c, w)

        return self.send(value, route)

    def gather_chips(self, value, share):
        pieces = [value[:share]]
        for k in range(1, self.seq):
            pieces.append(self.along(value[k * share : (k + 1) * share], k))
        half = self.half
        terms = [add(pieces[k], pieces[k + half]) for k in range(half)]
        if half == 2:
            even = self.place == 0
            ordered = [jnp.where(even, terms[0], terms[1]), jnp.where(even, terms[1], terms[0])]
            return jnp.stack(ordered)
        stacked = jnp.stack(terms)
        return stacked[self.place ^ jnp.arange(half)]


def add(first, second):
    return (first.astype(F32) + second.astype(F32)).astype(BF)


def after(value, *others):
    return lax.optimization_barrier((value,) + others)[0]


def pick(value, index, axis=0):
    return lax.dynamic_index_in_dim(value, index, axis, keepdims=False)


def cut(value, start, size, axis):
    return lax.dynamic_slice_in_dim(value, start, size, axis)


def on_device(
    ends_in,
    seq_lengths,
    deal_order,
    norm_w,
    in_w,
    conv_w,
    conv_b,
    dt_bias,
    a_log,
    d_skip,
    gnorm_w,
    out_w,
):
    plan = Plan()
    core = plan.core
    half = plan.half
    rank = plan.rank
    seq = plan.seq
    rows = ends_in.shape[3]
    total = rows * seq
    count = total // BLOCK
    heads = HEADS // seq
    width = heads * HEADDIM
    wide = max(width, LANES)
    side = 2 * wide + LANES
    first = 1 + core
    second = 2 - core
    spot = jnp.stack([core, plan.w, plan.z, plan.place, first, second, rank, 0 * rank])
    spot = spot.astype(jnp.int32)

    start = 2 * width * plan.place
    gate_cols = cut(in_w[0], start, 2 * width, 1)
    input_cols = cut(in_w[0], INNER + start, 2 * width, 1)
    pair_cols = in_w[0][:, 2 * INNER : 2 * INNER + PAIR]
    raw_cols = cut(in_w[0], 2 * INNER + PAIR + 2 * heads * plan.place, 2 * heads, 1)

    def padded(value, size):
        return jnp.pad(value, ((0, 0), (0, size - value.shape[1])))

    chunk = jnp.concatenate(
        [
            padded(gate_cols[:, :width], wide),
            padded(input_cols[:, :width], wide),
            padded(raw_cols[:, :heads], LANES),
            pair_cols,
            padded(gate_cols[:, width:], wide),
            padded(input_cols[:, width:], wide),
            padded(raw_cols[:, heads:], LANES),
        ],
        axis=1,
    )
    split_rows = chunk.shape[0] // 2
    chunk_keep = cut(chunk, core * split_rows, split_rows, 0)
    chunk_came = plan.swap(cut(chunk, (1 - core) * split_rows, split_rows, 0))
    chunk_parts = [plan.own(chunk_keep, chunk_came), plan.own(chunk_came, chunk_keep)]

    half_rows = rows // 2
    ends_keep = cut(ends_in[0, :, 0], core * half_rows, half_rows, 1)
    ends_came = plan.swap(cut(ends_in[0, :, 0], (1 - core) * half_rows, half_rows, 1))
    end_parts = [plan.own(ends_keep, ends_came), plan.own(ends_came, ends_keep)]

    order = pick(deal_order[:, 0], plan.batch)
    by_chip = order.reshape(seq, 2, half_rows)[plan.z ^ jnp.arange(seq)]
    orders = (
        pick(by_chip, core, 1).reshape(1, total // 2),
        pick(by_chip, 1 - core, 1).reshape(1, total // 2),
    )
    end_orders = (
        cut(order, rows * plan.z, rows, 0).reshape(rows, 1),
        cut(order, rows * (plan.z ^ half), rows, 0).reshape(rows, 1),
    )

    def collect(part):
        return plan.collect(pick(part, plan.batch), pick(part, 1 - plan.batch))

    started = collect(end_parts[0])

    def in_weights(part):
        near = plan.first_side(part)
        far = plan.second_side(jnp.stack([part, near]))
        give = jnp.stack([part, near, far[0], far[1]])
        theirs = plan.swap(cut(give, (1 - core) * side, side + PAIR, 2))
        return assemble(spot, part, near, far, theirs, wide), near

    def out_weights(part):
        if half == 2:
            low_shard = plan.w // 2

            def route(c, z, w):
                return (c, z, w ^ 2) if w // 2 == z % half else None

            came = plan.send(part, route)
            here = jnp.where(low_shard == plan.place, part, came)
            beside = plan.send(here, lambda c, z, w: (c, z, w ^ 1))
            same = plan.w % 2 == core
            mine = jnp.where(same, here, beside)
            theirs = plan.swap(jnp.where(same, beside, here))
            return jnp.concatenate([plan.own(mine, theirs), plan.own(theirs, mine)], axis=0)
        half_part = part.shape[0]
        near = plan.first_side(part)
        far = plan.second_side(jnp.stack([part, near]))
        pieces = jnp.stack([part, near, far[0], far[1]])
        shards = jnp.arange(4) ^ plan.w
        ordered = pieces[jnp.where((shards == 0) | (shards == 3), shards, jnp.where(core == 0, shards, 3 - shards))]
        other = plan.swap(ordered)
        whole = jnp.stack([plan.own(ordered, other), plan.own(other, ordered)], axis=1)
        whole = whole.reshape(8 * half_part, D)
        return jnp.pad(cut(whole, width * rank, width, 0), ((0, wide - width), (0, 0)))

    out_rows = out_w.shape[1] // 2
    out_keep = cut(out_w[0], core * out_rows, out_rows, 0)
    out_came = plan.swap(cut(out_w[0], (1 - core) * out_rows, out_rows, 0))
    out_parts = [plan.own(out_keep, out_came), plan.own(out_came, out_keep)]

    w_first, in_sent = in_weights(chunk_parts[0])
    w_out_first = out_weights(after(out_parts[0], in_sent))
    w_second, in_sent = in_weights(after(chunk_parts[1], w_first, w_out_first))
    w_out_second = out_weights(after(out_parts[1], in_sent))
    weights = [(w_first, w_out_first), (w_second, w_out_second)]

    tokens = place(orders, started)
    cotangent = place(orders, collect(after(end_parts[1], *started)))

    lengths = pick(seq_lengths[:, 0], plan.batch)
    ends = jnp.cumsum(lengths)
    at = iota((total,), 0)
    passed = at[:, None] >= ends[None, :]
    label = jnp.sum(passed.astype(jnp.int32), axis=1)
    begin = jnp.max(jnp.where(passed, ends[None, :], 0), axis=1)
    finished = jnp.min(jnp.where(passed, total, ends[None, :]), axis=1)
    channel_head = iota((LANES, wide), 1) // HEADDIM
    hot = (channel_head == iota((LANES, wide), 0)).astype(BF)
    env = types.SimpleNamespace(
        pos=jnp.stack([label, at - begin, finished - 1 - at], axis=1),
        label_row=label.reshape(count, 1, BLOCK),
        spread=jnp.concatenate([hot, hot], axis=0),
        fold=jnp.concatenate([hot.T, hot.T], axis=0),
    )

    own_small = jnp.concatenate(
        [
            norm_w[0],
            conv_w[0].reshape(-1),
            conv_b[0],
            dt_bias[0],
            a_log[0],
            d_skip[0],
            gnorm_w[0],
        ]
    )
    other_small = plan.swap(own_small)
    sizes = (D, (KCONV + 1) * (INNER + PAIR), HEADS, HEADS, HEADS, INNER)

    def pieces_of(flat):
        pieces = []
        begin = 0
        for size in sizes:
            pieces.append(flat[begin : begin + size])
            begin += size
        return pieces

    def vectors_of(layer):
        flat = jnp.where(core == layer, own_small, other_small)
        gain, taps, dtb, log_rate, skip, gated = pieces_of(flat)
        taps = taps.reshape(KCONV + 1, INNER + PAIR)
        channels = jnp.concatenate(
            [taps[:, INNER:], padded(cut(taps, rank * width, width, 1), wide)], axis=1
        )

        def lanes(value):
            return padded(cut(value, rank * heads, heads, 0)[None], LANES)

        terms = jnp.concatenate([lanes(dtb), lanes(-jnp.exp(log_rate))], axis=0)
        skips = jnp.repeat(cut(skip, rank * heads, heads, 0), HEADDIM)[None]
        wides = jnp.concatenate([skips, cut(gated, rank * width, width, 0)[None]], axis=0)
        return {
            "gain": gain[None],
            "taps": jnp.pad(channels, ((0, 8 - KCONV - 1), (0, 0))),
            "terms": jnp.pad(terms, ((0, 6), (0, 0))),
            "wides": jnp.pad(wides, ((0, 6), (0, wide - width))),
        }

    vectors = [vectors_of(0), vectors_of(1)]

    kept = [[], []]
    rows_summed = [[], []]
    summed = [[], []]
    turn = spot
    for layer in range(2):
        carried = None
        for part in range(2):
            before = None
            if layer == 1:
                before = summed[0][part] + (rows_summed[0][part],)
            carried = forward(
                layer, part, turn, env, tokens, before, weights[layer], vectors[layer], carried, cotangent
            )
            kept[layer].append(carried)
            rows_summed[layer].append(plan.total(carried.rows))
            folded = plan.fold(carried)
            if layer == 0:
                turn = after(spot, folded)
            summed[layer].append(plan.reduce(folded))

    grads_summed = [[None, None], [None, None]]
    turn = spot
    small_terms = [None, None]
    weight_terms = [None, None]
    douts = [None, None]
    for layer in (1, 0):
        carried = None
        gated = [None, None]
        scans = [None, None]
        for part in (1, 0):
            above = types.SimpleNamespace(dout=cotangent)
            if layer == 0:
                above.grad = grads_summed[1][part]
                above.summed = summed[0][part]
                above.tokens = kept[1][part].next
                above.gain = vectors[1]["gain"]
            gated[part] = ungate(
                layer,
                part,
                turn if part == 1 else spot,
                kept[layer][part],
                rows_summed[layer][part],
                weights[layer][1],
                vectors[layer],
                above,
            )
            carried = backward(
                part, turn, env, kept[layer][part], gated[part], weights[layer][0], vectors[layer], carried
            )
            scans[part] = carried
            folded = plan.fold(carried)
            turn = after(spot, folded)
            grads_summed[layer][part] = plan.reduce(folded)
        normed = [item.normed for item in kept[layer]]
        if layer == 1:
            dout_parts = ((cotangent, 0), (cotangent, 1))
        else:
            dout_parts = ((gated[0].dout, 0), (gated[1].dout, 0))
            douts = [item.dout for item in gated]
            gain_terms = gated[0].ggain + gated[1].ggain
        weight_terms[layer] = (
            weight_grads(
                spot,
                normed,
                [item.dgate for item in gated],
                seq,
                ([item.normed_out for item in gated], dout_parts),
                width // 4,
            ),
            weight_grads(spot, normed, [item.rest for item in scans], seq),
        )
        small_terms[layer] = (
            scans[0].gtaps + scans[1].gtaps,
            scans[0].gheads + scans[1].gheads,
            scans[0].gskip + scans[1].gskip,
            gated[0].ggated + gated[1].ggated,
        )

    result = None
    for part in (0, 1):
        values = types.SimpleNamespace(
            count=count // 2, summed=summed[1][part], rest=kept[1][part].next, rows=rows_summed[1][part]
        )
        result = finish("result", part, spot, end_orders, values, result)
    start_grad = None
    first_gain = None
    for part in (1, 0):
        values = types.SimpleNamespace(
            count=count // 2,
            summed=grads_summed[0][part],
            rest=douts[part],
            tokens=tokens,
            gain=vectors[0]["gain"],
        )
        start_grad = finish("grad", part, spot, end_orders, values, start_grad)
        gain = start_grad.ggain
        first_gain = gain if first_gain is None else first_gain + gain
    own_end = plan.own(start_grad.own, result.own)
    result_far = plan.along(result.across.astype(BF), half, (1,))
    grad_far = plan.along(start_grad.across.astype(BF), half, (0,))
    far_end = plan.own(grad_far, result_far).astype(F32)
    lower = plan.batch == 0
    ends_out = jnp.stack([jnp.where(lower, own_end, far_end), jnp.where(lower, far_end, own_end)])
    ends_out = ends_out[None, :, None]

    def reduced(terms):
        came = plan.first_side(terms.away)
        kept_back = add(terms.keep[0], came[0])
        given = add(terms.keep[1], came[1])
        return add(kept_back, plan.second_side(given))

    share = D // (4 * seq)
    gate_rows = D // 4
    in_grads = []
    out_grads = []
    for layer in range(2):
        gates, rest = weight_terms[layer]
        gates = reduced(gates)
        rest = reduced(rest)
        outs = gates[gate_rows:]
        outs = add(plan.home(outs, 0, layer), plan.home(outs, 1, layer)).astype(F32)
        size = width // 4
        pieces = [outs[k * size : (k + 1) * size] for k in range(D // wide)]
        out_grads.append(jnp.concatenate(pieces, axis=1))

        def both(value):
            came = plan.swap(value, (1 - layer,))
            return (value, came) if layer == 0 else (came, value)

        gate_sides = both(plan.gather_chips(gates, share))
        rest_sides = both(plan.gather_chips(rest, share))
        gate_list = []
        inputs = []
        raws = []
        pair = None
        for place_at in range(half):
            for gate_side, rest_side in zip(gate_sides, rest_sides):
                gate_list.append(gate_side[place_at][:, :width].astype(F32))
                part = rest_side[place_at].astype(F32)
                pair = part[:, :PAIR] if pair is None else pair + part[:, :PAIR]
                inputs.append(part[:, PAIR : PAIR + width])
                raws.append(part[:, PAIR + wide : PAIR + wide + heads])
        in_grads.append(jnp.concatenate(gate_list + inputs + [pair] + raws, axis=1))
    g_in = plan.own(in_grads[0], in_grads[1])
    g_out = plan.own(out_grads[0], out_grads[1])

    gains = [first_gain, gain_terms]

    def flat_of(layer):
        gtaps, gheads, gskip, ggated = small_terms[layer]
        zeros = lambda *shape: jnp.zeros(shape, F32)
        inner = lax.dynamic_update_slice_in_dim(
            zeros(KCONV + 1, INNER), gtaps[: KCONV + 1, PAIR : PAIR + width], rank * width, 1
        )
        channels = jnp.concatenate([inner, gtaps[: KCONV + 1, :PAIR]], axis=1)

        def per_head(value):
            return lax.dynamic_update_slice_in_dim(zeros(HEADS), value, rank * heads, 0)

        return jnp.concatenate(
            [
                channels.reshape(-1),
                per_head(gheads[0, :heads]),
                per_head(gheads[1, :heads]),
                per_head(jnp.sum(gskip[0, :width].reshape(heads, HEADDIM), axis=1)),
                lax.dynamic_update_slice_in_dim(zeros(INNER), ggated[0, :width], rank * width, 0),
            ]
        )

    def spread_sum(values):
        sums = plan.own(values[0], values[1]) + plan.swap(plan.own(values[1], values[0]))
        sums = sums + plan.first_side(sums)
        sums = sums + plan.second_side(sums)
        hop = 1
        while hop < seq:
            sums = sums + plan.along(sums, hop)
            hop *= 2
        return sums

    mine = (rank == 0).astype(F32)
    g_norm = spread_sum([gains[0][0] * mine, gains[1][0] * mine])
    sums = spread_sum([flat_of(0), flat_of(1)])
    _, g_taps, g_dt, g_log, g_skip, g_gated = pieces_of(jnp.concatenate([g_norm, sums]))
    g_taps = g_taps.reshape(KCONV + 1, INNER + PAIR)
    return (
        ends_out,
        g_norm[None],
        g_in[None],
        g_taps[None, :KCONV],
        g_taps[KCONV][None],
        g_dt[None],
        g_log[None],
        g_skip[None],
        g_gated[None],
        g_out[None],
    )


def solution(mesh):
    placed = (
        P("section", None, "wshard", "seq", None),
        P(None, "wshard", None),
        P(None, "wshard", None),
        P("section", None),
        P("section", "wshard", None),
        P("section", None, None),
        P("section", None),
        P("section", None),
        P("section", None),
        P("section", None),
        P("section", None),
        P("section", "wshard", None),
    )
    return jax.shard_map(
        on_device,
        mesh=mesh,
        in_specs=placed,
        out_specs=(
            P("section", None, "wshard", "seq", None),
            P("section", None),
            P("section", ("seq", "wshard"), None),
            P("section", None, None),
            P("section", None),
            P("section", None),
            P("section", None),
            P("section", None),
            P("section", None),
            P("section", ("seq", "wshard"), None),
        ),
        check_vma=False,
    )
```

time: 1920 us -> 556 us (0.29)
  waiting for transfers between devices: 643 us -> 94.2 us
  local copies, waits for them, and re-layouts: 409 us -> 60.1 us
  matrix products: 252 us -> 0 us
  blocking collectives: 223 us -> 0 us
  Pallas kernels: 0 us -> 200 us
  other arithmetic: 255 us -> 67.2 us
  starting transfers between devices: 71.3 us -> 121 us
  loops' own time: 34.8 us -> 0 us
    reduce_scatter x5 -> x0, waiting for transfers between devices: 381 us -> none  [the longest x1 381 us: on_device(): lax.psum_scatter(in_total, ('seq', 'wshard'), scatter_dimension=0, tiled=...]
    dot_general x150 -> x0, matrix products: 229 us -> none  [the longest x3 44.1 us: layer_backward(): in_grad = jnp.dot(normed.T, grad_proj, preferred_element_type=jnp.float32)]
    pallas_call x0 -> x24, Pallas kernels: none -> 200 us  [launch(): pl.pallas_call(kernel, grid=grid, in_specs=[item[2] for item in ins], out...]
    all_to_all x16 -> x0, waiting for transfers between devices: 161 us -> none  [the longest x3 70 us: layer_backward(): lax.all_to_all(grad_mixed.astype(jnp.bfloat16).reshape(tok_rows, shards,...]
    ppermute x4 -> x96, starting transfers between devices: 5.69 us -> 121 us  [send(): return lax.ppermute(value, AXES, pairs)]
    gather x27 -> x1, local copies, waits for them, and re-layouts: 96.8 us -> 0.57 us  [on_device(): by_chip = order.reshape(seq, 2, half_rows)[plan.z ^ jnp.arange(seq)]]
    all_gather x3 -> x0, blocking collectives: 92.8 us -> none  [on_device(): pair_dealt = lax.all_gather(layer_pair_rows, 'seq', axis=0, tiled=True)]
    all_gather x2 -> x0, waiting for transfers between devices: 92.6 us -> none  [the longest x1 92.6 us: on_device(): lax.all_gather(in_w[0], 'wshard', axis=0, tiled=True)]
  transfers between devices with their start and end apart: 27 -> 96, of which waited for: 15 -> 24; matrix products, arithmetic and copies ran while one was open for 16% -> 21% of each run, Pallas kernels for 0% -> 37%
where the time goes in v2:
time: 556 us; the launch traced here: 545 us
  Pallas kernels  200 us (36%)
  starting transfers between devices  121 us (22%)
  waiting for transfers between devices  94.2 us (17%)
  other arithmetic  67.2 us (12%)
  local copies, waits for them, and re-layouts  60.1 us (11%)
    pallas_call x24, Pallas kernels, launch(): pl.pallas_call(kernel, grid=grid, in_specs=[item[2] for item in ins], out...  200 us
    ppermute x96, starting transfers between devices, send(): return lax.ppermute(value, AXES, pairs)  121 us
    ppermute x96, waiting for transfers between devices, send(): return lax.ppermute(value, AXES, pairs)  94.2 us
    convert_element_type x24, other arithmetic, add(): return (first.astype(F32) + second.astype(F32)).astype(BF)  18.8 us
    unnamed x183, local copies, waits for them, and re-layouts  16.3 us
    dynamic_slice x14, local copies, waits for them, and re-layouts, cut(): return lax.dynamic_slice_in_dim(value, start, size, axis)  11.5 us
  transfers between devices with their start and end apart: 96, of which 24 were waited for; matrix products, arithmetic and copies ran while one was open for 21% of the time, Pallas kernels for 37%

profile of v2, /device:TPU:0, one launch (start us, length us, event | category | flops | bytes accessed | tf_op | source)
XLA Modules:
  0.0 545.1 jit_solution(4903178050739040301)
XLA Ops:
  3.0 3.0 copy.67
  6.0 2.1 constant_dynamic-slice_fusion.8
  24.7 2.9 collective-permute-start.1
  29.6 2.2 bitcast_select_fusion
  31.8 4.4 collective-permute-done.1.refs_2_
  37.4 2.0 collective-permute-start.2
  40.2 2.6 collective-permute-start.14
  42.8 2.3 bitcast_select_fusion.2
  45.0 3.2 collective-permute-start.5
  50.9 3.4 collective-permute-done.14
  57.6 2.6 collective-permute-done.13
  60.2 5.1 collective-permute-done.15
  73.5 10.4 %collective-permute-done.6 = bf16[256,1024]{1,0:T(8,128)(2,1)} collective-permute-done((bf16[256,1024]{1,0:T(8,128)(2,1)}, bf16[256,1024]{1,0:T(8,128)(2,1)}, u32[]{:S(2)}, u32[]{:S(2)}) %collective-permute-start.6) | collective-permute-done | bytes 524320 | tf_op jit(solution)/shard_map/ppermute | solution.py:773
  91.7 2.4 collective-permute-start.26
  94.0 6.5 %collective-permute-done.27 = bf16[128,1024]{1,0:T(8,128)(2,1)S(1)} collective-permute-done((bf16[128,1024]{1,0:T(8,128)(2,1)S(1)}, bf16[128,1024]{1,0:T(8,128)(2,1)S(1)}, u32[]{:S(2)}, u32[]{:S(2)}) %collective-permute-start.27) | collective-permute-done | bytes 262176 | tf_op jit(solution)/shard_map/ppermute | solution.py:773
  102.8 4.0 assemble.2.refs_3_.refs_1_
  107.3 5.3 place.2.refs_1_.refs_6_
  113.1 12.1 %forward.4 = (bf16[512,1024]{1,0:T(8,128)(2,1)}, f32[512,512]{1,0:T(8,128)}, f32[512,768]{1,0:T(8,128)}, bf16[512,768]{1,0:T(8,128)(2,1)}, bf16[512,128]{1,0:T(8...) custom-call(s32[8]{0:T(128)} %stack.112.refs_0_, ...), custom_call_target="tpu_custom_call" | custom-call | flops 3758096384 | bytes 8388608 | tf_op jit(solution)/shard_map/forward/pallas_call | solution.py:79
  128.1 4.4 collective-permute-start.19
  132.5 12.2 %forward.5 = (bf16[512,1024]{1,0:T(8,128)(2,1)}, f32[512,512]{1,0:T(8,128)}, f32[512,768]{1,0:T(8,128)}, bf16[512,768]{1,0:T(8,128)(2,1)}, bf16[512,128]{1,0:T(8...) custom-call(s32[8]{0:T(128)} %stack.112.refs_0_, ...), custom_call_target="tpu_custom_call" | custom-call | flops 3758096384 | bytes 8388608 | tf_op jit(solution)/shard_map/forward/pallas_call | solution.py:79
  149.5 5.3 place.3.refs_14_.refs_16_.refs_6_.refs_12_.refs_8_
  158.8 3.0 collective-permute-start.30
  161.8 8.7 %collective-permute-done.20 = bf16[256,1024]{1,0:T(8,128)(2,1)S(1)} collective-permute-done((bf16[256,1024]{1,0:T(8,128)(2,1)S(1)}, bf16[256,1024]{1,0:T(8,128)(2,1)S(1)}, u32[]{:S(2)}, u32[]{:S(2)}) %collective-permute-start.20) | collective-permute-done | bytes 524320 | tf_op jit(solution)/shard_map/ppermute | solution.py:773
  171.5 9.0 %collective-permute-done.30 = bf16[256,1024]{1,0:T(8,128)(2,1)S(1)} collective-permute-done((bf16[256,1024]{1,0:T(8,128)(2,1)S(1)}, bf16[256,1024]{1,0:T(8,128)(2,1)S(1)}, u32[]{:S(2)}, u32[]{:S(2)}) %collective-permute-start.30) | collective-permute-done | bytes 524320 | tf_op jit(solution)/shard_map/ppermute | solution.py:773
  183.1 4.4 assemble.3.refs_3_.refs_1_
  188.3 14.1 %forward.6 = (bf16[512,1024]{1,0:T(8,128)(2,1)}, f32[512,512]{1,0:T(8,128)}, f32[512,768]{1,0:T(8,128)}, bf16[512,768]{1,0:T(8,128)(2,1)}, bf16[512,128]{1,0:T(8...) custom-call(s32[8]{0:T(128)} %stack.112.refs_0_, ...), custom_call_target="tpu_custom_call" | custom-call | flops 3758096384 | bytes 8388608 | tf_op jit(solution)/shard_map/forward/pallas_call | solution.py:79
  203.8 14.2 %forward.7 = (bf16[512,1024]{1,0:T(8,128)(2,1)}, f32[512,512]{1,0:T(8,128)}, f32[512,768]{1,0:T(8,128)}, bf16[512,768]{1,0:T(8,128)(2,1)}, bf16[512,128]{1,0:T(8...) custom-call(s32[8]{0:T(128)} %stack.112.refs_0_, ...), custom_call_target="tpu_custom_call" | custom-call | flops 3758096384 | bytes 8388608 | tf_op jit(solution)/shard_map/forward/pallas_call | solution.py:79
  223.7 4.4 ungate.5
  228.6 4.5 ungate.4
  233.1 6.6 %weight_grads.6 = (bf16[2,512,512]{2,1,0:T(8,128)(2,1)}, bf16[2,512,512]{2,1,0:T(8,128)(2,1)}) custom-call(s32[8]{0:T(128)} %stack.112.refs_0_, bf16[512,1024]{1,0:T(8,128)(2,1)} %get-tuple-element.226.refs_1_, bf16[512,1024]{1,0:T(8,128)(2,1)} %get-tuple-element.227.refs_2_, bf16[512,512]{1,0:T(8,128)(2,1)} %get-tuple-element.167.refs_14_.refs_3_, ...), custom_call_target="tpu_custom_call" | custom-call | flops 1073741824 | bytes 2097152 | tf_op jit(solution)/shard_map/weight_grads/pallas_call | solution.py:79
  240.7 14.8 %backward.4 = (bf16[256,1024]{1,0:T(8,128)(2,1)}, bf16[256,1024]{1,0:T(8,128)(2,1)}, bf16[512,896]{1,0:T(8,128)(2,1)}, f32[8,768]{1,0:T(8,128)}, f32[8,128]{1,0:...) custom-call(s32[8]{0:T(128)} %stack.112.refs_0_, bf16[1024,1408]{1,0:T(8,128)(2,1)} %assemble.3.refs_3_.refs_1_, ...), custom_call_target="tpu_custom_call" | custom-call | flops 5637144576 | bytes 8388608 | tf_op jit(solution)/shard_map/backward/pallas_call | solution.py:79
  261.0 15.0 %backward.5 = (bf16[256,1024]{1,0:T(8,128)(2,1)}, bf16[256,1024]{1,0:T(8,128)(2,1)}, bf16[512,896]{1,0:T(8,128)(2,1)}, f32[8,768]{1,0:T(8,128)}, f32[8,128]{1,0:...) custom-call(s32[8]{0:T(128)} %stack.112.refs_0_, bf16[1024,1408]{1,0:T(8,128)(2,1)} %assemble.3.refs_3_.refs_1_, ...), custom_call_target="tpu_custom_call" | custom-call | flops 5637144576 | bytes 8388608 | tf_op jit(solution)/shard_map/backward/pallas_call | solution.py:79
  279.9 5.8 %weight_grads.7 = (bf16[2,256,896]{2,1,0:T(8,128)(2,1)}, bf16[2,256,896]{2,1,0:T(8,128)(2,1)}) custom-call(s32[8]{0:T(128)} %stack.112.refs_0_, bf16[512,1024]{1,0:T(8,128)(2,1)} %get-tuple-element.226.refs_1_, bf16[512,1024]{1,0:T(8,128)(2,1)} %get-tuple-element.227.refs_2_, bf16[512,896]{1,0:T(8,128)(2,1)} %get-tuple-element.232.refs_3_, ...), custom_call_target="tpu_custom_call" | custom-call | flops 1879048192 | bytes 3670016 | tf_op jit(solution)/shard_map/weight_grads/pallas_call | solution.py:79
  291.6 2.0 fusion.13
  297.3 6.3 %collective-permute-done.81 = bf16[2,256,896]{2,1,0:T(8,128)(2,1)S(1)} collective-permute-done((bf16[2,256,896]{2,1,0:T(8,128)(2,1)}, bf16[2,256,896]{2,1,0:T(8,128)(2,1)S(1)}, u32[]{:S(2)}, u32[]{:S(2)}) %collective-permute-start.81) | collective-permute-done | bytes 917536 | tf_op jit(solution)/shard_map/ppermute | solution.py:773
  305.4 3.1 collective-permute-start.82
  308.5 4.4 finish.6
  312.9 5.1 finish.7
  318.0 2.1 convert_element_type.532
  323.6 2.5 collective-permute-start.79
  326.0 7.1 %ungate.6 = (bf16[512,512]{1,0:T(8,128)(2,1)}, bf16[512,512]{1,0:T(8,128)(2,1)}, bf16[512,512]{1,0:T(8,128)(2,1)}, f32[1,512]{1,0:T(1,128)}, bf16[512,1024]{1,0:T(8,128)(2,1)}, /*index=5*/f32[1,1024]{1,0:T(1,128)}) custom-call(s32[8]{0:T(128)} %stack.112.refs_0_, f32[2,2,256]{2,1,0:T(2,128)} %add.409.refs_15_.refs_1_, ...), custom_call_target="tpu_custom_call" | custom-call | flops 536870912 | bytes 4718592 | tf_op jit(solution)/shard_map/ungate/pallas_call | solution.py:79
  333.1 15.2 %backward.6 = (bf16[256,1024]{1,0:T(8,128)(2,1)}, bf16[256,1024]{1,0:T(8,128)(2,1)}, bf16[512,896]{1,0:T(8,128)(2,1)}, f32[8,768]{1,0:T(8,128)}, f32[8,128]{1,0:...) custom-call(s32[8]{0:T(128)} %stack.112.refs_0_, bf16[1024,1408]{1,0:T(8,128)(2,1)} %assemble.2.refs_3_.refs_1_, ...), custom_call_target="tpu_custom_call" | custom-call | flops 5637144576 | bytes 8388608 | tf_op jit(solution)/shard_map/backward/pallas_call | solution.py:79
  352.2 4.8 collective-permute-start.80
  359.5 5.8 %collective-permute-start.83 = (bf16[64,896]{1,0:T(8,128)(2,1)S(1)}, bf16[64,896]{1,0:T(8,128)(2,1)S(1)}, u32[]{:S(2)}, u32[]{:S(2)}) collective-permute-start(bf16[64,896]{1,0:T(8,128)(2,1)S(1)} %get-tuple-element.341), channel_id=1, source_target_pairs={{0,8},{1,9},{2,10},{3,11},{4,12},{5,13},{6,14},{7,15},{8,0},{9,1},... | collective-permute-start | bytes 344072 | tf_op jit(solution)/shard_map/ppermute | solution.py:773
  366.9 3.7 collective-permute-done.83
  370.6 6.7 %collective-permute-start.42 = (bf16[256,1024]{1,0:T(8,128)(2,1)S(1)}, bf16[256,1024]{1,0:T(8,128)(2,1)S(1)}, u32[]{:S(2)}, u32[]{:S(2)}) collective-permute-start(bf16[256,1024]{1,0:T(8,128)(2,1)S(1)} %copy-done.87), channel_id=1, source_target_pairs={{0,16},{1,17},{2,18},{3,19},{4,20},{5,21},{6,22},{7,23},{8,24},{9,... | collective-permute-start | bytes 1572872 | tf_op jit(solution)/shard_map/ppermute | solution.py:773
  378.8 7.1 %collective-permute-start.86 = (bf16[2,64,896]{2,1,0:T(8,128)(2,1)}, bf16[2,64,896]{2,1,0:T(8,128)(2,1)}, u32[]{:S(2)}, u32[]{:S(2)}) collective-permute-start(bf16[2,64,896]{2,1,0:T(8,128)(2,1)} %pad_maximum_fusion.7), channel_id=1, source_target_pairs={{0,16},{1,17},{2,18},{3,19},{4,20},{5,21},{6,22},{7,23},{8,24},{9,... | collective-permute-start | bytes 688136 | tf_op jit(solution)/shard_map/ppermute | solution.py:773
  388.2 7.3 %ungate.7 = (bf16[512,512]{1,0:T(8,128)(2,1)}, bf16[512,512]{1,0:T(8,128)(2,1)}, bf16[512,512]{1,0:T(8,128)(2,1)}, f32[1,512]{1,0:T(1,128)}, bf16[512,1024]{1,0:T(8,128)(2,1)}, /*index=5*/f32[1,1024]{1,0:T(1,128)}) custom-call(s32[8]{0:T(128)} %stack.112.refs_0_, f32[2,2,256]{2,1,0:T(2,128)} %add.406.refs_13_.refs_1_, ...), custom_call_target="tpu_custom_call" | custom-call | flops 536870912 | bytes 4718592 | tf_op jit(solution)/shard_map/ungate/pallas_call | solution.py:79
  395.6 14.8 %backward.7 = (bf16[256,1024]{1,0:T(8,128)(2,1)}, bf16[256,1024]{1,0:T(8,128)(2,1)}, bf16[512,896]{1,0:T(8,128)(2,1)}, f32[8,768]{1,0:T(8,128)}, f32[8,128]{1,0:...) custom-call(s32[8]{0:T(128)} %stack.112.refs_0_, bf16[1024,1408]{1,0:T(8,128)(2,1)} %assemble.2.refs_3_.refs_1_, ...), custom_call_target="tpu_custom_call" | custom-call | flops 5637144576 | bytes 8388608 | tf_op jit(solution)/shard_map/backward/pallas_call | solution.py:79
  413.9 6.7 %weight_grads.4 = (bf16[2,512,512]{2,1,0:T(8,128)(2,1)}, bf16[2,512,512]{2,1,0:T(8,128)(2,1)}) custom-call(s32[8]{0:T(128)} %stack.112.refs_0_, bf16[512,1024]{1,0:T(8,128)(2,1)} %get-tuple-element.216.refs_1_, bf16[512,1024]{1,0:T(8,128)(2,1)} %get-tuple-element.217.refs_2_, bf16[512,512]{1,0:T(8,128)(2,1)} %get-tuple-element.193.refs_14_.refs_3_, ...), custom_call_target="tpu_custom_call" | custom-call | flops 1073741824 | bytes 2097152 | tf_op jit(solution)/shard_map/weight_grads/pallas_call | solution.py:79
  422.6 5.8 %weight_grads.5 = (bf16[2,256,896]{2,1,0:T(8,128)(2,1)}, bf16[2,256,896]{2,1,0:T(8,128)(2,1)}) custom-call(s32[8]{0:T(128)} %stack.112.refs_0_, bf16[512,1024]{1,0:T(8,128)(2,1)} %get-tuple-element.216.refs_1_, bf16[512,1024]{1,0:T(8,128)(2,1)} %get-tuple-element.217.refs_2_, bf16[512,896]{1,0:T(8,128)(2,1)} %get-tuple-element.222.refs_3_, ...), custom_call_target="tpu_custom_call" | custom-call | flops 1879048192 | bytes 3670016 | tf_op jit(solution)/shard_map/weight_grads/pallas_call | solution.py:79
  428.5 7.7 %collective-permute-done.88 = f32[13664]{0:T(1024)S(1)} collective-permute-done((f32[13664]{0:T(1024)S(1)}, f32[13664]{0:T(1024)S(1)}, u32[]{:S(2)}, u32[]{:S(2)}) %collective-permute-start.88) | collective-permute-done | bytes 54688 | tf_op jit(solution)/shard_map/ppermute | solution.py:773
  442.0 2.0 collective-permute-start.90
  446.9 2.3 collective-permute-start.91
  463.4 3.8 collective-permute-done.70
  469.2 2.3 collective-permute-start.71
  472.1 6.4 %collective-permute-done.46 = bf16[256,1024]{1,0:T(8,128)(2,1)S(1)} collective-permute-done((bf16[256,1024]{1,0:T(8,128)(2,1)S(1)}, bf16[256,1024]{1,0:T(8,128)(2,1)S(1)}, u32[]{:S(2)}, u32[]{:S(2)}) %collective-permute-start.46) | collective-permute-done | bytes 524320 | tf_op jit(solution)/shard_map/ppermute | solution.py:773
  482.4 5.2 finish.4
  490.4 5.9 %finish.5 = (f32[256,1024]{1,0:T(8,128)}, f32[256,1024]{1,0:T(8,128)}, f32[1,1024]{1,0:T(1,128)}) custom-call(s32[8]{0:T(128)} %stack.112.refs_0_, s32[256,1]{1,0:T(8,128)} %copy.78.refs_1_, s32[256,1]{1,0:T(8,128)} %copy.79.refs_2_, bf16[256,1024]{1,0:T(8,128)(2,1)} %copy-done.12, bf16[256,1024]{1,0:T(8,128)(2,1)} %copy-done.46, ...), custom_call_target="tpu_custom_call" | custom-call | flops 536870912 | bytes 4194304 | tf_op jit(solution)/shard_map/finish/pallas_call | solution.py:79
  505.6 2.5 collective-permute-start.65
  516.5 3.6 collective-permute-start.92
  521.4 5.5 %collective-permute-start.56 = (bf16[256,1024]{1,0:T(8,128)(2,1)}, bf16[256,1024]{1,0:T(8,128)(2,1)}, u32[]{:S(2)}, u32[]{:S(2)}) collective-permute-start(bf16[256,1024]{1,0:T(8,128)(2,1)} %convert_element_type.531), channel_id=1, source_target_pairs={{0,8},{1,9},{2,10},{3,11},{4,12},{5,13},{6,14},{7,15},{8,0},{9,1},... | collective-permute-start | bytes 1572872 | tf_op jit(solution)/shard_map/ppermute | solution.py:773
  533.8 2.5 collective-permute-done.93
  538.3 3.6 collective-permute-done.56
  (563 shorter events, 175.8 us)
Async XLA Ops:
  2.5 27.0 %collective-permute-start.12 = (bf16[2,128,1024]{2,1,0:T(8,128)(2,1)}, bf16[2,128,1024]{2,1,0:T(8,128)(2,1)}, u32[]{:S(2)}, u32[]{:S(2)}) collective-permute-start(bf16[2,128,1024]{2,1,0:T(8,128)(2,1)} %dynamic-slice_bitcast_fusion), channel_id=1, source_target_pairs={{0,16},{1,17},{2,18},{3,19},{4,20},{5,21},{6,22},{7,23},{8,24},{9,... | collective-permute-start | bytes 1572872 | tf_op jit(solution)/shard_map/ppermute | solution.py:773
  18.5 24.2 %collective-permute-start.4 = (bf16[256,1024]{1,0:T(8,128)(2,1)}, bf16[256,1024]{1,0:T(8,128)(2,1)}, u32[]{:S(2)}, u32[]{:S(2)}) collective-permute-start(bf16[256,1024]{1,0:T(8,128)(2,1)} %dynamic-slice_bitcast_fusion.1), channel_id=1, source_target_pairs={{0,16},{1,17},{2,18},{3,19},{4,20},{5,21},{6,22},{7,23},{8,24},{9,... | collective-permute-start | bytes 1572872 | tf_op jit(solution)/shard_map/ppermute | solution.py:773
  24.7 11.5 %collective-permute-start.1 = (bf16[128,2560]{1,0:T(8,128)(2,1)S(1)}, bf16[128,2560]{1,0:T(8,128)(2,1)S(1)}, u32[]{:S(2)}, u32[]{:S(2)}) collective-permute-start(bf16[128,2560]{1,0:T(8,128)(2,1)S(1)} %get-tuple-element.307.refs_1_), channel_id=1, source_target_pairs={{0,1},{1,0},{2,3},{3,2},{4,5},{5,4},{6,7},{7,6},{8,9},{9,8},{10,11... | collective-permute-start | bytes 1966088 | tf_op jit(solution)/shard_map/ppermute | solution.py:773
  37.4 33.5 %collective-permute-start.2 = (bf16[2,128,2560]{2,1,0:T(8,128)(2,1)}, bf16[2,128,2560]{2,1,0:T(8,128)(2,1)S(1)}, u32[]{:S(2)}, u32[]{:S(2)}) collective-permute-start(bf16[2,128,2560]{2,1,0:T(8,128)(2,1)} %pad_maximum_fusion), channel_id=1, source_target_pairs={{0,2},{1,3},{2,0},{3,1},{4,6},{5,7},{6,4},{7,5},{8,10},{9,11},{10,... | collective-permute-start | bytes 3932168 | tf_op jit(solution)/shard_map/ppermute | solution.py:773
  40.2 14.1 %collective-permute-start.14 = (bf16[128,1024]{1,0:T(8,128)(2,1)}, bf16[128,1024]{1,0:T(8,128)(2,1)}, u32[]{:S(2)}, u32[]{:S(2)}) collective-permute-start(bf16[128,1024]{1,0:T(8,128)(2,1)} %get-tuple-element.338), channel_id=1, source_target_pairs={{0,8},{1,9},{2,10},{3,11},{4,12},{5,13},{6,14},{7,15},{8,0},{9,1},... | collective-permute-start | bytes 786440 | tf_op jit(solution)/shard_map/ppermute | solution.py:773
  45.0 22.3 %collective-permute-start.5 = (bf16[256,1024]{1,0:T(8,128)(2,1)}, bf16[256,1024]{1,0:T(8,128)(2,1)}, u32[]{:S(2)}, u32[]{:S(2)}) collective-permute-start(bf16[256,1024]{1,0:T(8,128)(2,1)} %get-tuple-element.131), channel_id=1, source_target_pairs={{0,2},{1,3},{6,4},{7,5},{8,10},{9,11},{14,12},{15,13},{16,18},{17,... | collective-permute-start | bytes 1572872 | tf_op jit(solution)/shard_map/ppermute | solution.py:773
  67.3 17.8 %collective-permute-start.16 = (bf16[512,1024]{1,0:T(8,128)(2,1)}, bf16[512,1024]{1,0:T(8,128)(2,1)}, u32[]{:S(2)}, u32[]{:S(2)}) collective-permute-start(bf16[512,1024]{1,0:T(8,128)(2,1)} %pad_maximum_fusion.3.refs_2_), channel_id=1, source_target_pairs={{0,16},{1,17},{2,18},{3,19},{4,20},{5,21},{6,22},{7,23},{8,24},{9,... | collective-permute-start | bytes 3145736 | tf_op jit(solution)/shard_map/ppermute | solution.py:773
  69.2 14.7 %collective-permute-start.6 = (bf16[256,1024]{1,0:T(8,128)(2,1)}, bf16[256,1024]{1,0:T(8,128)(2,1)}, u32[]{:S(2)}, u32[]{:S(2)}) collective-permute-start(bf16[256,1024]{1,0:T(8,128)(2,1)} %broadcast_select_fusion.4), channel_id=1, source_target_pairs={{0,1},{1,0},{2,3},{3,2},{4,5},{5,4},{6,7},{7,6},{8,9},{9,8},{10,11... | collective-permute-start | bytes 1572872 | tf_op jit(solution)/shard_map/ppermute | solution.py:773
  72.5 30.3 %collective-permute-start.3 = (bf16[4,128,1408]{2,1,0:T(8,128)(2,1)}, bf16[4,128,1408]{2,1,0:T(8,128)(2,1)}, u32[]{:S(2)}, u32[]{:S(2)}) collective-permute-start(bf16[4,128,1408]{2,1,0:T(8,128)(2,1)} %fusion.3), channel_id=1, source_target_pairs={{0,16},{1,17},{2,18},{3,19},{4,20},{5,21},{6,22},{7,23},{8,24},{9,... | collective-permute-start | bytes 4325384 | tf_op jit(solution)/shard_map/ppermute | solution.py:773
  85.0 15.6 %collective-permute-start.7 = (bf16[256,1024]{1,0:T(8,128)(2,1)S(1)}, bf16[256,1024]{1,0:T(8,128)(2,1)S(1)}, u32[]{:S(2)}, u32[]{:S(2)}) collective-permute-start(bf16[256,1024]{1,0:T(8,128)(2,1)S(1)} %broadcast_select_fusion.7), channel_id=1, source_target_pairs={{0,16},{1,17},{2,18},{3,19},{4,20},{5,21},{6,22},{7,23},{8,24},{9,... | collective-permute-start | bytes 1572872 | tf_op jit(solution)/shard_map/ppermute | solution.py:773
  85.2 15.4 %collective-permute-start.27 = (bf16[128,1024]{1,0:T(8,128)(2,1)S(1)}, bf16[128,1024]{1,0:T(8,128)(2,1)S(1)}, u32[]{:S(2)}, u32[]{:S(2)}) collective-permute-start(bf16[128,1024]{1,0:T(8,128)(2,1)S(1)} %get-tuple-element.336), channel_id=1, source_target_pairs={{0,8},{1,9},{2,10},{3,11},{4,12},{5,13},{6,14},{7,15},{8,0},{9,1},... | collective-permute-start | bytes 786440 | tf_op jit(solution)/shard_map/ppermute | solution.py:773
  91.7 20.9 %collective-permute-start.26 = (bf16[128,1024]{1,0:T(8,128)(2,1)S(1)}, bf16[128,1024]{1,0:T(8,128)(2,1)S(1)}, u32[]{:S(2)}, u32[]{:S(2)}) collective-permute-start(bf16[128,1024]{1,0:T(8,128)(2,1)S(1)} %get-tuple-element.335), channel_id=1, source_target_pairs={{0,4},{1,5},{2,6},{3,7},{4,0},{5,1},{6,2},{7,3},{8,12},{9,13},{10,... | collective-permute-start | bytes 786440 | tf_op jit(solution)/shard_map/ppermute | solution.py:773
  100.5 12.0 %collective-permute-start.28 = (bf16[128,1024]{1,0:T(8,128)(2,1)S(1)}, bf16[128,1024]{1,0:T(8,128)(2,1)S(1)}, u32[]{:S(2)}, u32[]{:S(2)}) collective-permute-start(bf16[128,1024]{1,0:T(8,128)(2,1)S(1)} %collective-permute-done.27), channel_id=1, source_target_pairs={{0,4},{1,5},{2,6},{3,7},{4,0},{5,1},{6,2},{7,3},{8,12},{9,13},{10,... | collective-permute-start | bytes 786440 | tf_op jit(solution)/shard_map/ppermute | solution.py:773
  106.8 18.8 %collective-permute-start.8 = (bf16[128,2560]{1,0:T(8,128)(2,1)S(1)}, bf16[128,2560]{1,0:T(8,128)(2,1)S(1)}, u32[]{:S(2)}, u32[]{:S(2)}) collective-permute-start(bf16[128,2560]{1,0:T(8,128)(2,1)S(1)} %get-tuple-element.132.refs_1_), channel_id=1, source_target_pairs={{0,1},{1,0},{2,3},{3,2},{4,5},{5,4},{6,7},{7,6},{8,9},{9,8},{10,11... | collective-permute-start | bytes 1966088 | tf_op jit(solution)/shard_map/ppermute | solution.py:773
  112.6 36.9 %collective-permute-start.29 = (bf16[512,1024]{1,0:T(8,128)(2,1)S(1)}, bf16[512,1024]{1,0:T(8,128)(2,1)}, u32[]{:S(2)}, u32[]{:S(2)}) collective-permute-start(bf16[512,1024]{1,0:T(8,128)(2,1)S(1)} %pad_maximum_fusion.5.refs_2_), channel_id=1, source_target_pairs={{0,16},{1,17},{2,18},{3,19},{4,20},{5,21},{6,22},{7,23},{8,24},{9,... | collective-permute-start | bytes 3145736 | tf_op jit(solution)/shard_map/ppermute | solution.py:773
  125.7 31.6 %collective-permute-start.9 = (bf16[2,128,2560]{2,1,0:T(8,128)(2,1)S(1)}, bf16[2,128,2560]{2,1,0:T(8,128)(2,1)S(1)}, u32[]{:S(2)}, u32[]{:S(2)}) collective-permute-start(bf16[2,128,2560]{2,1,0:T(8,128)(2,1)S(1)} %pad_maximum_fusion.1), channel_id=1, source_target_pairs={{0,2},{1,3},{2,0},{3,1},{4,6},{5,7},{6,4},{7,5},{8,10},{9,11},{10,... | collective-permute-start | bytes 3932168 | tf_op jit(solution)/shard_map/ppermute | solution.py:773
  127.9 18.8 %collective-permute-start.24 = (f32[2,2,256]{2,1,0:T(2,128)S(1)}, f32[2,2,256]{2,1,0:T(2,128)S(1)}, u32[]{:S(2)}, u32[]{:S(2)}) collective-permute-start(f32[2,2,256]{2,1,0:T(2,128)S(1)} %copy-done.70), channel_id=1, source_target_pairs={{0,16},{1,17},{2,18},{3,19},{4,20},{5,21},{6,22},{7,23},{8,24},{9,... | collective-permute-start | bytes 12296 | tf_op jit(solution)/shard_map/ppermute | solution.py:773
  128.1 27.9 %collective-permute-start.19 = (bf16[256,1024]{1,0:T(8,128)(2,1)S(1)}, bf16[256,1024]{1,0:T(8,128)(2,1)}, u32[]{:S(2)}, u32[]{:S(2)}) collective-permute-start(bf16[256,1024]{1,0:T(8,128)(2,1)S(1)} %copy-done.15), channel_id=1, source_target_pairs={{0,2},{1,3},{6,4},{7,5},{8,10},{9,11},{14,12},{15,13},{16,18},{17,... | collective-permute-start | bytes 1572872 | tf_op jit(solution)/shard_map/ppermute | solution.py:773
  155.4 15.3 %collective-permute-start.22 = (bf16[256,1024]{1,0:T(8,128)(2,1)S(1)}, bf16[256,1024]{1,0:T(8,128)(2,1)S(1)}, u32[]{:S(2)}, u32[]{:S(2)}) collective-permute-start(bf16[256,1024]{1,0:T(8,128)(2,1)S(1)} %add_convert_fusion.19), channel_id=1, source_target_pairs={{0,4},{1,5},{2,6},{3,7},{4,0},{5,1},{6,2},{7,3},{8,12},{9,13},{10,... | collective-permute-start | bytes 1572872 | tf_op jit(solution)/shard_map/ppermute | solution.py:773
  156.1 14.4 %collective-permute-start.20 = (bf16[256,1024]{1,0:T(8,128)(2,1)S(1)}, bf16[256,1024]{1,0:T(8,128)(2,1)S(1)}, u32[]{:S(2)}, u32[]{:S(2)}) collective-permute-start(bf16[256,1024]{1,0:T(8,128)(2,1)S(1)} %broadcast_select_fusion.3), channel_id=1, source_target_pairs={{0,1},{1,0},{2,3},{3,2},{4,5},{5,4},{6,7},{7,6},{8,9},{9,8},{10,11... | collective-permute-start | bytes 1572872 | tf_op jit(solution)/shard_map/ppermute | solution.py:773
  158.4 23.6 %collective-permute-start.10 = (bf16[4,128,1408]{2,1,0:T(8,128)(2,1)S(1)}, bf16[4,128,1408]{2,1,0:T(8,128)(2,1)S(1)}, u32[]{:S(2)}, u32[]{:S(2)}) collective-permute-start(bf16[4,128,1408]{2,1,0:T(8,128)(2,1)S(1)} %fusion.1), channel_id=1, source_target_pairs={{0,16},{1,17},{2,18},{3,19},{4,20},{5,21},{6,22},{7,23},{8,24},{9,... | collective-permute-start | bytes 4325384 | tf_op jit(solution)/shard_map/ppermute | solution.py:773
  158.8 21.6 %collective-permute-start.30 = (bf16[256,1024]{1,0:T(8,128)(2,1)S(1)}, bf16[256,1024]{1,0:T(8,128)(2,1)S(1)}, u32[]{:S(2)}, u32[]{:S(2)}) collective-permute-start(bf16[256,1024]{1,0:T(8,128)(2,1)S(1)} %add_convert_fusion.18), channel_id=1, source_target_pairs={{0,4},{1,5},{2,6},{3,7},{4,0},{5,1},{6,2},{7,3},{8,12},{9,13},{10,... | collective-permute-start | bytes 1572872 | tf_op jit(solution)/shard_map/ppermute | solution.py:773
  170.9 16.6 %collective-permute-start.23 = (bf16[256,1024]{1,0:T(8,128)(2,1)S(1)}, bf16[256,1024]{1,0:T(8,128)(2,1)S(1)}, u32[]{:S(2)}, u32[]{:S(2)}) collective-permute-start(bf16[256,1024]{1,0:T(8,128)(2,1)S(1)} %add_convert_fusion.17.refs_11_.refs_8_), channel_id=1, source_target_pairs={{0,16},{1,17},{2,18},{3,19},{4,20},{5,21},{6,22},{7,23},{8,24},{9,... | collective-permute-start | bytes 1572872 | tf_op jit(solution)/shard_map/ppermute | solution.py:773
  180.6 22.3 %collective-permute-start.31 = (bf16[256,1024]{1,0:T(8,128)(2,1)S(1)}, bf16[256,1024]{1,0:T(8,128)(2,1)S(1)}, u32[]{:S(2)}, u32[]{:S(2)}) collective-permute-start(bf16[256,1024]{1,0:T(8,128)(2,1)S(1)} %add_convert_fusion.16.refs_13_.refs_8_), channel_id=1, source_target_pairs={{0,16},{1,17},{2,18},{3,19},{4,20},{5,21},{6,22},{7,23},{8,24},{9,... | collective-permute-start | bytes 1572872 | tf_op jit(solution)/shard_map/ppermute | solution.py:773
  202.4 15.7 %collective-permute-start.37 = (f32[2,2,256]{2,1,0:T(2,128)}, f32[2,2,256]{2,1,0:T(2,128)S(1)}, u32[]{:S(2)}, u32[]{:S(2)}) collective-permute-start(f32[2,2,256]{2,1,0:T(2,128)} %get-tuple-element.163), channel_id=1, source_target_pairs={{0,16},{1,17},{2,18},{3,19},{4,20},{5,21},{6,22},{7,23},{8,24},{9,... | collective-permute-start | bytes 12296 | tf_op jit(solution)/shard_map/ppermute | solution.py:773
  220.2 35.8 %collective-permute-start.53 = (bf16[256,1024]{1,0:T(8,128)(2,1)S(1)}, bf16[256,1024]{1,0:T(8,128)(2,1)S(1)}, u32[]{:S(2)}, u32[]{:S(2)}) collective-permute-start(bf16[256,1024]{1,0:T(8,128)(2,1)S(1)} %copy-done.86), channel_id=1, source_target_pairs={{0,16},{1,17},{2,18},{3,19},{4,20},{5,21},{6,22},{7,23},{8,24},{9,... | collective-permute-start | bytes 1572872 | tf_op jit(solution)/shard_map/ppermute | solution.py:773
  220.4 37.1 %collective-permute-start.50 = (bf16[256,1024]{1,0:T(8,128)(2,1)}, bf16[256,1024]{1,0:T(8,128)(2,1)S(1)}, u32[]{:S(2)}, u32[]{:S(2)}) collective-permute-start(bf16[256,1024]{1,0:T(8,128)(2,1)} %get-tuple-element.204), channel_id=1, source_target_pairs={{0,16},{1,17},{2,18},{3,19},{4,20},{5,21},{6,22},{7,23},{8,24},{9,... | collective-permute-start | bytes 1572872 | tf_op jit(solution)/shard_map/ppermute | solution.py:773
  239.7 51.5 %collective-permute-start.75 = (bf16[2,512,512]{2,1,0:T(8,128)(2,1)}, bf16[2,512,512]{2,1,0:T(8,128)(2,1)}, u32[]{:S(2)}, u32[]{:S(2)}) collective-permute-start(bf16[2,512,512]{2,1,0:T(8,128)(2,1)} %get-tuple-element.231), channel_id=1, source_target_pairs={{0,1},{1,0},{2,3},{3,2},{4,5},{5,4},{6,7},{7,6},{8,9},{9,8},{10,11... | collective-permute-start | bytes 3145736 | tf_op jit(solution)/shard_map/ppermute | solution.py:773
  256.2 29.5 %collective-permute-start.54 = (bf16[256,1024]{1,0:T(8,128)(2,1)S(1)}, bf16[256,1024]{1,0:T(8,128)(2,1)S(1)}, u32[]{:S(2)}, u32[]{:S(2)}) collective-permute-start(bf16[256,1024]{1,0:T(8,128)(2,1)S(1)} %add_convert_fusion.5), channel_id=1, source_target_pairs={{0,4},{1,5},{2,6},{3,7},{4,0},{5,1},{6,2},{7,3},{8,12},{9,13},{10,... | collective-permute-start | bytes 1572872 | tf_op jit(solution)/shard_map/ppermute | solution.py:773
  257.6 31.7 %collective-permute-start.51 = (bf16[256,1024]{1,0:T(8,128)(2,1)S(1)}, bf16[256,1024]{1,0:T(8,128)(2,1)}, u32[]{:S(2)}, u32[]{:S(2)}) collective-permute-start(bf16[256,1024]{1,0:T(8,128)(2,1)S(1)} %add_convert_fusion.7), channel_id=1, source_target_pairs={{0,4},{1,5},{2,6},{3,7},{4,0},{5,1},{6,2},{7,3},{8,12},{9,13},{10,... | collective-permute-start | bytes 1572872 | tf_op jit(solution)/shard_map/ppermute | solution.py:773
  259.8 35.7 %collective-permute-start.40 = (bf16[256,1024]{1,0:T(8,128)(2,1)S(1)}, bf16[256,1024]{1,0:T(8,128)(2,1)}, u32[]{:S(2)}, u32[]{:S(2)}) collective-permute-start(bf16[256,1024]{1,0:T(8,128)(2,1)S(1)} %add_convert_fusion.15), channel_id=1, source_target_pairs={{0,4},{1,5},{2,6},{3,7},{4,0},{5,1},{6,2},{7,3},{8,12},{9,13},{10,... | collective-permute-start | bytes 1572872 | tf_op jit(solution)/shard_map/ppermute | solution.py:773
  276.1 17.6 %collective-permute-start.39 = (bf16[256,1024]{1,0:T(8,128)(2,1)}, bf16[256,1024]{1,0:T(8,128)(2,1)}, u32[]{:S(2)}, u32[]{:S(2)}) collective-permute-start(bf16[256,1024]{1,0:T(8,128)(2,1)} %get-tuple-element.171), channel_id=1, source_target_pairs={{0,16},{1,17},{2,18},{3,19},{4,20},{5,21},{6,22},{7,23},{8,24},{9,... | collective-permute-start | bytes 1572872 | tf_op jit(solution)/shard_map/ppermute | solution.py:773
  286.6 17.1 %collective-permute-start.81 = (bf16[2,256,896]{2,1,0:T(8,128)(2,1)}, bf16[2,256,896]{2,1,0:T(8,128)(2,1)S(1)}, u32[]{:S(2)}, u32[]{:S(2)}) collective-permute-start(bf16[2,256,896]{2,1,0:T(8,128)(2,1)} %get-tuple-element.235), channel_id=1, source_target_pairs={{0,1},{1,0},{2,3},{3,2},{4,5},{5,4},{6,7},{7,6},{8,9},{9,8},{10,11... | collective-permute-start | bytes 2752520 | tf_op jit(solution)/shard_map/ppermute | solution.py:773
  289.3 15.2 %collective-permute-start.55 = (bf16[256,1024]{1,0:T(8,128)(2,1)S(1)}, bf16[256,1024]{1,0:T(8,128)(2,1)S(1)}, u32[]{:S(2)}, u32[]{:S(2)}) collective-permute-start(bf16[256,1024]{1,0:T(8,128)(2,1)S(1)} %add_convert_fusion.4.refs_3_), channel_id=1, source_target_pairs={{0,16},{1,17},{2,18},{3,19},{4,20},{5,21},{6,22},{7,23},{8,24},{9,... | collective-permute-start | bytes 1572872 | tf_op jit(solution)/shard_map/ppermute | solution.py:773
  291.3 21.6 %collective-permute-start.52 = (bf16[256,1024]{1,0:T(8,128)(2,1)S(1)}, bf16[256,1024]{1,0:T(8,128)(2,1)}, u32[]{:S(2)}, u32[]{:S(2)}) collective-permute-start(bf16[256,1024]{1,0:T(8,128)(2,1)S(1)} %add_convert_fusion.6.refs_3_), channel_id=1, source_target_pairs={{0,16},{1,17},{2,18},{3,19},{4,20},{5,21},{6,22},{7,23},{8,24},{9,... | collective-permute-start | bytes 1572872 | tf_op jit(solution)/shard_map/ppermute | solution.py:773
  293.6 26.4 %collective-permute-start.76 = (bf16[512,512]{1,0:T(8,128)(2,1)}, bf16[512,512]{1,0:T(8,128)(2,1)}, u32[]{:S(2)}, u32[]{:S(2)}) collective-permute-start(bf16[512,512]{1,0:T(8,128)(2,1)} %fusion.13), channel_id=1, source_target_pairs={{0,2},{1,3},{2,0},{3,1},{4,6},{5,7},{6,4},{7,5},{8,10},{9,11},{10,... | collective-permute-start | bytes 1572872 | tf_op jit(solution)/shard_map/ppermute | solution.py:773
  295.6 56.6 %collective-permute-start.43 = (bf16[256,1024]{1,0:T(8,128)(2,1)S(1)}, bf16[256,1024]{1,0:T(8,128)(2,1)S(1)}, u32[]{:S(2)}, u32[]{:S(2)}) collective-permute-start(bf16[256,1024]{1,0:T(8,128)(2,1)S(1)} %add_convert_fusion.14), channel_id=1, source_target_pairs={{0,4},{1,5},{2,6},{3,7},{4,0},{5,1},{6,2},{7,3},{8,12},{9,13},{10,... | collective-permute-start | bytes 1572872 | tf_op jit(solution)/shard_map/ppermute | solution.py:773
  303.7 19.9 %collective-permute-start.41 = (bf16[256,1024]{1,0:T(8,128)(2,1)S(1)}, bf16[256,1024]{1,0:T(8,128)(2,1)S(1)}, u32[]{:S(2)}, u32[]{:S(2)}) collective-permute-start(bf16[256,1024]{1,0:T(8,128)(2,1)S(1)} %add_convert_fusion.13.refs_6_), channel_id=1, source_target_pairs={{0,16},{1,17},{2,18},{3,19},{4,20},{5,21},{6,22},{7,23},{8,24},{9,... | collective-permute-start | bytes 1572872 | tf_op jit(solution)/shard_map/ppermute | solution.py:773
  305.4 53.9 %collective-permute-start.82 = (bf16[256,896]{1,0:T(8,128)(2,1)}, bf16[256,896]{1,0:T(8,128)(2,1)S(1)}, u32[]{:S(2)}, u32[]{:S(2)}) collective-permute-start(bf16[256,896]{1,0:T(8,128)(2,1)} %fusion.17), channel_id=1, source_target_pairs={{0,2},{1,3},{2,0},{3,1},{4,6},{5,7},{6,4},{7,5},{8,10},{9,11},{10,... | collective-permute-start | bytes 1376264 | tf_op jit(solution)/shard_map/ppermute | solution.py:773
  321.6 26.8 %collective-permute-start.77 = (bf16[64,512]{1,0:T(8,128)(2,1)S(1)}, bf16[64,512]{1,0:T(8,128)(2,1)S(1)}, u32[]{:S(2)}, u32[]{:S(2)}) collective-permute-start(bf16[64,512]{1,0:T(8,128)(2,1)S(1)} %get-tuple-element.329), channel_id=1, source_target_pairs={{0,8},{1,9},{2,10},{3,11},{4,12},{5,13},{6,14},{7,15},{8,0},{9,1},... | collective-permute-start | bytes 196616 | tf_op jit(solution)/shard_map/ppermute | solution.py:773
  322.0 27.8 %collective-permute-start.78 = (bf16[64,512]{1,0:T(8,128)(2,1)S(1)}, bf16[64,512]{1,0:T(8,128)(2,1)S(1)}, u32[]{:S(2)}, u32[]{:S(2)}) collective-permute-start(bf16[64,512]{1,0:T(8,128)(2,1)S(1)} %get-tuple-element.331), channel_id=1, source_target_pairs={{0,4},{1,5},{2,6},{3,7},{4,0},{5,1},{6,2},{7,3},{8,12},{9,13},{10,... | collective-permute-start | bytes 196616 | tf_op jit(solution)/shard_map/ppermute | solution.py:773
  323.6 27.8 %collective-permute-start.79 = (bf16[64,512]{1,0:T(8,128)(2,1)S(1)}, bf16[64,512]{1,0:T(8,128)(2,1)S(1)}, u32[]{:S(2)}, u32[]{:S(2)}) collective-permute-start(bf16[64,512]{1,0:T(8,128)(2,1)S(1)} %get-tuple-element.330), channel_id=1, source_target_pairs={{0,12},{1,13},{2,14},{3,15},{4,8},{5,9},{6,10},{7,11},{8,4},{9,5},... | collective-permute-start | bytes 196616 | tf_op jit(solution)/shard_map/ppermute | solution.py:773
  348.3 190.0 %collective-permute-start.57 = (bf16[256,1024]{1,0:T(8,128)(2,1)}, bf16[256,1024]{1,0:T(8,128)(2,1)}, u32[]{:S(2)}, u32[]{:S(2)}) collective-permute-start(bf16[256,1024]{1,0:T(8,128)(2,1)} %convert_element_type.532), channel_id=1, source_target_pairs={{16,24},{17,25},{18,26},{19,27},{20,28},{21,29},{22,30},{23,31},{2... | collective-permute-start | bytes 1572872 | tf_op jit(solution)/shard_map/ppermute | solution.py:773
  358.0 29.4 %collective-permute-start.44 = (bf16[256,1024]{1,0:T(8,128)(2,1)S(1)}, bf16[256,1024]{1,0:T(8,128)(2,1)S(1)}, u32[]{:S(2)}, u32[]{:S(2)}) collective-permute-start(bf16[256,1024]{1,0:T(8,128)(2,1)S(1)} %add_convert_fusion.11.refs_6_), channel_id=1, source_target_pairs={{0,16},{1,17},{2,18},{3,19},{4,20},{5,21},{6,22},{7,23},{8,24},{9,... | collective-permute-start | bytes 1572872 | tf_op jit(solution)/shard_map/ppermute | solution.py:773
  359.5 11.1 %collective-permute-start.83 = (bf16[64,896]{1,0:T(8,128)(2,1)S(1)}, bf16[64,896]{1,0:T(8,128)(2,1)S(1)}, u32[]{:S(2)}, u32[]{:S(2)}) collective-permute-start(bf16[64,896]{1,0:T(8,128)(2,1)S(1)} %get-tuple-element.341), channel_id=1, source_target_pairs={{0,8},{1,9},{2,10},{3,11},{4,12},{5,13},{6,14},{7,15},{8,0},{9,1},... | collective-permute-start | bytes 344072 | tf_op jit(solution)/shard_map/ppermute | solution.py:773
  365.3 12.0 %collective-permute-start.84 = (bf16[64,896]{1,0:T(8,128)(2,1)S(1)}, bf16[64,896]{1,0:T(8,128)(2,1)S(1)}, u32[]{:S(2)}, u32[]{:S(2)}) collective-permute-start(bf16[64,896]{1,0:T(8,128)(2,1)S(1)} %get-tuple-element.339), channel_id=1, source_target_pairs={{0,4},{1,5},{2,6},{3,7},{4,0},{5,1},{6,2},{7,3},{8,12},{9,13},{10,... | collective-permute-start | bytes 344072 | tf_op jit(solution)/shard_map/ppermute | solution.py:773
  365.3 12.0 %collective-permute-start.85 = (bf16[64,896]{1,0:T(8,128)(2,1)S(1)}, bf16[64,896]{1,0:T(8,128)(2,1)S(1)}, u32[]{:S(2)}, u32[]{:S(2)}) collective-permute-start(bf16[64,896]{1,0:T(8,128)(2,1)S(1)} %get-tuple-element.340), channel_id=1, source_target_pairs={{0,12},{1,13},{2,14},{3,15},{4,8},{5,9},{6,10},{7,11},{8,4},{9,5},... | collective-permute-start | bytes 344072 | tf_op jit(solution)/shard_map/ppermute | solution.py:773
  370.6 16.5 %collective-permute-start.42 = (bf16[256,1024]{1,0:T(8,128)(2,1)S(1)}, bf16[256,1024]{1,0:T(8,128)(2,1)S(1)}, u32[]{:S(2)}, u32[]{:S(2)}) collective-permute-start(bf16[256,1024]{1,0:T(8,128)(2,1)S(1)} %copy-done.87), channel_id=1, source_target_pairs={{0,16},{1,17},{2,18},{3,19},{4,20},{5,21},{6,22},{7,23},{8,24},{9,... | collective-permute-start | bytes 1572872 | tf_op jit(solution)/shard_map/ppermute | solution.py:773
  378.8 58.3 %collective-permute-start.86 = (bf16[2,64,896]{2,1,0:T(8,128)(2,1)}, bf16[2,64,896]{2,1,0:T(8,128)(2,1)}, u32[]{:S(2)}, u32[]{:S(2)}) collective-permute-start(bf16[2,64,896]{2,1,0:T(8,128)(2,1)} %pad_maximum_fusion.7), channel_id=1, source_target_pairs={{0,16},{1,17},{2,18},{3,19},{4,20},{5,21},{6,22},{7,23},{8,24},{9,... | collective-permute-start | bytes 688136 | tf_op jit(solution)/shard_map/ppermute | solution.py:773
  387.3 68.3 %collective-permute-start.48 = (bf16[256,1024]{1,0:T(8,128)(2,1)S(1)}, bf16[256,1024]{1,0:T(8,128)(2,1)}, u32[]{:S(2)}, u32[]{:S(2)}) collective-permute-start(bf16[256,1024]{1,0:T(8,128)(2,1)S(1)} %add_convert_fusion.12), channel_id=1, source_target_pairs={{0,4},{1,5},{2,6},{3,7},{4,0},{5,1},{6,2},{7,3},{8,12},{9,13},{10,... | collective-permute-start | bytes 1572872 | tf_op jit(solution)/shard_map/ppermute | solution.py:773
  420.5 42.7 %collective-permute-start.63 = (bf16[2,512,512]{2,1,0:T(8,128)(2,1)}, bf16[2,512,512]{2,1,0:T(8,128)(2,1)S(1)}, u32[]{:S(2)}, u32[]{:S(2)}) collective-permute-start(bf16[2,512,512]{2,1,0:T(8,128)(2,1)} %get-tuple-element.221), channel_id=1, source_target_pairs={{0,1},{1,0},{2,3},{3,2},{4,5},{5,4},{6,7},{7,6},{8,9},{9,8},{10,11... | collective-permute-start | bytes 3145736 | tf_op jit(solution)/shard_map/ppermute | solution.py:773
  421.5 14.6 %collective-permute-start.88 = (f32[13664]{0:T(1024)S(1)}, f32[13664]{0:T(1024)S(1)}, u32[]{:S(2)}, u32[]{:S(2)}) collective-permute-start(f32[13664]{0:T(1024)S(1)} %select_add_fusion), channel_id=1, source_target_pairs={{0,1},{1,0},{2,3},{3,2},{4,5},{5,4},{6,7},{7,6},{8,9},{9,8},{10,11... | collective-permute-start | bytes 163976 | tf_op jit(solution)/shard_map/ppermute | solution.py:773
  436.1 21.4 %collective-permute-start.69 = (bf16[2,256,896]{2,1,0:T(8,128)(2,1)}, bf16[2,256,896]{2,1,0:T(8,128)(2,1)}, u32[]{:S(2)}, u32[]{:S(2)}) collective-permute-start(bf16[2,256,896]{2,1,0:T(8,128)(2,1)} %get-tuple-element.225), channel_id=1, source_target_pairs={{0,1},{1,0},{2,3},{3,2},{4,5},{5,4},{6,7},{7,6},{8,9},{9,8},{10,11... | collective-permute-start | bytes 2752520 | tf_op jit(solution)/shard_map/ppermute | solution.py:773
  456.9 23.4 %collective-permute-start.49 = (bf16[256,1024]{1,0:T(8,128)(2,1)S(1)}, bf16[256,1024]{1,0:T(8,128)(2,1)S(1)}, u32[]{:S(2)}, u32[]{:S(2)}) collective-permute-start(bf16[256,1024]{1,0:T(8,128)(2,1)S(1)} %add_convert_fusion.8.refs_3_), channel_id=1, source_target_pairs={{0,16},{1,17},{2,18},{3,19},{4,20},{5,21},{6,22},{7,23},{8,24},{9,... | collective-permute-start | bytes 1572872 | tf_op jit(solution)/shard_map/ppermute | solution.py:773
  461.2 17.3 %collective-permute-start.46 = (bf16[256,1024]{1,0:T(8,128)(2,1)S(1)}, bf16[256,1024]{1,0:T(8,128)(2,1)S(1)}, u32[]{:S(2)}, u32[]{:S(2)}) collective-permute-start(bf16[256,1024]{1,0:T(8,128)(2,1)S(1)} %add_convert_fusion.10), channel_id=1, source_target_pairs={{0,4},{1,5},{2,6},{3,7},{4,0},{5,1},{6,2},{7,3},{8,12},{9,13},{10,... | collective-permute-start | bytes 1572872 | tf_op jit(solution)/shard_map/ppermute | solution.py:773
  469.2 18.4 %collective-permute-start.71 = (bf16[64,896]{1,0:T(8,128)(2,1)}, bf16[64,896]{1,0:T(8,128)(2,1)S(1)}, u32[]{:S(2)}, u32[]{:S(2)}) collective-permute-start(bf16[64,896]{1,0:T(8,128)(2,1)} %get-tuple-element.342), channel_id=1, source_target_pairs={{0,8},{1,9},{2,10},{3,11},{4,12},{5,13},{6,14},{7,15},{8,0},{9,1},... | collective-permute-start | bytes 344072 | tf_op jit(solution)/shard_map/ppermute | solution.py:773
  471.4 16.3 %collective-permute-start.72 = (bf16[64,896]{1,0:T(8,128)(2,1)}, bf16[64,896]{1,0:T(8,128)(2,1)S(1)}, u32[]{:S(2)}, u32[]{:S(2)}) collective-permute-start(bf16[64,896]{1,0:T(8,128)(2,1)} %get-tuple-element.344), channel_id=1, source_target_pairs={{0,4},{1,5},{2,6},{3,7},{4,0},{5,1},{6,2},{7,3},{8,12},{9,13},{10,... | collective-permute-start | bytes 344072 | tf_op jit(solution)/shard_map/ppermute | solution.py:773
  481.2 21.6 %collective-permute-start.64 = (bf16[512,512]{1,0:T(8,128)(2,1)S(1)}, bf16[512,512]{1,0:T(8,128)(2,1)}, u32[]{:S(2)}, u32[]{:S(2)}) collective-permute-start(bf16[512,512]{1,0:T(8,128)(2,1)S(1)} %fusion.11), channel_id=1, source_target_pairs={{0,2},{1,3},{2,0},{3,1},{4,6},{5,7},{6,4},{7,5},{8,10},{9,11},{10,... | collective-permute-start | bytes 1572872 | tf_op jit(solution)/shard_map/ppermute | solution.py:773
  508.1 12.0 %collective-permute-start.66 = (bf16[64,512]{1,0:T(8,128)(2,1)S(1)}, bf16[64,512]{1,0:T(8,128)(2,1)S(1)}, u32[]{:S(2)}, u32[]{:S(2)}) collective-permute-start(bf16[64,512]{1,0:T(8,128)(2,1)S(1)} %get-tuple-element.334), channel_id=1, source_target_pairs={{0,4},{1,5},{2,6},{3,7},{4,0},{5,1},{6,2},{7,3},{8,12},{9,13},{10,... | collective-permute-start | bytes 196616 | tf_op jit(solution)/shard_map/ppermute | solution.py:773
  508.1 13.3 %collective-permute-start.67 = (bf16[64,512]{1,0:T(8,128)(2,1)S(1)}, bf16[64,512]{1,0:T(8,128)(2,1)S(1)}, u32[]{:S(2)}, u32[]{:S(2)}) collective-permute-start(bf16[64,512]{1,0:T(8,128)(2,1)S(1)} %get-tuple-element.333), channel_id=1, source_target_pairs={{0,12},{1,13},{2,14},{3,15},{4,8},{5,9},{6,10},{7,11},{8,4},{9,5},... | collective-permute-start | bytes 196616 | tf_op jit(solution)/shard_map/ppermute | solution.py:773
  514.6 12.3 %collective-permute-start.74 = (bf16[2,64,896]{2,1,0:T(8,128)(2,1)S(1)}, bf16[2,64,896]{2,1,0:T(8,128)(2,1)S(1)}, u32[]{:S(2)}, u32[]{:S(2)}) collective-permute-start(bf16[2,64,896]{2,1,0:T(8,128)(2,1)S(1)} %pad_maximum_fusion.6), channel_id=1, source_target_pairs={{16,0},{17,1},{18,2},{19,3},{20,4},{21,5},{22,6},{23,7},{24,8},{25... | collective-permute-start | bytes 688136 | tf_op jit(solution)/shard_map/ppermute | solution.py:773
  516.5 17.3 %collective-permute-start.92 = (bf16[256,512]{1,0:T(8,128)(2,1)}, bf16[256,512]{1,0:T(8,128)(2,1)}, u32[]{:S(2)}, u32[]{:S(2)}) collective-permute-start(bf16[256,512]{1,0:T(8,128)(2,1)} %slice.523), channel_id=1, source_target_pairs={{0,0},{1,1},{2,2},{3,3},{4,8},{5,9},{6,10},{7,11},{16,4},{17,5},{1... | collective-permute-start | bytes 786440 | tf_op jit(solution)/shard_map/ppermute | solution.py:773
  520.1 16.2 %collective-permute-start.93 = (bf16[256,512]{1,0:T(8,128)(2,1)}, bf16[256,512]{1,0:T(8,128)(2,1)}, u32[]{:S(2)}, u32[]{:S(2)}) collective-permute-start(bf16[256,512]{1,0:T(8,128)(2,1)} %slice.523), channel_id=1, source_target_pairs={{8,0},{9,1},{10,2},{11,3},{12,8},{13,9},{14,10},{15,11},{24,4},{25... | collective-permute-start | bytes 786440 | tf_op jit(solution)/shard_map/ppermute | solution.py:773
  521.4 20.5 %collective-permute-start.56 = (bf16[256,1024]{1,0:T(8,128)(2,1)}, bf16[256,1024]{1,0:T(8,128)(2,1)}, u32[]{:S(2)}, u32[]{:S(2)}) collective-permute-start(bf16[256,1024]{1,0:T(8,128)(2,1)} %convert_element_type.531), channel_id=1, source_target_pairs={{0,8},{1,9},{2,10},{3,11},{4,12},{5,13},{6,14},{7,15},{8,0},{9,1},... | collective-permute-start | bytes 1572872 | tf_op jit(solution)/shard_map/ppermute | solution.py:773
  (122 other events, 1166.6 us)

commit v3 on v2

v3 whole, which is shorter than its diff:
```python
import functools
import types

import jax
import jax.numpy as jnp
from jax import lax
from jax.experimental import pallas as pl
from jax.experimental.pallas import tpu as pltpu
from jax.sharding import PartitionSpec as P

D = 1024
HEADDIM = 64
STATE = 128
KCONV = 4
BLOCK = 256
INNER = 2048
HEADS = 32
PAIR = 2 * STATE
LANES = 128
EPS = 1e-05
NEG = -1e30
BF = jnp.bfloat16
F32 = jnp.float32
HIGH = lax.Precision.HIGHEST
AXES = ("section", "seq", "wshard")
VMEM_LIMIT = 58 << 20
MICRO = 1.15e9


def nn(a, b, precision=None):
    return lax.dot_general(
        a, b, (((1,), (0,)), ((), ())), preferred_element_type=F32, precision=precision
    )


def nt(a, b):
    return lax.dot_general(a, b, (((1,), (1,)), ((), ())), preferred_element_type=F32)


def tn(a, b):
    return lax.dot_general(a, b, (((0,), (0,)), ((), ())), preferred_element_type=F32)


def two(x):
    hi = x.astype(BF)
    lo = (x - hi.astype(F32)).astype(BF)
    return jnp.concatenate([hi, lo], axis=1)


def iota(shape, dim):
    return lax.broadcasted_iota(jnp.int32, shape, dim)


def column(row):
    return jnp.broadcast_to(row, (LANES, row.shape[1])).T[:, :1]


def as_row(col):
    return jnp.broadcast_to(col, (col.shape[0], LANES)).T[:1]


def sigmoid(x):
    return 1.0 / (1.0 + jnp.exp(-x))


def softplus(x):
    return jnp.maximum(x, 0.0) + jnp.log1p(jnp.exp(-jnp.abs(x)))


def full(shape):
    return pl.BlockSpec(shape, lambda i: (0,) * len(shape))


class Names:
    def __getattr__(self, name):
        return name


N = Names()


def launch(name, body, grid, ins, outs, scratch=(), micros=1, aliases=()):
    names = [item[0] for item in ins] + [item[0] for item in outs] + [item[0] for item in scratch]

    def kernel(*refs):
        body(types.SimpleNamespace(**dict(zip(names, refs))))

    results = pl.pallas_call(
        kernel,
        grid=grid,
        in_specs=[item[2] for item in ins],
        out_specs=[item[3] for item in outs],
        out_shape=[jax.ShapeDtypeStruct(item[1], item[2]) for item in outs],
        scratch_shapes=[item[1] for item in scratch],
        compiler_params=pltpu.CompilerParams(
            dimension_semantics=(N.arbitrary,) * len(grid), vmem_limit_bytes=VMEM_LIMIT
        ),
        input_output_aliases=dict(aliases),
        cost_estimate=pl.CostEstimate(
            flops=int(micros * MICRO), bytes_accessed=1, transcendentals=0
        ),
        name=name,
    )(*[item[1] for item in ins])
    return types.SimpleNamespace(**dict(zip([item[0] for item in outs], results)))


def small():
    return pl.BlockSpec(memory_space=pltpu.SMEM)


def rows_of(width, first=0):
    return pl.BlockSpec((BLOCK, width), lambda i: (first + i, 0))


def turned(width, last):
    return pl.BlockSpec((BLOCK, width), lambda i: (last - i, 0))


def place(orders, halves):
    mine, theirs = halves
    total = 2 * mine.shape[0]

    def body(r):
        at = pl.program_id(0) * BLOCK + iota((BLOCK, total // 2), 0)
        first = (r.mine_order[...] == at).astype(BF)
        second = (r.their_order[...] == at).astype(BF)
        r.out[...] = (nn(first, r.mine[...]) + nn(second, r.theirs[...])).astype(BF)

    return launch(
        N.place,
        body,
        (total // BLOCK,),
        [
            (N.mine_order, orders[0], full((1, total // 2))),
            (N.their_order, orders[1], full((1, total // 2))),
            (N.mine, mine, full((total // 2, D))),
            (N.theirs, theirs, full((total // 2, D))),
        ],
        [(N.out, (total, D), BF, rows_of(D))],
        micros=5.3,
    ).out


def prepare_in(spot, in_w, seq):
    depth = in_w.shape[2] // 2
    heads = HEADS // seq
    width = heads * HEADDIM
    wide = max(width, LANES)
    side = 2 * wide + LANES
    shape = (2 * side + PAIR, depth)

    def body(r):
        core = r.spot[0]
        for at in range(seq // 2):

            @pl.when(r.spot[3] == at)
            def _():
                for half, ref in ((core, r.keep), (1 - core, r.give)):
                    span = pl.ds(pl.multiple_of(half * depth, depth), depth)
                    edge = r.w[0, 2 * INNER + PAIR :, span].astype(F32)

                    def piece(start):
                        value = r.w[0, start : start + width, span]
                        if width < wide:
                            room = jnp.zeros((wide - width, depth), BF)
                            value = jnp.concatenate([value, room], axis=0)
                        return value

                    for index in range(2):
                        head = 2 * at + index
                        base = index * (side + PAIR)
                        ref[base : base + wide] = piece(width * head)
                        ref[base + wide : base + 2 * wide] = piece(INNER + width * head)
                        raw = edge[heads * head : heads * (head + 1)]
                        room = jnp.zeros((LANES - heads, depth), F32)
                        raw = jnp.concatenate([raw, room], axis=0).astype(BF)
                        ref[base + 2 * wide : base + side] = raw
                    ref[side : side + PAIR] = r.w[0, 2 * INNER : 2 * INNER + PAIR, span]

    return launch(
        N.prepare_in,
        body,
        (1,),
        [(N.spot, spot, small()), (N.w, in_w, full(in_w.shape))],
        [(N.keep, shape, BF, full(shape)), (N.give, shape, BF, full(shape))],
        micros=3,
    )


def prepare_rest(spot, out_w, ends):
    out_shape = (out_w.shape[1] // 2, D)
    end_shape = (2, ends.shape[3] // 2, D)

    def body(r):
        core = r.spot[0]
        for half, out, end in ((core, r.out_keep, r.end_keep), (1 - core, r.out_give, r.end_give)):
            size = out_shape[0]
            out[...] = r.out_w[0, pl.ds(pl.multiple_of(half * size, size), size)]
            size = end_shape[1]
            span = pl.ds(pl.multiple_of(half * size, size), size)
            for batch in range(2):
                end[batch] = r.ends[0, batch, 0, span]

    return launch(
        N.prepare_rest,
        body,
        (1,),
        [
            (N.spot, spot, small()),
            (N.out_w, out_w, full(out_w.shape)),
            (N.ends, ends, full(ends.shape)),
        ],
        [
            (N.out_keep, out_shape, BF, full(out_shape)),
            (N.out_give, out_shape, BF, full(out_shape)),
            (N.end_keep, end_shape, BF, full(end_shape)),
            (N.end_give, end_shape, BF, full(end_shape)),
        ],
        micros=3,
    )


def assemble(spot, mine, theirs, wide, by_distance):
    depth = mine[0].shape[-1]
    side = 2 * wide + LANES
    total = PAIR + side
    count = 4

    def body(r):
        w = r.spot[1]
        named = vars(r)

        def parts_of(name, arrays):
            found = []
            for index, array in enumerate(arrays):
                ref = named[name + str(index)]
                if array.ndim == 2:
                    found.append(ref)
                else:
                    found += [ref.at[k] for k in range(array.shape[0])]
            return found

        def move(source, start, base, pair):
            span = pl.ds(pl.multiple_of(start, depth), depth)
            r.out[:wide, span] = source[base : base + wide]
            r.out[wide : wide + PAIR, span] = source[pair : pair + PAIR]
            r.out[wide + PAIR :, span] = source[base + wide : base + side]

        for core in range(2):

            @pl.when(r.spot[0] == core)
            def _():
                own = core * (side + PAIR)
                shards = list(range(count))
                other = shards
                if by_distance:
                    shards = (w, w ^ (1 + core), w ^ (2 - core), w ^ 3)
                    other = (w, w ^ (2 - core), w ^ (1 + core), w ^ 3)
                for source, shard in zip(parts_of(N.mine, mine), shards):
                    move(source, (2 * shard + core) * depth, own, side)
                for source, shard in zip(parts_of(N.theirs, theirs), other):
                    move(source, (2 * shard + 1 - core) * depth, core * PAIR, (1 - core) * side)

    return launch(
        N.assemble,
        body,
        (1,),
        [(N.spot, spot, small())]
        + [(N.mine + str(k), value, full(value.shape)) for k, value in enumerate(mine)]
        + [(N.theirs + str(k), value, full(value.shape)) for k, value in enumerate(theirs)],
        [(N.out, (total, 2 * count * depth), BF, full((total, 2 * count * depth)))],
        micros=4.5,
    ).out


def block_terms(raw, dtb, rate_sign, offset):
    rate = softplus(raw + dtb)
    lower = (iota((BLOCK, BLOCK), 1) <= iota((BLOCK, BLOCK), 0)).astype(F32)
    level = nn(lower, rate * rate_sign, HIGH)
    local = iota((BLOCK, 1), 0)
    end = level[BLOCK - 1 :]
    end_offset = offset[BLOCK - 1 :]
    head = jnp.where(offset > local, jnp.exp(level), 0.0)
    fade = jnp.where(local >= BLOCK - 1 - end_offset, jnp.exp(end - level), 0.0)
    carry = jnp.where(end_offset > BLOCK - 1, jnp.exp(end), 0.0)
    return rate, level, head, fade, carry


def either(flag, first, second):
    chosen = flag.astype(F32)
    return chosen * first.astype(F32) + (1.0 - chosen) * second.astype(F32)


def keep_or_give(r, core, block, split, value):
    slot = pl.ds(pl.multiple_of(block % split * BLOCK, BLOCK), BLOCK)

    @pl.when(block // split == core)
    def _():
        r.keep[slot] = value

    @pl.when(block // split != core)
    def _():
        r.away[slot] = value


def forward_body(layer, begin, wide, split, r):
    heads = wide // HEADDIM
    conv = PAIR + wide
    step = pl.program_id(0)
    core = r.spot[0]

    @pl.when(step == 0)
    def _():
        if begin:
            r.state[...] = jnp.zeros_like(r.state)
            r.halo[...] = jnp.zeros_like(r.halo)
        else:
            r.state[...] = r.state_in[...]
            r.halo[...] = r.halo_in[...]

    tokens = r.tokens[...].astype(F32)
    if layer == 1:
        scale = lax.rsqrt(column(r.last_rows[0][0:1]) / INNER + EPS)
        summed = either(step // split == core, r.mine[...], r.theirs[...])
        low = (tokens + summed * scale).astype(BF)
        r.next[...] = low
        tokens = low.astype(F32)
    scale = lax.rsqrt(jnp.mean(tokens * tokens, axis=1, keepdims=True) + EPS)
    x = (tokens * scale * r.gain[...]).astype(BF)
    r.normed[...] = x
    projected = nt(x, r.w[...])
    gate = projected[:, :wide]
    r.gate[...] = gate
    cin_low = projected[:, wide : wide + conv].astype(BF)
    r.cin[...] = cin_low
    raw_low = projected[:, wide + conv :].astype(BF)
    r.raw[...] = raw_low
    pos = r.pos[...]
    label_col = pos[:, 0:1]
    offset = pos[:, 1:2]
    cin = cin_low.astype(F32)
    longer = jnp.concatenate([r.halo[...], cin], axis=0)
    r.halo[...] = cin[BLOCK - 8 :]
    taps = r.taps[...]
    pre = taps[KCONV : KCONV + 1] + taps[KCONV - 1 : KCONV] * cin
    for index in range(KCONV - 1):
        delay = KCONV - 1 - index
        moved = longer[8 - delay : 8 - delay + BLOCK]
        pre = pre + jnp.where(offset >= delay, taps[index : index + 1] * moved, 0.0)
    r.pre[...] = pre
    mixed_conv = (pre * sigmoid(pre)).astype(BF)
    write = mixed_conv[:, :STATE]
    read = mixed_conv[:, STATE:PAIR]
    xs = mixed_conv[:, PAIR:]
    xs_float = xs.astype(F32)
    terms = r.terms[...]
    rate, level, head, fade, carry = block_terms(
        raw_low.astype(F32), terms[0:1], terms[1:2], offset
    )
    level_rows = level.T
    rate_rows = rate.T
    spread = r.spread[...]
    state = r.state[...]
    r.states[0] = state
    wides = r.wides[...]
    mixed = nn(two(head), spread) * nn(read, state.astype(BF)) + wides[0:1] * xs_float
    gram = nt(read, write)
    inside = (label_col == r.label[0]) & (iota((BLOCK, BLOCK), 1) <= iota((BLOCK, BLOCK), 0))
    closed = jnp.where(inside, 0.0, NEG)
    parts = []
    for first in range(0, heads, 2):
        span = xs[:, first * HEADDIM : (first + 2) * HEADDIM]
        mixing = []
        values = []
        for h in range(first, first + 2):
            weight = jnp.exp(level[:, h : h + 1] - level_rows[h : h + 1] + closed)
            mixing.append((gram * (weight * rate_rows[h : h + 1])).astype(BF))
            own = iota(span.shape, 1) // HEADDIM == h - first
            values.append(jnp.where(own, span, jnp.zeros_like(span)))
        parts.append(nn(jnp.concatenate(mixing, axis=1), jnp.concatenate(values, axis=0)))
    mixed = mixed + jnp.concatenate(parts, axis=1)
    mixed_low = mixed.astype(BF)
    r.mixed[...] = mixed_low
    carry_wide = nn(two(jnp.broadcast_to(carry, (8, LANES))), spread)[:1]
    written = (nn(two(fade * rate), spread) * xs_float).astype(BF)
    r.state[...] = carry_wide * state + tn(write, written)
    gv = mixed_low.astype(F32) * (gate * sigmoid(gate))
    r.rows[0, 0:1] = as_row(jnp.sum(gv * gv, axis=1, keepdims=True))
    scaled = gv * wides[1:2]
    if layer == 1:
        dotted = nt(r.dout[...], r.w_out[...]) * scaled
        r.rows[0, 1:2] = as_row(jnp.sum(dotted, axis=1, keepdims=True))
    else:
        r.rows[0, 1:2] = jnp.zeros((1, BLOCK), F32)
    keep_or_give(r, core, step, split, nn(scaled.astype(BF), r.w_out[...]).astype(BF))


def forward(layer, part, spot, env, tokens, before, weights, vectors, carried, dout):
    w, w_out = weights
    wide = w_out.shape[0]
    conv = PAIR + wide
    count = tokens.shape[0] // BLOCK // 2
    split = count // 2
    first = part * count
    total = count * BLOCK
    row = pl.BlockSpec((1, 2, BLOCK), lambda i: (i, 0, 0))
    ins = [
        (N.spot, spot, small()),
        (N.tokens, tokens, rows_of(D, first)),
        (N.gain, vectors[N.gain], full((1, D))),
        (N.w, w, full(w.shape)),
        (N.w_out, w_out, full(w_out.shape)),
        (N.taps, vectors[N.taps], full((8, conv))),
        (N.terms, vectors[N.terms], full((8, LANES))),
        (N.wides, vectors[N.wides], full((8, wide))),
        (N.spread, env.spread, full(env.spread.shape)),
        (N.pos, env.pos, rows_of(3, first)),
        (N.label, env.label_row, pl.BlockSpec((1, 1, BLOCK), lambda i: (first + i, 0, 0))),
    ]
    outs = [
        (N.normed, (total, D), BF, rows_of(D)),
        (N.gate, (total, wide), F32, rows_of(wide)),
        (N.pre, (total, conv), F32, rows_of(conv)),
        (N.cin, (total, conv), BF, rows_of(conv)),
        (N.raw, (total, LANES), BF, rows_of(LANES)),
        (N.mixed, (total, wide), BF, rows_of(wide)),
        (N.states, (count, STATE, wide), F32, pl.BlockSpec((1, STATE, wide), lambda i: (i, 0, 0))),
        (N.rows, (count, 2, BLOCK), F32, row),
        (N.state, (STATE, wide), F32, full((STATE, wide))),
        (N.halo, (8, conv), F32, full((8, conv))),
    ]
    joint = layer * total // 2
    side = pl.BlockSpec((total // 2, D), lambda i: (part * layer, 0))
    outs += [
        (N.keep, (total // 2 + joint, D), BF, side),
        (N.away, (total // 2 + joint, D), BF, side),
    ]
    aliases = []
    if part == 1:
        ins += [
            (N.state_in, carried.state, full((STATE, wide))),
            (N.halo_in, carried.halo, full((8, conv))),
        ]
        if layer == 1:
            anywhere = pl.BlockSpec(memory_space=pl.ANY)
            aliases = [(len(ins), len(outs) - 2), (len(ins) + 1, len(outs) - 1)]
            ins += [(N.keep_in, carried.keep, anywhere), (N.away_in, carried.away, anywhere)]
    if layer == 1:
        block = pl.BlockSpec((BLOCK, D), lambda i: (i % split, 0))
        mine, theirs, last_rows = before
        ins += [
            (N.mine, mine, block),
            (N.theirs, theirs, block),
            (N.last_rows, last_rows, row),
            (N.dout, dout, rows_of(D, first)),
        ]
        outs.append((N.next, (total, D), BF, rows_of(D)))
    return launch(
        N.forward,
        functools.partial(forward_body, layer, part == 0, wide, split),
        (count,),
        ins,
        outs,
        micros=12.5,
        aliases=aliases,
    )


def ungate_body(layer, wide, count, split, r):
    step = pl.program_id(0)
    block = count - 1 - step
    core = r.spot[0]

    @pl.when(step == 0)
    def _():
        r.ggated[...] = jnp.zeros_like(r.ggated)

    scale = lax.rsqrt(column(r.rows[0][0:1]) / INNER + EPS)
    if layer == 1:
        dout = r.dout[...]
        dots = column(r.rows[0][1:2])
    else:
        flag = block // split == core
        grad = either(flag, r.grad_mine[...], r.grad_theirs[...])
        dtokens = unnorm(r.tokens[...].astype(F32), r.gain[...], grad)
        dout = (r.dlater[...].astype(F32) + dtokens).astype(BF)
        r.dout[...] = dout
        summed = either(flag, r.mine[...], r.theirs[...])
        dots = jnp.sum(dout.astype(F32) * summed, axis=1, keepdims=True)
    gate = r.gate[...]
    gain = r.wides[1:2]
    mixed = r.mixed[...].astype(F32)
    sig = sigmoid(gate)
    act = gate * sig
    normal = mixed * act * scale
    grad_out = nt(dout, r.w_out[...])
    shared = dots * scale / INNER
    grad_gv = scale * (grad_out * gain - normal * shared)
    r.dmixed[...] = (grad_gv * act).astype(BF)
    r.dgate[...] = (grad_gv * mixed * (sig * (1.0 + gate * (1.0 - sig)))).astype(BF)
    r.ggated[...] += jnp.sum(grad_out * normal, axis=0, keepdims=True)
    r.normed_out[...] = (normal * gain).astype(BF)


def unnorm(tokens, gain, grad):
    scale = lax.rsqrt(jnp.mean(tokens * tokens, axis=1, keepdims=True) + EPS)
    normal = tokens * scale
    inner = grad * gain
    return scale * (inner - normal * jnp.mean(inner * normal, axis=1, keepdims=True))


def ungate(layer, part, spot, kept, rows, w_out, vectors, above):
    total, wide = kept.mixed.shape
    count = total // BLOCK
    split = count // 2
    last = count - 1
    row = pl.BlockSpec((1, 2, BLOCK), lambda i: (last - i, 0, 0))
    ins = [
        (N.spot, spot, small()),
        (N.rows, rows, row),
        (N.gate, kept.gate, turned(wide, last)),
        (N.mixed, kept.mixed, turned(wide, last)),
        (N.wides, vectors[N.wides], full((8, wide))),
        (N.w_out, w_out, full((wide, D))),
    ]
    outs = [
        (N.dmixed, (total, wide), BF, turned(wide, last)),
        (N.dgate, (total, wide), BF, turned(wide, last)),
        (N.normed_out, (total, wide), BF, turned(wide, last)),
        (N.ggated, (1, wide), F32, full((1, wide))),
    ]
    if layer == 1:
        ins.append((N.dout, above.dout, turned(D, part * count + last)))
    else:
        block = pl.BlockSpec((BLOCK, D), lambda i: ((last - i) % split, 0))
        ins += [
            (N.grad_mine, above.grad[0], block),
            (N.grad_theirs, above.grad[1], block),
            (N.mine, above.summed[0], block),
            (N.theirs, above.summed[1], block),
            (N.tokens, above.tokens, turned(D, last)),
            (N.gain, above.gain, full((1, D))),
            (N.dlater, above.dout, turned(D, part * count + last)),
        ]
        outs.append((N.dout, (total, D), BF, turned(D, last)))
    return launch(
        N.ungate,
        functools.partial(ungate_body, layer, wide, count, split),
        (count,),
        ins,
        outs,
        micros=5.5,
    )


def backward_body(begin, wide, count, split, r):
    heads = wide // HEADDIM
    conv = PAIR + wide
    step = pl.program_id(0)
    block = count - 1 - step
    core = r.spot[0]

    @pl.when(step == 0)
    def _():
        if begin:
            r.dstate[...] = jnp.zeros_like(r.dstate)
            r.halo[...] = jnp.zeros_like(r.halo)
        else:
            r.dstate[...] = r.dstate_in[...]
            r.halo[...] = r.halo_in[...]
        r.gtaps[...] = jnp.zeros_like(r.gtaps)
        r.gheads[...] = jnp.zeros_like(r.gheads)
        r.gskip[...] = jnp.zeros_like(r.gskip)
        r.ggain[...] = jnp.zeros_like(r.ggain)

    pos = r.pos[...]
    label_col = pos[:, 0:1]
    offset = pos[:, 1:2]
    remain = pos[:, 2:3]
    pre = r.pre[...]
    sig = sigmoid(pre)
    mixed_conv = (pre * sig).astype(BF)
    write = mixed_conv[:, :STATE]
    read = mixed_conv[:, STATE:PAIR]
    xs = mixed_conv[:, PAIR:]
    xs_float = xs.astype(F32)
    raw = r.raw[...].astype(F32)
    terms = r.terms[...]
    dtb = terms[0:1]
    sign = terms[1:2]
    rate, level, head, fade, carry = block_terms(raw, dtb, sign, offset)
    tail = fade * rate
    level_rows = level.T
    spread = r.spread[...]
    fold = r.fold[...]
    dy = r.dmixed[...]
    dy_float = dy.astype(F32)
    state = r.states[0]
    state_low = state.astype(BF)
    dstate = r.dstate[...]
    dstate_low = dstate.astype(BF)
    dhead = nn(two(dy_float * nn(read, state_low)), fold)
    tail_wide = nn(two(tail), spread)
    scaled = (nn(two(head), spread) * dy_float).astype(BF)
    written = (tail_wide * xs_float).astype(BF)
    through = nn(write, dstate_low)
    dtail = nn(two(xs_float * through), fold)
    r.gskip[...] += jnp.sum(dy_float * xs_float, axis=0, keepdims=True)
    carry_wide = nn(two(jnp.broadcast_to(carry, (8, LANES))), spread)[:1]
    held = jnp.broadcast_to(jnp.sum(state * dstate, axis=0, keepdims=True), (8, wide))
    dcarry = nn(two(held), fold)[:1]

    gram = nt(write, read)
    inside = (label_col == r.label[0]) & (iota((BLOCK, BLOCK), 0) <= iota((BLOCK, BLOCK), 1))
    closed = jnp.where(inside, 0.0, NEG)
    lane = iota((1, LANES), 1)
    drate = jnp.zeros((BLOCK, LANES), F32)
    level_sums = []
    parts = []
    dgram = jnp.zeros((BLOCK, BLOCK), F32)
    for first in range(0, heads, 2):
        cut_at = slice(first * HEADDIM, (first + 2) * HEADDIM)
        xs_span = xs[:, cut_at]
        dy_span = dy[:, cut_at]
        mixing = []
        values = []
        for h in range(first, first + 2):
            own = iota(xs_span.shape, 1) // HEADDIM == h - first
            xs_own = jnp.where(own, xs_span, jnp.zeros_like(xs_span))
            values.append(jnp.where(own, dy_span, jnp.zeros_like(dy_span)))
            decay = jnp.exp(level_rows[h : h + 1] - level[:, h : h + 1] + closed)
            rate_col = rate[:, h : h + 1]
            weight = decay * rate_col
            mixing.append((gram * weight).astype(BF))
            dmix = nt(xs_own, dy_span)
            dgram = dgram + dmix * weight
            bare = dmix * gram * decay
            drate = drate + jnp.sum(bare, axis=1, keepdims=True) * (lane == h).astype(F32)
            level_sums.append(jnp.sum(bare * rate_col, axis=0, keepdims=True))
        parts.append(nn(jnp.concatenate(mixing, axis=1), jnp.concatenate(values, axis=0)))
    dxs = jnp.concatenate(parts, axis=1) + r.wides[0:1] * dy_float + tail_wide * through
    dgram_low = dgram.astype(BF)
    dread = tn(dgram_low, write) + nt(scaled, state_low)
    dwrite = nn(dgram_low, read) + nt(written, dstate_low)
    r.dstate[...] = carry_wide * dstate + tn(read, scaled)

    level_sums.append(jnp.zeros((LANES - heads, BLOCK), F32))
    tail_flow = dtail * tail
    local = iota((BLOCK, 1), 0)
    last = jnp.sum(tail_flow, axis=0, keepdims=True) + dcarry * carry
    dlevel = jnp.concatenate(level_sums, axis=0).T - rate * drate + dhead * head - tail_flow
    dlevel = dlevel + jnp.where(local == BLOCK - 1, last, 0.0)
    upper = (iota((BLOCK, BLOCK), 0) <= iota((BLOCK, BLOCK), 1)).astype(F32)
    dsum = nn(upper, dlevel, HIGH)
    drate = drate + dtail * fade + sign * dsum
    draw = drate * sigmoid(raw + dtb)
    r.gheads[0:1] += jnp.sum(draw, axis=0, keepdims=True)
    r.gheads[1:2] += jnp.sum(rate * dsum, axis=0, keepdims=True) * sign

    dpre = jnp.concatenate([dwrite, dread, dxs], axis=1) * (sig * (1.0 + pre * (1.0 - sig)))
    longer = jnp.concatenate([dpre, r.halo[...]], axis=0)
    r.halo[...] = dpre[:8]
    cin = r.cin[...].astype(F32)
    taps = r.taps[...]
    r.gtaps[KCONV : KCONV + 1] += jnp.sum(dpre, axis=0, keepdims=True)
    r.gtaps[KCONV - 1 : KCONV] += jnp.sum(dpre * cin, axis=0, keepdims=True)
    dcin = taps[KCONV - 1 : KCONV] * dpre
    for index in range(KCONV - 1):
        delay = KCONV - 1 - index
        moved = jnp.where(remain >= delay, longer[delay : delay + BLOCK], 0.0)
        dcin = dcin + taps[index : index + 1] * moved
        r.gtaps[index : index + 1] += jnp.sum(moved * cin, axis=0, keepdims=True)
    rest = jnp.concatenate([dcin, draw], axis=1).astype(BF)
    r.rest[...] = rest
    w = r.w[...]
    dnormed = nn(r.dgate[...], w[:wide]) + nn(rest, w[wide:])
    r.ggain[...] += jnp.sum(dnormed * r.normed[...].astype(F32), axis=0, keepdims=True)
    keep_or_give(r, core, block, split, dnormed.astype(BF))


def backward(part, spot, env, kept, grads, w, vectors, carried):
    total, wide = kept.mixed.shape
    conv = PAIR + wide
    count = total // BLOCK
    split = count // 2
    last = count - 1
    top = part * count + last
    ins = [
        (N.spot, spot, small()),
        (N.w, w, full(w.shape)),
        (N.taps, vectors[N.taps], full((8, conv))),
        (N.terms, vectors[N.terms], full((8, LANES))),
        (N.wides, vectors[N.wides], full((8, wide))),
        (N.spread, env.spread, full(env.spread.shape)),
        (N.fold, env.fold, full(env.fold.shape)),
        (N.pos, env.pos, turned(3, top)),
        (N.label, env.label_row, pl.BlockSpec((1, 1, BLOCK), lambda i: (top - i, 0, 0))),
        (N.pre, kept.pre, turned(conv, last)),
        (N.cin, kept.cin, turned(conv, last)),
        (N.raw, kept.raw, turned(LANES, last)),
        (N.states, kept.states, pl.BlockSpec((1, STATE, wide), lambda i: (last - i, 0, 0))),
        (N.normed, kept.normed, turned(D, last)),
        (N.dmixed, grads.dmixed, turned(wide, last)),
        (N.dgate, grads.dgate, turned(wide, last)),
    ]
    if part == 0:
        ins += [
            (N.dstate_in, carried.dstate, full((STATE, wide))),
            (N.halo_in, carried.halo, full((8, conv))),
        ]
    outs = [
        (N.keep, (total // 2, D), BF, full((total // 2, D))),
        (N.away, (total // 2, D), BF, full((total // 2, D))),
        (N.rest, (total, conv + LANES), BF, turned(conv + LANES, last)),
        (N.gtaps, (8, conv), F32, full((8, conv))),
        (N.gheads, (8, LANES), F32, full((8, LANES))),
        (N.gskip, (1, wide), F32, full((1, wide))),
        (N.ggain, (1, D), F32, full((1, D))),
        (N.dstate, (STATE, wide), F32, full((STATE, wide))),
        (N.halo, (8, conv), F32, full((8, conv))),
    ]
    return launch(
        N.backward,
        functools.partial(backward_body, part == 1, wide, count, split),
        (count,),
        ins,
        outs,
        micros=14.5,
    )


def weight_grads(spot, lefts, rights, seq, outer=None, size=0):
    depth = lefts[0].shape[1]
    spans = []
    wide = 0
    for pair in rights:
        spans.append((wide, pair[0].shape[1]))
        wide += pair[0].shape[1]
    share = depth // (4 * seq)
    rows = depth // 4
    room = 0 if outer is None else outer[0][0].shape[1]

    def body(r):
        w = r.spot[1]
        z = r.spot[2]
        named = vars(r)
        sides = ((r.keep, (0, r.spot[5])), (r.away, (r.spot[4], 3)))
        for index, (base, width) in enumerate(spans):
            right = [named[N.right + str(index) + str(part)] for part in range(2)]
            r.total[:, base : base + width] = tn(r.left0[...], right[0][...]) + tn(
                r.left1[...], right[1][...]
            )
        for ref, shards in sides:
            for index, shard in enumerate(shards):
                for turn in range(seq):
                    start = ((z ^ turn) * 4 + (w ^ shard)) * share
                    piece = r.total[pl.ds(pl.multiple_of(start, share), share)]
                    ref[index, turn * share : (turn + 1) * share, :wide] = piece.astype(BF)
        if outer is None:
            return
        for part in range(D // room):
            cols = slice(part * room, (part + 1) * room)
            r.outer[...] = tn(r.out0[...], r.dout0[...][:, cols]) + tn(
                r.out1[...], r.dout1[...][:, cols]
            )
            for ref, shards in sides:
                for index, shard in enumerate(shards):
                    start = pl.multiple_of((w ^ shard) * size, size)
                    ref[index, part * size : (part + 1) * size, wide:] = r.outer[
                        pl.ds(start, size)
                    ].astype(BF)
        if size * (D // room) < rows:
            for ref, _ in sides:
                ref[:, size * (D // room) :, wide:] = jnp.zeros(
                    (2, rows - size * (D // room), room), BF
                )

    ins = [(N.spot, spot, small())]
    for index in range(2):
        ins.append((N.left + str(index), lefts[index], full(lefts[index].shape)))
    for index, pair in enumerate(rights):
        for part in range(2):
            ins.append((N.right + str(index) + str(part), pair[part], full(pair[part].shape)))
    scratch = [(N.total, pltpu.VMEM((depth, wide), F32))]
    if outer is not None:
        outs, douts = outer
        height = outs[0].shape[0]
        for index in range(2):
            ins.append((N.out + str(index), outs[index], full(outs[index].shape)))
            array, at = douts[index]
            spec = pl.BlockSpec((height, D), functools.partial(lambda at, i: (at, 0), at))
            ins.append((N.dout + str(index), array, spec))
        scratch.append((N.outer, pltpu.VMEM((room, room), F32)))
    shape = (2, rows, wide + room)
    return launch(
        N.weight_grads,
        body,
        (1,),
        ins,
        [(N.keep, shape, BF, full(shape)), (N.away, shape, BF, full(shape))],
        scratch=scratch,
        micros=6 if len(rights) == 1 else 11,
    )


def finish(kind, part, spot, orders, values, before):
    count = values.count
    split = count // 2
    total = count * BLOCK

    def body(r):
        step = pl.program_id(0)
        core = r.spot[0]

        @pl.when(step == 0)
        def _():
            if before is None:
                r.own[...] = jnp.zeros_like(r.own)
                r.across[...] = jnp.zeros_like(r.across)
            else:
                r.own[...] = r.own_in[...]
                r.across[...] = r.across_in[...]

        summed = either(step // split == core, r.mine[...], r.theirs[...])
        if kind == N.grad:
            dtokens = unnorm(r.tokens[...].astype(F32), r.gain[...], summed)
            value = r.rest[...].astype(F32) + dtokens
        else:
            scale = lax.rsqrt(column(r.rows[0][0:1]) / INNER + EPS)
            value = r.rest[...].astype(F32) + summed * scale
        low = value.astype(BF)
        at = (part * count + step) * BLOCK + iota((BLOCK, BLOCK), 1)
        r.own[...] += nn((r.own_order[...] == at).astype(BF), low).astype(BF)
        r.across[...] += nn((r.far_order[...] == at).astype(BF), low).astype(BF)

    block = pl.BlockSpec((BLOCK, D), lambda i: (values.first + i % split, 0))
    ins = [
        (N.spot, spot, small()),
        (N.own_order, orders[0], full((BLOCK, 1))),
        (N.far_order, orders[1], full((BLOCK, 1))),
        (N.mine, values.summed[0], block),
        (N.theirs, values.summed[1], block),
        (N.rest, values.rest, rows_of(D)),
    ]
    outs = [
        (N.own, (BLOCK, D), BF, full((BLOCK, D))),
        (N.across, (BLOCK, D), BF, full((BLOCK, D))),
    ]
    if kind == N.grad:
        ins += [
            (N.tokens, values.tokens, rows_of(D, part * count)),
            (N.gain, values.gain, full((1, D))),
        ]
    else:
        ins.append((N.rows, values.rows, pl.BlockSpec((1, 2, BLOCK), lambda i: (i, 0, 0))))
    if before is not None:
        ins += [
            (N.own_in, before.own, full((BLOCK, D))),
            (N.across_in, before.across, full((BLOCK, D))),
        ]
    return launch(
        N.finish, body, (count,), ins, outs, micros=5,
    )


def settle(spot, ends):
    rows = ends[0].shape[0]

    def body(r):
        core = r.spot[0]
        batch = r.spot[7]
        for layer, own, far in ((0, r.own0, r.far0), (1, r.own1, r.far1)):
            for at in range(2):

                @pl.when((core == layer) & (batch == at))
                def _():
                    r.out[0, at, 0] = own[...].astype(F32)
                    r.out[0, 1 - at, 0] = far[...].astype(F32)

    names = (N.own0, N.far0, N.own1, N.far1)
    shape = (1, 2, 1, rows, D)
    return launch(
        N.settle,
        body,
        (1,),
        [(N.spot, spot, small())]
        + [(name, value, full(value.shape)) for name, value in zip(names, ends)],
        [(N.out, shape, F32, full(shape))],
        micros=2,
    ).out


def gather_columns(spot, sides, seq):
    half = seq // 2
    heads = HEADS // seq
    width = heads * HEADDIM
    wide = max(width, LANES)
    share = sides[0][0].shape[1]
    shape = (1, share, 2 * INNER + PAIR + HEADS)

    def body(r):
        named = vars(r)
        for layer in range(2):

            @pl.when(r.spot[0] == layer)
            def _():
                raws = []
                pair = jnp.zeros((share, PAIR), F32)
                for place_at in range(half):
                    for side in range(2):
                        rank = 2 * place_at + side
                        part = named[N.side + str(layer) + str(side)][place_at].astype(F32)
                        r.out[0, :, width * rank : width * (rank + 1)] = part[:, :width]
                        start = wide + PAIR
                        r.out[0, :, INNER + width * rank : INNER + width * (rank + 1)] = part[
                            :, start : start + width
                        ]
                        pair = pair + part[:, wide : wide + PAIR]
                        raws.append(part[:, start + wide : start + wide + heads])
                r.out[0, :, 2 * INNER : 2 * INNER + PAIR] = pair
                r.out[0, :, 2 * INNER + PAIR :] = jnp.concatenate(raws, axis=1)

    ins = [(N.spot, spot, small())]
    for layer in range(2):
        for side in range(2):
            value = sides[layer][side]
            ins.append((N.side + str(layer) + str(side), value, full(value.shape)))
    return launch(
        N.gather_columns, body, (1,), ins, [(N.out, shape, F32, full(shape))], micros=2
    ).out


def pack(spot, fold, gains, scans, gated, seq):
    heads = HEADS // seq
    width = heads * HEADDIM
    wide = max(width, LANES)
    conv = PAIR + wide
    shape = (KCONV + 3, INNER + PAIR)
    ins = [(N.spot, spot, small()), (N.fold, fold, full(fold.shape))]
    for layer in range(2):
        ins.append((N.gain + str(layer), gains[layer], full((1, D))))
        for part in range(2):
            scan = scans[layer][part]
            for name, value in (
                (N.gtaps, scan.gtaps),
                (N.gheads, scan.gheads),
                (N.gskip, scan.gskip),
                (N.ggain, scan.ggain),
                (N.ggated, gated[layer][part].ggated),
            ):
                ins.append((name + str(layer) + str(part), value, full(value.shape)))

    def body(r):
        named = vars(r)

        def both(name, layer):
            return named[name + str(layer) + "0"][...] + named[name + str(layer) + "1"][...]

        for layer in range(2):
            taps = both(N.gtaps, layer)
            by_head = both(N.gheads, layer)
            skips = jnp.broadcast_to(both(N.gskip, layer), (8, wide))
            skips = nn(two(skips), r.fold[...])[:1]
            gated_row = both(N.ggated, layer)
            gain_row = both(N.ggain, layer) / named[N.gain + str(layer)][...]

            def fill(ref):
                ref[...] = jnp.zeros(shape, F32)
                ref[: KCONV + 1, INNER:] = taps[: KCONV + 1, :PAIR]
                ref[KCONV + 2 :, :D] = gain_row
                for rank in range(seq):

                    @pl.when(r.spot[6] == rank)
                    def _():
                        cols = slice(rank * width, (rank + 1) * width)
                        ref[: KCONV + 1, cols] = taps[: KCONV + 1, PAIR : PAIR + width]
                        ref[KCONV + 1 : KCONV + 2, cols] = gated_row[:, :width]
                        row = []
                        for value in (by_head[0:1], by_head[1:2], skips):
                            if rank:
                                row.append(jnp.zeros((1, rank * heads), F32))
                            row.append(value[:, :heads])
                            if rank < seq - 1:
                                row.append(jnp.zeros((1, HEADS - (rank + 1) * heads), F32))
                        row.append(jnp.zeros((1, PAIR - 3 * HEADS), F32))
                        ref[KCONV + 1 : KCONV + 2, INNER:] = jnp.concatenate(row, axis=1)

            @pl.when(r.spot[0] == layer)
            def _():
                fill(r.mine)

            @pl.when(r.spot[0] != layer)
            def _():
                fill(r.give)

    return launch(
        N.pack,
        body,
        (1,),
        ins,
        [(N.mine, shape, F32, full(shape)), (N.give, shape, F32, full(shape))],
        micros=2,
    )


class Plan:
    def __init__(self):
        self.seq = lax.axis_size(N.seq)
        self.shards = lax.axis_size(N.wshard)
        self.half = self.seq // 2
        self.core = lax.axis_index(N.section)
        self.z = lax.axis_index(N.seq)
        self.w = lax.axis_index(N.wshard)
        self.batch = self.z // self.half
        self.place = self.z % self.half
        self.rank = 2 * self.place + self.core

    def send(self, value, route, cores=(0, 1)):
        pairs = []
        for c in range(2):
            for z in range(self.seq):
                for w in range(self.shards):
                    target = route(c, z, w)
                    if c in cores and target is not None:
                        source = (c * self.seq + z) * self.shards + w
                        tc, tz, tw = target
                        pairs.append((source, (tc * self.seq + tz) * self.shards + tw))
        return lax.ppermute(value, AXES, pairs)

    def swap(self, value, cores=(0, 1)):
        return self.send(value, lambda c, z, w: (1 - c, z, w), cores)

    def along(self, value, k, cores=(0, 1)):
        return self.send(value, lambda c, z, w: (c, z ^ k, w), cores)

    def first_side(self, value):
        return self.send(value, lambda c, z, w: (c, z, w ^ (1 + c)))

    def second_side(self, value):
        return self.send(value, lambda c, z, w: (c, z, w ^ (2 - c)))

    def own(self, first, second):
        return jnp.where(self.core == 0, first, second)

    def reach(self, near, far):
        pieces = [self.along(near, k) for k in range(1, self.half)]
        return near, pieces, self.along(far, self.half)

    def collect(self, reached, mark, late):
        near, pieces, came = reached
        came = after(came, mark)
        more = [self.along(came, k) for k in range(1, self.half)]
        mine = jnp.concatenate([near] + pieces + [came] + [after(piece, late) for piece in more], axis=0)
        return mine, self.swap(mine)

    def fold(self, terms):
        return add(terms.keep, self.swap(terms.away))

    def reduce(self, total, *marks):
        hop = 1
        while hop < self.half:
            total = add(total, after(self.along(total, hop), *marks))
            hop *= 2
        return total, self.swap(total)

    def chip_total(self, value):
        return value + self.swap(value)

    def total(self, value, *marks):
        hop = 1
        while hop < self.half:
            value = value + after(self.along(value, hop), *marks)
            hop *= 2
        return value

    def home(self, value, batch, layer):
        half = self.half

        def route(c, z, w):
            if z // half != batch:
                return None
            return (layer, 2 * (z % half) + c, w)

        return self.send(value, route)

    def gather_chips(self, value, share):
        pieces = [value[:share]]
        for k in range(1, self.seq):
            pieces.append(self.along(value[k * share : (k + 1) * share], k))
        half = self.half
        terms = [add(pieces[k], pieces[k + half]) for k in range(half)]
        if half == 2:
            even = self.place == 0
            ordered = [jnp.where(even, terms[0], terms[1]), jnp.where(even, terms[1], terms[0])]
            return jnp.stack(ordered)
        stacked = jnp.stack(terms)
        return stacked[self.place ^ jnp.arange(half)]


def add(first, second):
    return (first.astype(F32) + second.astype(F32)).astype(BF)


def after(value, *others):
    return lax.optimization_barrier((value,) + others)[0]


def pick(value, index, axis=0):
    return lax.dynamic_index_in_dim(value, index, axis, keepdims=False)


def cut(value, start, size, axis):
    return lax.dynamic_slice_in_dim(value, start, size, axis)


def on_device(
    ends_in,
    seq_lengths,
    deal_order,
    norm_w,
    in_w,
    conv_w,
    conv_b,
    dt_bias,
    a_log,
    d_skip,
    gnorm_w,
    out_w,
):
    plan = Plan()
    core = plan.core
    half = plan.half
    rank = plan.rank
    seq = plan.seq
    rows = ends_in.shape[3]
    total = rows * seq
    count = total // BLOCK
    heads = HEADS // seq
    width = heads * HEADDIM
    wide = max(width, LANES)
    side = 2 * wide + LANES
    first = 1 + core
    second = 2 - core
    spot = jnp.stack([core, plan.w, plan.z, plan.place, first, second, rank, plan.batch])
    spot = spot.astype(jnp.int32)

    def padded(value, size):
        return jnp.pad(value, ((0, 0), (0, size - value.shape[1])))

    held = prepare_in(spot, jnp.swapaxes(in_w, 1, 2), seq)
    came = plan.swap(held.give)
    chunk_parts = [plan.own(held.keep, came), plan.own(came, held.keep)]
    held = prepare_rest(after(spot, held.give), out_w, ends_in)
    came = plan.swap(held.end_give)
    end_parts = [plan.own(held.end_keep, came), plan.own(came, held.end_keep)]
    came = plan.swap(held.out_give)
    out_parts = [plan.own(held.out_keep, came), plan.own(came, held.out_keep)]
    half_rows = rows // 2

    order = pick(deal_order[:, 0], plan.batch)
    by_chip = order.reshape(seq, 2, half_rows)[plan.z ^ jnp.arange(seq)]
    orders = (
        pick(by_chip, core, 1).reshape(1, total // 2),
        pick(by_chip, 1 - core, 1).reshape(1, total // 2),
    )
    end_orders = (
        cut(order, rows * plan.z, rows, 0).reshape(rows, 1),
        cut(order, rows * (plan.z ^ half), rows, 0).reshape(rows, 1),
    )

    def give(value):
        return plan.swap(cut(value, (1 - core) * side, side + PAIR, value.ndim - 2))

    def in_weights(part):
        near = plan.first_side(part)
        beyond = plan.second_side(part)
        far = plan.second_side(near)
        theirs = (give(jnp.stack([part, near, beyond])), give(far))
        return assemble(spot, (part, near, beyond, far), theirs, wide, True), near, far

    def later_in_weights(part):
        every = lax.all_gather(part, N.wshard)
        return assemble(spot, (every,), (give(every),), wide, False)

    def chosen_rows(every):
        half_part = every.shape[1]
        if half == 2:
            mine = pick(every, rank)
            theirs = plan.swap(pick(every, rank ^ 1))
            return jnp.concatenate([plan.own(mine, theirs), plan.own(theirs, mine)], axis=0)
        other = plan.swap(every)
        whole = jnp.stack([plan.own(every, other), plan.own(other, every)], axis=1)
        whole = whole.reshape(8 * half_part, D)
        return jnp.pad(cut(whole, width * rank, width, 0), ((0, wide - width), (0, 0)))

    def out_weights(part):
        if half == 2:
            low_shard = plan.w // 2

            def route(c, z, w):
                return (c, z, w ^ 2) if w // 2 == z % half else None

            came = plan.send(part, route)
            here = jnp.where(low_shard == plan.place, part, came)
            beside = plan.send(here, lambda c, z, w: (c, z, w ^ 1))
            same = plan.w % 2 == core
            mine = jnp.where(same, here, beside)
            theirs = plan.swap(jnp.where(same, beside, here))
            return jnp.concatenate([plan.own(mine, theirs), plan.own(theirs, mine)], axis=0)
        return chosen_rows(lax.all_gather(part, N.wshard))

    def reach(part):
        return plan.reach(pick(part, plan.batch), pick(part, 1 - plan.batch))

    w_first, in_near, in_far = in_weights(chunk_parts[0])
    started = plan.collect(reach(end_parts[0]), in_far, in_far)
    w_out_first = out_weights(after(out_parts[0], in_near))
    w_second = later_in_weights(after(chunk_parts[1], in_far))
    w_out_second = out_weights(after(out_parts[1], w_out_first))
    weights = [(w_first, w_out_first), (w_second, w_out_second)]

    tokens = place(orders, started)

    lengths = pick(seq_lengths[:, 0], plan.batch)
    ends = jnp.cumsum(lengths)
    at = iota((total,), 0)
    passed = at[:, None] >= ends[None, :]
    label = jnp.sum(passed.astype(jnp.int32), axis=1)
    begin = jnp.max(jnp.where(passed, ends[None, :], 0), axis=1)
    finished = jnp.min(jnp.where(passed, total, ends[None, :]), axis=1)
    channel_head = iota((LANES, wide), 1) // HEADDIM
    hot = (channel_head == iota((LANES, wide), 0)).astype(BF)
    env = types.SimpleNamespace(
        pos=jnp.stack([label, at - begin, finished - 1 - at], axis=1),
        label_row=label.reshape(count, 1, BLOCK),
        spread=jnp.concatenate([hot, hot], axis=0),
        fold=jnp.concatenate([hot.T, hot.T], axis=0),
    )

    own_small = jnp.concatenate(
        [
            norm_w[0],
            conv_w[0].reshape(-1),
            conv_b[0],
            dt_bias[0],
            a_log[0],
            d_skip[0],
            gnorm_w[0],
        ]
    )
    other_small = plan.swap(own_small)
    sizes = (D, (KCONV + 1) * (INNER + PAIR), HEADS, HEADS, HEADS, INNER)

    def pieces_of(flat):
        pieces = []
        begin = 0
        for size in sizes:
            pieces.append(flat[begin : begin + size])
            begin += size
        return pieces

    def vectors_of(layer):
        flat = jnp.where(core == layer, own_small, other_small)
        gain, taps, dtb, log_rate, skip, gated = pieces_of(flat)
        taps = taps.reshape(KCONV + 1, INNER + PAIR)
        channels = jnp.concatenate(
            [taps[:, INNER:], padded(cut(taps, rank * width, width, 1), wide)], axis=1
        )

        def lanes(value):
            return padded(cut(value, rank * heads, heads, 0)[None], LANES)

        terms = jnp.concatenate([lanes(dtb), lanes(-jnp.exp(log_rate))], axis=0)
        skips = jnp.repeat(cut(skip, rank * heads, heads, 0), HEADDIM)[None]
        wides = jnp.concatenate([skips, cut(gated, rank * width, width, 0)[None]], axis=0)
        return {
            N.gain: gain[None],
            N.taps: jnp.pad(channels, ((0, 8 - KCONV - 1), (0, 0))),
            N.terms: jnp.pad(terms, ((0, 6), (0, 0))),
            N.wides: jnp.pad(wides, ((0, 6), (0, wide - width))),
        }

    vectors = [vectors_of(0), vectors_of(1)]

    kept = [[], []]
    rows_summed = [[], []]
    summed = [[], []]
    def pass_on(layer, part, turn, before, dout):
        carried = kept[layer][0] if part == 1 else None
        done = forward(
            layer, part, turn, env, tokens, before, weights[layer], vectors[layer], carried, dout
        )
        kept[layer].append(done)
        return done

    reached = reach(after(end_parts[1], *started))
    done = pass_on(0, 0, spot, None, None)
    mark = done.rows
    rows_low = plan.chip_total(done.rows)
    folded = plan.fold(done)
    done = pass_on(0, 1, after(spot, folded, rows_low), None, None)
    rows_summed[0].append(plan.total(rows_low, done.rows))
    summed[0].append(plan.reduce(folded, done.rows))
    cotangent = place(orders, plan.collect(reached, mark, done.rows))
    folded = plan.fold(done)
    rows_summed[0].append(plan.total(plan.chip_total(done.rows)))
    turn = after(spot, folded, rows_summed[0][1])
    done = pass_on(1, 0, turn, summed[0][0] + (rows_summed[0][0],), cotangent)
    summed[0].append(plan.reduce(folded, done.rows))
    rows_low = plan.chip_total(done.rows)
    turn = after(spot, rows_low)
    done = pass_on(1, 1, turn, summed[0][1] + (rows_summed[0][1],), cotangent)
    rows_summed[1].append(plan.total(rows_low, done.rows))
    rows_summed[1].append(plan.total(plan.chip_total(done.rows)))
    last_fold = after(plan.fold(done), *rows_summed[1])

    grads_summed = [[None, None], [None, None]]
    gated = [[None, None], [None, None]]
    scans = [[None, None], [None, None]]
    grad_parts = [[None, None], [None, None]]

    def ungate_part(layer, part, turn):
        above = types.SimpleNamespace(dout=cotangent)
        if layer == 0:
            above.grad = grads_summed[1][part]
            above.summed = summed[0][part]
            above.tokens = kept[1][part].next
            above.gain = vectors[1][N.gain]
        gated[layer][part] = ungate(
            layer,
            part,
            turn,
            kept[layer][part],
            rows_summed[layer][part],
            weights[layer][1],
            vectors[layer],
            above,
        )

    def scan_part(layer, part, turn):
        carried = scans[layer][1] if part == 0 else None
        scan = backward(
            part, turn, env, kept[layer][part], gated[layer][part], weights[layer][0], vectors[layer], carried
        )
        scans[layer][part] = scan
        return plan.fold(scan)

    def outer_of(layer):
        douts = [(cotangent, 0), (cotangent, 1)]
        if layer == 0:
            douts = [(item.dout, 0) for item in gated[0]]
        return [item.normed_out for item in gated[layer]], douts

    def normed_of(layer):
        return [item.normed for item in kept[layer]]

    def gates_of(layer):
        return [item.dgate for item in gated[layer]]

    def rests_of(layer):
        return [item.rest for item in scans[layer]]

    def first_hop(terms):
        return plan.first_side(terms.away)

    def first_add(terms, came):
        return add(terms.keep[0], came[0]), add(terms.keep[1], came[1])

    def finish_part(kind, part, turn, before):
        if kind == N.result:
            values = types.SimpleNamespace(
                summed=last_sums,
                rest=kept[1][part].next,
                rows=rows_summed[1][part],
                first=part * (count // 4),
            )
        else:
            values = types.SimpleNamespace(
                summed=grads_summed[0][part],
                rest=gated[0][part].dout,
                tokens=tokens,
                gain=vectors[0][N.gain],
                first=0,
            )
        values.count = count // 2
        return finish(kind, part, turn, end_orders, values, before)

    share = D // (4 * seq)
    gate_span = wide
    rest_span = side + PAIR - wide
    def homed(outs, layer, *marks):
        return add(
            after(plan.home(outs, 0, layer), *marks), after(plan.home(outs, 1, layer), *marks)
        )

    ungate_part(1, 0, spot)
    ungate_part(1, 1, spot)
    folded = scan_part(1, 1, spot)
    last_sums = plan.reduce(last_fold, scans[1][1].gskip)
    upper = folded
    folded = scan_part(1, 0, after(spot, folded, *last_sums))
    mark = scans[1][0].gskip
    grads_summed[1][1] = plan.reduce(upper, mark)
    result = finish_part(N.result, 0, after(spot, mark), None)
    result = finish_part(N.result, 1, spot, result)
    terms = weight_grads(
        after(spot, result.own, folded),
        normed_of(1),
        (gates_of(1), rests_of(1)),
        seq,
        outer_of(1),
        width // 4,
    )
    came = first_hop(terms)
    grads_summed[1][0] = plan.reduce(folded, terms.away)
    ungate_part(0, 1, after(spot, terms.away))
    result_far = plan.along(result.across, half, (1,))
    folded = scan_part(0, 1, after(spot, gated[0][1].ggated, *grads_summed[1][0]))
    pair = first_add(terms, after(came, scans[0][1].gskip))
    given = plan.second_side(pair[1])
    ungate_part(0, 0, after(spot, folded, pair[1]))
    gate_terms = weight_grads(
        after(spot, gated[0][0].ggated), normed_of(0), (gates_of(0),), seq, outer_of(0), width // 4
    )
    gate_came = first_hop(gate_terms)
    grads_summed[0][1] = plan.reduce(folded, gate_terms.away)
    later_last = add(pair[0], after(given, gate_terms.away))
    start_grad = finish_part(N.grad, 1, after(spot, later_last), None)
    folded = scan_part(0, 0, after(spot, start_grad.own, result_far))
    mark = scans[0][0].gskip
    chips_later = plan.gather_chips(later_last[:, : gate_span + rest_span], share)
    came_later = plan.swap(chips_later, (0,))
    outs_later = homed(later_last[:, gate_span + rest_span :], 1)
    rest_terms = weight_grads(
        after(spot, mark, chips_later, outs_later, folded), normed_of(0), (rests_of(0),), seq
    )
    rest_came = first_hop(rest_terms)
    grads_summed[0][0] = plan.reduce(folded, rest_terms.away)
    gate_pair = first_add(gate_terms, after(gate_came, mark))
    gate_given = plan.second_side(gate_pair[1])
    rest_pair = first_add(rest_terms, rest_came)
    rest_given = plan.second_side(rest_pair[1])
    gate_last = add(gate_pair[0], after(gate_given, rest_terms.away))
    start_grad = finish_part(N.grad, 0, after(spot, rest_pair[1]), start_grad)
    rest_last = add(rest_pair[0], rest_given)
    joined = jnp.concatenate([gate_last[:, :gate_span], rest_last], axis=1)
    chips_first = plan.gather_chips(joined, share)
    weight_sums = [
        (homed(gate_last[:, gate_span:], 0, rest_last), chips_first, plan.swap(chips_first, (1,))),
        (outs_later, chips_later, came_later),
    ]

    grad_far = plan.along(start_grad.across, half, (0,))
    ends_out = settle(spot, (start_grad.own, grad_far, result.own, result_far))

    both_sides = []
    out_grads = []
    for layer in range(2):
        outs, chips, came = weight_sums[layer]
        size = width // 4
        pieces = [outs[k * size : (k + 1) * size] for k in range(D // wide)]
        out_grads.append(jnp.concatenate(pieces, axis=1).astype(F32))
        both_sides.append((chips, came) if layer == 0 else (came, chips))
    g_in = gather_columns(spot, both_sides, seq)
    g_out = plan.own(out_grads[0], out_grads[1])

    packed = pack(after(spot, folded), env.fold, [item[N.gain] for item in vectors], scans, gated, seq)
    sums = packed.mine + plan.swap(packed.give)
    sums = sums + after(plan.first_side(after(sums, rest_terms.away)), rest_pair[1])
    sums = sums + plan.second_side(after(sums, rest_last))
    hop = 1
    while hop < seq:
        sums = sums + after(plan.along(sums, hop), grad_far)
        hop *= 2
    heads_at = INNER + HEADS
    return (
        ends_out,
        sums[KCONV + 2 :, :D],
        g_in,
        sums[None, :KCONV],
        sums[KCONV][None],
        sums[KCONV + 1 : KCONV + 2, INNER:heads_at],
        sums[KCONV + 1 : KCONV + 2, heads_at : heads_at + HEADS],
        sums[KCONV + 1 : KCONV + 2, heads_at + HEADS : heads_at + 2 * HEADS],
        sums[KCONV + 1 : KCONV + 2, :INNER],
        g_out[None],
    )


def solution(mesh):
    placed = (
        P("section", None, "wshard", "seq", None),
        P(None, "wshard", None),
        P(None, "wshard", None),
        P("section", None),
        P("section", "wshard", None),
        P("section", None, None),
        P("section", None),
        P("section", None),
        P("section", None),
        P("section", None),
        P("section", None),
        P("section", "wshard", None),
    )
    return jax.shard_map(
        on_device,
        mesh=mesh,
        in_specs=placed,
        out_specs=(
            P("section", None, "wshard", "seq", None),
            P("section", None),
            P("section", ("seq", "wshard"), None),
            P("section", None, None),
            P("section", None),
            P("section", None),
            P("section", None),
            P("section", None),
            P("section", None),
            P("section", ("seq", "wshard"), None),
        ),
        check_vma=False,
    )
```

time: 556 us -> 452 us (0.81)
  local copies, waits for them, and re-layouts: 60.1 us -> 24.3 us
  starting transfers between devices: 121 us -> 88.5 us
  other arithmetic: 67.2 us -> 35.3 us
  waiting for transfers between devices: 94.2 us -> 71.4 us
  between operations: 2.69 us -> 15.7 us
  Pallas kernels: 200 us -> 211 us
    ppermute x96 -> x78, starting transfers between devices: 121 us -> 88.4 us  [send(): return lax.ppermute(value, AXES, pairs)]
    ppermute x96 -> x78, waiting for transfers between devices: 94.2 us -> 71.4 us  [send(): return lax.ppermute(value, AXES, pairs)]
    unnamed x183 -> x102, local copies, waits for them, and re-layouts: 16.3 us -> 4.92 us
    concatenate x23 -> x2, local copies, waits for them, and re-layouts: 11.6 us -> 0.7 us  [on_device(): out_grads.append(jnp.concatenate(pieces, axis=1).astype(F32))]
    pallas_call x24 -> x28, Pallas kernels: 200 us -> 211 us  [launch(): pl.pallas_call(kernel, grid=grid, in_specs=[item[2] for item in ins], out...]
    convert_element_type x24 -> x22, other arithmetic: 18.8 us -> 9.28 us  [add(): return (first.astype(F32) + second.astype(F32)).astype(BF)]
    dynamic_slice x14 -> x8, local copies, waits for them, and re-layouts: 11.5 us -> 3.17 us  [cut(): return lax.dynamic_slice_in_dim(value, start, size, axis)]
    convert_element_type x10 -> x0, other arithmetic: 7.63 us -> none  [the longest x4 2.73 us: on_device(): part = rest_side[place_at].astype(F32)]
  transfers between devices with their start and end apart: 96 -> 79, of which waited for: 24 -> 22; matrix products, arithmetic and copies ran while one was open for 21% -> 12% of each run, Pallas kernels for 37% -> 43%
where the time goes in v3:
time: 452 us; the launch traced here: 446 us
  Pallas kernels  211 us (47%)
  starting transfers between devices  88.5 us (20%)
  waiting for transfers between devices  71.4 us (16%)
  other arithmetic  35.3 us (8%)
  local copies, waits for them, and re-layouts  24.3 us (5%)
  between operations  15.7 us (3%)
    pallas_call x28, Pallas kernels, launch(): pl.pallas_call(kernel, grid=grid, in_specs=[item[2] for item in ins], out...  211 us
    ppermute x78, starting transfers between devices, send(): return lax.ppermute(value, AXES, pairs)  88.4 us
    ppermute x78, waiting for transfers between devices, send(): return lax.ppermute(value, AXES, pairs)  71.4 us
    convert_element_type x22, other arithmetic, add(): return (first.astype(F32) + second.astype(F32)).astype(BF)  9.28 us
  transfers between devices with their start and end apart: 79, of which 22 were waited for; matrix products, arithmetic and copies ran while one was open for 12% of the time, Pallas kernels for 43%

profile of v3, /device:TPU:0, one launch (start us, length us, event | category | flops | bytes accessed | tf_op | source)
XLA Modules:
  0.0 446.0 jit_solution(1083632818650594603)
XLA Ops:
  8.0 2.9 prepare_in.1
  11.5 3.1 prepare_rest.1
  22.8 2.9 collective-permute-start.4
  30.8 7.4 %collective-permute-done.4.refs_2_ = bf16[2560,128]{1,0:T(8,128)(2,1)} collective-permute-done((bf16[2560,128]{1,0:T(8,128)(2,1)S(1)}, bf16[2560,128]{1,0:T(8,128)(2,1)}, u32[]{:S(2)}, u32[]{:S(2)}) %collective-permute-start.4) | collective-permute-done | bytes 655392 | tf_op jit(solution)/shard_map/ppermute | solution.py:1028
  38.2 5.7 %collective-permute-start.13 = (bf16[256,1024]{1,0:T(8,128)(2,1)S(1)}, bf16[256,1024]{1,0:T(8,128)(2,1)S(1)}, u32[]{:S(2)}, u32[]{:S(2)}) collective-permute-start(bf16[256,1024]{1,0:T(8,128)(2,1)S(1)} %get-tuple-element.182), channel_id=1, source_target_pairs={{0,2},{1,3},{6,4},{7,5},{8,10},{9,11},{14,12},{15,13},{16,18},{17,... | collective-permute-start | bytes 1572872 | tf_op jit(solution)/shard_map/ppermute | solution.py:1028
  44.1 2.4 collective-permute-start.2
  48.0 3.2 collective-permute-done.13
  51.3 2.5 collective-permute-start.14
  53.8 2.5 collective-permute-start.1
  56.3 2.0 collective-permute-done.5.refs_4_
  58.3 2.4 collective-permute-start.6
  60.9 6.2 %collective-permute-done.6 = bf16[128,1024]{1,0:T(8,128)(2,1)S(1)} collective-permute-done((bf16[128,1024]{1,0:T(8,128)(2,1)S(1)}, bf16[128,1024]{1,0:T(8,128)(2,1)S(1)}, u32[]{:S(2)}, u32[]{:S(2)}) %collective-permute-start.6) | collective-permute-done | bytes 262176 | tf_op jit(solution)/shard_map/ppermute | solution.py:1028
  72.1 4.5 %assemble.2.refs_3_.refs_1_ = bf16[1408,1024]{1,0:T(8,128)(2,1)} custom-call(s32[8]{0:T(128)} %stack.73.refs_0_, bf16[2560,128]{1,0:T(8,128)(2,1)} %copy-done.2, bf16[2560,128]{1,0:T(8,128)(2,1)} %collective-permute-done.4.refs_2_, bf16[2560,128]{1,0:T(8,128)(2,1)} %copy-done.9, bf16[2560,128]{1,0:T(8,128)(2,1)} %copy-done.27, ...), custom_call_target="tpu_custom_call" | custom-call | flops 5175000064 | bytes 1 | tf_op jit(solution)/shard_map/assemble/pallas_call | solution.py:88
  78.9 2.6 collective-permute-start.22
  81.5 5.3 %place.2.refs_1_.refs_6_ = bf16[1024,1024]{1,0:T(8,128)(2,1)} custom-call(s32[1,512]{1,0:T(1,128)} %get-tuple-element.383.refs_0_, s32[1,512]{1,0:T(1,128)} %get-tuple-element.382.refs_1_, bf16[512,1024]{1,0:T(8,128)(2,1)} %pad_maximum_fusion.refs_2_, bf16[512,1024]{1,0:T(8,128)(2,1)} %collective-permute-done.7.refs_3_), custom_call_target="tpu_custom_call" | custom-call | flops 6095000064 | bytes 1 | tf_op jit(solution)/shard_map/place/pallas_call | solution.py:88
  86.8 12.1 %forward.4 = (bf16[512,1024]{1,0:T(8,128)(2,1)}, f32[512,512]{1,0:T(8,128)}, f32[512,768]{1,0:T(8,128)}, bf16[512,768]{1,0:T(8,128)(2,1)}, bf16[512,128]{1,0:T(8...) custom-call(s32[8]{0:T(128)} %stack.73.refs_0_, ...), custom_call_target="tpu_custom_call" | custom-call | flops 14375000064 | bytes 1 | tf_op jit(solution)/shard_map/forward/pallas_call | solution.py:88
  102.2 2.2 collective-permute-start.29
  105.1 2.0 collective-permute-start.27
  107.2 2.4 collective-permute-start.23
  109.6 6.5 %collective-permute-done.29 = bf16[128,1024]{1,0:T(8,128)(2,1)S(1)} collective-permute-done((bf16[128,1024]{1,0:T(8,128)(2,1)S(1)}, bf16[128,1024]{1,0:T(8,128)(2,1)S(1)}, u32[]{:S(2)}, u32[]{:S(2)}) %collective-permute-start.29) | collective-permute-done | bytes 262176 | tf_op jit(solution)/shard_map/ppermute | solution.py:1028
  116.3 2.1 collective-permute-start.25
  118.4 12.2 %forward.5 = (bf16[512,1024]{1,0:T(8,128)(2,1)}, f32[512,512]{1,0:T(8,128)}, f32[512,768]{1,0:T(8,128)}, bf16[512,768]{1,0:T(8,128)(2,1)}, bf16[512,128]{1,0:T(8...) custom-call(s32[8]{0:T(128)} %stack.73.refs_0_, ...), custom_call_target="tpu_custom_call" | custom-call | flops 14375000064 | bytes 1 | tf_op jit(solution)/shard_map/forward/pallas_call | solution.py:88
  134.6 3.4 collective-permute-done.20
  145.7 5.3 %place.3.refs_14_.refs_18_.refs_6_.refs_8_.refs_10_.refs_12_ = bf16[1024,1024]{1,0:T(8,128)(2,1)} custom-call(s32[1,512]{1,0:T(1,128)} %get-tuple-element.383.refs_0_, s32[1,512]{1,0:T(1,128)} %get-tuple-element.382.refs_1_, bf16[512,1024]{1,0:T(8,128)(2,1)} %copy-done.7, bf16[512,1024]{1,0:T(8,128)(2,1)} %collective-permute-done.31.refs_3_), custom_call_target="tpu_custom_call" | custom-call | flops 6095000064 | bytes 1 | tf_op jit(solution)/shard_map/place/pallas_call | solution.py:88
  151.0 4.8 %assemble.3.refs_3_.refs_1_ = bf16[1408,1024]{1,0:T(8,128)(2,1)} custom-call(s32[8]{0:T(128)} %stack.73.refs_0_, bf16[4,2560,128]{2,1,0:T(8,128)(2,1)} %bitcast.97, bf16[4,1408,128]{2,1,0:T(8,128)(2,1)} %collective-permute-done.21.refs_2_), custom_call_target="tpu_custom_call" | custom-call | flops 5175000064 | bytes 1 | tf_op jit(solution)/shard_map/assemble/pallas_call | solution.py:88
  155.8 14.2 %forward.6 = (bf16[512,1024]{1,0:T(8,128)(2,1)}, f32[512,512]{1,0:T(8,128)}, f32[512,768]{1,0:T(8,128)}, bf16[512,768]{1,0:T(8,128)(2,1)}, bf16[512,128]{1,0:T(8...) custom-call(s32[8]{0:T(128)} %stack.73.refs_0_, ...), custom_call_target="tpu_custom_call" | custom-call | flops 14375000064 | bytes 1 | tf_op jit(solution)/shard_map/forward/pallas_call | solution.py:88
  173.8 14.3 %forward.7 = (bf16[512,1024]{1,0:T(8,128)(2,1)}, f32[512,512]{1,0:T(8,128)}, f32[512,768]{1,0:T(8,128)}, bf16[512,768]{1,0:T(8,128)(2,1)}, bf16[512,128]{1,0:T(8...) custom-call(s32[8]{0:T(128)} %stack.73.refs_0_, ...), custom_call_target="tpu_custom_call", output_to_operand_aliasing={{10}: (13, {}), {11}: (14, {})} | custom-call | flops 14375000064 | bytes 1 | tf_op jit(solution)/shard_map/forward/pallas_call | solution.py:88
  188.9 2.0 collective-permute-start.36
  191.7 2.0 collective-permute-start.38
  195.9 4.4 ungate.4
  200.8 2.0 collective-permute-start.39
  202.8 15.4 %backward.4 = (bf16[256,1024]{1,0:T(8,128)(2,1)}, bf16[256,1024]{1,0:T(8,128)(2,1)}, bf16[512,896]{1,0:T(8,128)(2,1)}, f32[8,768]{1,0:T(8,128)}, f32[8,128]{1,0:...) custom-call(s32[8]{0:T(128)} %stack.73.refs_0_, ...), custom_call_target="tpu_custom_call" | custom-call | flops 16675000320 | bytes 1 | tf_op jit(solution)/shard_map/backward/pallas_call | solution.py:88
  218.1 7.3 %collective-permute-done.39 = bf16[512,1024]{1,0:T(8,128)(2,1)S(1)} collective-permute-done((bf16[512,1024]{1,0:T(8,128)(2,1)S(1)}, bf16[512,1024]{1,0:T(8,128)(2,1)S(1)}, u32[]{:S(2)}, u32[]{:S(2)}) %collective-permute-start.39) | collective-permute-done | bytes 1048608 | tf_op jit(solution)/shard_map/ppermute | solution.py:1028
  228.8 4.4 ungate.5
  234.9 15.3 %backward.5 = (bf16[256,1024]{1,0:T(8,128)(2,1)}, bf16[256,1024]{1,0:T(8,128)(2,1)}, bf16[512,896]{1,0:T(8,128)(2,1)}, f32[8,768]{1,0:T(8,128)}, f32[8,128]{1,0:...) custom-call(s32[8]{0:T(128)} %stack.73.refs_0_, ...), custom_call_target="tpu_custom_call" | custom-call | flops 16675000320 | bytes 1 | tf_op jit(solution)/shard_map/backward/pallas_call | solution.py:88
  251.1 4.0 finish.4
  255.1 4.3 finish.5
  260.3 9.9 %weight_grads.3 = (bf16[2,256,1920]{2,1,0:T(8,128)(2,1)}, bf16[2,256,1920]{2,1,0:T(8,128)(2,1)}) custom-call(s32[8]{0:T(128)} %stack.73.refs_0_, bf16[512,1024]{1,0:T(8,128)(2,1)} %get-tuple-element.231.refs_13_.refs_1_, bf16[512,1024]{1,0:T(8,128)(2,1)} %get-tuple-element.216.refs_13_.refs_2_, bf16[512,512]{1,0:T(8,128)(2,1)} %get-tuple-element.235.refs_15_.refs_3_, ...), custom_call_target="tpu_custom_call" | custom-call | flops 12650000384 | bytes 1 | tf_op jit(solution)/shard_map/weight_grads/pallas_call | solution.py:88
  270.3 2.0 collective-permute-start.43
  274.9 7.1 %ungate.6 = (bf16[512,512]{1,0:T(8,128)(2,1)}, bf16[512,512]{1,0:T(8,128)(2,1)}, bf16[512,512]{1,0:T(8,128)(2,1)}, f32[1,512]{1,0:T(1,128)}, bf16[512,1024]{1,0:T(8,128)(2,1)}) custom-call(s32[8]{0:T(128)} %stack.73.refs_0_, f32[2,2,256]{2,1,0:T(2,128)} %add.263.refs_17_.refs_1_, f32[512,512]{1,0:T(8,128)} %get-tuple-element.254.refs_2_, ...), custom_call_target="tpu_custom_call" | custom-call | flops 6325000192 | bytes 1 | tf_op jit(solution)/shard_map/ungate/pallas_call | solution.py:88
  282.0 15.2 %backward.6 = (bf16[256,1024]{1,0:T(8,128)(2,1)}, bf16[256,1024]{1,0:T(8,128)(2,1)}, bf16[512,896]{1,0:T(8,128)(2,1)}, f32[8,768]{1,0:T(8,128)}, f32[8,128]{1,0:...) custom-call(s32[8]{0:T(128)} %stack.73.refs_0_, ...), custom_call_target="tpu_custom_call" | custom-call | flops 16675000320 | bytes 1 | tf_op jit(solution)/shard_map/backward/pallas_call | solution.py:88
  303.6 7.3 %ungate.7 = (bf16[512,512]{1,0:T(8,128)(2,1)}, bf16[512,512]{1,0:T(8,128)(2,1)}, bf16[512,512]{1,0:T(8,128)(2,1)}, f32[1,512]{1,0:T(1,128)}, bf16[512,1024]{1,0:T(8,128)(2,1)}) custom-call(s32[8]{0:T(128)} %stack.73.refs_0_, f32[2,2,256]{2,1,0:T(2,128)} %add.265.refs_13_.refs_1_, f32[512,512]{1,0:T(8,128)} %get-tuple-element.272.refs_2_, ...), custom_call_target="tpu_custom_call" | custom-call | flops 6325000192 | bytes 1 | tf_op jit(solution)/shard_map/ungate/pallas_call | solution.py:88
  310.9 6.6 %weight_grads.4 = (bf16[2,256,1024]{2,1,0:T(8,128)(2,1)}, bf16[2,256,1024]{2,1,0:T(8,128)(2,1)}) custom-call(s32[8]{0:T(128)} %stack.73.refs_0_, bf16[512,1024]{1,0:T(8,128)(2,1)} %get-tuple-element.276.refs_1_.refs_13_, bf16[512,1024]{1,0:T(8,128)(2,1)} %get-tuple-element.264.refs_13_.refs_2_, bf16[512,512]{1,0:T(8,128)(2,1)} %get-tuple-element.277.refs_3_.refs_15_, ...), custom_call_target="tpu_custom_call" | custom-call | flops 6899999744 | bytes 1 | tf_op jit(solution)/shard_map/weight_grads/pallas_call | solution.py:88
  317.5 1.9 collective-permute-start.69
  323.9 2.0 collective-permute-start.56
  327.5 4.6 %finish.6 = (bf16[256,1024]{1,0:T(8,128)(2,1)}, bf16[256,1024]{1,0:T(8,128)(2,1)}) custom-call(s32[8]{0:T(128)} %stack.73.refs_0_, s32[256,1]{1,0:T(8,128)} %copy.59.refs_1_, s32[256,1]{1,0:T(8,128)} %copy.60.refs_2_, bf16[256,1024]{1,0:T(8,128)(2,1)} %copy-done.22, bf16[256,1024]{1,0:T(8,128)(2,1)} %copy-done.49, ...), custom_call_target="tpu_custom_call" | custom-call | flops 5750000128 | bytes 1 | tf_op jit(solution)/shard_map/finish/pallas_call | solution.py:88
  332.1 4.2 collective-permute-start.53
  336.3 15.0 %backward.7 = (bf16[256,1024]{1,0:T(8,128)(2,1)}, bf16[256,1024]{1,0:T(8,128)(2,1)}, bf16[512,896]{1,0:T(8,128)(2,1)}, f32[8,768]{1,0:T(8,128)}, f32[8,128]{1,0:...) custom-call(s32[8]{0:T(128)} %stack.73.refs_0_, ...), custom_call_target="tpu_custom_call" | custom-call | flops 16675000320 | bytes 1 | tf_op jit(solution)/shard_map/backward/pallas_call | solution.py:88
  353.9 5.6 %collective-permute-done.55 = bf16[64,1408]{1,0:T(8,128)(2,1)S(1)} collective-permute-done((bf16[64,1408]{1,0:T(8,128)(2,1)S(1)}, bf16[64,1408]{1,0:T(8,128)(2,1)S(1)}, u32[]{:S(2)}, u32[]{:S(2)}) %collective-permute-start.55) | collective-permute-done | bytes 180256 | tf_op jit(solution)/shard_map/ppermute | solution.py:1028
  361.4 2.2 collective-permute-start.75
  363.9 3.8 collective-permute-start.60
  367.6 5.8 %weight_grads.5 = (bf16[2,256,896]{2,1,0:T(8,128)(2,1)}, bf16[2,256,896]{2,1,0:T(8,128)(2,1)}) custom-call(s32[8]{0:T(128)} %stack.73.refs_0_, bf16[512,1024]{1,0:T(8,128)(2,1)} %get-tuple-element.276.refs_1_.refs_13_, bf16[512,1024]{1,0:T(8,128)(2,1)} %get-tuple-element.264.refs_13_.refs_2_, bf16[512,896]{1,0:T(8,128)(2,1)} %get-tuple-element.300.refs_3_, ...), custom_call_target="tpu_custom_call" | custom-call | flops 6899999744 | bytes 1 | tf_op jit(solution)/shard_map/weight_grads/pallas_call | solution.py:88
  373.4 2.7 collective-permute-start.59
  376.1 2.2 pack.1
  382.8 4.9 %collective-permute-done.59 = bf16[2,256,896]{2,1,0:T(8,128)(2,1)S(1)} collective-permute-done((bf16[2,256,896]{2,1,0:T(8,128)(2,1)}, bf16[2,256,896]{2,1,0:T(8,128)(2,1)S(1)}, u32[]{:S(2)}, u32[]{:S(2)}) %collective-permute-start.59) | collective-permute-done | bytes 917536 | tf_op jit(solution)/shard_map/ppermute | solution.py:1028
  390.9 4.9 %finish.7 = (bf16[256,1024]{1,0:T(8,128)(2,1)}, bf16[256,1024]{1,0:T(8,128)(2,1)}) custom-call(s32[8]{0:T(128)} %stack.73.refs_0_, s32[256,1]{1,0:T(8,128)} %copy.59.refs_1_, s32[256,1]{1,0:T(8,128)} %copy.60.refs_2_, bf16[256,1024]{1,0:T(8,128)(2,1)} %copy-done.21, bf16[256,1024]{1,0:T(8,128)(2,1)} %copy-done.48, ...), custom_call_target="tpu_custom_call" | custom-call | flops 5750000128 | bytes 1 | tf_op jit(solution)/shard_map/finish/pallas_call | solution.py:88
  395.8 1.9 collective-permute-done.65
  397.9 3.6 collective-permute-start.71
  405.0 2.6 collective-permute-done.66
  407.6 3.8 collective-permute-start.62
  415.7 3.2 collective-permute-done.67
  418.9 8.5 %collective-permute-done.62.refs_2_ = bf16[256,1024]{1,0:T(8,128)(2,1)S(1)} collective-permute-done((bf16[256,1024]{1,0:T(8,128)(2,1)S(1)}, bf16[256,1024]{1,0:T(8,128)(2,1)S(1)}, u32[]{:S(2)}, u32[]{:S(2)}) %collective-permute-start.62) | collective-permute-done | bytes 524320 | tf_op jit(solution)/shard_map/ppermute | solution.py:1028
  428.2 3.0 settle.1
  436.5 2.4 gather_columns.1
  (353 shorter events, 94.9 us)
Async XLA Ops:
  7.2 132.2 %all-gather.3.cloned.1.call-start = ((), (), s32[]{:S(2)}) async-start(), calls=%async_computation | async-start | bytes 3276800 | tf_op jit(solution)/shard_map/all_gather | solution.py:1182
  10.9 10.9 %collective-permute-start.3 = (bf16[2560,128]{1,0:T(8,128)(2,1)}, bf16[2560,128]{1,0:T(8,128)(2,1)S(1)}, u32[]{:S(2)}, u32[]{:S(2)}) collective-permute-start(bf16[2560,128]{1,0:T(8,128)(2,1)} %get-tuple-element.173), channel_id=1, source_target_pairs={{0,16},{1,17},{2,18},{3,19},{4,20},{5,21},{6,22},{7,23},{8,24},{9,... | collective-permute-start | bytes 1966088 | tf_op jit(solution)/shard_map/ppermute | solution.py:1028
  14.6 14.9 %collective-permute-start.12 = (bf16[256,1024]{1,0:T(8,128)(2,1)}, bf16[256,1024]{1,0:T(8,128)(2,1)}, u32[]{:S(2)}, u32[]{:S(2)}) collective-permute-start(bf16[256,1024]{1,0:T(8,128)(2,1)} %get-tuple-element.181), channel_id=1, source_target_pairs={{0,16},{1,17},{2,18},{3,19},{4,20},{5,21},{6,22},{7,23},{8,24},{9,... | collective-permute-start | bytes 1572872 | tf_op jit(solution)/shard_map/ppermute | solution.py:1028
  14.6 29.3 %collective-permute-start = (bf16[2,128,1024]{2,1,0:T(8,128)(2,1)}, bf16[2,128,1024]{2,1,0:T(8,128)(2,1)S(1)}, u32[]{:S(2)}, u32[]{:S(2)}) collective-permute-start(bf16[2,128,1024]{2,1,0:T(8,128)(2,1)} %get-tuple-element.176), channel_id=1, source_target_pairs={{0,16},{1,17},{2,18},{3,19},{4,20},{5,21},{6,22},{7,23},{8,24},{9,... | collective-permute-start | bytes 1572872 | tf_op jit(solution)/shard_map/ppermute | solution.py:1028
  22.8 15.4 %collective-permute-start.4 = (bf16[2560,128]{1,0:T(8,128)(2,1)S(1)}, bf16[2560,128]{1,0:T(8,128)(2,1)}, u32[]{:S(2)}, u32[]{:S(2)}) collective-permute-start(bf16[2560,128]{1,0:T(8,128)(2,1)S(1)} %get-tuple-element.346.refs_1_), channel_id=1, source_target_pairs={{0,1},{1,0},{2,3},{3,2},{4,5},{5,4},{6,7},{7,6},{8,9},{9,8},{10,11... | collective-permute-start | bytes 1966088 | tf_op jit(solution)/shard_map/ppermute | solution.py:1028
  28.0 18.6 %collective-permute-start.9 = (bf16[2560,128]{1,0:T(8,128)(2,1)S(1)}, bf16[2560,128]{1,0:T(8,128)(2,1)S(1)}, u32[]{:S(2)}, u32[]{:S(2)}) collective-permute-start(bf16[2560,128]{1,0:T(8,128)(2,1)S(1)} %get-tuple-element.346.refs_1_), channel_id=1, source_target_pairs={{0,2},{1,3},{2,0},{3,1},{4,6},{5,7},{6,4},{7,5},{8,10},{9,11},{10,... | collective-permute-start | bytes 1966088 | tf_op jit(solution)/shard_map/ppermute | solution.py:1028
  38.2 13.0 %collective-permute-start.13 = (bf16[256,1024]{1,0:T(8,128)(2,1)S(1)}, bf16[256,1024]{1,0:T(8,128)(2,1)S(1)}, u32[]{:S(2)}, u32[]{:S(2)}) collective-permute-start(bf16[256,1024]{1,0:T(8,128)(2,1)S(1)} %get-tuple-element.182), channel_id=1, source_target_pairs={{0,2},{1,3},{6,4},{7,5},{8,10},{9,11},{14,12},{15,13},{16,18},{17,... | collective-permute-start | bytes 1572872 | tf_op jit(solution)/shard_map/ppermute | solution.py:1028
  44.0 14.3 %collective-permute-start.5 = (bf16[2560,128]{1,0:T(8,128)(2,1)}, bf16[2560,128]{1,0:T(8,128)(2,1)S(1)}, u32[]{:S(2)}, u32[]{:S(2)}) collective-permute-start(bf16[2560,128]{1,0:T(8,128)(2,1)} %collective-permute-done.4.refs_2_), channel_id=1, source_target_pairs={{0,2},{1,3},{2,0},{3,1},{4,6},{5,7},{6,4},{7,5},{8,10},{9,11},{10,... | collective-permute-start | bytes 1966088 | tf_op jit(solution)/shard_map/ppermute | solution.py:1028
  44.1 12.2 %collective-permute-start.2 = (bf16[128,1024]{1,0:T(8,128)(2,1)S(1)}, bf16[128,1024]{1,0:T(8,128)(2,1)S(1)}, u32[]{:S(2)}, u32[]{:S(2)}) collective-permute-start(bf16[128,1024]{1,0:T(8,128)(2,1)S(1)} %get-tuple-element.364), channel_id=1, source_target_pairs={{0,8},{1,9},{2,10},{3,11},{4,12},{5,13},{6,14},{7,15},{8,0},{9,1},... | collective-permute-start | bytes 786440 | tf_op jit(solution)/shard_map/ppermute | solution.py:1028
  47.9 24.2 %collective-permute-start.10 = (bf16[3,1408,128]{2,1,0:T(8,128)(2,1)S(1)}, bf16[3,1408,128]{2,1,0:T(8,128)(2,1)}, u32[]{:S(2)}, u32[]{:S(2)}) collective-permute-start(bf16[3,1408,128]{2,1,0:T(8,128)(2,1)S(1)} %fusion.2), channel_id=1, source_target_pairs={{0,16},{1,17},{2,18},{3,19},{4,20},{5,21},{6,22},{7,23},{8,24},{9,... | collective-permute-start | bytes 3244040 | tf_op jit(solution)/shard_map/ppermute | solution.py:1028
  51.3 16.9 %collective-permute-start.14 = (bf16[256,1024]{1,0:T(8,128)(2,1)S(1)}, bf16[256,1024]{1,0:T(8,128)(2,1)S(1)}, u32[]{:S(2)}, u32[]{:S(2)}) collective-permute-start(bf16[256,1024]{1,0:T(8,128)(2,1)S(1)} %broadcast_select_fusion.3), channel_id=1, source_target_pairs={{0,1},{1,0},{2,3},{3,2},{4,5},{5,4},{6,7},{7,6},{8,9},{9,8},{10,11... | collective-permute-start | bytes 1572872 | tf_op jit(solution)/shard_map/ppermute | solution.py:1028
  53.8 13.3 %collective-permute-start.1 = (bf16[128,1024]{1,0:T(8,128)(2,1)S(1)}, bf16[128,1024]{1,0:T(8,128)(2,1)S(1)}, u32[]{:S(2)}, u32[]{:S(2)}) collective-permute-start(bf16[128,1024]{1,0:T(8,128)(2,1)S(1)} %get-tuple-element.363), channel_id=1, source_target_pairs={{0,4},{1,5},{2,6},{3,7},{4,0},{5,1},{6,2},{7,3},{8,12},{9,13},{10,... | collective-permute-start | bytes 786440 | tf_op jit(solution)/shard_map/ppermute | solution.py:1028
  58.3 8.8 %collective-permute-start.6 = (bf16[128,1024]{1,0:T(8,128)(2,1)S(1)}, bf16[128,1024]{1,0:T(8,128)(2,1)S(1)}, u32[]{:S(2)}, u32[]{:S(2)}) collective-permute-start(bf16[128,1024]{1,0:T(8,128)(2,1)S(1)} %collective-permute-done.2), channel_id=1, source_target_pairs={{0,4},{1,5},{2,6},{3,7},{4,0},{5,1},{6,2},{7,3},{8,12},{9,13},{10,... | collective-permute-start | bytes 786440 | tf_op jit(solution)/shard_map/ppermute | solution.py:1028
  60.8 11.2 %collective-permute-start.11 = (bf16[1408,128]{1,0:T(8,128)(2,1)S(1)}, bf16[1408,128]{1,0:T(8,128)(2,1)}, u32[]{:S(2)}, u32[]{:S(2)}) collective-permute-start(bf16[1408,128]{1,0:T(8,128)(2,1)S(1)} %constant_dynamic-slice_fusion.4), channel_id=1, source_target_pairs={{0,16},{1,17},{2,18},{3,19},{4,20},{5,21},{6,22},{7,23},{8,24},{9,... | collective-permute-start | bytes 1081352 | tf_op jit(solution)/shard_map/ppermute | solution.py:1028
  68.1 13.3 %collective-permute-start.7 = (bf16[512,1024]{1,0:T(8,128)(2,1)}, bf16[512,1024]{1,0:T(8,128)(2,1)}, u32[]{:S(2)}, u32[]{:S(2)}) collective-permute-start(bf16[512,1024]{1,0:T(8,128)(2,1)} %pad_maximum_fusion.refs_2_), channel_id=1, source_target_pairs={{0,16},{1,17},{2,18},{3,19},{4,20},{5,21},{6,22},{7,23},{8,24},{9,... | collective-permute-start | bytes 3145736 | tf_op jit(solution)/shard_map/ppermute | solution.py:1028
  69.1 7.5 %collective-permute-start.15 = (bf16[256,1024]{1,0:T(8,128)(2,1)}, bf16[256,1024]{1,0:T(8,128)(2,1)}, u32[]{:S(2)}, u32[]{:S(2)}) collective-permute-start(bf16[256,1024]{1,0:T(8,128)(2,1)} %broadcast_select_fusion.6), channel_id=1, source_target_pairs={{0,16},{1,17},{2,18},{3,19},{4,20},{5,21},{6,22},{7,23},{8,24},{9,... | collective-permute-start | bytes 1572872 | tf_op jit(solution)/shard_map/ppermute | solution.py:1028
  78.9 28.3 %collective-permute-start.22 = (bf16[256,1024]{1,0:T(8,128)(2,1)S(1)}, bf16[256,1024]{1,0:T(8,128)(2,1)S(1)}, u32[]{:S(2)}, u32[]{:S(2)}) collective-permute-start(bf16[256,1024]{1,0:T(8,128)(2,1)S(1)} %get-tuple-element.194), channel_id=1, source_target_pairs={{0,2},{1,3},{6,4},{7,5},{8,10},{9,11},{14,12},{15,13},{16,18},{17,... | collective-permute-start | bytes 1572872 | tf_op jit(solution)/shard_map/ppermute | solution.py:1028
  99.0 17.1 %collective-permute-start.16 = (bf16[256,1024]{1,0:T(8,128)(2,1)}, bf16[256,1024]{1,0:T(8,128)(2,1)S(1)}, u32[]{:S(2)}, u32[]{:S(2)}) collective-permute-start(bf16[256,1024]{1,0:T(8,128)(2,1)} %get-tuple-element.184), channel_id=1, source_target_pairs={{0,16},{1,17},{2,18},{3,19},{4,20},{5,21},{6,22},{7,23},{8,24},{9,... | collective-permute-start | bytes 1572872 | tf_op jit(solution)/shard_map/ppermute | solution.py:1028
  102.2 13.8 %collective-permute-start.29 = (bf16[128,1024]{1,0:T(8,128)(2,1)S(1)}, bf16[128,1024]{1,0:T(8,128)(2,1)S(1)}, u32[]{:S(2)}, u32[]{:S(2)}) collective-permute-start(bf16[128,1024]{1,0:T(8,128)(2,1)S(1)} %get-tuple-element.362), channel_id=1, source_target_pairs={{0,8},{1,9},{2,10},{3,11},{4,12},{5,13},{6,14},{7,15},{8,0},{9,1},... | collective-permute-start | bytes 786440 | tf_op jit(solution)/shard_map/ppermute | solution.py:1028
  104.4 30.0 %collective-permute-start.28 = (bf16[128,1024]{1,0:T(8,128)(2,1)S(1)}, bf16[128,1024]{1,0:T(8,128)(2,1)S(1)}, u32[]{:S(2)}, u32[]{:S(2)}) collective-permute-start(bf16[128,1024]{1,0:T(8,128)(2,1)S(1)} %get-tuple-element.361), channel_id=1, source_target_pairs={{0,4},{1,5},{2,6},{3,7},{4,0},{5,1},{6,2},{7,3},{8,12},{9,13},{10,... | collective-permute-start | bytes 786440 | tf_op jit(solution)/shard_map/ppermute | solution.py:1028
  105.1 25.5 %collective-permute-start.27 = (f32[2,2,256]{2,1,0:T(2,128)S(1)}, f32[2,2,256]{2,1,0:T(2,128)S(1)}, u32[]{:S(2)}, u32[]{:S(2)}) collective-permute-start(f32[2,2,256]{2,1,0:T(2,128)S(1)} %add.260), channel_id=1, source_target_pairs={{0,4},{1,5},{2,6},{3,7},{4,0},{5,1},{6,2},{7,3},{8,12},{9,13},{10,... | collective-permute-start | bytes 12296 | tf_op jit(solution)/shard_map/ppermute | solution.py:1028
  107.2 31.3 %collective-permute-start.23 = (bf16[256,1024]{1,0:T(8,128)(2,1)S(1)}, bf16[256,1024]{1,0:T(8,128)(2,1)S(1)}, u32[]{:S(2)}, u32[]{:S(2)}) collective-permute-start(bf16[256,1024]{1,0:T(8,128)(2,1)S(1)} %broadcast_select_fusion.2), channel_id=1, source_target_pairs={{0,1},{1,0},{2,3},{3,2},{4,5},{5,4},{6,7},{7,6},{8,9},{9,8},{10,11... | collective-permute-start | bytes 1572872 | tf_op jit(solution)/shard_map/ppermute | solution.py:1028
  116.1 17.1 %collective-permute-start.30 = (bf16[128,1024]{1,0:T(8,128)(2,1)S(1)}, bf16[128,1024]{1,0:T(8,128)(2,1)S(1)}, u32[]{:S(2)}, u32[]{:S(2)}) collective-permute-start(bf16[128,1024]{1,0:T(8,128)(2,1)S(1)} %collective-permute-done.29), channel_id=1, source_target_pairs={{0,4},{1,5},{2,6},{3,7},{4,0},{5,1},{6,2},{7,3},{8,12},{9,13},{10,... | collective-permute-start | bytes 786440 | tf_op jit(solution)/shard_map/ppermute | solution.py:1028
  116.3 23.1 %collective-permute-start.25 = (bf16[256,1024]{1,0:T(8,128)(2,1)S(1)}, bf16[256,1024]{1,0:T(8,128)(2,1)S(1)}, u32[]{:S(2)}, u32[]{:S(2)}) collective-permute-start(bf16[256,1024]{1,0:T(8,128)(2,1)S(1)} %add_convert_fusion.17), channel_id=1, source_target_pairs={{0,4},{1,5},{2,6},{3,7},{4,0},{5,1},{6,2},{7,3},{8,12},{9,13},{10,... | collective-permute-start | bytes 1572872 | tf_op jit(solution)/shard_map/ppermute | solution.py:1028
  133.2 8.6 %collective-permute-start.18 = (bf16[256,1024]{1,0:T(8,128)(2,1)}, bf16[256,1024]{1,0:T(8,128)(2,1)}, u32[]{:S(2)}, u32[]{:S(2)}) collective-permute-start(bf16[256,1024]{1,0:T(8,128)(2,1)} %get-tuple-element.190), channel_id=1, source_target_pairs={{0,16},{1,17},{2,18},{3,19},{4,20},{5,21},{6,22},{7,23},{8,24},{9,... | collective-permute-start | bytes 1572872 | tf_op jit(solution)/shard_map/ppermute | solution.py:1028
  134.5 11.2 %collective-permute-start.31 = (bf16[512,1024]{1,0:T(8,128)(2,1)S(1)}, bf16[512,1024]{1,0:T(8,128)(2,1)}, u32[]{:S(2)}, u32[]{:S(2)}) collective-permute-start(bf16[512,1024]{1,0:T(8,128)(2,1)S(1)} %pad_maximum_fusion.3.refs_2_), channel_id=1, source_target_pairs={{0,16},{1,17},{2,18},{3,19},{4,20},{5,21},{6,22},{7,23},{8,24},{9,... | collective-permute-start | bytes 3145736 | tf_op jit(solution)/shard_map/ppermute | solution.py:1028
  141.0 10.0 %collective-permute-start.21 = (bf16[4,1408,128]{2,1,0:T(8,128)(2,1)S(1)}, bf16[4,1408,128]{2,1,0:T(8,128)(2,1)}, u32[]{:S(2)}, u32[]{:S(2)}) collective-permute-start(bf16[4,1408,128]{2,1,0:T(8,128)(2,1)S(1)} %constant_dynamic-slice_fusion.1), channel_id=1, source_target_pairs={{0,16},{1,17},{2,18},{3,19},{4,20},{5,21},{6,22},{7,23},{8,24},{9,... | collective-permute-start | bytes 4325384 | tf_op jit(solution)/shard_map/ppermute | solution.py:1028
  141.7 14.0 %collective-permute-start.26 = (bf16[256,1024]{1,0:T(8,128)(2,1)S(1)}, bf16[256,1024]{1,0:T(8,128)(2,1)}, u32[]{:S(2)}, u32[]{:S(2)}) collective-permute-start(bf16[256,1024]{1,0:T(8,128)(2,1)S(1)} %add_convert_fusion.15.refs_11_.refs_8_), channel_id=1, source_target_pairs={{0,16},{1,17},{2,18},{3,19},{4,20},{5,21},{6,22},{7,23},{8,24},{9,... | collective-permute-start | bytes 1572872 | tf_op jit(solution)/shard_map/ppermute | solution.py:1028
  143.2 26.8 %collective-permute-start.33 = (bf16[256,1024]{1,0:T(8,128)(2,1)S(1)}, bf16[256,1024]{1,0:T(8,128)(2,1)S(1)}, u32[]{:S(2)}, u32[]{:S(2)}) collective-permute-start(bf16[256,1024]{1,0:T(8,128)(2,1)S(1)} %add_convert_fusion.16), channel_id=1, source_target_pairs={{0,4},{1,5},{2,6},{3,7},{4,0},{5,1},{6,2},{7,3},{8,12},{9,13},{10,... | collective-permute-start | bytes 1572872 | tf_op jit(solution)/shard_map/ppermute | solution.py:1028
  188.1 12.2 %collective-permute-start.35 = (bf16[512,1024]{1,0:T(8,128)(2,1)}, bf16[512,1024]{1,0:T(8,128)(2,1)S(1)}, u32[]{:S(2)}, u32[]{:S(2)}) collective-permute-start(bf16[512,1024]{1,0:T(8,128)(2,1)} %get-tuple-element.208), channel_id=1, source_target_pairs={{0,16},{1,17},{2,18},{3,19},{4,20},{5,21},{6,22},{7,23},{8,24},{9,... | collective-permute-start | bytes 3145736 | tf_op jit(solution)/shard_map/ppermute | solution.py:1028
  200.8 24.7 %collective-permute-start.39 = (bf16[512,1024]{1,0:T(8,128)(2,1)S(1)}, bf16[512,1024]{1,0:T(8,128)(2,1)S(1)}, u32[]{:S(2)}, u32[]{:S(2)}) collective-permute-start(bf16[512,1024]{1,0:T(8,128)(2,1)S(1)} %add_convert_fusion.1), channel_id=1, source_target_pairs={{0,4},{1,5},{2,6},{3,7},{4,0},{5,1},{6,2},{7,3},{8,12},{9,13},{10,... | collective-permute-start | bytes 3145736 | tf_op jit(solution)/shard_map/ppermute | solution.py:1028
  225.9 9.0 %collective-permute-start.40 = (bf16[512,1024]{1,0:T(8,128)(2,1)S(1)}, bf16[512,1024]{1,0:T(8,128)(2,1)S(1)}, u32[]{:S(2)}, u32[]{:S(2)}) collective-permute-start(bf16[512,1024]{1,0:T(8,128)(2,1)S(1)} %add_convert_fusion.refs_3_), channel_id=1, source_target_pairs={{0,16},{1,17},{2,18},{3,19},{4,20},{5,21},{6,22},{7,23},{8,24},{9,... | collective-permute-start | bytes 3145736 | tf_op jit(solution)/shard_map/ppermute | solution.py:1028
  233.4 16.9 %collective-permute-start.44 = (bf16[256,1024]{1,0:T(8,128)(2,1)S(1)}, bf16[256,1024]{1,0:T(8,128)(2,1)S(1)}, u32[]{:S(2)}, u32[]{:S(2)}) collective-permute-start(bf16[256,1024]{1,0:T(8,128)(2,1)S(1)} %add_convert_fusion.13), channel_id=1, source_target_pairs={{0,4},{1,5},{2,6},{3,7},{4,0},{5,1},{6,2},{7,3},{8,12},{9,13},{10,... | collective-permute-start | bytes 1572872 | tf_op jit(solution)/shard_map/ppermute | solution.py:1028
  250.2 9.2 %collective-permute-start.42 = (bf16[256,1024]{1,0:T(8,128)(2,1)}, bf16[256,1024]{1,0:T(8,128)(2,1)S(1)}, u32[]{:S(2)}, u32[]{:S(2)}) collective-permute-start(bf16[256,1024]{1,0:T(8,128)(2,1)} %get-tuple-element.245), channel_id=1, source_target_pairs={{0,16},{1,17},{2,18},{3,19},{4,20},{5,21},{6,22},{7,23},{8,24},{9,... | collective-permute-start | bytes 1572872 | tf_op jit(solution)/shard_map/ppermute | solution.py:1028
  250.5 23.4 %collective-permute-start.45 = (bf16[256,1024]{1,0:T(8,128)(2,1)S(1)}, bf16[256,1024]{1,0:T(8,128)(2,1)S(1)}, u32[]{:S(2)}, u32[]{:S(2)}) collective-permute-start(bf16[256,1024]{1,0:T(8,128)(2,1)S(1)} %add_convert_fusion.11.refs_6_), channel_id=1, source_target_pairs={{0,16},{1,17},{2,18},{3,19},{4,20},{5,21},{6,22},{7,23},{8,24},{9,... | collective-permute-start | bytes 1572872 | tf_op jit(solution)/shard_map/ppermute | solution.py:1028
  259.6 14.0 %collective-permute-start.46 = (bf16[256,1024]{1,0:T(8,128)(2,1)S(1)}, bf16[256,1024]{1,0:T(8,128)(2,1)S(1)}, u32[]{:S(2)}, u32[]{:S(2)}) collective-permute-start(bf16[256,1024]{1,0:T(8,128)(2,1)S(1)} %add_convert_fusion.12), channel_id=1, source_target_pairs={{0,4},{1,5},{2,6},{3,7},{4,0},{5,1},{6,2},{7,3},{8,12},{9,13},{10,... | collective-permute-start | bytes 1572872 | tf_op jit(solution)/shard_map/ppermute | solution.py:1028
  270.3 31.2 %collective-permute-start.43 = (bf16[2,256,1920]{2,1,0:T(8,128)(2,1)}, bf16[2,256,1920]{2,1,0:T(8,128)(2,1)}, u32[]{:S(2)}, u32[]{:S(2)}) collective-permute-start(bf16[2,256,1920]{2,1,0:T(8,128)(2,1)} %get-tuple-element.252), channel_id=1, source_target_pairs={{0,1},{1,0},{2,3},{3,2},{4,5},{5,4},{6,7},{7,6},{8,9},{9,8},{10,11... | collective-permute-start | bytes 5898248 | tf_op jit(solution)/shard_map/ppermute | solution.py:1028
  273.9 8.1 %collective-permute-start.47 = (bf16[256,1024]{1,0:T(8,128)(2,1)S(1)}, bf16[256,1024]{1,0:T(8,128)(2,1)S(1)}, u32[]{:S(2)}, u32[]{:S(2)}) collective-permute-start(bf16[256,1024]{1,0:T(8,128)(2,1)S(1)} %add_convert_fusion.10.refs_6_), channel_id=1, source_target_pairs={{0,16},{1,17},{2,18},{3,19},{4,20},{5,21},{6,22},{7,23},{8,24},{9,... | collective-permute-start | bytes 1572872 | tf_op jit(solution)/shard_map/ppermute | solution.py:1028
  297.8 34.4 %collective-permute-start.52 = (bf16[256,1024]{1,0:T(8,128)(2,1)}, bf16[256,1024]{1,0:T(8,128)(2,1)}, u32[]{:S(2)}, u32[]{:S(2)}) collective-permute-start(bf16[256,1024]{1,0:T(8,128)(2,1)} %get-tuple-element.287), channel_id=1, source_target_pairs={{16,24},{17,25},{18,26},{19,27},{20,28},{21,29},{22,30},{23,31},{2... | collective-permute-start | bytes 1572872 | tf_op jit(solution)/shard_map/ppermute | solution.py:1028
  300.7 19.6 %collective-permute-start.50 = (bf16[256,1024]{1,0:T(8,128)(2,1)S(1)}, bf16[256,1024]{1,0:T(8,128)(2,1)S(1)}, u32[]{:S(2)}, u32[]{:S(2)}) collective-permute-start(bf16[256,1024]{1,0:T(8,128)(2,1)S(1)} %add_convert_fusion.9), channel_id=1, source_target_pairs={{0,4},{1,5},{2,6},{3,7},{4,0},{5,1},{6,2},{7,3},{8,12},{9,13},{10,... | collective-permute-start | bytes 1572872 | tf_op jit(solution)/shard_map/ppermute | solution.py:1028
  302.9 19.3 %collective-permute-start.48 = (bf16[256,1920]{1,0:T(8,128)(2,1)S(1)}, bf16[256,1920]{1,0:T(8,128)(2,1)S(1)}, u32[]{:S(2)}, u32[]{:S(2)}) collective-permute-start(bf16[256,1920]{1,0:T(8,128)(2,1)S(1)} %fusion.5), channel_id=1, source_target_pairs={{0,2},{1,3},{2,0},{3,1},{4,6},{5,7},{6,4},{7,5},{8,10},{9,11},{10,... | collective-permute-start | bytes 2949128 | tf_op jit(solution)/shard_map/ppermute | solution.py:1028
  317.5 33.9 %collective-permute-start.69 = (bf16[2,256,1024]{2,1,0:T(8,128)(2,1)}, bf16[2,256,1024]{2,1,0:T(8,128)(2,1)S(1)}, u32[]{:S(2)}, u32[]{:S(2)}) collective-permute-start(bf16[2,256,1024]{2,1,0:T(8,128)(2,1)} %get-tuple-element.282), channel_id=1, source_target_pairs={{0,1},{1,0},{2,3},{3,2},{4,5},{5,4},{6,7},{7,6},{8,9},{9,8},{10,11... | collective-permute-start | bytes 3145736 | tf_op jit(solution)/shard_map/ppermute | solution.py:1028
  320.5 6.2 %collective-permute-start.51 = (bf16[256,1024]{1,0:T(8,128)(2,1)S(1)}, bf16[256,1024]{1,0:T(8,128)(2,1)S(1)}, u32[]{:S(2)}, u32[]{:S(2)}) collective-permute-start(bf16[256,1024]{1,0:T(8,128)(2,1)S(1)} %add_convert_fusion.8.refs_3_), channel_id=1, source_target_pairs={{0,16},{1,17},{2,18},{3,19},{4,20},{5,21},{6,22},{7,23},{8,24},{9,... | collective-permute-start | bytes 1572872 | tf_op jit(solution)/shard_map/ppermute | solution.py:1028
  323.9 39.6 %collective-permute-start.56 = (bf16[256,512]{1,0:T(8,128)(2,1)S(1)}, bf16[256,512]{1,0:T(8,128)(2,1)S(1)}, u32[]{:S(2)}, u32[]{:S(2)}) collective-permute-start(bf16[256,512]{1,0:T(8,128)(2,1)S(1)} %slice.217), channel_id=1, source_target_pairs={{0,16},{1,17},{2,18},{3,19},{4,24},{5,25},{6,26},{7,27},{16,20},{1... | collective-permute-start | bytes 786440 | tf_op jit(solution)/shard_map/ppermute | solution.py:1028
  326.0 37.6 %collective-permute-start.57 = (bf16[256,512]{1,0:T(8,128)(2,1)S(1)}, bf16[256,512]{1,0:T(8,128)(2,1)S(1)}, u32[]{:S(2)}, u32[]{:S(2)}) collective-permute-start(bf16[256,512]{1,0:T(8,128)(2,1)S(1)} %slice.217), channel_id=1, source_target_pairs={{8,16},{9,17},{10,18},{11,19},{12,24},{13,25},{14,26},{15,27},{24,... | collective-permute-start | bytes 786440 | tf_op jit(solution)/shard_map/ppermute | solution.py:1028
  332.1 21.0 %collective-permute-start.53 = (bf16[64,1408]{1,0:T(8,128)(2,1)S(1)}, bf16[64,1408]{1,0:T(8,128)(2,1)S(1)}, u32[]{:S(2)}, u32[]{:S(2)}) collective-permute-start(bf16[64,1408]{1,0:T(8,128)(2,1)S(1)} %get-tuple-element.353), channel_id=1, source_target_pairs={{0,8},{1,9},{2,10},{3,11},{4,12},{5,13},{6,14},{7,15},{8,0},{9,1},... | collective-permute-start | bytes 540680 | tf_op jit(solution)/shard_map/ppermute | solution.py:1028
  336.3 16.9 %collective-permute-start.54 = (bf16[64,1408]{1,0:T(8,128)(2,1)S(1)}, bf16[64,1408]{1,0:T(8,128)(2,1)}, u32[]{:S(2)}, u32[]{:S(2)}) collective-permute-start(bf16[64,1408]{1,0:T(8,128)(2,1)S(1)} %get-tuple-element.355), channel_id=1, source_target_pairs={{0,4},{1,5},{2,6},{3,7},{4,0},{5,1},{6,2},{7,3},{8,12},{9,13},{10,... | collective-permute-start | bytes 540680 | tf_op jit(solution)/shard_map/ppermute | solution.py:1028
  351.4 8.2 %collective-permute-start.55 = (bf16[64,1408]{1,0:T(8,128)(2,1)S(1)}, bf16[64,1408]{1,0:T(8,128)(2,1)S(1)}, u32[]{:S(2)}, u32[]{:S(2)}) collective-permute-start(bf16[64,1408]{1,0:T(8,128)(2,1)S(1)} %get-tuple-element.354), channel_id=1, source_target_pairs={{0,12},{1,13},{2,14},{3,15},{4,8},{5,9},{6,10},{7,11},{8,4},{9,5},... | collective-permute-start | bytes 540680 | tf_op jit(solution)/shard_map/ppermute | solution.py:1028
  353.2 10.5 %collective-permute-start.58 = (bf16[256,1024]{1,0:T(8,128)(2,1)}, bf16[256,1024]{1,0:T(8,128)(2,1)S(1)}, u32[]{:S(2)}, u32[]{:S(2)}) collective-permute-start(bf16[256,1024]{1,0:T(8,128)(2,1)} %get-tuple-element.298), channel_id=1, source_target_pairs={{0,16},{1,17},{2,18},{3,19},{4,20},{5,21},{6,22},{7,23},{8,24},{9,... | collective-permute-start | bytes 1572872 | tf_op jit(solution)/shard_map/ppermute | solution.py:1028
  353.3 27.6 %collective-permute-start.70 = (bf16[256,1024]{1,0:T(8,128)(2,1)S(1)}, bf16[256,1024]{1,0:T(8,128)(2,1)S(1)}, u32[]{:S(2)}, u32[]{:S(2)}) collective-permute-start(bf16[256,1024]{1,0:T(8,128)(2,1)S(1)} %fusion.8), channel_id=1, source_target_pairs={{0,2},{1,3},{2,0},{3,1},{4,6},{5,7},{6,4},{7,5},{8,10},{9,11},{10,... | collective-permute-start | bytes 1572872 | tf_op jit(solution)/shard_map/ppermute | solution.py:1028
  361.4 74.4 %collective-permute-start.75 = (bf16[2,64,1408]{2,1,0:T(8,128)(2,1)}, bf16[2,64,1408]{2,1,0:T(8,128)(2,1)}, u32[]{:S(2)}, u32[]{:S(2)}) collective-permute-start(bf16[2,64,1408]{2,1,0:T(8,128)(2,1)} %pad_maximum_fusion.4.refs_4_), channel_id=1, source_target_pairs={{0,16},{1,17},{2,18},{3,19},{4,20},{5,21},{6,22},{7,23},{8,24},{9,... | collective-permute-start | bytes 1081352 | tf_op jit(solution)/shard_map/ppermute | solution.py:1028
  363.9 17.0 %collective-permute-start.60 = (bf16[256,1024]{1,0:T(8,128)(2,1)S(1)}, bf16[256,1024]{1,0:T(8,128)(2,1)S(1)}, u32[]{:S(2)}, u32[]{:S(2)}) collective-permute-start(bf16[256,1024]{1,0:T(8,128)(2,1)S(1)} %add_convert_fusion.7), channel_id=1, source_target_pairs={{0,4},{1,5},{2,6},{3,7},{4,0},{5,1},{6,2},{7,3},{8,12},{9,13},{10,... | collective-permute-start | bytes 1572872 | tf_op jit(solution)/shard_map/ppermute | solution.py:1028
  373.4 14.3 %collective-permute-start.59 = (bf16[2,256,896]{2,1,0:T(8,128)(2,1)}, bf16[2,256,896]{2,1,0:T(8,128)(2,1)S(1)}, u32[]{:S(2)}, u32[]{:S(2)}) collective-permute-start(bf16[2,256,896]{2,1,0:T(8,128)(2,1)} %get-tuple-element.303), channel_id=1, source_target_pairs={{0,1},{1,0},{2,3},{3,2},{4,5},{5,4},{6,7},{7,6},{8,9},{9,8},{10,11... | collective-permute-start | bytes 2752520 | tf_op jit(solution)/shard_map/ppermute | solution.py:1028
  380.7 8.4 %collective-permute-start.64 = (f32[7,2304]{1,0:T(8,128)S(1)}, f32[7,2304]{1,0:T(8,128)S(1)}, u32[]{:S(2)}, u32[]{:S(2)}) collective-permute-start(f32[7,2304]{1,0:T(8,128)S(1)} %add.288), channel_id=1, source_target_pairs={{0,1},{1,0},{2,3},{3,2},{4,5},{5,4},{6,7},{7,6},{8,9},{9,8},{10,11... | collective-permute-start | bytes 193544 | tf_op jit(solution)/shard_map/ppermute | solution.py:1028
  381.1 9.0 %collective-permute-start.61 = (bf16[256,1024]{1,0:T(8,128)(2,1)S(1)}, bf16[256,1024]{1,0:T(8,128)(2,1)S(1)}, u32[]{:S(2)}, u32[]{:S(2)}) collective-permute-start(bf16[256,1024]{1,0:T(8,128)(2,1)S(1)} %add_convert_fusion.6.refs_3_), channel_id=1, source_target_pairs={{0,16},{1,17},{2,18},{3,19},{4,20},{5,21},{6,22},{7,23},{8,24},{9,... | collective-permute-start | bytes 1572872 | tf_op jit(solution)/shard_map/ppermute | solution.py:1028
  382.1 15.7 %collective-permute-start.76 = (bf16[256,512]{1,0:T(8,128)(2,1)S(1)}, bf16[256,512]{1,0:T(8,128)(2,1)S(1)}, u32[]{:S(2)}, u32[]{:S(2)}) collective-permute-start(bf16[256,512]{1,0:T(8,128)(2,1)S(1)} %get-tuple-element.359), channel_id=1, source_target_pairs={{0,0},{1,1},{2,2},{3,3},{4,8},{5,9},{6,10},{7,11},{16,4},{17,5},{1... | collective-permute-start | bytes 786440 | tf_op jit(solution)/shard_map/ppermute | solution.py:1028
  387.7 10.2 %collective-permute-start.77 = (bf16[256,512]{1,0:T(8,128)(2,1)S(1)}, bf16[256,512]{1,0:T(8,128)(2,1)S(1)}, u32[]{:S(2)}, u32[]{:S(2)}) collective-permute-start(bf16[256,512]{1,0:T(8,128)(2,1)S(1)} %get-tuple-element.359), channel_id=1, source_target_pairs={{8,0},{9,1},{10,2},{11,3},{12,8},{13,9},{14,10},{15,11},{24,4},{25... | collective-permute-start | bytes 786440 | tf_op jit(solution)/shard_map/ppermute | solution.py:1028
  389.1 8.5 %collective-permute-start.65 = (bf16[256,896]{1,0:T(8,128)(2,1)S(1)}, bf16[256,896]{1,0:T(8,128)(2,1)S(1)}, u32[]{:S(2)}, u32[]{:S(2)}) collective-permute-start(bf16[256,896]{1,0:T(8,128)(2,1)S(1)} %fusion.9), channel_id=1, source_target_pairs={{0,2},{1,3},{2,0},{3,1},{4,6},{5,7},{6,4},{7,5},{8,10},{9,11},{10,... | collective-permute-start | bytes 1376264 | tf_op jit(solution)/shard_map/ppermute | solution.py:1028
  397.9 13.5 %collective-permute-start.71 = (bf16[64,1408]{1,0:T(8,128)(2,1)S(1)}, bf16[64,1408]{1,0:T(8,128)(2,1)S(1)}, u32[]{:S(2)}, u32[]{:S(2)}) collective-permute-start(bf16[64,1408]{1,0:T(8,128)(2,1)S(1)} %get-tuple-element.356), channel_id=1, source_target_pairs={{0,8},{1,9},{2,10},{3,11},{4,12},{5,13},{6,14},{7,15},{8,0},{9,1},... | collective-permute-start | bytes 540680 | tf_op jit(solution)/shard_map/ppermute | solution.py:1028
  401.5 12.7 %collective-permute-start.72 = (bf16[64,1408]{1,0:T(8,128)(2,1)S(1)}, bf16[64,1408]{1,0:T(8,128)(2,1)S(1)}, u32[]{:S(2)}, u32[]{:S(2)}) collective-permute-start(bf16[64,1408]{1,0:T(8,128)(2,1)S(1)} %get-tuple-element.358), channel_id=1, source_target_pairs={{0,4},{1,5},{2,6},{3,7},{4,0},{5,1},{6,2},{7,3},{8,12},{9,13},{10,... | collective-permute-start | bytes 540680 | tf_op jit(solution)/shard_map/ppermute | solution.py:1028
  401.5 12.7 %collective-permute-start.73 = (bf16[64,1408]{1,0:T(8,128)(2,1)S(1)}, bf16[64,1408]{1,0:T(8,128)(2,1)S(1)}, u32[]{:S(2)}, u32[]{:S(2)}) collective-permute-start(bf16[64,1408]{1,0:T(8,128)(2,1)S(1)} %get-tuple-element.357), channel_id=1, source_target_pairs={{0,12},{1,13},{2,14},{3,15},{4,8},{5,9},{6,10},{7,11},{8,4},{9,5},... | collective-permute-start | bytes 540680 | tf_op jit(solution)/shard_map/ppermute | solution.py:1028
  407.6 19.8 %collective-permute-start.62 = (bf16[256,1024]{1,0:T(8,128)(2,1)S(1)}, bf16[256,1024]{1,0:T(8,128)(2,1)S(1)}, u32[]{:S(2)}, u32[]{:S(2)}) collective-permute-start(bf16[256,1024]{1,0:T(8,128)(2,1)S(1)} %copy-done.43), channel_id=1, source_target_pairs={{0,8},{1,9},{2,10},{3,11},{4,12},{5,13},{6,14},{7,15},{8,0},{9,1},... | collective-permute-start | bytes 1572872 | tf_op jit(solution)/shard_map/ppermute | solution.py:1028
  411.5 7.4 %collective-permute-start.67 = (f32[7,2304]{1,0:T(8,128)S(1)}, f32[7,2304]{1,0:T(8,128)S(1)}, u32[]{:S(2)}, u32[]{:S(2)}) collective-permute-start(f32[7,2304]{1,0:T(8,128)S(1)} %add.292), channel_id=1, source_target_pairs={{0,4},{1,5},{2,6},{3,7},{4,0},{5,1},{6,2},{7,3},{8,12},{9,13},{10,... | collective-permute-start | bytes 193544 | tf_op jit(solution)/shard_map/ppermute | solution.py:1028
  414.4 21.4 %collective-permute-start.74 = (bf16[2,64,1408]{2,1,0:T(8,128)(2,1)S(1)}, bf16[2,64,1408]{2,1,0:T(8,128)(2,1)S(1)}, u32[]{:S(2)}, u32[]{:S(2)}) collective-permute-start(bf16[2,64,1408]{2,1,0:T(8,128)(2,1)S(1)} %pad_maximum_fusion.5.refs_1_), channel_id=1, source_target_pairs={{16,0},{17,1},{18,2},{19,3},{20,4},{21,5},{22,6},{23,7},{24,8},{25... | collective-permute-start | bytes 1081352 | tf_op jit(solution)/shard_map/ppermute | solution.py:1028
  (66 other events, 447.6 us)
Sparse Core Ops, SparseCore 0:
  72.2 53.8 all-gather.2

commit v4 on v3

--- a/solution.py
+++ b/solution.py
@@ -47,6 +47,14 @@
     return jnp.concatenate([hi, lo], axis=1)
 
 
+def sums(choice, x):
+    first = x.astype(BF)
+    rest = x - first.astype(F32)
+    second = rest.astype(BF)
+    third = (rest - second.astype(F32)).astype(BF)
+    return nn(choice, first) + nn(choice, second) + nn(choice, third)
+
+
 def iota(shape, dim):
     return lax.broadcasted_iota(jnp.int32, shape, dim)
 
@@ -60,7 +68,7 @@
 
 
 def sigmoid(x):
-    return 1.0 / (1.0 + jnp.exp(-x))
+    return 0.5 * jnp.tanh(0.5 * x) + 0.5
 
 
 def softplus(x):
@@ -275,8 +283,8 @@
 
 def block_terms(raw, dtb, rate_sign, offset):
     rate = softplus(raw + dtb)
-    lower = (iota((BLOCK, BLOCK), 1) <= iota((BLOCK, BLOCK), 0)).astype(F32)
-    level = nn(lower, rate * rate_sign, HIGH)
+    lower = (iota((BLOCK, BLOCK), 1) <= iota((BLOCK, BLOCK), 0)).astype(BF)
+    level = sums(lower, rate * rate_sign)
     local = iota((BLOCK, 1), 0)
     end = level[BLOCK - 1 :]
     end_offset = offset[BLOCK - 1 :]
@@ -650,8 +658,8 @@
     last = jnp.sum(tail_flow, axis=0, keepdims=True) + dcarry * carry
     dlevel = jnp.concatenate(level_sums, axis=0).T - rate * drate + dhead * head - tail_flow
     dlevel = dlevel + jnp.where(local == BLOCK - 1, last, 0.0)
-    upper = (iota((BLOCK, BLOCK), 0) <= iota((BLOCK, BLOCK), 1)).astype(F32)
-    dsum = nn(upper, dlevel, HIGH)
+    upper = (iota((BLOCK, BLOCK), 0) <= iota((BLOCK, BLOCK), 1)).astype(BF)
+    dsum = sums(upper, dlevel)
     drate = drate + dtail * fade + sign * dsum
     draw = drate * sigmoid(raw + dtb)
     r.gheads[0:1] += jnp.sum(draw, axis=0, keepdims=True)
@@ -1046,9 +1054,8 @@
         pieces = [self.along(near, k) for k in range(1, self.half)]
         return near, pieces, self.along(far, self.half)
 
-    def collect(self, reached, mark, late):
+    def collect(self, reached, late):
         near, pieces, came = reached
-        came = after(came, mark)
         more = [self.along(came, k) for k in range(1, self.half)]
         mine = jnp.concatenate([near] + pieces + [came] + [after(piece, late) for piece in more], axis=0)
         return mine, self.swap(mine)
@@ -1083,10 +1090,11 @@
 
         return self.send(value, route)
 
-    def gather_chips(self, value, share):
+    def gather_chips(self, value, share, *marks):
         pieces = [value[:share]]
         for k in range(1, self.seq):
-            pieces.append(self.along(value[k * share : (k + 1) * share], k))
+            piece = self.along(value[k * share : (k + 1) * share], k)
+            pieces.append(after(piece, *marks))
         half = self.half
         terms = [add(pieces[k], pieces[k + half]) for k in range(half)]
         if half == 2:
@@ -1193,16 +1201,16 @@
         whole = whole.reshape(8 * half_part, D)
         return jnp.pad(cut(whole, width * rank, width, 0), ((0, wide - width), (0, 0)))
 
-    def out_weights(part):
+    def out_weights(part, *marks):
         if half == 2:
             low_shard = plan.w // 2
 
             def route(c, z, w):
                 return (c, z, w ^ 2) if w // 2 == z % half else None
 
-            came = plan.send(part, route)
+            came = after(plan.send(part, route), *marks[:1])
             here = jnp.where(low_shard == plan.place, part, came)
-            beside = plan.send(here, lambda c, z, w: (c, z, w ^ 1))
+            beside = after(plan.send(here, lambda c, z, w: (c, z, w ^ 1)), *marks[1:])
             same = plan.w % 2 == core
             mine = jnp.where(same, here, beside)
             theirs = plan.swap(jnp.where(same, beside, here))
@@ -1213,11 +1221,11 @@
         return plan.reach(pick(part, plan.batch), pick(part, 1 - plan.batch))
 
     w_first, in_near, in_far = in_weights(chunk_parts[0])
-    started = plan.collect(reach(end_parts[0]), in_far, in_far)
+    near, pieces, came = reach(end_parts[0])
+    started = plan.collect((near, pieces, after(came, in_far)), in_far)
     w_out_first = out_weights(after(out_parts[0], in_near))
     w_second = later_in_weights(after(chunk_parts[1], in_far))
-    w_out_second = out_weights(after(out_parts[1], w_out_first))
-    weights = [(w_first, w_out_first), (w_second, w_out_second)]
+    weights = [(w_first, w_out_first)]
 
     tokens = place(orders, started)
 
@@ -1295,13 +1303,18 @@
 
     reached = reach(after(end_parts[1], *started))
     done = pass_on(0, 0, spot, None, None)
-    mark = done.rows
+    near, pieces, came = reached
+    came = after(came, done.rows)
+    done.away = after(done.away, came)
     rows_low = plan.chip_total(done.rows)
     folded = plan.fold(done)
+    mark = done.rows
     done = pass_on(0, 1, after(spot, folded, rows_low), None, None)
+    w_out_second = out_weights(after(out_parts[1], w_out_first), mark, done.rows)
+    weights.append((w_second, w_out_second))
     rows_summed[0].append(plan.total(rows_low, done.rows))
     summed[0].append(plan.reduce(folded, done.rows))
-    cotangent = place(orders, plan.collect(reached, mark, done.rows))
+    cotangent = place(orders, plan.collect((near, pieces, came), done.rows))
     folded = plan.fold(done)
     rows_summed[0].append(plan.total(plan.chip_total(done.rows)))
     turn = after(spot, folded, rows_summed[0][1])
@@ -1396,7 +1409,7 @@
     ungate_part(1, 0, spot)
     ungate_part(1, 1, spot)
     folded = scan_part(1, 1, spot)
-    last_sums = plan.reduce(last_fold, scans[1][1].gskip)
+    last_sums = plan.reduce(last_fold, scans[1][1].gskip, gated[1][0].ggated)
     upper = folded
     folded = scan_part(1, 0, after(spot, folded, *last_sums))
     mark = scans[1][0].gskip
@@ -1428,12 +1441,12 @@
     start_grad = finish_part(N.grad, 1, after(spot, later_last), None)
     folded = scan_part(0, 0, after(spot, start_grad.own, result_far))
     mark = scans[0][0].gskip
-    chips_later = plan.gather_chips(later_last[:, : gate_span + rest_span], share)
+    outs_later = homed(later_last[:, gate_span + rest_span :], 1)
+    rest_terms = weight_grads(after(spot, mark, folded), normed_of(0), (rests_of(0),), seq)
+    chips_later = plan.gather_chips(
+        later_last[:, : gate_span + rest_span], share, rest_terms.away
+    )
     came_later = plan.swap(chips_later, (0,))
-    outs_later = homed(later_last[:, gate_span + rest_span :], 1)
-    rest_terms = weight_grads(
-        after(spot, mark, chips_later, outs_later, folded), normed_of(0), (rests_of(0),), seq
-    )
     rest_came = first_hop(rest_terms)
     grads_summed[0][0] = plan.reduce(folded, rest_terms.away)
     gate_pair = first_add(gate_terms, after(gate_came, mark))

time: 452 us -> 436 us (0.965)
  Pallas kernels: 211 us -> 204 us
  waiting for transfers between devices: 71.4 us -> 64.5 us
    ppermute x78, waiting for transfers between devices: 71.4 us -> 64.5 us  [send(): return lax.ppermute(value, AXES, pairs)]
    pallas_call x28, Pallas kernels: 211 us -> 204 us  [launch(): pl.pallas_call(kernel, grid=grid, in_specs=[item[2] for item in ins], out...]
  transfers between devices with their start and end apart: 79 -> 79, of which waited for: 22 -> 21; matrix products, arithmetic and copies ran while one was open for 12% -> 13% of each run, Pallas kernels for 43% -> 46%
where the time goes in v4:
time: 436 us; the launch traced here: 431 us
  Pallas kernels  204 us (47%)
  starting transfers between devices  85.2 us (20%)
  waiting for transfers between devices  64.5 us (15%)
  other arithmetic  35.6 us (8%)
  local copies, waits for them, and re-layouts  25.8 us (6%)
  between operations  15.6 us (4%)
    pallas_call x28, Pallas kernels, launch(): pl.pallas_call(kernel, grid=grid, in_specs=[item[2] for item in ins], out...  204 us
    ppermute x78, starting transfers between devices, send(): return lax.ppermute(value, AXES, pairs)  85.2 us
    ppermute x78, waiting for transfers between devices, send(): return lax.ppermute(value, AXES, pairs)  64.5 us
    convert_element_type x22, other arithmetic, add(): return (first.astype(F32) + second.astype(F32)).astype(BF)  10.2 us
  transfers between devices with their start and end apart: 79, of which 21 were waited for; matrix products, arithmetic and copies ran while one was open for 13% of the time, Pallas kernels for 46%

profile of v4, /device:TPU:0, one launch (start us, length us, event | category | flops | bytes accessed | tf_op | source)
XLA Modules:
  0.0 430.9 jit_solution(9744942816759993402)
XLA Ops:
  7.9 2.9 prepare_in.1
  11.4 3.0 prepare_rest.1
  22.7 2.9 collective-permute-start.4
  30.7 7.4 %collective-permute-done.4.refs_2_ = bf16[2560,128]{1,0:T(8,128)(2,1)} collective-permute-done((bf16[2560,128]{1,0:T(8,128)(2,1)S(1)}, bf16[2560,128]{1,0:T(8,128)(2,1)}, u32[]{:S(2)}, u32[]{:S(2)}) %collective-permute-start.4) | collective-permute-done | bytes 655392 | tf_op jit(solution)/shard_map/ppermute | solution.py:1036
  38.1 5.7 %collective-permute-start.13 = (bf16[256,1024]{1,0:T(8,128)(2,1)S(1)}, bf16[256,1024]{1,0:T(8,128)(2,1)S(1)}, u32[]{:S(2)}, u32[]{:S(2)}) collective-permute-start(bf16[256,1024]{1,0:T(8,128)(2,1)S(1)} %get-tuple-element.188), channel_id=1, source_target_pairs={{0,2},{1,3},{6,4},{7,5},{8,10},{9,11},{14,12},{15,13},{16,18},{17,... | collective-permute-start | bytes 1572872 | tf_op jit(solution)/shard_map/ppermute | solution.py:1036
  44.1 2.5 collective-permute-start.2
  47.9 3.2 collective-permute-done.13
  51.2 2.5 collective-permute-start.14
  53.7 2.5 collective-permute-start.1
  56.3 2.0 collective-permute-done.5.refs_4_
  58.3 2.4 collective-permute-start.6
  60.8 6.2 %collective-permute-done.6 = bf16[128,1024]{1,0:T(8,128)(2,1)S(1)} collective-permute-done((bf16[128,1024]{1,0:T(8,128)(2,1)S(1)}, bf16[128,1024]{1,0:T(8,128)(2,1)S(1)}, u32[]{:S(2)}, u32[]{:S(2)}) %collective-permute-start.6) | collective-permute-done | bytes 262176 | tf_op jit(solution)/shard_map/ppermute | solution.py:1036
  71.9 4.6 %assemble.2.refs_3_.refs_1_ = bf16[1408,1024]{1,0:T(8,128)(2,1)} custom-call(s32[8]{0:T(128)} %stack.73.refs_0_, bf16[2560,128]{1,0:T(8,128)(2,1)} %copy-done.2, bf16[2560,128]{1,0:T(8,128)(2,1)} %collective-permute-done.4.refs_2_, bf16[2560,128]{1,0:T(8,128)(2,1)} %copy-done.9, bf16[2560,128]{1,0:T(8,128)(2,1)} %copy-done.27, ...), custom_call_target="tpu_custom_call" | custom-call | flops 5175000064 | bytes 1 | tf_op jit(solution)/shard_map/assemble/pallas_call | solution.py:96
  78.8 2.6 collective-permute-start.23
  81.5 2.2 collective-permute-start.16
  83.7 5.3 %place.2.refs_1_.refs_6_ = bf16[1024,1024]{1,0:T(8,128)(2,1)} custom-call(s32[1,512]{1,0:T(1,128)} %get-tuple-element.395.refs_0_, s32[1,512]{1,0:T(1,128)} %get-tuple-element.394.refs_1_, bf16[512,1024]{1,0:T(8,128)(2,1)} %pad_maximum_fusion.refs_2_, bf16[512,1024]{1,0:T(8,128)(2,1)} %collective-permute-done.7.refs_3_), custom_call_target="tpu_custom_call" | custom-call | flops 6095000064 | bytes 1 | tf_op jit(solution)/shard_map/place/pallas_call | solution.py:96
  89.0 11.6 %forward.4 = (bf16[512,1024]{1,0:T(8,128)(2,1)}, f32[512,512]{1,0:T(8,128)}, f32[512,768]{1,0:T(8,128)}, bf16[512,768]{1,0:T(8,128)(2,1)}, bf16[512,128]{1,0:T(8...) custom-call(s32[8]{0:T(128)} %stack.73.refs_0_, ...), custom_call_target="tpu_custom_call" | custom-call | flops 14375000064 | bytes 1 | tf_op jit(solution)/shard_map/forward/pallas_call | solution.py:96
  106.4 2.0 collective-permute-start.28
  108.5 2.4 collective-permute-start.24
  112.2 2.1 collective-permute-start.26
  114.2 11.7 %forward.5 = (bf16[512,1024]{1,0:T(8,128)(2,1)}, f32[512,512]{1,0:T(8,128)}, f32[512,768]{1,0:T(8,128)}, bf16[512,768]{1,0:T(8,128)(2,1)}, bf16[512,128]{1,0:T(8...) custom-call(s32[8]{0:T(128)} %stack.73.refs_0_, ...), custom_call_target="tpu_custom_call" | custom-call | flops 14375000064 | bytes 1 | tf_op jit(solution)/shard_map/forward/pallas_call | solution.py:96
  126.6 2.3 collective-permute-done.24
  129.0 1.6 collective-permute-start.21
  136.8 1.6 collective-permute-start.33
  140.6 5.3 %place.3.refs_14_.refs_18_.refs_6_.refs_8_.refs_10_.refs_12_ = bf16[1024,1024]{1,0:T(8,128)(2,1)} custom-call(s32[1,512]{1,0:T(1,128)} %get-tuple-element.395.refs_0_, s32[1,512]{1,0:T(1,128)} %get-tuple-element.394.refs_1_, bf16[512,1024]{1,0:T(8,128)(2,1)} %copy-done.7, bf16[512,1024]{1,0:T(8,128)(2,1)} %collective-permute-done.31.refs_3_), custom_call_target="tpu_custom_call" | custom-call | flops 6095000064 | bytes 1 | tf_op jit(solution)/shard_map/place/pallas_call | solution.py:96
  146.0 5.0 %assemble.3.refs_3_.refs_1_ = bf16[1408,1024]{1,0:T(8,128)(2,1)} custom-call(s32[8]{0:T(128)} %stack.73.refs_0_, bf16[4,2560,128]{2,1,0:T(8,128)(2,1)} %bitcast.97, bf16[4,1408,128]{2,1,0:T(8,128)(2,1)} %collective-permute-done.22.refs_2_), custom_call_target="tpu_custom_call" | custom-call | flops 5175000064 | bytes 1 | tf_op jit(solution)/shard_map/assemble/pallas_call | solution.py:96
  151.7 13.6 %forward.6 = (bf16[512,1024]{1,0:T(8,128)(2,1)}, f32[512,512]{1,0:T(8,128)}, f32[512,768]{1,0:T(8,128)}, bf16[512,768]{1,0:T(8,128)(2,1)}, bf16[512,128]{1,0:T(8...) custom-call(s32[8]{0:T(128)} %stack.73.refs_0_, ...), custom_call_target="tpu_custom_call" | custom-call | flops 14375000064 | bytes 1 | tf_op jit(solution)/shard_map/forward/pallas_call | solution.py:96
  169.7 13.7 %forward.7 = (bf16[512,1024]{1,0:T(8,128)(2,1)}, f32[512,512]{1,0:T(8,128)}, f32[512,768]{1,0:T(8,128)}, bf16[512,768]{1,0:T(8,128)(2,1)}, bf16[512,128]{1,0:T(8...) custom-call(s32[8]{0:T(128)} %stack.73.refs_0_, ...), custom_call_target="tpu_custom_call", output_to_operand_aliasing={{10}: (13, {}), {11}: (14, {})} | custom-call | flops 14375000064 | bytes 1 | tf_op jit(solution)/shard_map/forward/pallas_call | solution.py:96
  187.5 4.3 ungate.5
  192.4 4.4 %ungate.4 = (bf16[512,512]{1,0:T(8,128)(2,1)}, bf16[512,512]{1,0:T(8,128)(2,1)}, bf16[512,512]{1,0:T(8,128)(2,1)}, f32[1,512]{1,0:T(1,128)}) custom-call(s32[8]{0:T(128)} %stack.73.refs_0_, f32[2,2,256]{2,1,0:T(2,128)} %add.271.refs_1_.refs_6_, f32[512,512]{1,0:T(8,128)} %get-tuple-element.226.refs_2_, bf16[512,512]{1,0:T(8,128)(2,1)} %get-tuple-element.227.refs_3_, ...), custom_call_target="tpu_custom_call" | custom-call | flops 6325000192 | bytes 1 | tf_op jit(solution)/shard_map/ungate/pallas_call | solution.py:96
  197.8 14.1 %backward.4 = (bf16[256,1024]{1,0:T(8,128)(2,1)}, bf16[256,1024]{1,0:T(8,128)(2,1)}, bf16[512,896]{1,0:T(8,128)(2,1)}, f32[8,768]{1,0:T(8,128)}, f32[8,128]{1,0:...) custom-call(s32[8]{0:T(128)} %stack.73.refs_0_, ...), custom_call_target="tpu_custom_call" | custom-call | flops 16675000320 | bytes 1 | tf_op jit(solution)/shard_map/backward/pallas_call | solution.py:96
  212.0 10.1 %collective-permute-done.39 = bf16[512,1024]{1,0:T(8,128)(2,1)S(1)} collective-permute-done((bf16[512,1024]{1,0:T(8,128)(2,1)S(1)}, bf16[512,1024]{1,0:T(8,128)(2,1)S(1)}, u32[]{:S(2)}, u32[]{:S(2)}) %collective-permute-start.39) | collective-permute-done | bytes 1048608 | tf_op jit(solution)/shard_map/ppermute | solution.py:1036
  227.0 14.3 %backward.5 = (bf16[256,1024]{1,0:T(8,128)(2,1)}, bf16[256,1024]{1,0:T(8,128)(2,1)}, bf16[512,896]{1,0:T(8,128)(2,1)}, f32[8,768]{1,0:T(8,128)}, f32[8,128]{1,0:...) custom-call(s32[8]{0:T(128)} %stack.73.refs_0_, ...), custom_call_target="tpu_custom_call" | custom-call | flops 16675000320 | bytes 1 | tf_op jit(solution)/shard_map/backward/pallas_call | solution.py:96
  242.2 4.0 finish.4
  246.2 4.7 %finish.5 = (bf16[256,1024]{1,0:T(8,128)(2,1)}, bf16[256,1024]{1,0:T(8,128)(2,1)}) custom-call(s32[8]{0:T(128)} %stack.73.refs_0_, s32[256,1]{1,0:T(8,128)} %copy.59.refs_1_, s32[256,1]{1,0:T(8,128)} %copy.60.refs_2_, bf16[512,1024]{1,0:T(8,128)(2,1)} %copy-done.4, bf16[512,1024]{1,0:T(8,128)(2,1)} %copy-done.42, ...), custom_call_target="tpu_custom_call" | custom-call | flops 5750000128 | bytes 1 | tf_op jit(solution)/shard_map/finish/pallas_call | solution.py:96
  251.1 1.6 collective-permute-start.46
  252.6 10.0 %weight_grads.3 = (bf16[2,256,1920]{2,1,0:T(8,128)(2,1)}, bf16[2,256,1920]{2,1,0:T(8,128)(2,1)}) custom-call(s32[8]{0:T(128)} %stack.73.refs_0_, bf16[512,1024]{1,0:T(8,128)(2,1)} %get-tuple-element.243.refs_13_.refs_1_, bf16[512,1024]{1,0:T(8,128)(2,1)} %get-tuple-element.225.refs_13_.refs_2_, bf16[512,512]{1,0:T(8,128)(2,1)} %get-tuple-element.245.refs_15_.refs_3_, ...), custom_call_target="tpu_custom_call" | custom-call | flops 12650000384 | bytes 1 | tf_op jit(solution)/shard_map/weight_grads/pallas_call | solution.py:96
  263.1 2.0 collective-permute-done.46
  266.3 7.0 %ungate.6 = (bf16[512,512]{1,0:T(8,128)(2,1)}, bf16[512,512]{1,0:T(8,128)(2,1)}, bf16[512,512]{1,0:T(8,128)(2,1)}, f32[1,512]{1,0:T(1,128)}, bf16[512,1024]{1,0:T(8,128)(2,1)}) custom-call(s32[8]{0:T(128)} %stack.73.refs_0_, f32[2,2,256]{2,1,0:T(2,128)} %add.263.refs_17_.refs_1_, f32[512,512]{1,0:T(8,128)} %get-tuple-element.264.refs_2_, ...), custom_call_target="tpu_custom_call" | custom-call | flops 6325000192 | bytes 1 | tf_op jit(solution)/shard_map/ungate/pallas_call | solution.py:96
  273.3 14.1 %backward.6 = (bf16[256,1024]{1,0:T(8,128)(2,1)}, bf16[256,1024]{1,0:T(8,128)(2,1)}, bf16[512,896]{1,0:T(8,128)(2,1)}, f32[8,768]{1,0:T(8,128)}, f32[8,128]{1,0:...) custom-call(s32[8]{0:T(128)} %stack.73.refs_0_, ...), custom_call_target="tpu_custom_call" | custom-call | flops 16675000320 | bytes 1 | tf_op jit(solution)/shard_map/backward/pallas_call | solution.py:96
  287.9 1.6 collective-permute-start.52
  290.9 1.6 collective-permute-start.50
  295.5 6.9 %ungate.7 = (bf16[512,512]{1,0:T(8,128)(2,1)}, bf16[512,512]{1,0:T(8,128)(2,1)}, bf16[512,512]{1,0:T(8,128)(2,1)}, f32[1,512]{1,0:T(1,128)}, bf16[512,1024]{1,0:T(8,128)(2,1)}) custom-call(s32[8]{0:T(128)} %stack.73.refs_0_, f32[2,2,256]{2,1,0:T(2,128)} %add.265.refs_13_.refs_1_, f32[512,512]{1,0:T(8,128)} %get-tuple-element.282.refs_2_, ...), custom_call_target="tpu_custom_call" | custom-call | flops 6325000192 | bytes 1 | tf_op jit(solution)/shard_map/ungate/pallas_call | solution.py:96
  302.4 6.6 %weight_grads.4 = (bf16[2,256,1024]{2,1,0:T(8,128)(2,1)}, bf16[2,256,1024]{2,1,0:T(8,128)(2,1)}) custom-call(s32[8]{0:T(128)} %stack.73.refs_0_, bf16[512,1024]{1,0:T(8,128)(2,1)} %get-tuple-element.286.refs_1_.refs_13_, bf16[512,1024]{1,0:T(8,128)(2,1)} %get-tuple-element.274.refs_13_.refs_2_, bf16[512,512]{1,0:T(8,128)(2,1)} %get-tuple-element.287.refs_3_.refs_15_, ...), custom_call_target="tpu_custom_call" | custom-call | flops 6899999744 | bytes 1 | tf_op jit(solution)/shard_map/weight_grads/pallas_call | solution.py:96
  309.8 1.8 collective-permute-start.51
  311.6 1.6 fusion
  313.3 2.0 collective-permute-start.76
  316.8 4.7 %finish.6 = (bf16[256,1024]{1,0:T(8,128)(2,1)}, bf16[256,1024]{1,0:T(8,128)(2,1)}) custom-call(s32[8]{0:T(128)} %stack.73.refs_0_, s32[256,1]{1,0:T(8,128)} %copy.59.refs_1_, s32[256,1]{1,0:T(8,128)} %copy.60.refs_2_, bf16[256,1024]{1,0:T(8,128)(2,1)} %copy-done.21, bf16[256,1024]{1,0:T(8,128)(2,1)} %copy-done.50, ...), custom_call_target="tpu_custom_call" | custom-call | flops 5750000128 | bytes 1 | tf_op jit(solution)/shard_map/finish/pallas_call | solution.py:96
  321.5 14.0 %backward.7 = (bf16[256,1024]{1,0:T(8,128)(2,1)}, bf16[256,1024]{1,0:T(8,128)(2,1)}, bf16[512,896]{1,0:T(8,128)(2,1)}, f32[8,768]{1,0:T(8,128)}, f32[8,128]{1,0:...) custom-call(s32[8]{0:T(128)} %stack.73.refs_0_, ...), custom_call_target="tpu_custom_call" | custom-call | flops 16675000320 | bytes 1 | tf_op jit(solution)/shard_map/backward/pallas_call | solution.py:96
  337.3 5.3 %collective-permute-start.70 = (bf16[64,1408]{1,0:T(8,128)(2,1)}, bf16[64,1408]{1,0:T(8,128)(2,1)}, u32[]{:S(2)}, u32[]{:S(2)}) collective-permute-start(bf16[64,1408]{1,0:T(8,128)(2,1)} %get-tuple-element.365), channel_id=1, source_target_pairs={{0,8},{1,9},{2,10},{3,11},{4,12},{5,13},{6,14},{7,15},{8,0},{9,1},... | collective-permute-start | bytes 540680 | tf_op jit(solution)/shard_map/ppermute | solution.py:1036
  347.4 5.8 %weight_grads.5 = (bf16[2,256,896]{2,1,0:T(8,128)(2,1)}, bf16[2,256,896]{2,1,0:T(8,128)(2,1)}) custom-call(s32[8]{0:T(128)} %stack.73.refs_0_, bf16[512,1024]{1,0:T(8,128)(2,1)} %get-tuple-element.286.refs_1_.refs_13_, bf16[512,1024]{1,0:T(8,128)(2,1)} %get-tuple-element.274.refs_13_.refs_2_, bf16[512,896]{1,0:T(8,128)(2,1)} %get-tuple-element.310.refs_3_, ...), custom_call_target="tpu_custom_call" | custom-call | flops 6899999744 | bytes 1 | tf_op jit(solution)/shard_map/weight_grads/pallas_call | solution.py:96
  353.9 3.8 collective-permute-done.71
  357.6 2.2 pack.1
  361.9 3.1 collective-permute-start.73
  372.8 5.0 %finish.7 = (bf16[256,1024]{1,0:T(8,128)(2,1)}, bf16[256,1024]{1,0:T(8,128)(2,1)}) custom-call(s32[8]{0:T(128)} %stack.73.refs_0_, s32[256,1]{1,0:T(8,128)} %copy.59.refs_1_, s32[256,1]{1,0:T(8,128)} %copy.60.refs_2_, bf16[256,1024]{1,0:T(8,128)(2,1)} %copy-done.20, bf16[256,1024]{1,0:T(8,128)(2,1)} %copy-done.49, ...), custom_call_target="tpu_custom_call" | custom-call | flops 5750000128 | bytes 1 | tf_op jit(solution)/shard_map/finish/pallas_call | solution.py:96
  380.5 2.4 collective-permute-start.66
  382.9 2.0 collective-permute-start.68
  387.4 2.0 collective-permute-done.61
  389.5 3.3 collective-permute-start.57
  394.3 2.6 collective-permute-done.67
  398.4 3.6 collective-permute-done.62
  402.0 10.3 %collective-permute-done.57.refs_2_ = bf16[256,1024]{1,0:T(8,128)(2,1)S(1)} collective-permute-done((bf16[256,1024]{1,0:T(8,128)(2,1)S(1)}, bf16[256,1024]{1,0:T(8,128)(2,1)S(1)}, u32[]{:S(2)}, u32[]{:S(2)}) %collective-permute-start.57) | collective-permute-done | bytes 524320 | tf_op jit(solution)/shard_map/ppermute | solution.py:1036
  413.0 3.0 settle.1
  421.4 2.4 gather_columns.1
  (355 shorter events, 96.5 us)
Async XLA Ops:
  7.2 126.0 %all-gather.3.cloned.1.call-start = ((), (), s32[]{:S(2)}) async-start(), calls=%async_computation | async-start | bytes 3276800 | tf_op jit(solution)/shard_map/all_gather | solution.py:1190
  10.9 10.8 %collective-permute-start.3 = (bf16[2560,128]{1,0:T(8,128)(2,1)}, bf16[2560,128]{1,0:T(8,128)(2,1)S(1)}, u32[]{:S(2)}, u32[]{:S(2)}) collective-permute-start(bf16[2560,128]{1,0:T(8,128)(2,1)} %get-tuple-element.179), channel_id=1, source_target_pairs={{0,16},{1,17},{2,18},{3,19},{4,20},{5,21},{6,22},{7,23},{8,24},{9,... | collective-permute-start | bytes 1966088 | tf_op jit(solution)/shard_map/ppermute | solution.py:1036
  14.5 15.0 %collective-permute-start.12 = (bf16[256,1024]{1,0:T(8,128)(2,1)}, bf16[256,1024]{1,0:T(8,128)(2,1)}, u32[]{:S(2)}, u32[]{:S(2)}) collective-permute-start(bf16[256,1024]{1,0:T(8,128)(2,1)} %get-tuple-element.187), channel_id=1, source_target_pairs={{0,16},{1,17},{2,18},{3,19},{4,20},{5,21},{6,22},{7,23},{8,24},{9,... | collective-permute-start | bytes 1572872 | tf_op jit(solution)/shard_map/ppermute | solution.py:1036
  14.5 29.3 %collective-permute-start = (bf16[2,128,1024]{2,1,0:T(8,128)(2,1)}, bf16[2,128,1024]{2,1,0:T(8,128)(2,1)S(1)}, u32[]{:S(2)}, u32[]{:S(2)}) collective-permute-start(bf16[2,128,1024]{2,1,0:T(8,128)(2,1)} %get-tuple-element.182), channel_id=1, source_target_pairs={{0,16},{1,17},{2,18},{3,19},{4,20},{5,21},{6,22},{7,23},{8,24},{9,... | collective-permute-start | bytes 1572872 | tf_op jit(solution)/shard_map/ppermute | solution.py:1036
  22.7 15.4 %collective-permute-start.4 = (bf16[2560,128]{1,0:T(8,128)(2,1)S(1)}, bf16[2560,128]{1,0:T(8,128)(2,1)}, u32[]{:S(2)}, u32[]{:S(2)}) collective-permute-start(bf16[2560,128]{1,0:T(8,128)(2,1)S(1)} %get-tuple-element.358.refs_1_), channel_id=1, source_target_pairs={{0,1},{1,0},{2,3},{3,2},{4,5},{5,4},{6,7},{7,6},{8,9},{9,8},{10,11... | collective-permute-start | bytes 1966088 | tf_op jit(solution)/shard_map/ppermute | solution.py:1036
  27.9 18.6 %collective-permute-start.9 = (bf16[2560,128]{1,0:T(8,128)(2,1)S(1)}, bf16[2560,128]{1,0:T(8,128)(2,1)S(1)}, u32[]{:S(2)}, u32[]{:S(2)}) collective-permute-start(bf16[2560,128]{1,0:T(8,128)(2,1)S(1)} %get-tuple-element.358.refs_1_), channel_id=1, source_target_pairs={{0,2},{1,3},{2,0},{3,1},{4,6},{5,7},{6,4},{7,5},{8,10},{9,11},{10,... | collective-permute-start | bytes 1966088 | tf_op jit(solution)/shard_map/ppermute | solution.py:1036
  38.1 13.0 %collective-permute-start.13 = (bf16[256,1024]{1,0:T(8,128)(2,1)S(1)}, bf16[256,1024]{1,0:T(8,128)(2,1)S(1)}, u32[]{:S(2)}, u32[]{:S(2)}) collective-permute-start(bf16[256,1024]{1,0:T(8,128)(2,1)S(1)} %get-tuple-element.188), channel_id=1, source_target_pairs={{0,2},{1,3},{6,4},{7,5},{8,10},{9,11},{14,12},{15,13},{16,18},{17,... | collective-permute-start | bytes 1572872 | tf_op jit(solution)/shard_map/ppermute | solution.py:1036
  43.9 14.3 %collective-permute-start.5 = (bf16[2560,128]{1,0:T(8,128)(2,1)}, bf16[2560,128]{1,0:T(8,128)(2,1)S(1)}, u32[]{:S(2)}, u32[]{:S(2)}) collective-permute-start(bf16[2560,128]{1,0:T(8,128)(2,1)} %collective-permute-done.4.refs_2_), channel_id=1, source_target_pairs={{0,2},{1,3},{2,0},{3,1},{4,6},{5,7},{6,4},{7,5},{8,10},{9,11},{10,... | collective-permute-start | bytes 1966088 | tf_op jit(solution)/shard_map/ppermute | solution.py:1036
  44.1 12.2 %collective-permute-start.2 = (bf16[128,1024]{1,0:T(8,128)(2,1)S(1)}, bf16[128,1024]{1,0:T(8,128)(2,1)S(1)}, u32[]{:S(2)}, u32[]{:S(2)}) collective-permute-start(bf16[128,1024]{1,0:T(8,128)(2,1)S(1)} %get-tuple-element.376), channel_id=1, source_target_pairs={{0,8},{1,9},{2,10},{3,11},{4,12},{5,13},{6,14},{7,15},{8,0},{9,1},... | collective-permute-start | bytes 786440 | tf_op jit(solution)/shard_map/ppermute | solution.py:1036
  47.9 24.1 %collective-permute-start.10 = (bf16[3,1408,128]{2,1,0:T(8,128)(2,1)S(1)}, bf16[3,1408,128]{2,1,0:T(8,128)(2,1)}, u32[]{:S(2)}, u32[]{:S(2)}) collective-permute-start(bf16[3,1408,128]{2,1,0:T(8,128)(2,1)S(1)} %fusion.2), channel_id=1, source_target_pairs={{0,16},{1,17},{2,18},{3,19},{4,20},{5,21},{6,22},{7,23},{8,24},{9,... | collective-permute-start | bytes 3244040 | tf_op jit(solution)/shard_map/ppermute | solution.py:1036
  51.2 16.9 %collective-permute-start.14 = (bf16[256,1024]{1,0:T(8,128)(2,1)S(1)}, bf16[256,1024]{1,0:T(8,128)(2,1)S(1)}, u32[]{:S(2)}, u32[]{:S(2)}) collective-permute-start(bf16[256,1024]{1,0:T(8,128)(2,1)S(1)} %broadcast_select_fusion.3), channel_id=1, source_target_pairs={{0,1},{1,0},{2,3},{3,2},{4,5},{5,4},{6,7},{7,6},{8,9},{9,8},{10,11... | collective-permute-start | bytes 1572872 | tf_op jit(solution)/shard_map/ppermute | solution.py:1036
  53.7 13.3 %collective-permute-start.1 = (bf16[128,1024]{1,0:T(8,128)(2,1)S(1)}, bf16[128,1024]{1,0:T(8,128)(2,1)S(1)}, u32[]{:S(2)}, u32[]{:S(2)}) collective-permute-start(bf16[128,1024]{1,0:T(8,128)(2,1)S(1)} %get-tuple-element.375), channel_id=1, source_target_pairs={{0,4},{1,5},{2,6},{3,7},{4,0},{5,1},{6,2},{7,3},{8,12},{9,13},{10,... | collective-permute-start | bytes 786440 | tf_op jit(solution)/shard_map/ppermute | solution.py:1036
  58.3 8.8 %collective-permute-start.6 = (bf16[128,1024]{1,0:T(8,128)(2,1)S(1)}, bf16[128,1024]{1,0:T(8,128)(2,1)S(1)}, u32[]{:S(2)}, u32[]{:S(2)}) collective-permute-start(bf16[128,1024]{1,0:T(8,128)(2,1)S(1)} %collective-permute-done.2), channel_id=1, source_target_pairs={{0,4},{1,5},{2,6},{3,7},{4,0},{5,1},{6,2},{7,3},{8,12},{9,13},{10,... | collective-permute-start | bytes 786440 | tf_op jit(solution)/shard_map/ppermute | solution.py:1036
  60.7 11.2 %collective-permute-start.11 = (bf16[1408,128]{1,0:T(8,128)(2,1)S(1)}, bf16[1408,128]{1,0:T(8,128)(2,1)}, u32[]{:S(2)}, u32[]{:S(2)}) collective-permute-start(bf16[1408,128]{1,0:T(8,128)(2,1)S(1)} %constant_dynamic-slice_fusion.4), channel_id=1, source_target_pairs={{0,16},{1,17},{2,18},{3,19},{4,20},{5,21},{6,22},{7,23},{8,24},{9,... | collective-permute-start | bytes 1081352 | tf_op jit(solution)/shard_map/ppermute | solution.py:1036
  68.1 13.4 %collective-permute-start.7 = (bf16[512,1024]{1,0:T(8,128)(2,1)}, bf16[512,1024]{1,0:T(8,128)(2,1)}, u32[]{:S(2)}, u32[]{:S(2)}) collective-permute-start(bf16[512,1024]{1,0:T(8,128)(2,1)} %pad_maximum_fusion.refs_2_), channel_id=1, source_target_pairs={{0,16},{1,17},{2,18},{3,19},{4,20},{5,21},{6,22},{7,23},{8,24},{9,... | collective-permute-start | bytes 3145736 | tf_op jit(solution)/shard_map/ppermute | solution.py:1036
  69.0 7.6 %collective-permute-start.15 = (bf16[256,1024]{1,0:T(8,128)(2,1)}, bf16[256,1024]{1,0:T(8,128)(2,1)}, u32[]{:S(2)}, u32[]{:S(2)}) collective-permute-start(bf16[256,1024]{1,0:T(8,128)(2,1)} %broadcast_select_fusion.6), channel_id=1, source_target_pairs={{0,16},{1,17},{2,18},{3,19},{4,20},{5,21},{6,22},{7,23},{8,24},{9,... | collective-permute-start | bytes 1572872 | tf_op jit(solution)/shard_map/ppermute | solution.py:1036
  78.8 29.7 %collective-permute-start.23 = (bf16[256,1024]{1,0:T(8,128)(2,1)S(1)}, bf16[256,1024]{1,0:T(8,128)(2,1)S(1)}, u32[]{:S(2)}, u32[]{:S(2)}) collective-permute-start(bf16[256,1024]{1,0:T(8,128)(2,1)S(1)} %get-tuple-element.203), channel_id=1, source_target_pairs={{0,2},{1,3},{6,4},{7,5},{8,10},{9,11},{14,12},{15,13},{16,18},{17,... | collective-permute-start | bytes 1572872 | tf_op jit(solution)/shard_map/ppermute | solution.py:1036
  81.5 19.1 %collective-permute-start.16 = (bf16[128,1024]{1,0:T(8,128)(2,1)S(1)}, bf16[128,1024]{1,0:T(8,128)(2,1)S(1)}, u32[]{:S(2)}, u32[]{:S(2)}) collective-permute-start(bf16[128,1024]{1,0:T(8,128)(2,1)S(1)} %get-tuple-element.374), channel_id=1, source_target_pairs={{0,8},{1,9},{2,10},{3,11},{4,12},{5,13},{6,14},{7,15},{8,0},{9,1},... | collective-permute-start | bytes 786440 | tf_op jit(solution)/shard_map/ppermute | solution.py:1036
  100.6 10.3 %collective-permute-start.17 = (bf16[256,1024]{1,0:T(8,128)(2,1)}, bf16[256,1024]{1,0:T(8,128)(2,1)S(1)}, u32[]{:S(2)}, u32[]{:S(2)}) collective-permute-start(bf16[256,1024]{1,0:T(8,128)(2,1)} %get-tuple-element.194), channel_id=1, source_target_pairs={{0,16},{1,17},{2,18},{3,19},{4,20},{5,21},{6,22},{7,23},{8,24},{9,... | collective-permute-start | bytes 1572872 | tf_op jit(solution)/shard_map/ppermute | solution.py:1036
  105.7 20.3 %collective-permute-start.29 = (bf16[128,1024]{1,0:T(8,128)(2,1)S(1)}, bf16[128,1024]{1,0:T(8,128)(2,1)S(1)}, u32[]{:S(2)}, u32[]{:S(2)}) collective-permute-start(bf16[128,1024]{1,0:T(8,128)(2,1)S(1)} %get-tuple-element.373), channel_id=1, source_target_pairs={{0,4},{1,5},{2,6},{3,7},{4,0},{5,1},{6,2},{7,3},{8,12},{9,13},{10,... | collective-permute-start | bytes 786440 | tf_op jit(solution)/shard_map/ppermute | solution.py:1036
  106.4 24.9 %collective-permute-start.28 = (f32[2,2,256]{2,1,0:T(2,128)S(1)}, f32[2,2,256]{2,1,0:T(2,128)S(1)}, u32[]{:S(2)}, u32[]{:S(2)}) collective-permute-start(f32[2,2,256]{2,1,0:T(2,128)S(1)} %add.260), channel_id=1, source_target_pairs={{0,4},{1,5},{2,6},{3,7},{4,0},{5,1},{6,2},{7,3},{8,12},{9,13},{10,... | collective-permute-start | bytes 12296 | tf_op jit(solution)/shard_map/ppermute | solution.py:1036
  108.5 20.4 %collective-permute-start.24 = (bf16[256,1024]{1,0:T(8,128)(2,1)S(1)}, bf16[256,1024]{1,0:T(8,128)(2,1)S(1)}, u32[]{:S(2)}, u32[]{:S(2)}) collective-permute-start(bf16[256,1024]{1,0:T(8,128)(2,1)S(1)} %broadcast_select_fusion.2), channel_id=1, source_target_pairs={{0,1},{1,0},{2,3},{3,2},{4,5},{5,4},{6,7},{7,6},{8,9},{9,8},{10,11... | collective-permute-start | bytes 1572872 | tf_op jit(solution)/shard_map/ppermute | solution.py:1036
  110.9 15.0 %collective-permute-start.30 = (bf16[128,1024]{1,0:T(8,128)(2,1)S(1)}, bf16[128,1024]{1,0:T(8,128)(2,1)S(1)}, u32[]{:S(2)}, u32[]{:S(2)}) collective-permute-start(bf16[128,1024]{1,0:T(8,128)(2,1)S(1)} %collective-permute-done.16), channel_id=1, source_target_pairs={{0,4},{1,5},{2,6},{3,7},{4,0},{5,1},{6,2},{7,3},{8,12},{9,13},{10,... | collective-permute-start | bytes 786440 | tf_op jit(solution)/shard_map/ppermute | solution.py:1036
  112.2 21.1 %collective-permute-start.26 = (bf16[256,1024]{1,0:T(8,128)(2,1)S(1)}, bf16[256,1024]{1,0:T(8,128)(2,1)S(1)}, u32[]{:S(2)}, u32[]{:S(2)}) collective-permute-start(bf16[256,1024]{1,0:T(8,128)(2,1)S(1)} %add_convert_fusion.17), channel_id=1, source_target_pairs={{0,4},{1,5},{2,6},{3,7},{4,0},{5,1},{6,2},{7,3},{8,12},{9,13},{10,... | collective-permute-start | bytes 1572872 | tf_op jit(solution)/shard_map/ppermute | solution.py:1036
  126.1 14.6 %collective-permute-start.31 = (bf16[512,1024]{1,0:T(8,128)(2,1)S(1)}, bf16[512,1024]{1,0:T(8,128)(2,1)}, u32[]{:S(2)}, u32[]{:S(2)}) collective-permute-start(bf16[512,1024]{1,0:T(8,128)(2,1)S(1)} %pad_maximum_fusion.3.refs_2_), channel_id=1, source_target_pairs={{0,16},{1,17},{2,18},{3,19},{4,20},{5,21},{6,22},{7,23},{8,24},{9,... | collective-permute-start | bytes 3145736 | tf_op jit(solution)/shard_map/ppermute | solution.py:1036
  132.0 6.4 %collective-permute-start.25 = (bf16[256,1024]{1,0:T(8,128)(2,1)}, bf16[256,1024]{1,0:T(8,128)(2,1)}, u32[]{:S(2)}, u32[]{:S(2)}) collective-permute-start(bf16[256,1024]{1,0:T(8,128)(2,1)} %broadcast_select_fusion.4), channel_id=1, source_target_pairs={{0,16},{1,17},{2,18},{3,19},{4,20},{5,21},{6,22},{7,23},{8,24},{9,... | collective-permute-start | bytes 1572872 | tf_op jit(solution)/shard_map/ppermute | solution.py:1036
  134.8 11.2 %collective-permute-start.22 = (bf16[4,1408,128]{2,1,0:T(8,128)(2,1)S(1)}, bf16[4,1408,128]{2,1,0:T(8,128)(2,1)}, u32[]{:S(2)}, u32[]{:S(2)}) collective-permute-start(bf16[4,1408,128]{2,1,0:T(8,128)(2,1)S(1)} %constant_dynamic-slice_fusion.1), channel_id=1, source_target_pairs={{0,16},{1,17},{2,18},{3,19},{4,20},{5,21},{6,22},{7,23},{8,24},{9,... | collective-permute-start | bytes 4325384 | tf_op jit(solution)/shard_map/ppermute | solution.py:1036
  135.1 15.9 %collective-permute-start.27 = (bf16[256,1024]{1,0:T(8,128)(2,1)S(1)}, bf16[256,1024]{1,0:T(8,128)(2,1)S(1)}, u32[]{:S(2)}, u32[]{:S(2)}) collective-permute-start(bf16[256,1024]{1,0:T(8,128)(2,1)S(1)} %add_convert_fusion.15.refs_11_.refs_8_), channel_id=1, source_target_pairs={{0,16},{1,17},{2,18},{3,19},{4,20},{5,21},{6,22},{7,23},{8,24},{9,... | collective-permute-start | bytes 1572872 | tf_op jit(solution)/shard_map/ppermute | solution.py:1036
  136.8 28.5 %collective-permute-start.33 = (bf16[256,1024]{1,0:T(8,128)(2,1)S(1)}, bf16[256,1024]{1,0:T(8,128)(2,1)S(1)}, u32[]{:S(2)}, u32[]{:S(2)}) collective-permute-start(bf16[256,1024]{1,0:T(8,128)(2,1)S(1)} %add_convert_fusion.16), channel_id=1, source_target_pairs={{0,4},{1,5},{2,6},{3,7},{4,0},{5,1},{6,2},{7,3},{8,12},{9,13},{10,... | collective-permute-start | bytes 1572872 | tf_op jit(solution)/shard_map/ppermute | solution.py:1036
  168.4 15.9 %collective-permute-start.36 = (f32[2,2,256]{2,1,0:T(2,128)S(1)}, f32[2,2,256]{2,1,0:T(2,128)S(1)}, u32[]{:S(2)}, u32[]{:S(2)}) collective-permute-start(f32[2,2,256]{2,1,0:T(2,128)S(1)} %add.266), channel_id=1, source_target_pairs={{0,4},{1,5},{2,6},{3,7},{4,0},{5,1},{6,2},{7,3},{8,12},{9,13},{10,... | collective-permute-start | bytes 12296 | tf_op jit(solution)/shard_map/ppermute | solution.py:1036
  184.8 12.0 %collective-permute-start.35 = (bf16[512,1024]{1,0:T(8,128)(2,1)}, bf16[512,1024]{1,0:T(8,128)(2,1)S(1)}, u32[]{:S(2)}, u32[]{:S(2)}) collective-permute-start(bf16[512,1024]{1,0:T(8,128)(2,1)} %get-tuple-element.217), channel_id=1, source_target_pairs={{0,16},{1,17},{2,18},{3,19},{4,20},{5,21},{6,22},{7,23},{8,24},{9,... | collective-permute-start | bytes 3145736 | tf_op jit(solution)/shard_map/ppermute | solution.py:1036
  186.0 5.8 %collective-permute-start.38 = (f32[2,2,256]{2,1,0:T(2,128)S(1)}, f32[2,2,256]{2,1,0:T(2,128)S(1)}, u32[]{:S(2)}, u32[]{:S(2)}) collective-permute-start(f32[2,2,256]{2,1,0:T(2,128)S(1)} %add.270), channel_id=1, source_target_pairs={{0,4},{1,5},{2,6},{3,7},{4,0},{5,1},{6,2},{7,3},{8,12},{9,13},{10,... | collective-permute-start | bytes 12296 | tf_op jit(solution)/shard_map/ppermute | solution.py:1036
  197.2 24.9 %collective-permute-start.39 = (bf16[512,1024]{1,0:T(8,128)(2,1)S(1)}, bf16[512,1024]{1,0:T(8,128)(2,1)S(1)}, u32[]{:S(2)}, u32[]{:S(2)}) collective-permute-start(bf16[512,1024]{1,0:T(8,128)(2,1)S(1)} %add_convert_fusion.1), channel_id=1, source_target_pairs={{0,4},{1,5},{2,6},{3,7},{4,0},{5,1},{6,2},{7,3},{8,12},{9,13},{10,... | collective-permute-start | bytes 3145736 | tf_op jit(solution)/shard_map/ppermute | solution.py:1036
  226.4 15.0 %collective-permute-start.44 = (bf16[256,1024]{1,0:T(8,128)(2,1)S(1)}, bf16[256,1024]{1,0:T(8,128)(2,1)S(1)}, u32[]{:S(2)}, u32[]{:S(2)}) collective-permute-start(bf16[256,1024]{1,0:T(8,128)(2,1)S(1)} %add_convert_fusion.13), channel_id=1, source_target_pairs={{0,4},{1,5},{2,6},{3,7},{4,0},{5,1},{6,2},{7,3},{8,12},{9,13},{10,... | collective-permute-start | bytes 1572872 | tf_op jit(solution)/shard_map/ppermute | solution.py:1036
  241.3 9.5 %collective-permute-start.42 = (bf16[256,1024]{1,0:T(8,128)(2,1)}, bf16[256,1024]{1,0:T(8,128)(2,1)S(1)}, u32[]{:S(2)}, u32[]{:S(2)}) collective-permute-start(bf16[256,1024]{1,0:T(8,128)(2,1)} %get-tuple-element.255), channel_id=1, source_target_pairs={{0,16},{1,17},{2,18},{3,19},{4,20},{5,21},{6,22},{7,23},{8,24},{9,... | collective-permute-start | bytes 1572872 | tf_op jit(solution)/shard_map/ppermute | solution.py:1036
  241.6 23.7 %collective-permute-start.45 = (bf16[256,1024]{1,0:T(8,128)(2,1)S(1)}, bf16[256,1024]{1,0:T(8,128)(2,1)S(1)}, u32[]{:S(2)}, u32[]{:S(2)}) collective-permute-start(bf16[256,1024]{1,0:T(8,128)(2,1)S(1)} %add_convert_fusion.11.refs_6_), channel_id=1, source_target_pairs={{0,16},{1,17},{2,18},{3,19},{4,20},{5,21},{6,22},{7,23},{8,24},{9,... | collective-permute-start | bytes 1572872 | tf_op jit(solution)/shard_map/ppermute | solution.py:1036
  251.1 14.0 %collective-permute-start.46 = (bf16[256,1024]{1,0:T(8,128)(2,1)S(1)}, bf16[256,1024]{1,0:T(8,128)(2,1)S(1)}, u32[]{:S(2)}, u32[]{:S(2)}) collective-permute-start(bf16[256,1024]{1,0:T(8,128)(2,1)S(1)} %add_convert_fusion.12), channel_id=1, source_target_pairs={{0,4},{1,5},{2,6},{3,7},{4,0},{5,1},{6,2},{7,3},{8,12},{9,13},{10,... | collective-permute-start | bytes 1572872 | tf_op jit(solution)/shard_map/ppermute | solution.py:1036
  262.6 29.9 %collective-permute-start.43 = (bf16[2,256,1920]{2,1,0:T(8,128)(2,1)}, bf16[2,256,1920]{2,1,0:T(8,128)(2,1)}, u32[]{:S(2)}, u32[]{:S(2)}) collective-permute-start(bf16[2,256,1920]{2,1,0:T(8,128)(2,1)} %get-tuple-element.262), channel_id=1, source_target_pairs={{0,1},{1,0},{2,3},{3,2},{4,5},{5,4},{6,7},{7,6},{8,9},{9,8},{10,11... | collective-permute-start | bytes 5898248 | tf_op jit(solution)/shard_map/ppermute | solution.py:1036
  265.3 8.0 %collective-permute-start.47 = (bf16[256,1024]{1,0:T(8,128)(2,1)S(1)}, bf16[256,1024]{1,0:T(8,128)(2,1)S(1)}, u32[]{:S(2)}, u32[]{:S(2)}) collective-permute-start(bf16[256,1024]{1,0:T(8,128)(2,1)S(1)} %add_convert_fusion.10.refs_6_), channel_id=1, source_target_pairs={{0,16},{1,17},{2,18},{3,19},{4,20},{5,21},{6,22},{7,23},{8,24},{9,... | collective-permute-start | bytes 1572872 | tf_op jit(solution)/shard_map/ppermute | solution.py:1036
  287.9 33.6 %collective-permute-start.52 = (bf16[256,1024]{1,0:T(8,128)(2,1)}, bf16[256,1024]{1,0:T(8,128)(2,1)}, u32[]{:S(2)}, u32[]{:S(2)}) collective-permute-start(bf16[256,1024]{1,0:T(8,128)(2,1)} %get-tuple-element.297), channel_id=1, source_target_pairs={{16,24},{17,25},{18,26},{19,27},{20,28},{21,29},{22,30},{23,31},{2... | collective-permute-start | bytes 1572872 | tf_op jit(solution)/shard_map/ppermute | solution.py:1036
  290.9 18.7 %collective-permute-start.50 = (bf16[256,1024]{1,0:T(8,128)(2,1)S(1)}, bf16[256,1024]{1,0:T(8,128)(2,1)S(1)}, u32[]{:S(2)}, u32[]{:S(2)}) collective-permute-start(bf16[256,1024]{1,0:T(8,128)(2,1)S(1)} %add_convert_fusion.9), channel_id=1, source_target_pairs={{0,4},{1,5},{2,6},{3,7},{4,0},{5,1},{6,2},{7,3},{8,12},{9,13},{10,... | collective-permute-start | bytes 1572872 | tf_op jit(solution)/shard_map/ppermute | solution.py:1036
  294.0 17.6 %collective-permute-start.48 = (bf16[256,1920]{1,0:T(8,128)(2,1)S(1)}, bf16[256,1920]{1,0:T(8,128)(2,1)S(1)}, u32[]{:S(2)}, u32[]{:S(2)}) collective-permute-start(bf16[256,1920]{1,0:T(8,128)(2,1)S(1)} %fusion.5), channel_id=1, source_target_pairs={{0,2},{1,3},{2,0},{3,1},{4,6},{5,7},{6,4},{7,5},{8,10},{9,11},{10,... | collective-permute-start | bytes 2949128 | tf_op jit(solution)/shard_map/ppermute | solution.py:1036
  309.0 33.5 %collective-permute-start.64 = (bf16[2,256,1024]{2,1,0:T(8,128)(2,1)}, bf16[2,256,1024]{2,1,0:T(8,128)(2,1)S(1)}, u32[]{:S(2)}, u32[]{:S(2)}) collective-permute-start(bf16[2,256,1024]{2,1,0:T(8,128)(2,1)} %get-tuple-element.292), channel_id=1, source_target_pairs={{0,1},{1,0},{2,3},{3,2},{4,5},{5,4},{6,7},{7,6},{8,9},{9,8},{10,11... | collective-permute-start | bytes 3145736 | tf_op jit(solution)/shard_map/ppermute | solution.py:1036
  309.8 6.2 %collective-permute-start.51 = (bf16[256,1024]{1,0:T(8,128)(2,1)S(1)}, bf16[256,1024]{1,0:T(8,128)(2,1)S(1)}, u32[]{:S(2)}, u32[]{:S(2)}) collective-permute-start(bf16[256,1024]{1,0:T(8,128)(2,1)S(1)} %add_convert_fusion.8.refs_3_), channel_id=1, source_target_pairs={{0,16},{1,17},{2,18},{3,19},{4,20},{5,21},{6,22},{7,23},{8,24},{9,... | collective-permute-start | bytes 1572872 | tf_op jit(solution)/shard_map/ppermute | solution.py:1036
  313.3 29.5 %collective-permute-start.76 = (bf16[256,512]{1,0:T(8,128)(2,1)S(1)}, bf16[256,512]{1,0:T(8,128)(2,1)S(1)}, u32[]{:S(2)}, u32[]{:S(2)}) collective-permute-start(bf16[256,512]{1,0:T(8,128)(2,1)S(1)} %slice.236), channel_id=1, source_target_pairs={{0,16},{1,17},{2,18},{3,19},{4,24},{5,25},{6,26},{7,27},{16,20},{1... | collective-permute-start | bytes 786440 | tf_op jit(solution)/shard_map/ppermute | solution.py:1036
  315.3 29.0 %collective-permute-start.77 = (bf16[256,512]{1,0:T(8,128)(2,1)S(1)}, bf16[256,512]{1,0:T(8,128)(2,1)S(1)}, u32[]{:S(2)}, u32[]{:S(2)}) collective-permute-start(bf16[256,512]{1,0:T(8,128)(2,1)S(1)} %slice.236), channel_id=1, source_target_pairs={{8,16},{9,17},{10,18},{11,19},{12,24},{13,25},{14,26},{15,27},{24,... | collective-permute-start | bytes 786440 | tf_op jit(solution)/shard_map/ppermute | solution.py:1036
  335.5 11.0 %collective-permute-start.53 = (bf16[256,1024]{1,0:T(8,128)(2,1)}, bf16[256,1024]{1,0:T(8,128)(2,1)S(1)}, u32[]{:S(2)}, u32[]{:S(2)}) collective-permute-start(bf16[256,1024]{1,0:T(8,128)(2,1)} %get-tuple-element.308), channel_id=1, source_target_pairs={{0,16},{1,17},{2,18},{3,19},{4,20},{5,21},{6,22},{7,23},{8,24},{9,... | collective-permute-start | bytes 1572872 | tf_op jit(solution)/shard_map/ppermute | solution.py:1036
  337.3 16.0 %collective-permute-start.70 = (bf16[64,1408]{1,0:T(8,128)(2,1)}, bf16[64,1408]{1,0:T(8,128)(2,1)}, u32[]{:S(2)}, u32[]{:S(2)}) collective-permute-start(bf16[64,1408]{1,0:T(8,128)(2,1)} %get-tuple-element.365), channel_id=1, source_target_pairs={{0,8},{1,9},{2,10},{3,11},{4,12},{5,13},{6,14},{7,15},{8,0},{9,1},... | collective-permute-start | bytes 540680 | tf_op jit(solution)/shard_map/ppermute | solution.py:1036
  342.5 15.1 %collective-permute-start.71 = (bf16[64,1408]{1,0:T(8,128)(2,1)}, bf16[64,1408]{1,0:T(8,128)(2,1)}, u32[]{:S(2)}, u32[]{:S(2)}) collective-permute-start(bf16[64,1408]{1,0:T(8,128)(2,1)} %get-tuple-element.367), channel_id=1, source_target_pairs={{0,4},{1,5},{2,6},{3,7},{4,0},{5,1},{6,2},{7,3},{8,12},{9,13},{10,... | collective-permute-start | bytes 540680 | tf_op jit(solution)/shard_map/ppermute | solution.py:1036
  342.7 14.9 %collective-permute-start.72 = (bf16[64,1408]{1,0:T(8,128)(2,1)}, bf16[64,1408]{1,0:T(8,128)(2,1)}, u32[]{:S(2)}, u32[]{:S(2)}) collective-permute-start(bf16[64,1408]{1,0:T(8,128)(2,1)} %get-tuple-element.366), channel_id=1, source_target_pairs={{0,12},{1,13},{2,14},{3,15},{4,8},{5,9},{6,10},{7,11},{8,4},{9,5},... | collective-permute-start | bytes 540680 | tf_op jit(solution)/shard_map/ppermute | solution.py:1036
  344.3 22.1 %collective-permute-start.65 = (bf16[256,1024]{1,0:T(8,128)(2,1)S(1)}, bf16[256,1024]{1,0:T(8,128)(2,1)S(1)}, u32[]{:S(2)}, u32[]{:S(2)}) collective-permute-start(bf16[256,1024]{1,0:T(8,128)(2,1)S(1)} %fusion.8), channel_id=1, source_target_pairs={{0,2},{1,3},{2,0},{3,1},{4,6},{5,7},{6,4},{7,5},{8,10},{9,11},{10,... | collective-permute-start | bytes 1572872 | tf_op jit(solution)/shard_map/ppermute | solution.py:1036
  346.8 20.7 %collective-permute-start.55 = (bf16[256,1024]{1,0:T(8,128)(2,1)S(1)}, bf16[256,1024]{1,0:T(8,128)(2,1)S(1)}, u32[]{:S(2)}, u32[]{:S(2)}) collective-permute-start(bf16[256,1024]{1,0:T(8,128)(2,1)S(1)} %add_convert_fusion.7), channel_id=1, source_target_pairs={{0,4},{1,5},{2,6},{3,7},{4,0},{5,1},{6,2},{7,3},{8,12},{9,13},{10,... | collective-permute-start | bytes 1572872 | tf_op jit(solution)/shard_map/ppermute | solution.py:1036
  353.3 15.5 %collective-permute-start.54 = (bf16[2,256,896]{2,1,0:T(8,128)(2,1)}, bf16[2,256,896]{2,1,0:T(8,128)(2,1)S(1)}, u32[]{:S(2)}, u32[]{:S(2)}) collective-permute-start(bf16[2,256,896]{2,1,0:T(8,128)(2,1)} %get-tuple-element.313), channel_id=1, source_target_pairs={{0,1},{1,0},{2,3},{3,2},{4,5},{5,4},{6,7},{7,6},{8,9},{9,8},{10,11... | collective-permute-start | bytes 2752520 | tf_op jit(solution)/shard_map/ppermute | solution.py:1036
  361.9 58.7 %collective-permute-start.73 = (bf16[2,64,1408]{2,1,0:T(8,128)(2,1)}, bf16[2,64,1408]{2,1,0:T(8,128)(2,1)}, u32[]{:S(2)}, u32[]{:S(2)}) collective-permute-start(bf16[2,64,1408]{2,1,0:T(8,128)(2,1)} %pad_maximum_fusion.5.refs_4_), channel_id=1, source_target_pairs={{0,16},{1,17},{2,18},{3,19},{4,20},{5,21},{6,22},{7,23},{8,24},{9,... | collective-permute-start | bytes 1081352 | tf_op jit(solution)/shard_map/ppermute | solution.py:1036
  368.1 11.1 %collective-permute-start.74 = (bf16[256,512]{1,0:T(8,128)(2,1)S(1)}, bf16[256,512]{1,0:T(8,128)(2,1)S(1)}, u32[]{:S(2)}, u32[]{:S(2)}) collective-permute-start(bf16[256,512]{1,0:T(8,128)(2,1)S(1)} %get-tuple-element.371), channel_id=1, source_target_pairs={{0,0},{1,1},{2,2},{3,3},{4,8},{5,9},{6,10},{7,11},{16,4},{17,5},{1... | collective-permute-start | bytes 786440 | tf_op jit(solution)/shard_map/ppermute | solution.py:1036
  368.8 11.6 %collective-permute-start.75 = (bf16[256,512]{1,0:T(8,128)(2,1)S(1)}, bf16[256,512]{1,0:T(8,128)(2,1)S(1)}, u32[]{:S(2)}, u32[]{:S(2)}) collective-permute-start(bf16[256,512]{1,0:T(8,128)(2,1)S(1)} %get-tuple-element.371), channel_id=1, source_target_pairs={{8,0},{9,1},{10,2},{11,3},{12,8},{13,9},{14,10},{15,11},{24,4},{25... | collective-permute-start | bytes 786440 | tf_op jit(solution)/shard_map/ppermute | solution.py:1036
  370.5 8.5 %collective-permute-start.60 = (bf16[256,896]{1,0:T(8,128)(2,1)S(1)}, bf16[256,896]{1,0:T(8,128)(2,1)S(1)}, u32[]{:S(2)}, u32[]{:S(2)}) collective-permute-start(bf16[256,896]{1,0:T(8,128)(2,1)S(1)} %fusion.9), channel_id=1, source_target_pairs={{0,2},{1,3},{2,0},{3,1},{4,6},{5,7},{6,4},{7,5},{8,10},{9,11},{10,... | collective-permute-start | bytes 1376264 | tf_op jit(solution)/shard_map/ppermute | solution.py:1036
  380.5 13.8 %collective-permute-start.66 = (bf16[64,1408]{1,0:T(8,128)(2,1)S(1)}, bf16[64,1408]{1,0:T(8,128)(2,1)S(1)}, u32[]{:S(2)}, u32[]{:S(2)}) collective-permute-start(bf16[64,1408]{1,0:T(8,128)(2,1)S(1)} %get-tuple-element.368), channel_id=1, source_target_pairs={{0,8},{1,9},{2,10},{3,11},{4,12},{5,13},{6,14},{7,15},{8,0},{9,1},... | collective-permute-start | bytes 540680 | tf_op jit(solution)/shard_map/ppermute | solution.py:1036
  382.9 14.0 %collective-permute-start.67 = (bf16[64,1408]{1,0:T(8,128)(2,1)S(1)}, bf16[64,1408]{1,0:T(8,128)(2,1)S(1)}, u32[]{:S(2)}, u32[]{:S(2)}) collective-permute-start(bf16[64,1408]{1,0:T(8,128)(2,1)S(1)} %get-tuple-element.370), channel_id=1, source_target_pairs={{0,4},{1,5},{2,6},{3,7},{4,0},{5,1},{6,2},{7,3},{8,12},{9,13},{10,... | collective-permute-start | bytes 540680 | tf_op jit(solution)/shard_map/ppermute | solution.py:1036
  382.9 14.0 %collective-permute-start.68 = (bf16[64,1408]{1,0:T(8,128)(2,1)S(1)}, bf16[64,1408]{1,0:T(8,128)(2,1)S(1)}, u32[]{:S(2)}, u32[]{:S(2)}) collective-permute-start(bf16[64,1408]{1,0:T(8,128)(2,1)S(1)} %get-tuple-element.369), channel_id=1, source_target_pairs={{0,12},{1,13},{2,14},{3,15},{4,8},{5,9},{6,10},{7,11},{8,4},{9,5},... | collective-permute-start | bytes 540680 | tf_op jit(solution)/shard_map/ppermute | solution.py:1036
  389.5 22.8 %collective-permute-start.57 = (bf16[256,1024]{1,0:T(8,128)(2,1)S(1)}, bf16[256,1024]{1,0:T(8,128)(2,1)S(1)}, u32[]{:S(2)}, u32[]{:S(2)}) collective-permute-start(bf16[256,1024]{1,0:T(8,128)(2,1)S(1)} %copy-done.45), channel_id=1, source_target_pairs={{0,8},{1,9},{2,10},{3,11},{4,12},{5,13},{6,14},{7,15},{8,0},{9,1},... | collective-permute-start | bytes 1572872 | tf_op jit(solution)/shard_map/ppermute | solution.py:1036
  394.3 7.6 %collective-permute-start.62 = (f32[7,2304]{1,0:T(8,128)S(1)}, f32[7,2304]{1,0:T(8,128)S(1)}, u32[]{:S(2)}, u32[]{:S(2)}) collective-permute-start(f32[7,2304]{1,0:T(8,128)S(1)} %add.289), channel_id=1, source_target_pairs={{0,4},{1,5},{2,6},{3,7},{4,0},{5,1},{6,2},{7,3},{8,12},{9,13},{10,... | collective-permute-start | bytes 193544 | tf_op jit(solution)/shard_map/ppermute | solution.py:1036
  397.1 23.5 %collective-permute-start.69 = (bf16[2,64,1408]{2,1,0:T(8,128)(2,1)S(1)}, bf16[2,64,1408]{2,1,0:T(8,128)(2,1)S(1)}, u32[]{:S(2)}, u32[]{:S(2)}) collective-permute-start(bf16[2,64,1408]{2,1,0:T(8,128)(2,1)S(1)} %pad_maximum_fusion.4.refs_1_), channel_id=1, source_target_pairs={{16,0},{17,1},{18,2},{19,3},{20,4},{21,5},{22,6},{23,7},{24,8},{25... | collective-permute-start | bytes 1081352 | tf_op jit(solution)/shard_map/ppermute | solution.py:1036
  412.3 5.3 %collective-permute-start.63 = (f32[7,2304]{1,0:T(8,128)S(1)}, f32[7,2304]{1,0:T(8,128)S(1)}, u32[]{:S(2)}, u32[]{:S(2)}) collective-permute-start(f32[7,2304]{1,0:T(8,128)S(1)} %add.290), channel_id=1, source_target_pairs={{0,8},{1,9},{2,10},{3,11},{4,12},{5,13},{6,14},{7,15},{8,0},{9,1},... | collective-permute-start | bytes 193544 | tf_op jit(solution)/shard_map/ppermute | solution.py:1036
  (67 other events, 455.3 us)
Sparse Core Ops, SparseCore 0:
  72.0 52.2 all-gather.2
